TPU v7x, 256 devices: a whole 4x4x8 slice. The times are simulated.
256 devices in a mesh: dp: 16 (over y, x), group: 16 (over z, core).
Axes of the slice: x: 4, y: 4, z: 8, core: 2. Of those that a mesh axis runs over, the one named last changes fastest.
Arguments:
- layer_input: bfloat16 [65536, 1280], P(('dp', 'group')), may hold values from -6 to 6
- grad_packed: bfloat16 [65536, 1280], P(('dp', 'group')), may hold values from -6 to 6
- source_row: int32 [16, 4096], P('dp'), may hold values from 0 to 4095, each once within a row
- window_id: int32 [16, 4096], P('dp'), may hold values from 0 to 4095, as said below
- w_qkv: bfloat16 [3, 1280, 1280], P(None, None, 'group'), may hold values from -1 to 1
- gain: float32 [1280], replicated, may hold values from 0.25 to 1.75
Outputs:
- grad_input: bfloat16 [65536, 1280], P(('dp', 'group'))
- grad_weight: float32 [3, 1280, 1280], P(None, None, 'group')
- grad_gain: float32 [1280], replicated
Inputs may be any that keep to these rules, and one draw needn't show every extreme that they name: `source_row`: each batch's row is named once. `window_id`: window numbers never decrease along a batch's rows; each window is a run of consecutive rows inside one aligned block of 64 rows; the last window of every batch is numbered 4096 - 1.
All inputs are finite; a program needn't handle non-finite values.
Results may differ from a plain program's by a relative error of at most 0.018.
Values may be sent and summed in bfloat16 or wider, within the bound.
No kernel may reach another device: no remote copies, remote signals or barrier semaphores. Data moves between devices by JAX's collectives and lax.ppermute only.
A program may use at most 128 MiB of HBM per device.

v0:
```python
import jax
import jax.numpy as jnp
from jax import lax
from jax.sharding import PartitionSpec as P

HEADS = 16
WIN = 64


epsilon = 1e-06


def normalize(rows_in, gain):
    values = rows_in.astype(jnp.float32)
    inverse = lax.rsqrt(jnp.mean(values * values, axis=-1, keepdims=True) + epsilon)
    scaled = values * inverse
    normed = (scaled * gain).astype(jnp.bfloat16)
    return (scaled, inverse, normed)


def attention_grad(stacked, grad_out, windows, head_size):
    total_rows = stacked.shape[1]
    window_rows = WIN
    blocks = total_rows // window_rows
    local_heads = stacked.shape[2] // head_size
    shaped = stacked.reshape(3, blocks, window_rows, local_heads, head_size)
    query, keys, values = (shaped[0], shaped[1], shaped[2])
    upstream = grad_out.reshape(blocks, window_rows, local_heads, head_size)
    labels = windows.reshape(blocks, window_rows)
    same_window = labels[:, :, None] == labels[:, None, :]
    scaling = head_size ** (-0.5)
    scores = (
        jnp.einsum("bqhe,bkhe->bhqk", query, keys, preferred_element_type=jnp.float32) * scaling
    )
    scores = jnp.where(same_window[:, None], scores, -1e30)
    probs = jax.nn.softmax(scores, axis=-1)
    grad_probs = jnp.einsum("bqhe,bkhe->bhqk", upstream, values, preferred_element_type=jnp.float32)
    row_dot = jnp.sum(probs * grad_probs, axis=-1, keepdims=True)
    grad_scores = (probs * (grad_probs - row_dot)).astype(jnp.bfloat16)
    probs_low = probs.astype(jnp.bfloat16)
    grad_values = jnp.einsum(
        "bhqk,bqhe->bkhe", probs_low, upstream, preferred_element_type=jnp.float32
    )
    grad_query = (
        jnp.einsum("bhqk,bkhe->bqhe", grad_scores, keys, preferred_element_type=jnp.float32)
        * scaling
    )
    grad_keys = (
        jnp.einsum("bhqk,bqhe->bkhe", grad_scores, query, preferred_element_type=jnp.float32)
        * scaling
    )
    joined = jnp.stack(
        [
            grad_query.astype(jnp.bfloat16),
            grad_keys.astype(jnp.bfloat16),
            grad_values.astype(jnp.bfloat16),
        ]
    )
    return joined.reshape(3, total_rows, local_heads * head_size)


def on_device(layer_input, grad_packed, source_row, window_id, w_qkv, gain):
    width = layer_input.shape[1]
    head_size = width // HEADS
    scaled, inverse, normed = normalize(layer_input, gain)
    gathered = lax.all_gather(normed, "group", axis=0, tiled=True)
    projected = jnp.einsum(
        "rd,jde->jre", gathered, w_qkv, preferred_element_type=jnp.float32
    ).astype(jnp.bfloat16)
    head_grads = lax.all_to_all(grad_packed, "group", split_axis=1, concat_axis=0, tiled=True)
    grad_out = jnp.take(head_grads, source_row[0], axis=0)
    grad_qkv = attention_grad(projected, grad_out, window_id[0], head_size)
    weight_part = jnp.einsum("rd,jre->jde", gathered, grad_qkv, preferred_element_type=jnp.float32)
    grad_weight = lax.psum(weight_part.astype(jnp.bfloat16), "dp").astype(jnp.float32)
    returned = lax.all_to_all(grad_qkv, "group", split_axis=1, concat_axis=2, tiled=True)
    grad_normed = jnp.einsum(
        "jre,jde->rd",
        returned,
        lax.all_gather(w_qkv, "group", axis=2, tiled=True),
        preferred_element_type=jnp.float32,
    )
    grad_scaled = grad_normed * gain
    mixed = jnp.mean(grad_scaled * scaled, axis=-1, keepdims=True)
    grad_input = (inverse * (grad_scaled - scaled * mixed)).astype(jnp.bfloat16)
    grad_gain = lax.psum(jnp.sum(grad_normed * scaled, axis=0), ("dp", "group"))
    return (grad_input, grad_weight, grad_gain)


def solution(mesh):
    return jax.shard_map(
        on_device,
        mesh=mesh,
        in_specs=(
            P(("dp", "group"), None),
            P(("dp", "group"), None),
            P("dp", None),
            P("dp", None),
            P(None, None, "group"),
            P(),
        ),
        out_specs=(P(("dp", "group"), None), P(None, None, "group"), P()),
        check_vma=False,
    )
```

profile of v0, /device:TPU:2, one launch (start us, length us, event | category | flops | bytes accessed | tf_op | source)
XLA Modules:
  0.0 366.9 jit_solution(12103016686699925205)
XLA Ops:
  7.2 1.4 fusion.20
  8.6 2.2 fusion.14
  10.8 1.1 copy.48
  11.9 8.6 %all-to-all-start = ((bf16[256,16,80]{0,2,1:T(8,128)(2,1)}), bf16[256,16,80]{0,2,1:T(8,128)(2,1)S(1)}, u32[]{:S(2)}, u32[]{:S(2)}) async-start(bf16[256,16,80]{0,2,1:T(8,128)(2,1)} %bitcast.4), calls=%async_computation | async-start | bytes 1310720 | tf_op jit(solution)/shard_map/all_to_all | solution.py:70
  21.0 0.7 reduce.13
  21.8 0.7 reduce.12
  22.6 20.1 %all-to-all-done = bf16[256,16,80]{0,2,1:T(8,128)(2,1)S(1)} async-done(((bf16[256,16,80]{0,2,1:T(8,128)(2,1)}), bf16[256,16,80]{0,2,1:T(8,128)(2,1)S(1)}, u32[]{:S(2)}, u32[]{:S(2)}) %all-to-all-start) | async-done | bytes 655392 | tf_op jit(solution)/shard_map/all_to_all | solution.py:70
  43.4 15.0 %gather_fusion = bf16[4096,80]{1,0:T(8,128)(2,1)} fusion(bf16[4096,80]{1,0:T(8,128)(2,1)S(1)} %bitcast.60, s32[4096]{0:T(1024)S(1)} %broadcast_clamp_fusion), kind=kCustom, calls=%fused_computation | custom fusion | bytes 1327104 | tf_op jit(solution)/shard_map/jit(_take)/gather | solution.py:71
  58.4 31.3 %all-gather.3.cloned.1.call-done = bf16[4096,1280]{1,0:T(8,128)(2,1)} async-done(((bf16[256,1280]{1,0:T(8,128)(2,1)}), bf16[4096,1280]{1,0:T(8,128)(2,1)}) %all-gather.3.cloned.1.call-update) | async-done | bytes 10485776 | tf_op jit(solution)/shard_map/all_gather | solution.py:66
  89.8 5.6 %fusion.37 = f32[4096,240]{0,1:S(1)} fusion(bf16[4096,1280]{1,0:T(8,128)(2,1)} %all-gather.3.cloned.1.call-done, bf16[1280,240]{0,1:T(8,128)(2,1)S(1)} %bitcast.76), kind=kOutput, calls=%fused_computation.53 | convolution fusion | flops 2516582400 | bytes 15032320
  95.8 0.6 copy.66
  97.1 1.3 copy.63
  98.5 2.0 fusion.36
  100.5 2.6 multiply_reduce_fusion
  103.1 0.7 multiply_convert_fusion.2
  104.8 0.8 copy-done.4
  105.5 1.8 convolution_convert_fusion
  108.3 1.5 copy.56
  109.8 7.5 %fusion.6 = bf16[3,1280,80]{1,2,0:T(8,128)(2,1)} fusion(bf16[4096,1280]{1,0:T(8,128)(2,1)} %all-gather.3.cloned.1.call-done, bf16[1,4096,80]{1,2,0:T(8,128)(2,1)S(1)} %copy.56, bf16[1,4096,80]{1,2,0:T(8,128)(2,1)S(1)} %copy.55, bf16[1,4096,80]{1,2,0:T(8,128)(2,1)S(1)} %copy.54), kind=kOutput, calls=%fused_computation.6 | convolution fusion | flops 2518855680 | bytes 13066240 | tf_op jit(solution)/shard_map/rd,jre->jde/dot_general | solution.py:73
  117.4 0.7 all-gather.5.cloned.1.call-update
  118.1 1.3 pad_maximum_fusion
  119.4 4.7 %copy.57 = bf16[3,4096,80]{2,0,1:T(4,128)(2,1)} copy(bf16[3,4096,80]{1,2,0:T(8,128)(2,1)S(1)} %pad_maximum_fusion) | data formatting | bytes 3932160 | tf_op jit(solution)/shard_map/stack | solution.py:52
  124.1 8.9 %reshape.179 = bf16[16,2,30720]{2,1,0:T(2,128)(2,1)} reshape(bf16[4096,3,80]{2,1,0:T(4,128)(2,1)} %bitcast.61) | data formatting | bytes 3932160
  132.9 4.6 %all-to-all-start.1 = ((bf16[16,2,30720]{2,1,0:T(2,128)(2,1)}), bf16[16,2,30720]{2,1,0:T(2,128)(2,1)S(1)}, u32[]{:S(2)}, u32[]{:S(2)}) async-start(bf16[16,2,30720]{2,1,0:T(2,128)(2,1)} %reshape.179), calls=%async_computation.1 | async-start | bytes 3932160 | tf_op jit(solution)/shard_map/all_to_all | solution.py:75
  137.6 73.2 %all-reduce.2.cloned.1.call-done = bf16[3,1280,80]{1,2,0:T(8,128)(2,1)} async-done(((bf16[3,1280,80]{1,2,0:T(8,128)(2,1)}), bf16[3,1280,80]{1,2,0:T(8,128)(2,1)}) %all-reduce.2.cloned.1.call-update) | async-done | bytes 614416 | tf_op jit(solution)/shard_map/psum | solution.py:74
  210.8 2.2 convert_element_type.77
  213.0 7.5 %reshape.180 = bf16[4096,3,80]{2,1,0:T(4,128)(2,1)} reshape(bf16[16,2,30720]{2,1,0:T(2,128)(2,1)S(1)} %all-to-all-done.1) | data formatting | bytes 3932160
  220.5 5.7 %copy.65 = bf16[3,16,256,80]{2,3,1,0:T(8,128)(2,1)S(1)} copy(bf16[3,16,256,80]{3,0,2,1:T(4,128)(2,1)} %bitcast.62) | data formatting | bytes 3932160 | tf_op jit(solution)/shard_map/all_to_all | solution.py:75
  226.2 49.0 %all-gather.5.cloned.1.call-done = bf16[3,1280,1280]{1,2,0:T(8,128)(2,1)} async-done(((bf16[3,1280,80]{1,2,0:T(8,128)(2,1)}), bf16[3,1280,1280]{1,2,0:T(8,128)(2,1)}) %all-gather.5.cloned.1.call-update) | async-done | bytes 9830416 | tf_op jit(solution)/shard_map/all_gather | solution.py:79
  275.2 7.7 %fusion.19 = (f32[1280]{0:T(1024)S(1)}, f32[256]{0:T(256)S(1)}, f32[256,1280]{1,0:T(8,128)}) fusion(bf16[256,1280]{1,0:T(8,128)(2,1)S(1)} %copy-done, f32[256]{0:T(256)S(1)} %add_rsqrt_fusion, f32[1280]{0:T(1024)S(1)} %copy-done.7, bf16[3,256,1280]{1,2,0:T(8,128)(2,1)S(1)} %bitcast.63, bf16[3,1280,1280]{1,2,0:T(8,128)(2,1)} %all-gather.5.cloned.1.call-done), kind=kOutput, calls=%fused_computation.28 | convolution fusion | flops 2518874624 | bytes 13774848 | tf_op jit(solution)/shard_map/jre,jde->rd/dot_general | solution.py:76
  283.0 74.9 %psum.15 = f32[1280]{0:T(1024)} all-reduce(f32[1280]{0:T(1024)S(1)} %get-tuple-element.3), channel_id=1, replica_groups=mesh['dp'=16,'group'=16] {'dp','group'}, use_global_device_ids=true, to_apply=%region_7.8 | all-reduce | flops 1280 | bytes 10240 | tf_op jit(solution)/shard_map/psum | solution.py:85
  357.9 2.5 fusion.18
  (41 shorter events, 4.5 us)
Async XLA Ops:
  7.2 3.7 copy-start.5
  7.2 82.6 %all-gather.3.cloned.1.call-start = ((), (), s32[]{:S(2)}) async-start(), calls=%async_computation.2 | async-start | bytes 11141120 | tf_op jit(solution)/shard_map/all_gather | solution.py:66
  8.6 12.5 %copy-start.9 = (s32[1,4096]{1,0:T(1,128)S(1)}, s32[1,4096]{1,0:T(1,128)}, u32[]{:S(2)}) copy-start(s32[1,4096]{1,0:T(1,128)} %param.9) | copy-start | bytes 49156
  8.6 13.2 %copy-start.8 = (s32[1,4096]{1,0:T(1,128)S(1)}, s32[1,4096]{1,0:T(1,128)}, u32[]{:S(2)}) copy-start(s32[1,4096]{1,0:T(1,128)} %param.8) | copy-start | bytes 49156
  11.9 30.8 %all-to-all-start = ((bf16[256,16,80]{0,2,1:T(8,128)(2,1)}), bf16[256,16,80]{0,2,1:T(8,128)(2,1)S(1)}, u32[]{:S(2)}, u32[]{:S(2)}) async-start(bf16[256,16,80]{0,2,1:T(8,128)(2,1)} %bitcast.4), calls=%async_computation | async-start | bytes 1310720 | tf_op jit(solution)/shard_map/all_to_all | solution.py:70
  20.5 190.3 %all-reduce.2.cloned.1.call-start = ((), (), s32[]{:S(2)}) async-start(), calls=%async_computation.4 | async-start | bytes 1228800 | tf_op jit(solution)/shard_map/psum | solution.py:74
  43.4 46.4 %copy-start.6 = (bf16[3,1280,80]{1,2,0:T(8,128)(2,1)S(1)}, bf16[3,1280,80]{1,2,0:T(8,128)(2,1)}, u32[]{:S(2)}) copy-start(bf16[3,1280,80]{1,2,0:T(8,128)(2,1)} %param.10) | copy-start | bytes 1843204
  98.5 2.0 copy-start.3
  100.5 2.6 copy-start.2
  104.3 1.2 copy-start.4
  107.8 9.5 %copy-start.1 = (bf16[1,4096,80]{1,2,0:T(8,128)(2,1)}, bf16[1,4096,80]{1,2,0:T(8,128)(2,1)S(1)}, u32[]{:S(2)}) copy-start(bf16[1,4096,80]{1,2,0:T(8,128)(2,1)S(1)} %copy.54) | copy-start | bytes 1966084
  117.3 157.9 %all-gather.5.cloned.1.call-start = ((), (), s32[]{:S(2)}) async-start(), calls=%async_computation.3 | async-start | bytes 10444800 | tf_op jit(solution)/shard_map/all_gather | solution.py:79
  132.9 80.1 %all-to-all-start.1 = ((bf16[16,2,30720]{2,1,0:T(2,128)(2,1)}), bf16[16,2,30720]{2,1,0:T(2,128)(2,1)S(1)}, u32[]{:S(2)}, u32[]{:S(2)}) async-start(bf16[16,2,30720]{2,1,0:T(2,128)(2,1)} %reshape.179), calls=%async_computation.1 | async-start | bytes 3932160 | tf_op jit(solution)/shard_map/all_to_all | solution.py:75
  220.5 54.7 %copy-start = (bf16[256,1280]{1,0:T(8,128)(2,1)S(1)}, bf16[256,1280]{1,0:T(8,128)(2,1)}, u32[]{:S(2)}) copy-start(bf16[256,1280]{1,0:T(8,128)(2,1)} %param.6) | copy-start | bytes 1966084
  220.5 54.7 %copy-start.7 = (f32[1280]{0:T(1024)S(1)}, f32[1280]{0:T(1024)}, u32[]{:S(2)}) copy-start(f32[1280]{0:T(1024)} %param.11) | copy-start | bytes 15364
Sparse Core Ops, SparseCore 0:
  10.9 78.7 all-gather.2
  117.4 93.3 all-reduce.1
  212.7 62.4 all-gather.4
where the time goes:
time: 370 us; the launch traced here: 367 us
  waiting for transfers between devices  174 us (47%)
  blocking collectives  74.9 us (20%)
  local copies, waits for them, and re-layouts  50.2 us (14%)
  matrix products  28.2 us (8%)
  between operations  14 us (4%)
  starting transfers between devices  13.3 us (4%)
  other arithmetic  11.8 us (3%)
    psum x1, blocking collectives, on_device(): grad_gain = lax.psum(jnp.sum(grad_normed * scaled, axis=0), ('dp', 'group'))  74.9 us
    psum x1, waiting for transfers between devices, on_device(): lax.psum(weight_part.astype(jnp.bfloat16), 'dp').astype(jnp.float32)  73.2 us
    all_gather x1, waiting for transfers between devices, on_device(): lax.all_gather(w_qkv, 'group', axis=2, tiled=True)  49 us
    all_gather x1, waiting for transfers between devices, on_device(): gathered = lax.all_gather(normed, 'group', axis=0, tiled=True)  31.3 us
    all_to_all x1, waiting for transfers between devices, on_device(): lax.all_to_all(grad_packed, 'group', split_axis=1, concat_axis=0, tiled=T...  20.1 us
    unnamed x24, local copies, waits for them, and re-layouts  18.8 us
    gather x1, local copies, waits for them, and re-layouts, on_device(): grad_out = jnp.take(head_grads, source_row[0], axis=0)  15 us
    all_to_all x1, starting transfers between devices, on_device(): lax.all_to_all(grad_packed, 'group', split_axis=1, concat_axis=0, tiled=T...  8.57 us
  transfers between devices with their start and end apart: 5, of which 4 were waited for; matrix products, arithmetic and copies ran while one was open for 13% of the time, Pallas kernels for 0%

commit v1 on v0

v1 whole, which is shorter than its diff:
```python
import functools

import jax
import jax.numpy as jnp
from jax import lax
from jax.experimental import pallas as pl
from jax.experimental.pallas import tpu as pltpu
from jax.sharding import Mesh, PartitionSpec as P

HEAD = 80
HEADS = 16
SUPER = 128
CHUNK = 256
SLOTS = 4
RING = 4
LINES = 160
PADDED = 256
XOR_ORDER = (0, 2, 1, 3)
epsilon = 1e-06
bf16 = jnp.bfloat16
f32 = jnp.float32
NT = (((1,), (1,)), ((), ()))
TN = (((0,), (0,)), ((), ()))
NN = (((1,), (0,)), ((), ()))
BIG = 56 * 1024 * 1024


def dot(a, b, dims):
    return lax.dot_general(a, b, dims, preferred_element_type=f32)


def lanes(shape):
    return lax.broadcasted_iota(jnp.int32, shape, len(shape) - 1)


def roll(x, shift):
    shift = shift % x.shape[-1]
    return x if shift == 0 else pltpu.roll(x, shift, x.ndim - 1)


def pack(rows):
    top = jnp.where(lanes((128, 128)) < 64, rows[:128], roll(rows[128:], 64))
    group = lanes((32, 128)) // 16
    low = roll(rows[:32], -64)
    for k in range(1, 8):
        low = jnp.where(group == k, roll(rows[32 * k : 32 * k + 32], 16 * k - 64), low)
    return top, low


def unpack(top, low, place):
    at = lanes((128, 128))
    upper = roll(top, place)
    lower = roll(top, place - 64)
    tail = [roll(low, place + 64 - 16 * k) for k in range(8)]
    first = jnp.concatenate(tail[:4], axis=0)
    second = jnp.concatenate(tail[4:], axis=0)
    wide = (at >= place) & (at < place + 64)
    rest = (at >= place + 64) & (at < place + HEAD)
    one = jnp.where(wide, upper, jnp.where(rest, first, 0.0))
    two = jnp.where(wide, lower, jnp.where(rest, second, 0.0))
    return one, two


def pack_kernel(rows_ref, out_ref):
    for g in range(HEADS):
        start = (HEAD * g) // 128 * 128
        shift = HEAD * g - start
        size = 128 if shift + HEAD <= 128 else 256
        window = rows_ref[:, start : start + size].astype(f32)
        window = roll(window, -shift)[:, :128]
        top, low = pack(window)
        out_ref[g, :128, :] = top.astype(bf16)
        out_ref[g, 128:, :] = low.astype(bf16)


def permute_kernel(place_ref, source_ref, in_ref, out_ref, table, picked):
    slot = place_ref[1]
    for src in range(HEADS):
        one, two = unpack(
            in_ref[src, :128, :].astype(f32), in_ref[src, 128:, :].astype(f32), 0
        )
        table[CHUNK * src : CHUNK * src + 128, :] = one
        table[CHUNK * src + 128 : CHUNK * src + 256, :] = two
    for q in range(RING):
        for o, off in enumerate(XOR_ORDER):
            base = q * SLOTS * CHUNK + (slot ^ off) * CHUNK

            def step(i, carry):
                at = i * 16
                for u in range(16):
                    row = source_ref[base + at + u]
                    picked[pl.ds(at + u, 1), :] = table[pl.ds(row, 1), :]
                return carry

            lax.fori_loop(0, CHUNK // 16, step, 0)
            top, low = pack(picked[...])
            out_ref[q, o, :128, :] = top.astype(bf16)
            out_ref[q, o, 128:, :] = low.astype(bf16)


def norm_kernel(rows_ref, gain_ref, out_ref):
    values = rows_ref[...].astype(f32)
    inverse = lax.rsqrt(jnp.mean(values * values, axis=-1, keepdims=True) + epsilon)
    out_ref[...] = (values * inverse * gain_ref[...]).astype(bf16)


def head_kernel(
    place_ref, normed_ref, w_ref, up_ref, window_ref, grad_ref, weight_ref, gain_ref,
    first, second, key_at, query_at, upstream,
):
    head = pl.program_id(0)
    ring, slot = place_ref[0], place_ref[1]
    scaling = HEAD ** (-0.5)
    w = w_ref[0]
    for c in range(SLOTS):
        rows = slice(CHUNK * c, CHUNK * c + CHUNK)
        all_three = dot(normed_ref[rows, :], w, NT)
        low = all_three.astype(bf16)
        first[rows, :] = low[:, :128]
        second[rows, :] = low[:, 128:]
        rounded = low.astype(f32)
        at = lanes((CHUNK, PADDED))
        moved = jnp.where(at < HEAD, roll(rounded, -HEAD), 0.0)
        key_at[rows, :] = moved[:, :128].astype(bf16)
        query_at[rows, :] = jnp.where(
            (at >= HEAD) & (at < 2 * HEAD), roll(rounded, HEAD), 0.0
        ).astype(bf16)
        one, two = unpack(
            up_ref[0, c, :128, :].astype(f32), up_ref[0, c, 128:, :].astype(f32), 32
        )
        upstream[CHUNK * c : CHUNK * c + 128, :] = one.astype(bf16)
        upstream[CHUNK * c + 128 : CHUNK * c + 256, :] = two.astype(bf16)
    for b in range(SLOTS * CHUNK // SUPER):
        rows = slice(SUPER * b, SUPER * b + SUPER)
        line = ring * 8 + (slot ^ XOR_ORDER[b // 2]) * 2 + b % 2
        labels = jnp.broadcast_to(window_ref[pl.ds(line, 1), :], (SUPER, SUPER))
        same = labels == labels.T
        keys = key_at[rows, :]
        up = upstream[rows, :]
        scores = dot(first[rows, :], keys, NT) * scaling
        scores = jnp.where(same, scores, -1e30)
        top = jnp.max(scores, axis=-1, keepdims=True)
        powers = jnp.exp(scores - top)
        probs = powers / jnp.sum(powers, axis=-1, keepdims=True)
        grad_probs = dot(up, second[rows, :], NT)
        row_dot = jnp.sum(probs * grad_probs, axis=-1, keepdims=True)
        grad_scores = (probs * (grad_probs - row_dot)).astype(bf16)
        grad_query = dot(grad_scores, keys, NN)
        grad_key = dot(grad_scores, query_at[rows, :], TN)
        grad_value = dot(probs.astype(bf16), up, TN)
        grad_ref[0, rows, :128] = ((grad_query + grad_key[:, :128]) * scaling).astype(bf16)
        grad_ref[0, rows, 128:] = (grad_key[:, 128:] * scaling + grad_value).astype(bf16)
    grads = grad_ref[0]
    for n in range(5):
        cols = slice(256 * n, 256 * n + 256)
        part = dot(grads, normed_ref[:, cols], TN)
        weight_ref[:, 0, :, cols] = part.astype(bf16).reshape(16, 16, 256)
        gained = jnp.sum(part * w[:, cols].astype(f32), axis=0, keepdims=True)

        @pl.when(head == 0)
        def _():
            gain_ref[:, cols] = gained

        @pl.when(head > 0)
        def _():
            gain_ref[:, cols] += gained


def back_kernel(grad_ref, w_ref, keep_ref, send_ref):
    for c in range(SLOTS):
        rows = slice(CHUNK * c, CHUNK * c + CHUNK)
        total = dot(grad_ref[0, rows, :], w_ref[0], NN)
        for h in range(1, RING):
            total += dot(grad_ref[h, rows, :], w_ref[h], NN)
        if c < 2:
            keep_ref[rows, :] = total
        else:
            send_ref[CHUNK * (c - 2) : CHUNK * (c - 1), :] = total.astype(bf16)


def final_kernel(rows_ref, gain_ref, keep_ref, core_ref, pair_ref, out_ref):
    values = rows_ref[...].astype(f32)
    inverse = lax.rsqrt(jnp.mean(values * values, axis=-1, keepdims=True) + epsilon)
    scaled = values * inverse
    normed_grad = keep_ref[...] + core_ref[...].astype(f32) + pair_ref[...].astype(f32)
    grad_scaled = normed_grad * gain_ref[...]
    mixed = jnp.mean(grad_scaled * scaled, axis=-1, keepdims=True)
    out_ref[...] = (inverse * (grad_scaled - scaled * mixed)).astype(bf16)


def vmem():
    return pl.BlockSpec(memory_space=pltpu.VMEM)


def smem():
    return pl.BlockSpec(memory_space=pltpu.SMEM)


def params():
    return pltpu.CompilerParams(vmem_limit_bytes=BIG)


def pack_call(rows):
    return pl.pallas_call(
        pack_kernel,
        out_shape=jax.ShapeDtypeStruct((HEADS, LINES, 128), bf16),
        in_specs=[vmem()],
        out_specs=vmem(),
        compiler_params=params(),
    )(rows)


def permute_call(place, source, received):
    return pl.pallas_call(
        permute_kernel,
        out_shape=jax.ShapeDtypeStruct((RING, SLOTS, LINES, 128), bf16),
        in_specs=[smem(), smem(), vmem()],
        out_specs=vmem(),
        scratch_shapes=[pltpu.VMEM((HEADS * CHUNK, 128), f32), pltpu.VMEM((CHUNK, 128), f32)],
        compiler_params=params(),
    )(place, source, received)


def norm_call(rows, gain):
    return pl.pallas_call(
        norm_kernel,
        out_shape=jax.ShapeDtypeStruct(rows.shape, bf16),
        in_specs=[vmem(), vmem()],
        out_specs=vmem(),
        compiler_params=params(),
    )(rows, gain)


def head_call(place, normed, weights, upstream, windows):
    rows, width = normed.shape
    return pl.pallas_call(
        head_kernel,
        grid=(RING,),
        out_shape=(
            jax.ShapeDtypeStruct((RING, rows, PADDED), bf16),
            jax.ShapeDtypeStruct((16, RING, 16, width), bf16),
            jax.ShapeDtypeStruct((1, width), f32),
        ),
        in_specs=[
            smem(),
            pl.BlockSpec((rows, width), lambda h: (0, 0)),
            pl.BlockSpec((1, PADDED, width), lambda h: (h, 0, 0)),
            pl.BlockSpec((1, SLOTS, LINES, 128), lambda h: (h, 0, 0, 0)),
            pl.BlockSpec((32, 128), lambda h: (0, 0)),
        ],
        out_specs=(
            pl.BlockSpec((1, rows, PADDED), lambda h: (h, 0, 0)),
            pl.BlockSpec((16, 1, 16, width), lambda h: (0, h, 0, 0)),
            pl.BlockSpec((1, width), lambda h: (0, 0)),
        ),
        scratch_shapes=[
            pltpu.VMEM((rows, 128), bf16),
            pltpu.VMEM((rows, 128), bf16),
            pltpu.VMEM((rows, 128), bf16),
            pltpu.VMEM((rows, PADDED), bf16),
            pltpu.VMEM((rows, 128), bf16),
        ],
        compiler_params=params(),
    )(place, normed, weights, upstream, windows)


def back_call(grads, weights):
    width = weights.shape[-1]
    return pl.pallas_call(
        back_kernel,
        out_shape=(
            jax.ShapeDtypeStruct((2 * CHUNK, width), f32),
            jax.ShapeDtypeStruct((2 * CHUNK, width), bf16),
        ),
        in_specs=[vmem(), vmem()],
        out_specs=(vmem(), vmem()),
        compiler_params=params(),
    )(grads, weights)


def final_call(rows, gain, keep, from_core, from_pair):
    return pl.pallas_call(
        final_kernel,
        out_shape=jax.ShapeDtypeStruct(rows.shape, bf16),
        in_specs=[vmem()] * 5,
        out_specs=vmem(),
        compiler_params=params(),
    )(rows, gain, keep, from_core, from_pair)


def swap(x, axis):
    return lax.ppermute(x, axis, [(0, 1), (1, 0)])


def on_device(layer_input, grad_packed, source_row, window_id, w_qkv, gain):
    width = layer_input.shape[1]
    dp = lax.axis_index("y") * 4 + lax.axis_index("x")
    ring = lax.axis_index("zq")
    slot = lax.axis_index("zp") * 2 + lax.axis_index("core")
    place = jnp.stack([ring, slot]).astype(jnp.int32)
    gain_row = gain.reshape(1, width)

    flipped = jnp.swapaxes(w_qkv, 1, 2).reshape(3 * HEAD, width)
    flipped = jnp.pad(flipped, ((0, PADDED - 3 * HEAD), (0, 0)))
    share = lax.dynamic_slice(flipped, (16 * dp, 0), (16, width))
    weights = lax.all_gather(share, ("zq", "y", "x"), axis=0, tiled=True)
    weights = weights.reshape(RING, PADDED, width)

    packed = pack_call(grad_packed)
    by_head = lax.all_to_all(packed, ("zq", "zp", "core"), split_axis=0, concat_axis=0)
    permuted = permute_call(place, source_row.reshape(-1), by_head)
    upstream = lax.all_to_all(permuted, "zq", split_axis=0, concat_axis=0)

    own = norm_call(layer_input, gain_row)
    half = jnp.concatenate([own, swap(own, "zp")], axis=0)
    normed = jnp.concatenate([half, swap(half, "core")], axis=0)

    windows = window_id.reshape(32, 128).astype(f32)
    grads, weight_part, gain_part = head_call(place, normed, weights, upstream, windows)

    arrived = lax.all_to_all(weight_part, ("y", "x"), split_axis=0, concat_axis=0)
    summed = jnp.sum(arrived.astype(f32), axis=0).astype(bf16)
    gain_part = gain_part + swap(gain_part, "core")
    gain_part = gain_part + swap(gain_part, "zp")
    beside = jnp.pad(gain_part.reshape(10, 128), ((0, 6), (0, 0))).astype(bf16)
    beside = jnp.broadcast_to(beside[None], (RING, 16, 128))
    message = jnp.concatenate([summed, beside], axis=2)
    arrived = lax.all_to_all(message, "zq", split_axis=0, concat_axis=0)
    summed = jnp.sum(arrived.astype(f32), axis=0).astype(bf16)
    copies = jnp.broadcast_to(summed[None], (16,) + summed.shape)
    whole = lax.all_to_all(copies, ("y", "x"), split_axis=0, concat_axis=0)
    gradient = whole[:, :, :width].reshape(PADDED, width)[: 3 * HEAD].astype(f32)
    grad_weight = jnp.swapaxes(gradient.reshape(3, HEAD, width), 1, 2)
    grad_gain = jnp.sum(whole[:, :10, width:].astype(f32), axis=0).reshape(width) / gain

    keep, send = back_call(grads, weights)
    from_core = swap(send, "core")
    pair = (keep[CHUNK:] + from_core[CHUNK:].astype(f32)).astype(bf16)
    from_pair = swap(pair, "zp")
    grad_input = final_call(layer_input, gain_row, keep[:CHUNK], from_core[:CHUNK], from_pair)
    return (grad_input, grad_weight, grad_gain)


def solution(mesh):
    fine = Mesh(mesh.devices.reshape(4, 4, 4, 2, 2), ("y", "x", "zq", "zp", "core"))
    dp, group = ("y", "x"), ("zq", "zp", "core")
    rows = P(dp + group, None)
    return jax.shard_map(
        on_device,
        mesh=fine,
        in_specs=(rows, rows, P(dp, None), P(dp, None), P(None, None, group), P()),
        out_specs=(rows, P(None, None, group), P()),
        check_vma=False,
    )
```

time: 370 us -> 223 us (0.60)
  waiting for transfers between devices: 174 us -> 90.5 us
  blocking collectives: 74.9 us -> 12.5 us
  Pallas kernels: 0 us -> 54.2 us
  local copies, waits for them, and re-layouts: 50.2 us -> 7.38 us
  matrix products: 28.2 us -> 0 us
  starting transfers between devices: 13.3 us -> 35.2 us
    psum x1 -> x0, blocking collectives: 74.9 us -> none  [on_device(): grad_gain = lax.psum(jnp.sum(grad_normed * scaled, axis=0), ('dp', 'group'))]
    psum x1 -> x0, waiting for transfers between devices: 73.2 us -> none  [on_device(): lax.psum(weight_part.astype(jnp.bfloat16), 'dp').astype(jnp.float32)]
    all_gather x2 -> x1, waiting for transfers between devices: 80.4 us -> 21.5 us  [on_device(): weights = lax.all_gather(share, ('zq', 'y', 'x'), axis=0, tiled=True)]
    pallas_call x0 -> x6, Pallas kernels: none -> 54.2 us  [the longest x1 30.3 us: head_call(): pl.pallas_call(head_kernel, grid=(RING,), out_shape=(jax.ShapeDtypeStruct...]
    all_to_all x2 -> x4, waiting for transfers between devices: 20.1 us -> 47.9 us  [the longest x1 19.5 us: on_device(): lax.all_to_all(weight_part, ('y', 'x'), split_axis=0, concat_axis=0)]
    ppermute x0 -> x6, waiting for transfers between devices: none -> 21.1 us  [swap(): return lax.ppermute(x, axis, [(0, 1), (1, 0)])]
    dot_general x6 -> x0, matrix products: 20.5 us -> none  [the longest x1 7.74 us: on_device(): jnp.einsum('jre,jde->rd', returned, lax.all_gather(w_qkv, 'group', axis=2...]
    unnamed x24 -> x16, local copies, waits for them, and re-layouts: 18.8 us -> 1.72 us
  transfers between devices with their start and end apart: 5 -> 11, of which waited for: 4 -> 8; matrix products, arithmetic and copies ran while one was open for 13% -> 5% of each run, Pallas kernels for 0% -> 11%
where the time goes in v1:
time: 223 us; the launch traced here: 222 us
  waiting for transfers between devices  90.5 us (41%)
  Pallas kernels  54.2 us (24%)
  starting transfers between devices  35.2 us (16%)
  between operations  14.1 us (6%)
  blocking collectives  12.5 us (6%)
  other arithmetic  8.54 us (4%)
  local copies, waits for them, and re-layouts  7.38 us (3%)
    pallas_call x1, Pallas kernels, head_call(): pl.pallas_call(head_kernel, grid=(RING,), out_shape=(jax.ShapeDtypeStruct...  30.3 us
    all_gather x1, waiting for transfers between devices, on_device(): weights = lax.all_gather(share, ('zq', 'y', 'x'), axis=0, tiled=True)  21.5 us
    ppermute x6, waiting for transfers between devices, swap(): return lax.ppermute(x, axis, [(0, 1), (1, 0)])  21.1 us
    all_to_all x1, waiting for transfers between devices, on_device(): lax.all_to_all(weight_part, ('y', 'x'), split_axis=0, concat_axis=0)  19.5 us
    all_to_all x1, waiting for transfers between devices, on_device(): upstream = lax.all_to_all(permuted, 'zq', split_axis=0, concat_axis=0)  16.1 us
    all_to_all x1, blocking collectives, on_device(): arrived = lax.all_to_all(message, 'zq', split_axis=0, concat_axis=0)  12.5 us
    all_to_all x1, waiting for transfers between devices, on_device(): lax.all_to_all(packed, ('zq', 'zp', 'core'), split_axis=0, concat_axis=0)  12.4 us
    all_to_all x1, starting transfers between devices, on_device(): whole = lax.all_to_all(copies, ('y', 'x'), split_axis=0, concat_axis=0)  8.78 us
  transfers between devices with their start and end apart: 11, of which 8 were waited for; matrix products, arithmetic and copies ran while one was open for 5% of the time, Pallas kernels for 11%

profile of v1, /device:TPU:2, one launch (start us, length us, event | category | flops | bytes accessed | tf_op | source)
XLA Modules:
  0.0 222.4 jit_solution(4337160055110171434)
XLA Ops:
  7.2 1.4 pad_dynamic-slice_fusion
  8.7 1.3 reshape.35.gain_ref
  10.0 2.2 shard_map.85
  12.1 1.9 collective-permute-start
  14.1 3.6 %shard_map.86 = bf16[16,160,128]{2,1,0:T(8,128)(2,1)} custom-call(bf16[256,1280]{1,0:T(8,128)(2,1)} %rows_ref.4), custom_call_target="tpu_custom_call" | custom-call | tf_op jit(solution)/shard_map/pallas_call | solution.py:204
  17.7 7.7 %all-to-all-start = ((bf16[16,160,128]{2,1,0:T(8,128)(2,1)}), bf16[16,160,128]{2,1,0:T(8,128)(2,1)S(1)}, u32[]{:S(2)}, u32[]{:S(2)}) async-start(bf16[16,160,128]{2,1,0:T(8,128)(2,1)} %shard_map.86), calls=%async_computation | async-start | bytes 1310720 | tf_op jit(solution)/shard_map/all_to_all | solution.py:310
  25.3 6.3 %collective-permute-done = bf16[256,1280]{1,0:T(8,128)(2,1)S(1)} collective-permute-done((bf16[256,1280]{1,0:T(8,128)(2,1)}, bf16[256,1280]{1,0:T(8,128)(2,1)S(1)}, u32[]{:S(2)}, u32[]{:S(2)}) %collective-permute-start) | collective-permute-done | bytes 655392 | tf_op jit(solution)/shard_map/ppermute | solution.py:292
  31.7 1.1 pad_maximum_fusion.1
  33.4 12.4 %all-to-all-done.in_ref = bf16[16,160,128]{2,1,0:T(8,128)(2,1)S(1)} async-done(((bf16[16,160,128]{2,1,0:T(8,128)(2,1)}), bf16[16,160,128]{2,1,0:T(8,128)(2,1)S(1)}, u32[]{:S(2)}, u32[]{:S(2)}) %all-to-all-start) | async-done | bytes 655392 | tf_op jit(solution)/shard_map/all_to_all | solution.py:310
  45.8 0.8 copy-done.3
  46.6 8.3 %shard_map.87 = bf16[4,4,160,128]{3,2,1,0:T(8,128)(2,1)} custom-call(s32[2]{0:T(128)} %pad_add_fusion.place_ref, s32[4096]{0:T(1024)} %bitcast.22, bf16[16,160,128]{2,1,0:T(8,128)(2,1)} %copy-done.3), custom_call_target="tpu_custom_call" | custom-call | tf_op jit(solution)/shard_map/pallas_call | solution.py:214
  54.9 5.1 %all-to-all-start.1 = ((bf16[4,4,160,128]{3,2,1,0:T(8,128)(2,1)}), bf16[4,4,160,128]{3,2,1,0:T(8,128)(2,1)S(1)}, u32[]{:S(2)}, u32[]{:S(2)}) async-start(bf16[4,4,160,128]{3,2,1,0:T(8,128)(2,1)} %shard_map.87), calls=%async_computation.1 | async-start | bytes 1310720 | tf_op jit(solution)/shard_map/all_to_all | solution.py:312
  60.6 1.6 pad_maximum_fusion.normed_ref
  62.3 16.1 %all-to-all-done.1.up_ref = bf16[4,4,160,128]{3,2,1,0:T(8,128)(2,1)S(1)} async-done(((bf16[4,4,160,128]{3,2,1,0:T(8,128)(2,1)}), bf16[4,4,160,128]{3,2,1,0:T(8,128)(2,1)S(1)}, u32[]{:S(2)}, u32[]{:S(2)}) %all-to-all-start.1) | async-done | bytes 655392 | tf_op jit(solution)/shard_map/all_to_all | solution.py:312
  78.3 21.5 %all-gather.2.cloned.1.call-done = bf16[1024,1280]{1,0:T(8,128)(2,1)} async-done(((bf16[16,1280]{1,0:T(8,128)(2,1)}), bf16[1024,1280]{1,0:T(8,128)(2,1)}) %all-gather.2.cloned.1.call-update) | async-done | bytes 2621456 | tf_op jit(solution)/shard_map/all_gather | solution.py:306
  99.8 30.3 %shard_map.88 = (bf16[4,1024,256]{2,1,0:T(8,128)(2,1)}, bf16[16,4,16,1280]{3,2,1,0:T(8,128)(2,1)}, f32[1,1280]{1,0:T(1,128)}) custom-call(s32[2]{0:T(128)} %pad_add_fusion.place_ref, bf16[1024,1280]{1,0:T(8,128)(2,1)} %pad_maximum_fusion.normed_ref, bf16[4,256,1280]{2,1,0:T(8,128)(2,1)} %bitcast.17, bf16[4,4,160,128]{3,2,1,0:T(8,128)(2,1)} %copy-done.1, ...), custom_call_target="tpu_custom_call" | custom-call | tf_op jit(solution)/shard_map/pallas_call | solution.py:236
  130.2 7.3 %all-to-all-start.2 = ((bf16[16,4,16,1280]{3,2,1,0:T(8,128)(2,1)}), bf16[16,4,16,1280]{3,2,1,0:T(8,128)(2,1)S(1)}, u32[]{:S(2)}, u32[]{:S(2)}) async-start(bf16[16,4,16,1280]{3,2,1,0:T(8,128)(2,1)} %get-tuple-element.11), calls=%async_computation.2 | async-start | bytes 5242880 | tf_op jit(solution)/shard_map/all_to_all | solution.py:321
  137.5 6.3 %shard_map.89 = (f32[512,1280]{1,0:T(8,128)}, bf16[512,1280]{1,0:T(8,128)(2,1)}) custom-call(bf16[4,1024,256]{2,1,0:T(8,128)(2,1)} %get-tuple-element.8.grad_ref, bf16[4,256,1280]{2,1,0:T(8,128)(2,1)} %bitcast.18), custom_call_target="tpu_custom_call" | custom-call | tf_op jit(solution)/shard_map/pallas_call | solution.py:269
  144.3 2.2 collective-permute-done.4
  146.5 1.0 collective-permute-start.5
  147.5 2.6 %collective-permute-done.5 = f32[1,1280]{1,0:T(1,128)S(1)} collective-permute-done((f32[1,1280]{1,0:T(1,128)S(1)}, f32[1,1280]{1,0:T(1,128)S(1)}, u32[]{:S(2)}, u32[]{:S(2)}) %collective-permute-start.5) | collective-permute-done | bytes 5152 | tf_op jit(solution)/shard_map/ppermute | solution.py:292
  150.1 19.5 %all-to-all-done.2 = bf16[16,4,16,1280]{3,2,1,0:T(8,128)(2,1)S(1)} async-done(((bf16[16,4,16,1280]{3,2,1,0:T(8,128)(2,1)}), bf16[16,4,16,1280]{3,2,1,0:T(8,128)(2,1)S(1)}, u32[]{:S(2)}, u32[]{:S(2)}) %all-to-all-start.2) | async-done | bytes 2621472 | tf_op jit(solution)/shard_map/all_to_all | solution.py:321
  170.0 12.5 %all_to_all.25 = bf16[4,16,1408]{2,1,0:T(8,128)(2,1)S(1)} all-to-all(bf16[4,16,1408]{2,1,0:T(8,128)(2,1)S(1)} %pad_maximum_fusion.2), channel_id=1, replica_groups=mesh['y'=4,'x'=4,'zq'=4,'zp'=2,'core'=2] {'zq'}, dimensions={0} | all-to-all | bytes 360448 | tf_op jit(solution)/shard_map/all_to_all | solution.py:328
  182.6 0.9 broadcast_in_dim.5
  183.5 8.8 %all-to-all-start.4 = ((bf16[16,16,1408]{2,1,0:T(8,128)(2,1)}), bf16[16,16,1408]{2,1,0:T(8,128)(2,1)S(1)}, u32[]{:S(2)}, u32[]{:S(2)}) async-start(bf16[16,16,1408]{2,1,0:T(8,128)(2,1)} %broadcast_in_dim.5), calls=%async_computation.4 | async-start | bytes 1441792 | tf_op jit(solution)/shard_map/all_to_all | solution.py:331
  192.3 2.3 %add_convert_fusion = (bf16[256,1280]{1,0:T(8,128)(2,1)S(1)}, f32[256,1280]{1,0:T(8,128)}) fusion(f32[512,1280]{1,0:T(8,128)S(1)} %copy-done.2, bf16[512,1280]{1,0:T(8,128)(2,1)} %collective-permute-done.2), kind=kLoop, calls=%fused_computation.2 | loop fusion | flops 983040 | bytes 5242880 | tf_op jit(solution)/shard_map/convert_element_type | solution.py:338
  194.6 2.9 %collective-permute-start.3 = (bf16[256,1280]{1,0:T(8,128)(2,1)S(1)}, bf16[256,1280]{1,0:T(8,128)(2,1)S(1)}, u32[]{:S(2)}, u32[]{:S(2)}) collective-permute-start(bf16[256,1280]{1,0:T(8,128)(2,1)S(1)} %get-tuple-element.13), channel_id=1, source_target_pairs={{0,2},{2,0},{1,3},{3,1},{4,6},{6,4},{5,7},{7,5},{8,10},{10,8},{9,1... | collective-permute-start | bytes 1966088 | tf_op jit(solution)/shard_map/ppermute | solution.py:292
  197.5 2.0 slice.27.core_ref
  199.5 9.9 %collective-permute-done.3.pair_ref = bf16[256,1280]{1,0:T(8,128)(2,1)S(1)} collective-permute-done((bf16[256,1280]{1,0:T(8,128)(2,1)S(1)}, bf16[256,1280]{1,0:T(8,128)(2,1)S(1)}, u32[]{:S(2)}, u32[]{:S(2)}) %collective-permute-start.3) | collective-permute-done | bytes 655392 | tf_op jit(solution)/shard_map/ppermute | solution.py:292
  209.5 0.9 copy-done.4
  210.3 3.4 %shard_map.90 = bf16[256,1280]{1,0:T(8,128)(2,1)} custom-call(bf16[256,1280]{1,0:T(8,128)(2,1)} %rows_ref.5, f32[1,1280]{1,0:T(1,128)} %reshape.35.gain_ref, f32[256,1280]{1,0:T(8,128)} %get-tuple-element.14.keep_ref, bf16[256,1280]{1,0:T(8,128)(2,1)} %slice.27.core_ref, bf16[256,1280]{1,0:T(8,128)(2,1)} %copy-done.4), custom_call_target="tpu_custom_call" | custom-call | tf_op jit(solution)/shard_map/pallas_call | solution.py:282
  213.8 1.1 convert_bitcast_fusion
  (34 shorter events, 3.0 us)
Async XLA Ops:
  7.2 92.7 %all-gather.2.cloned.1.call-start = ((), (), s32[]{:S(2)}) async-start(), calls=%async_computation.5 | async-start | bytes 2662400 | tf_op jit(solution)/shard_map/all_gather | solution.py:306
  12.1 19.5 %copy-start = (bf16[256,1280]{1,0:T(8,128)(2,1)S(1)}, bf16[256,1280]{1,0:T(8,128)(2,1)}, u32[]{:S(2)}) copy-start(bf16[256,1280]{1,0:T(8,128)(2,1)} %shard_map.85) | copy-start | bytes 1966084
  12.1 19.5 %collective-permute-start = (bf16[256,1280]{1,0:T(8,128)(2,1)}, bf16[256,1280]{1,0:T(8,128)(2,1)S(1)}, u32[]{:S(2)}, u32[]{:S(2)}) collective-permute-start(bf16[256,1280]{1,0:T(8,128)(2,1)} %shard_map.85), channel_id=1, source_target_pairs={{0,2},{2,0},{1,3},{3,1},{4,6},{6,4},{5,7},{7,5},{8,10},{10,8},{9,1... | collective-permute-start | bytes 1966088 | tf_op jit(solution)/shard_map/ppermute | solution.py:292
  17.7 28.1 %all-to-all-start = ((bf16[16,160,128]{2,1,0:T(8,128)(2,1)}), bf16[16,160,128]{2,1,0:T(8,128)(2,1)S(1)}, u32[]{:S(2)}, u32[]{:S(2)}) async-start(bf16[16,160,128]{2,1,0:T(8,128)(2,1)} %shard_map.86), calls=%async_computation | async-start | bytes 1310720 | tf_op jit(solution)/shard_map/all_to_all | solution.py:310
  25.3 34.7 %copy-start.6 = (s32[1,4096]{1,0:T(1,128)S(1)}, s32[1,4096]{1,0:T(1,128)}, u32[]{:S(2)}) copy-start(s32[1,4096]{1,0:T(1,128)} %param.9) | copy-start | bytes 49156
  32.8 27.8 %collective-permute-start.1 = (bf16[512,1280]{1,0:T(8,128)(2,1)}, bf16[512,1280]{1,0:T(8,128)(2,1)S(1)}, u32[]{:S(2)}, u32[]{:S(2)}) collective-permute-start(bf16[512,1280]{1,0:T(8,128)(2,1)} %pad_maximum_fusion.1), channel_id=1, source_target_pairs={{0,1},{1,0},{2,3},{3,2},{4,5},{5,4},{6,7},{7,6},{8,9},{9,8},{10,11... | collective-permute-start | bytes 3932168 | tf_op jit(solution)/shard_map/ppermute | solution.py:292
  45.8 0.8 copy-start.3
  54.9 23.4 %all-to-all-start.1 = ((bf16[4,4,160,128]{3,2,1,0:T(8,128)(2,1)}), bf16[4,4,160,128]{3,2,1,0:T(8,128)(2,1)S(1)}, u32[]{:S(2)}, u32[]{:S(2)}) async-start(bf16[4,4,160,128]{3,2,1,0:T(8,128)(2,1)} %shard_map.87), calls=%async_computation.1 | async-start | bytes 1310720 | tf_op jit(solution)/shard_map/all_to_all | solution.py:312
  78.3 21.5 %copy-start.1 = (bf16[4,4,160,128]{3,2,1,0:T(8,128)(2,1)}, bf16[4,4,160,128]{3,2,1,0:T(8,128)(2,1)S(1)}, u32[]{:S(2)}) copy-start(bf16[4,4,160,128]{3,2,1,0:T(8,128)(2,1)S(1)} %all-to-all-done.1.up_ref) | copy-start | bytes 1966084
  130.2 39.4 %all-to-all-start.2 = ((bf16[16,4,16,1280]{3,2,1,0:T(8,128)(2,1)}), bf16[16,4,16,1280]{3,2,1,0:T(8,128)(2,1)S(1)}, u32[]{:S(2)}, u32[]{:S(2)}) async-start(bf16[16,4,16,1280]{3,2,1,0:T(8,128)(2,1)} %get-tuple-element.11), calls=%async_computation.2 | async-start | bytes 5242880 | tf_op jit(solution)/shard_map/all_to_all | solution.py:321
  137.5 6.3 %copy-start.7 = (f32[1,1280]{1,0:T(1,128)S(1)}, f32[1,1280]{1,0:T(1,128)}, u32[]{:S(2)}) copy-start(f32[1,1280]{1,0:T(1,128)} %get-tuple-element.12) | copy-start | bytes 15364
  143.8 48.5 %collective-permute-start.2 = (bf16[512,1280]{1,0:T(8,128)(2,1)}, bf16[512,1280]{1,0:T(8,128)(2,1)}, u32[]{:S(2)}, u32[]{:S(2)}) collective-permute-start(bf16[512,1280]{1,0:T(8,128)(2,1)} %get-tuple-element.10), channel_id=1, source_target_pairs={{0,1},{1,0},{2,3},{3,2},{4,5},{5,4},{6,7},{7,6},{8,9},{9,8},{10,11... | collective-permute-start | bytes 3932168 | tf_op jit(solution)/shard_map/ppermute | solution.py:292
  143.8 2.7 %collective-permute-start.4 = (f32[1,1280]{1,0:T(1,128)S(1)}, f32[1,1280]{1,0:T(1,128)S(1)}, u32[]{:S(2)}, u32[]{:S(2)}) collective-permute-start(f32[1,1280]{1,0:T(1,128)S(1)} %copy-done.7), channel_id=1, source_target_pairs={{0,1},{1,0},{2,3},{3,2},{4,5},{5,4},{6,7},{7,6},{8,9},{9,8},{10,11... | collective-permute-start | bytes 15368 | tf_op jit(solution)/shard_map/ppermute | solution.py:292
  146.5 3.6 %collective-permute-start.5 = (f32[1,1280]{1,0:T(1,128)S(1)}, f32[1,1280]{1,0:T(1,128)S(1)}, u32[]{:S(2)}, u32[]{:S(2)}) collective-permute-start(f32[1,1280]{1,0:T(1,128)S(1)} %add.26), channel_id=1, source_target_pairs={{0,2},{2,0},{1,3},{3,1},{4,6},{6,4},{5,7},{7,5},{8,10},{10,8},{9,1... | collective-permute-start | bytes 15368 | tf_op jit(solution)/shard_map/ppermute | solution.py:292
  170.0 22.3 %copy-start.2 = (f32[512,1280]{1,0:T(8,128)S(1)}, f32[512,1280]{1,0:T(8,128)}, u32[]{:S(2)}) copy-start(f32[512,1280]{1,0:T(8,128)} %get-tuple-element.9) | copy-start | bytes 7864324
  183.5 30.3 %all-to-all-start.4 = ((bf16[16,16,1408]{2,1,0:T(8,128)(2,1)}), bf16[16,16,1408]{2,1,0:T(8,128)(2,1)S(1)}, u32[]{:S(2)}, u32[]{:S(2)}) async-start(bf16[16,16,1408]{2,1,0:T(8,128)(2,1)} %broadcast_in_dim.5), calls=%async_computation.4 | async-start | bytes 1441792 | tf_op jit(solution)/shard_map/all_to_all | solution.py:331
  194.6 14.8 %collective-permute-start.3 = (bf16[256,1280]{1,0:T(8,128)(2,1)S(1)}, bf16[256,1280]{1,0:T(8,128)(2,1)S(1)}, u32[]{:S(2)}, u32[]{:S(2)}) collective-permute-start(bf16[256,1280]{1,0:T(8,128)(2,1)S(1)} %get-tuple-element.13), channel_id=1, source_target_pairs={{0,2},{2,0},{1,3},{3,1},{4,6},{6,4},{5,7},{7,5},{8,10},{10,8},{9,1... | collective-permute-start | bytes 1966088 | tf_op jit(solution)/shard_map/ppermute | solution.py:292
  209.5 0.9 copy-start.4
  210.3 4.6 %copy-start.5 = (f32[1280]{0:T(1024)S(1)}, f32[1280]{0:T(1024)}, u32[]{:S(2)}) copy-start(f32[1280]{0:T(1024)} %param.11) | copy-start | bytes 15364
Sparse Core Ops, SparseCore 0:
  11.3 88.4 all-gather.1

commit v2 on v1

--- a/solution.py
+++ b/solution.py
@@ -22,7 +22,7 @@
 NT = (((1,), (1,)), ((), ()))
 TN = (((0,), (0,)), ((), ()))
 NN = (((1,), (0,)), ((), ()))
-BIG = 56 * 1024 * 1024
+BIG = 28 * 1024 * 1024
 
 
 def dot(a, b, dims):
@@ -111,71 +111,60 @@
     head = pl.program_id(0)
     ring, slot = place_ref[0], place_ref[1]
     scaling = HEAD ** (-0.5)
-    w = w_ref[0]
+    w = w_ref[:, 0].reshape(PADDED, w_ref.shape[-1])
+    total_rows = SLOTS * CHUNK
+    low = dot(normed_ref[...], w, NT).astype(bf16)
+    first[...] = low[:, :128]
+    second[...] = low[:, 128:]
+    rounded = low.astype(f32)
+    at = lanes((total_rows, PADDED))
+    key_at[...] = jnp.where(at < HEAD, roll(rounded, -HEAD), 0.0)[:, :128].astype(bf16)
+    query_at[...] = jnp.where(
+        (at >= HEAD) & (at < 2 * HEAD), roll(rounded, HEAD), 0.0
+    ).astype(bf16)
     for c in range(SLOTS):
-        rows = slice(CHUNK * c, CHUNK * c + CHUNK)
-        all_three = dot(normed_ref[rows, :], w, NT)
-        low = all_three.astype(bf16)
-        first[rows, :] = low[:, :128]
-        second[rows, :] = low[:, 128:]
-        rounded = low.astype(f32)
-        at = lanes((CHUNK, PADDED))
-        moved = jnp.where(at < HEAD, roll(rounded, -HEAD), 0.0)
-        key_at[rows, :] = moved[:, :128].astype(bf16)
-        query_at[rows, :] = jnp.where(
-            (at >= HEAD) & (at < 2 * HEAD), roll(rounded, HEAD), 0.0
-        ).astype(bf16)
         one, two = unpack(
             up_ref[0, c, :128, :].astype(f32), up_ref[0, c, 128:, :].astype(f32), 32
         )
         upstream[CHUNK * c : CHUNK * c + 128, :] = one.astype(bf16)
         upstream[CHUNK * c + 128 : CHUNK * c + 256, :] = two.astype(bf16)
-    for b in range(SLOTS * CHUNK // SUPER):
-        rows = slice(SUPER * b, SUPER * b + SUPER)
+    blocks = [slice(SUPER * b, SUPER * b + SUPER) for b in range(total_rows // SUPER)]
+    scores = [dot(first[r, :], key_at[r, :], NT) for r in blocks]
+    grad_probs = [dot(upstream[r, :], second[r, :], NT) for r in blocks]
+    probs, grad_scores = [], []
+    for b in range(len(blocks)):
         line = ring * 8 + (slot ^ XOR_ORDER[b // 2]) * 2 + b % 2
         labels = jnp.broadcast_to(window_ref[pl.ds(line, 1), :], (SUPER, SUPER))
-        same = labels == labels.T
-        keys = key_at[rows, :]
-        up = upstream[rows, :]
-        scores = dot(first[rows, :], keys, NT) * scaling
-        scores = jnp.where(same, scores, -1e30)
-        top = jnp.max(scores, axis=-1, keepdims=True)
-        powers = jnp.exp(scores - top)
-        probs = powers / jnp.sum(powers, axis=-1, keepdims=True)
-        grad_probs = dot(up, second[rows, :], NT)
-        row_dot = jnp.sum(probs * grad_probs, axis=-1, keepdims=True)
-        grad_scores = (probs * (grad_probs - row_dot)).astype(bf16)
-        grad_query = dot(grad_scores, keys, NN)
-        grad_key = dot(grad_scores, query_at[rows, :], TN)
-        grad_value = dot(probs.astype(bf16), up, TN)
-        grad_ref[0, rows, :128] = ((grad_query + grad_key[:, :128]) * scaling).astype(bf16)
-        grad_ref[0, rows, 128:] = (grad_key[:, 128:] * scaling + grad_value).astype(bf16)
-    grads = grad_ref[0]
-    for n in range(5):
-        cols = slice(256 * n, 256 * n + 256)
-        part = dot(grads, normed_ref[:, cols], TN)
-        weight_ref[:, 0, :, cols] = part.astype(bf16).reshape(16, 16, 256)
-        gained = jnp.sum(part * w[:, cols].astype(f32), axis=0, keepdims=True)
-
-        @pl.when(head == 0)
-        def _():
-            gain_ref[:, cols] = gained
-
-        @pl.when(head > 0)
-        def _():
-            gain_ref[:, cols] += gained
+        masked = jnp.where(labels == labels.T, scores[b] * scaling, -1e30)
+        powers = jnp.exp(masked - jnp.max(masked, axis=-1, keepdims=True))
+        prob = powers / jnp.sum(powers, axis=-1, keepdims=True)
+        row_dot = jnp.sum(prob * grad_probs[b], axis=-1, keepdims=True)
+        grad_scores.append((prob * (grad_probs[b] - row_dot)).astype(bf16))
+        probs.append(prob.astype(bf16))
+    for b, r in enumerate(blocks):
+        grad_query = dot(grad_scores[b], key_at[r, :], NN)
+        grad_key = dot(grad_scores[b], query_at[r, :], TN)
+        grad_value = dot(probs[b], upstream[r, :], TN)
+        grad_ref[r, :128] = ((grad_query + grad_key[:, :128]) * scaling).astype(bf16)
+        grad_ref[r, 128:] = (grad_key[:, 128:] * scaling + grad_value).astype(bf16)
+    part = dot(grad_ref[...], normed_ref[...], TN)
+    weight_ref[:, 0] = part.astype(bf16).reshape(16, 16, part.shape[1])
+    gained = jnp.sum(part * w.astype(f32), axis=0, keepdims=True)
+
+    @pl.when(head == 0)
+    def _():
+        gain_ref[...] = gained
+
+    @pl.when(head > 0)
+    def _():
+        gain_ref[...] += gained
 
 
 def back_kernel(grad_ref, w_ref, keep_ref, send_ref):
-    for c in range(SLOTS):
-        rows = slice(CHUNK * c, CHUNK * c + CHUNK)
-        total = dot(grad_ref[0, rows, :], w_ref[0], NN)
-        for h in range(1, RING):
-            total += dot(grad_ref[h, rows, :], w_ref[h], NN)
-        if c < 2:
-            keep_ref[rows, :] = total
-        else:
-            send_ref[CHUNK * (c - 2) : CHUNK * (c - 1), :] = total.astype(bf16)
+    parts = [w_ref[:, h].reshape(PADDED, w_ref.shape[-1]) for h in range(RING)]
+    total = dot(grad_ref[...], jnp.concatenate(parts, axis=0), NN)
+    keep_ref[...] = total[: 2 * CHUNK]
+    send_ref[...] = total[2 * CHUNK :].astype(bf16)
 
 
 def final_kernel(rows_ref, gain_ref, keep_ref, core_ref, pair_ref, out_ref):
@@ -237,19 +226,19 @@
         head_kernel,
         grid=(RING,),
         out_shape=(
-            jax.ShapeDtypeStruct((RING, rows, PADDED), bf16),
+            jax.ShapeDtypeStruct((rows, RING * PADDED), bf16),
             jax.ShapeDtypeStruct((16, RING, 16, width), bf16),
             jax.ShapeDtypeStruct((1, width), f32),
         ),
         in_specs=[
             smem(),
             pl.BlockSpec((rows, width), lambda h: (0, 0)),
-            pl.BlockSpec((1, PADDED, width), lambda h: (h, 0, 0)),
+            pl.BlockSpec((16, 1, 16, width), lambda h: (0, h, 0, 0)),
             pl.BlockSpec((1, SLOTS, LINES, 128), lambda h: (h, 0, 0, 0)),
             pl.BlockSpec((32, 128), lambda h: (0, 0)),
         ],
         out_specs=(
-            pl.BlockSpec((1, rows, PADDED), lambda h: (h, 0, 0)),
+            pl.BlockSpec((rows, PADDED), lambda h: (0, h)),
             pl.BlockSpec((16, 1, 16, width), lambda h: (0, h, 0, 0)),
             pl.BlockSpec((1, width), lambda h: (0, 0)),
         ),
@@ -265,15 +254,23 @@
 
 
 def back_call(grads, weights):
-    width = weights.shape[-1]
+    rows, width = grads.shape[0], weights.shape[-1]
+    piece = 256
     return pl.pallas_call(
         back_kernel,
+        grid=(width // piece,),
         out_shape=(
             jax.ShapeDtypeStruct((2 * CHUNK, width), f32),
             jax.ShapeDtypeStruct((2 * CHUNK, width), bf16),
         ),
-        in_specs=[vmem(), vmem()],
-        out_specs=(vmem(), vmem()),
+        in_specs=[
+            pl.BlockSpec((rows, RING * PADDED), lambda n: (0, 0)),
+            pl.BlockSpec((16, RING, 16, piece), lambda n: (0, 0, 0, n)),
+        ],
+        out_specs=(
+            pl.BlockSpec((2 * CHUNK, piece), lambda n: (0, n)),
+            pl.BlockSpec((2 * CHUNK, piece), lambda n: (0, n)),
+        ),
         compiler_params=params(),
     )(grads, weights)
 
@@ -303,15 +300,19 @@
     flipped = jnp.swapaxes(w_qkv, 1, 2).reshape(3 * HEAD, width)
     flipped = jnp.pad(flipped, ((0, PADDED - 3 * HEAD), (0, 0)))
     share = lax.dynamic_slice(flipped, (16 * dp, 0), (16, width))
-    weights = lax.all_gather(share, ("zq", "y", "x"), axis=0, tiled=True)
-    weights = weights.reshape(RING, PADDED, width)
+    others = [lax.ppermute(share, "zq", [(i, (i + k) % RING) for i in range(RING)]) for k in (3, 2, 1)]
+    circle = jnp.concatenate([share] + others + [share] + others, axis=0)
+    ordered = lax.dynamic_slice(circle, (16 * ((RING - ring) % RING), 0), (16 * RING, width))
+    weights = lax.all_gather(ordered, ("y", "x"), axis=0, tiled=True)
+    weights = weights.reshape(16, RING, 16, width)
 
     packed = pack_call(grad_packed)
+    packed, rows_in = lax.optimization_barrier((packed, layer_input))
     by_head = lax.all_to_all(packed, ("zq", "zp", "core"), split_axis=0, concat_axis=0)
     permuted = permute_call(place, source_row.reshape(-1), by_head)
     upstream = lax.all_to_all(permuted, "zq", split_axis=0, concat_axis=0)
 
-    own = norm_call(layer_input, gain_row)
+    own = norm_call(rows_in, gain_row)
     half = jnp.concatenate([own, swap(own, "zp")], axis=0)
     normed = jnp.concatenate([half, swap(half, "core")], axis=0)
 
@@ -324,7 +325,13 @@
     gain_part = gain_part + swap(gain_part, "zp")
     beside = jnp.pad(gain_part.reshape(10, 128), ((0, 6), (0, 0))).astype(bf16)
     beside = jnp.broadcast_to(beside[None], (RING, 16, 128))
+    keep, send = back_call(grads, weights)
+    from_core = swap(send, "core")
+    pair = (keep[CHUNK:] + from_core[CHUNK:].astype(f32)).astype(bf16)
+    from_pair = swap(pair, "zp")
+    grad_input = final_call(layer_input, gain_row, keep[:CHUNK], from_core[:CHUNK], from_pair)
     message = jnp.concatenate([summed, beside], axis=2)
+    message, grad_input = lax.optimization_barrier((message, grad_input))
     arrived = lax.all_to_all(message, "zq", split_axis=0, concat_axis=0)
     summed = jnp.sum(arrived.astype(f32), axis=0).astype(bf16)
     copies = jnp.broadcast_to(summed[None], (16,) + summed.shape)
@@ -333,11 +340,6 @@
     grad_weight = jnp.swapaxes(gradient.reshape(3, HEAD, width), 1, 2)
     grad_gain = jnp.sum(whole[:, :10, width:].astype(f32), axis=0).reshape(width) / gain
 
-    keep, send = back_call(grads, weights)
-    from_core = swap(send, "core")
-    pair = (keep[CHUNK:] + from_core[CHUNK:].astype(f32)).astype(bf16)
-    from_pair = swap(pair, "zp")
-    grad_input = final_call(layer_input, gain_row, keep[:CHUNK], from_core[:CHUNK], from_pair)
     return (grad_input, grad_weight, grad_gain)
 
 

time: 223 us -> 201 us (0.901); the launches traced: 222 us -> 198 us
  waiting for transfers between devices: 90.5 us -> 63.3 us
  blocking collectives: 12.5 us -> 34.5 us
  Pallas kernels: 54.2 us -> 34.8 us
  starting transfers between devices: 35.2 us -> 37.6 us
    all_gather x1, waiting for transfers between devices: 21.5 us -> 0.01 us  [on_device(): weights = lax.all_gather(ordered, ('y', 'x'), axis=0, tiled=True)]
    all_to_all x0 -> x1, blocking collectives: none -> 18.2 us  [on_device(): whole = lax.all_to_all(copies, ('y', 'x'), split_axis=0, concat_axis=0)]
    pallas_call x1, Pallas kernels: 30.3 us -> 17.9 us  [head_call(): pl.pallas_call(head_kernel, grid=(RING,), out_shape=(jax.ShapeDtypeStruct...]
    ppermute x0 -> x3, starting transfers between devices: none -> 10.2 us  [on_device(): lax.ppermute(share, 'zq', [(i, (i + k) % RING) for i in range(RING)])]
    ppermute x6, waiting for transfers between devices: 21.1 us -> 30.4 us  [swap(): return lax.ppermute(x, axis, [(0, 1), (1, 0)])]
    all_to_all x1, waiting for transfers between devices: 19.5 us -> 10.5 us  [on_device(): lax.all_to_all(weight_part, ('y', 'x'), split_axis=0, concat_axis=0)]
    all_to_all x1 -> x0, starting transfers between devices: 8.78 us -> none  [on_device(): whole = lax.all_to_all(copies, ('y', 'x'), split_axis=0, concat_axis=0)]
    all_to_all x1, waiting for transfers between devices: 12.4 us -> 5.31 us  [on_device(): lax.all_to_all(packed, ('zq', 'zp', 'core'), split_axis=0, concat_axis=0)]
  transfers between devices with their start and end apart: 11 -> 13, of which waited for: 8 -> 7; matrix products, arithmetic and copies ran while one was open for 5% -> 3% of each run, Pallas kernels for 11% -> 6%
where the time goes in v2:
time: 201 us; the launch traced here: 198 us
  waiting for transfers between devices  63.3 us (31%)
  starting transfers between devices  37.6 us (19%)
  Pallas kernels  34.8 us (17%)
  blocking collectives  34.5 us (17%)
  between operations  14.2 us (7%)
  other arithmetic  7.14 us (4%)
  local copies, waits for them, and re-layouts  6.35 us (3%)
    ppermute x6, waiting for transfers between devices, swap(): return lax.ppermute(x, axis, [(0, 1), (1, 0)])  30.4 us
    all_to_all x1, blocking collectives, on_device(): whole = lax.all_to_all(copies, ('y', 'x'), split_axis=0, concat_axis=0)  18.2 us
    pallas_call x1, Pallas kernels, head_call(): pl.pallas_call(head_kernel, grid=(RING,), out_shape=(jax.ShapeDtypeStruct...  17.9 us
    all_to_all x1, blocking collectives, on_device(): arrived = lax.all_to_all(message, 'zq', split_axis=0, concat_axis=0)  16.3 us
    all_to_all x1, waiting for transfers between devices, on_device(): upstream = lax.all_to_all(permuted, 'zq', split_axis=0, concat_axis=0)  13.1 us
    all_to_all x1, waiting for transfers between devices, on_device(): lax.all_to_all(weight_part, ('y', 'x'), split_axis=0, concat_axis=0)  10.5 us
    ppermute x3, starting transfers between devices, on_device(): lax.ppermute(share, 'zq', [(i, (i + k) % RING) for i in range(RING)])  10.2 us
    ppermute x6, starting transfers between devices, swap(): return lax.ppermute(x, axis, [(0, 1), (1, 0)])  9.36 us
  transfers between devices with their start and end apart: 13, of which 7 were waited for; matrix products, arithmetic and copies ran while one was open for 3% of the time, Pallas kernels for 6%

profile of v2, /device:TPU:2, one launch (start us, length us, event | category | flops | bytes accessed | tf_op | source)
XLA Modules:
  0.0 197.9 jit_solution(9148324145476773573)
XLA Ops:
  7.2 0.9 constant_dynamic-update-slice_fusion.7
  8.1 6.4 %collective-permute-start.2 = (bf16[16,1280]{1,0:T(8,128)(2,1)S(1)}, bf16[16,1280]{1,0:T(8,128)(2,1)S(1)}, u32[]{:S(2)}, u32[]{:S(2)}) collective-permute-start(bf16[16,1280]{1,0:T(8,128)(2,1)S(1)} %get-tuple-element.22), channel_id=1, source_target_pairs={{0,12},{4,0},{8,4},{12,8},{1,13},{5,1},{9,5},{13,9},{2,14},{6,2},{... | collective-permute-start | bytes 122888 | tf_op jit(solution)/shard_map/ppermute | solution.py:303
  14.5 3.8 %collective-permute-start.3 = (bf16[16,1280]{1,0:T(8,128)(2,1)S(1)}, bf16[16,1280]{1,0:T(8,128)(2,1)S(1)}, u32[]{:S(2)}, u32[]{:S(2)}) collective-permute-start(bf16[16,1280]{1,0:T(8,128)(2,1)S(1)} %get-tuple-element.22), channel_id=1, source_target_pairs={{0,8},{4,12},{8,0},{12,4},{1,9},{5,13},{9,1},{13,5},{2,10},{6,14},... | collective-permute-start | bytes 122888 | tf_op jit(solution)/shard_map/ppermute | solution.py:303
  18.3 4.1 %collective-permute-done.3 = bf16[16,1280]{1,0:T(8,128)(2,1)S(1)} collective-permute-done((bf16[16,1280]{1,0:T(8,128)(2,1)S(1)}, bf16[16,1280]{1,0:T(8,128)(2,1)S(1)}, u32[]{:S(2)}, u32[]{:S(2)}) %collective-permute-start.3) | collective-permute-done | bytes 40992 | tf_op jit(solution)/shard_map/ppermute | solution.py:303
  22.4 0.7 constant_dynamic-slice_fusion
  23.1 0.7 reshape.35.gain_ref
  23.8 1.1 copy-done.4
  24.9 2.5 %shard_map.85 = bf16[16,160,128]{2,1,0:T(8,128)(2,1)} custom-call(bf16[256,1280]{1,0:T(8,128)(2,1)S(1)} %copy-done.4), custom_call_target="tpu_custom_call" | custom-call | tf_op jit(solution)/shard_map/pallas_call | solution.py:193
  27.7 1.3 collective-permute-start
  29.0 5.4 %all-to-all-start = ((bf16[16,160,128]{2,1,0:T(8,128)(2,1)}), bf16[16,160,128]{2,1,0:T(8,128)(2,1)S(1)}, u32[]{:S(2)}, u32[]{:S(2)}) async-start(bf16[16,160,128]{2,1,0:T(8,128)(2,1)} %shard_map.85), calls=%async_computation | async-start | bytes 1310720 | tf_op jit(solution)/shard_map/all_to_all | solution.py:311
  34.4 15.7 %collective-permute-done = bf16[256,1280]{1,0:T(8,128)(2,1)S(1)} collective-permute-done((bf16[256,1280]{1,0:T(8,128)(2,1)S(1)}, bf16[256,1280]{1,0:T(8,128)(2,1)S(1)}, u32[]{:S(2)}, u32[]{:S(2)}) %collective-permute-start) | collective-permute-done | bytes 655392 | tf_op jit(solution)/shard_map/ppermute | solution.py:289
  50.3 5.3 %all-to-all-done.in_ref = bf16[16,160,128]{2,1,0:T(8,128)(2,1)S(1)} async-done(((bf16[16,160,128]{2,1,0:T(8,128)(2,1)}), bf16[16,160,128]{2,1,0:T(8,128)(2,1)S(1)}, u32[]{:S(2)}, u32[]{:S(2)}) %all-to-all-start) | async-done | bytes 655392 | tf_op jit(solution)/shard_map/all_to_all | solution.py:311
  55.7 8.0 %shard_map.87 = bf16[4,4,160,128]{3,2,1,0:T(8,128)(2,1)} custom-call(s32[2]{0:T(128)S(1)} %pad_add_fusion.place_ref, s32[4096]{0:T(1024)S(1)} %bitcast.20, bf16[16,160,128]{2,1,0:T(8,128)(2,1)S(1)} %all-to-all-done.in_ref), custom_call_target="tpu_custom_call" | custom-call | tf_op jit(solution)/shard_map/pallas_call | solution.py:203
  63.7 5.1 %all-to-all-start.1 = ((bf16[4,4,160,128]{3,2,1,0:T(8,128)(2,1)}), bf16[4,4,160,128]{3,2,1,0:T(8,128)(2,1)}, u32[]{:S(2)}, u32[]{:S(2)}) async-start(bf16[4,4,160,128]{3,2,1,0:T(8,128)(2,1)} %shard_map.87), calls=%async_computation.1 | async-start | bytes 1310720 | tf_op jit(solution)/shard_map/all_to_all | solution.py:313
  68.9 1.7 pad_maximum_fusion.normed_ref
  70.5 13.1 %all-to-all-done.1.up_ref = bf16[4,4,160,128]{3,2,1,0:T(8,128)(2,1)} async-done(((bf16[4,4,160,128]{3,2,1,0:T(8,128)(2,1)}), bf16[4,4,160,128]{3,2,1,0:T(8,128)(2,1)}, u32[]{:S(2)}, u32[]{:S(2)}) %all-to-all-start.1) | async-done | bytes 655392 | tf_op jit(solution)/shard_map/all_to_all | solution.py:313
  83.6 1.7 copy-done
  85.4 17.9 %shard_map.88 = (bf16[1024,1024]{1,0:T(8,128)(2,1)S(1)}, bf16[16,4,16,1280]{3,2,1,0:T(8,128)(2,1)}, f32[1,1280]{1,0:T(1,128)S(1)}) custom-call(s32[2]{0:T(128)S(1)} %pad_add_fusion.place_ref, bf16[1024,1280]{1,0:T(8,128)(2,1)S(1)} %pad_maximum_fusion.normed_ref, bf16[16,4,16,1280]{3,2,1,0:T(8,128)(2,1)S(1)} %bitcast.17, ...), custom_call_target="tpu_custom_call" | custom-call | tf_op jit(solution)/shard_map/pallas_call | solution.py:225
  103.2 4.6 %shard_map.89 = (f32[512,1280]{1,0:T(8,128)S(1)}, bf16[512,1280]{1,0:T(8,128)(2,1)}) custom-call(bf16[1024,1024]{1,0:T(8,128)(2,1)S(1)} %get-tuple-element.16.grad_ref, bf16[16,4,16,1280]{3,2,1,0:T(8,128)(2,1)S(1)} %bitcast.18), custom_call_target="tpu_custom_call" | custom-call | tf_op jit(solution)/shard_map/pallas_call | solution.py:259
  107.9 1.6 collective-permute-start.7
  109.5 7.5 %all-to-all-start.2 = ((bf16[16,4,16,1280]{3,2,1,0:T(8,128)(2,1)}), bf16[16,4,16,1280]{3,2,1,0:T(8,128)(2,1)}, u32[]{:S(2)}, u32[]{:S(2)}) async-start(bf16[16,4,16,1280]{3,2,1,0:T(8,128)(2,1)} %get-tuple-element.14), calls=%async_computation.2 | async-start | bytes 5242880 | tf_op jit(solution)/shard_map/all_to_all | solution.py:322
  117.0 1.3 add_convert_fusion
  118.3 6.2 %collective-permute-start.8 = (bf16[256,1280]{1,0:T(8,128)(2,1)S(1)}, bf16[256,1280]{1,0:T(8,128)(2,1)S(1)}, u32[]{:S(2)}, u32[]{:S(2)}) collective-permute-start(bf16[256,1280]{1,0:T(8,128)(2,1)S(1)} %get-tuple-element.23), channel_id=1, source_target_pairs={{0,2},{2,0},{1,3},{3,1},{4,6},{6,4},{5,7},{7,5},{8,10},{10,8},{9,1... | collective-permute-start | bytes 1966088 | tf_op jit(solution)/shard_map/ppermute | solution.py:289
  124.5 1.2 collective-permute-done.5
  125.8 13.5 %collective-permute-done.6 = f32[1,1280]{1,0:T(1,128)S(1)} collective-permute-done((f32[1,1280]{1,0:T(1,128)S(1)}, f32[1,1280]{1,0:T(1,128)S(1)}, u32[]{:S(2)}, u32[]{:S(2)}) %collective-permute-start.6) | collective-permute-done | bytes 5152 | tf_op jit(solution)/shard_map/ppermute | solution.py:289
  139.4 1.1 slice.27.core_ref
  140.6 1.5 shard_map.90
  142.1 10.5 %all-to-all-done.2 = bf16[16,4,16,1280]{3,2,1,0:T(8,128)(2,1)} async-done(((bf16[16,4,16,1280]{3,2,1,0:T(8,128)(2,1)}), bf16[16,4,16,1280]{3,2,1,0:T(8,128)(2,1)}, u32[]{:S(2)}, u32[]{:S(2)}) %all-to-all-start.2) | async-done | bytes 2621472 | tf_op jit(solution)/shard_map/all_to_all | solution.py:322
  152.5 2.1 %reduce_sum.33 = bf16[4,16,1280]{2,1,0:T(8,128)(2,1)S(1)} reduce(bf16[16,4,16,1280]{3,2,1,0:T(8,128)(2,1)} %all-to-all-done.2, bf16[]{:T(256)} %constant.39.clone.1), dimensions={0}, to_apply=%region_0.1 | reduce | flops 1228800 | bytes 2785282 | tf_op jit(solution)/shard_map/reduce_sum | solution.py:323
  154.7 16.3 %all_to_all.25 = bf16[4,16,1408]{2,1,0:T(8,128)(2,1)S(1)} all-to-all(bf16[4,16,1408]{2,1,0:T(8,128)(2,1)S(1)} %pad_maximum_fusion.2), channel_id=1, replica_groups=mesh['y'=4,'x'=4,'zq'=4,'zp'=2,'core'=2] {'zq'}, dimensions={0} | all-to-all | bytes 360448 | tf_op jit(solution)/shard_map/all_to_all | solution.py:335
  171.1 18.2 %all_to_all.26 = bf16[16,16,1408]{2,1,0:T(8,128)(2,1)S(1)} all-to-all(bf16[16,16,1408]{2,1,0:T(8,128)(2,1)S(1)} %broadcast_in_dim.5), channel_id=1, replica_groups=mesh['y'=4,'x'=4,'zq'=4,'zp'=2,'core'=2] {'y','x'}, dimensions={0} | all-to-all | bytes 1441792 | tf_op jit(solution)/shard_map/all_to_all | solution.py:338
  190.0 1.1 convert_bitcast_fusion
  (49 shorter events, 1.7 us)
Async XLA Ops:
  7.2 20.3 %copy-start.2 = (bf16[256,1280]{1,0:T(8,128)(2,1)S(1)}, bf16[256,1280]{1,0:T(8,128)(2,1)}, u32[]{:S(2)}) copy-start(bf16[256,1280]{1,0:T(8,128)(2,1)} %rows_ref.4) | copy-start | bytes 1966084
  7.2 76.4 %all-gather.2.cloned.1.call-start = ((), (), s32[]{:S(2)}) async-start(), calls=%async_computation.5 | async-start | bytes 2785280 | tf_op jit(solution)/shard_map/all_gather | solution.py:306
  8.1 10.2 %collective-permute-start.2 = (bf16[16,1280]{1,0:T(8,128)(2,1)S(1)}, bf16[16,1280]{1,0:T(8,128)(2,1)S(1)}, u32[]{:S(2)}, u32[]{:S(2)}) collective-permute-start(bf16[16,1280]{1,0:T(8,128)(2,1)S(1)} %get-tuple-element.22), channel_id=1, source_target_pairs={{0,12},{4,0},{8,4},{12,8},{1,13},{5,1},{9,5},{13,9},{2,14},{6,2},{... | collective-permute-start | bytes 122888 | tf_op jit(solution)/shard_map/ppermute | solution.py:303
  14.5 7.9 %collective-permute-start.4 = (bf16[16,1280]{1,0:T(8,128)(2,1)S(1)}, bf16[16,1280]{1,0:T(8,128)(2,1)S(1)}, u32[]{:S(2)}, u32[]{:S(2)}) collective-permute-start(bf16[16,1280]{1,0:T(8,128)(2,1)S(1)} %get-tuple-element.22), channel_id=1, source_target_pairs={{0,4},{4,8},{8,12},{12,0},{1,5},{5,9},{9,13},{13,1},{2,6},{6,10},{... | collective-permute-start | bytes 122888 | tf_op jit(solution)/shard_map/ppermute | solution.py:303
  14.5 7.9 %collective-permute-start.3 = (bf16[16,1280]{1,0:T(8,128)(2,1)S(1)}, bf16[16,1280]{1,0:T(8,128)(2,1)S(1)}, u32[]{:S(2)}, u32[]{:S(2)}) collective-permute-start(bf16[16,1280]{1,0:T(8,128)(2,1)S(1)} %get-tuple-element.22), channel_id=1, source_target_pairs={{0,8},{4,12},{8,0},{12,4},{1,9},{5,13},{9,1},{13,5},{2,10},{6,14},... | collective-permute-start | bytes 122888 | tf_op jit(solution)/shard_map/ppermute | solution.py:303
  23.8 1.1 copy-start.4
  27.4 28.2 %copy-start.5 = (s32[1,4096]{1,0:T(1,128)S(1)}, s32[1,4096]{1,0:T(1,128)}, u32[]{:S(2)}) copy-start(s32[1,4096]{1,0:T(1,128)} %param.8) | copy-start | bytes 49156
  27.7 22.4 %collective-permute-start = (bf16[256,1280]{1,0:T(8,128)(2,1)S(1)}, bf16[256,1280]{1,0:T(8,128)(2,1)S(1)}, u32[]{:S(2)}, u32[]{:S(2)}) collective-permute-start(bf16[256,1280]{1,0:T(8,128)(2,1)S(1)} %shard_map.86), channel_id=1, source_target_pairs={{0,2},{2,0},{1,3},{3,1},{4,6},{6,4},{5,7},{7,5},{8,10},{10,8},{9,1... | collective-permute-start | bytes 1966088 | tf_op jit(solution)/shard_map/ppermute | solution.py:289
  29.0 26.7 %all-to-all-start = ((bf16[16,160,128]{2,1,0:T(8,128)(2,1)}), bf16[16,160,128]{2,1,0:T(8,128)(2,1)S(1)}, u32[]{:S(2)}, u32[]{:S(2)}) async-start(bf16[16,160,128]{2,1,0:T(8,128)(2,1)} %shard_map.85), calls=%async_computation | async-start | bytes 1310720 | tf_op jit(solution)/shard_map/all_to_all | solution.py:311
  34.4 34.4 %copy-start.8 = (s32[1,4096]{1,0:T(1,128)S(1)}, s32[1,4096]{1,0:T(1,128)}, u32[]{:S(2)}) copy-start(s32[1,4096]{1,0:T(1,128)} %param.9) | copy-start | bytes 49156
  50.1 18.8 %copy-start.6 = (bf16[256,1280]{1,0:T(8,128)(2,1)}, bf16[256,1280]{1,0:T(8,128)(2,1)S(1)}, u32[]{:S(2)}) copy-start(bf16[256,1280]{1,0:T(8,128)(2,1)S(1)} %collective-permute-done) | copy-start | bytes 1966084
  50.2 18.7 %collective-permute-start.1 = (bf16[512,1280]{1,0:T(8,128)(2,1)S(1)}, bf16[512,1280]{1,0:T(8,128)(2,1)}, u32[]{:S(2)}, u32[]{:S(2)}) collective-permute-start(bf16[512,1280]{1,0:T(8,128)(2,1)S(1)} %pad_maximum_fusion.1), channel_id=1, source_target_pairs={{0,1},{1,0},{2,3},{3,2},{4,5},{5,4},{6,7},{7,6},{8,9},{9,8},{10,11... | collective-permute-start | bytes 3932168 | tf_op jit(solution)/shard_map/ppermute | solution.py:289
  63.7 19.9 %all-to-all-start.1 = ((bf16[4,4,160,128]{3,2,1,0:T(8,128)(2,1)}), bf16[4,4,160,128]{3,2,1,0:T(8,128)(2,1)}, u32[]{:S(2)}, u32[]{:S(2)}) async-start(bf16[4,4,160,128]{3,2,1,0:T(8,128)(2,1)} %shard_map.87), calls=%async_computation.1 | async-start | bytes 1310720 | tf_op jit(solution)/shard_map/all_to_all | solution.py:313
  83.6 1.7 copy-start
  85.4 17.9 %copy-start.1 = (bf16[1024,1280]{1,0:T(8,128)(2,1)S(1)}, bf16[1024,1280]{1,0:T(8,128)(2,1)}, u32[]{:S(2)}) copy-start(bf16[1024,1280]{1,0:T(8,128)(2,1)} %all-gather.2.cloned.1.call-done) | copy-start | bytes 7864324
  107.9 9.1 %collective-permute-start.7 = (bf16[512,1280]{1,0:T(8,128)(2,1)}, bf16[512,1280]{1,0:T(8,128)(2,1)}, u32[]{:S(2)}, u32[]{:S(2)}) collective-permute-start(bf16[512,1280]{1,0:T(8,128)(2,1)} %get-tuple-element.18), channel_id=1, source_target_pairs={{0,1},{1,0},{2,3},{3,2},{4,5},{5,4},{6,7},{7,6},{8,9},{9,8},{10,11... | collective-permute-start | bytes 3932168 | tf_op jit(solution)/shard_map/ppermute | solution.py:289
  109.5 43.1 %all-to-all-start.2 = ((bf16[16,4,16,1280]{3,2,1,0:T(8,128)(2,1)}), bf16[16,4,16,1280]{3,2,1,0:T(8,128)(2,1)}, u32[]{:S(2)}, u32[]{:S(2)}) async-start(bf16[16,4,16,1280]{3,2,1,0:T(8,128)(2,1)} %get-tuple-element.14), calls=%async_computation.2 | async-start | bytes 5242880 | tf_op jit(solution)/shard_map/all_to_all | solution.py:322
  116.9 23.6 %copy-start.3 = (bf16[256,1280]{1,0:T(8,128)(2,1)S(1)}, bf16[256,1280]{1,0:T(8,128)(2,1)}, u32[]{:S(2)}) copy-start(bf16[256,1280]{1,0:T(8,128)(2,1)} %rows_ref.4) | copy-start | bytes 1966084
  118.3 22.2 %collective-permute-start.8 = (bf16[256,1280]{1,0:T(8,128)(2,1)S(1)}, bf16[256,1280]{1,0:T(8,128)(2,1)S(1)}, u32[]{:S(2)}, u32[]{:S(2)}) collective-permute-start(bf16[256,1280]{1,0:T(8,128)(2,1)S(1)} %get-tuple-element.23), channel_id=1, source_target_pairs={{0,2},{2,0},{1,3},{3,1},{4,6},{6,4},{5,7},{7,5},{8,10},{10,8},{9,1... | collective-permute-start | bytes 1966088 | tf_op jit(solution)/shard_map/ppermute | solution.py:289
  124.5 1.2 collective-permute-start.5
  125.7 13.7 %collective-permute-start.6 = (f32[1,1280]{1,0:T(1,128)S(1)}, f32[1,1280]{1,0:T(1,128)S(1)}, u32[]{:S(2)}, u32[]{:S(2)}) collective-permute-start(f32[1,1280]{1,0:T(1,128)S(1)} %add.34), channel_id=1, source_target_pairs={{0,2},{2,0},{1,3},{3,1},{4,6},{6,4},{5,7},{7,5},{8,10},{10,8},{9,1... | collective-permute-start | bytes 15368 | tf_op jit(solution)/shard_map/ppermute | solution.py:289
  142.1 47.2 %copy-start.7 = (f32[1280]{0:T(1024)S(1)}, f32[1280]{0:T(1024)}, u32[]{:S(2)}) copy-start(f32[1280]{0:T(1024)} %param.11) | copy-start | bytes 15364
Sparse Core Ops, SparseCore 0:
  23.3 51.0 all-gather.1

commit v3 on v2

--- a/solution.py
+++ b/solution.py
@@ -104,67 +104,99 @@
     out_ref[...] = (values * inverse * gain_ref[...]).astype(bf16)
 
 
+def shifted(shape, move):
+    row = lax.broadcasted_iota(jnp.int32, shape, 0)
+    return jnp.where(move(row, lanes(shape)), 1.0, 0.0).astype(bf16)
+
+
 def head_kernel(
-    place_ref, normed_ref, w_ref, up_ref, window_ref, grad_ref, weight_ref, gain_ref,
-    first, second, key_at, query_at, upstream,
+    place_ref, normed_ref, turned_ref, w_ref, up_ref, window_ref, grad_ref, weight_ref,
+    first, second, key_at, query_at, upstream, same,
 ):
-    head = pl.program_id(0)
     ring, slot = place_ref[0], place_ref[1]
     scaling = HEAD ** (-0.5)
-    w = w_ref[:, 0].reshape(PADDED, w_ref.shape[-1])
     total_rows = SLOTS * CHUNK
-    low = dot(normed_ref[...], w, NT).astype(bf16)
-    first[...] = low[:, :128]
-    second[...] = low[:, 128:]
-    rounded = low.astype(f32)
-    at = lanes((total_rows, PADDED))
-    key_at[...] = jnp.where(at < HEAD, roll(rounded, -HEAD), 0.0)[:, :128].astype(bf16)
-    query_at[...] = jnp.where(
-        (at >= HEAD) & (at < 2 * HEAD), roll(rounded, HEAD), 0.0
-    ).astype(bf16)
-    for c in range(SLOTS):
-        one, two = unpack(
-            up_ref[0, c, :128, :].astype(f32), up_ref[0, c, 128:, :].astype(f32), 32
-        )
-        upstream[CHUNK * c : CHUNK * c + 128, :] = one.astype(bf16)
-        upstream[CHUNK * c + 128 : CHUNK * c + 256, :] = two.astype(bf16)
+    width = w_ref.shape[-1]
     blocks = [slice(SUPER * b, SUPER * b + SUPER) for b in range(total_rows // SUPER)]
-    scores = [dot(first[r, :], key_at[r, :], NT) for r in blocks]
-    grad_probs = [dot(upstream[r, :], second[r, :], NT) for r in blocks]
-    probs, grad_scores = [], []
-    for b in range(len(blocks)):
+    to_key = shifted((PADDED, 128), lambda r, c: (c < HEAD) & (r == c + HEAD))
+    to_query = shifted(
+        (128, PADDED), lambda r, c: (c >= HEAD) & (c < 2 * HEAD) & (r == c - HEAD)
+    )
+    to_wide = shifted(
+        (128, 128), lambda r, c: (c >= 32) & (c < 96) & (r % 64 == c - 32)
+    )
+    to_rest = shifted(
+        (128, 128), lambda r, c: (c >= 96) & (c < 112) & (r % 16 == c - 96)
+    )
+    row = lax.broadcasted_iota(jnp.int32, (CHUNK, 128), 0)
+    keep_wide = row // 128 == lanes((CHUNK, 128)) // 64
+    keep_rest = row // 32 == lanes((CHUNK, 128)) // 16
+
+    def project(h):
+        w = w_ref[:, h].reshape(PADDED, width)
+        low = dot(normed_ref[...], w, NT).astype(bf16)
+        first[h] = low[:, :128]
+        second[h] = low[:, 128:]
+        rounded = low.astype(f32)
+        at = lanes((total_rows, PADDED))
+        key_at[h] = jnp.where(at < HEAD, roll(rounded, -HEAD), 0.0)[:, :128].astype(bf16)
+        query_at[h] = jnp.where(
+            (at >= HEAD) & (at < 2 * HEAD), roll(rounded, HEAD), 0.0
+        ).astype(bf16)
+
+    def spread(h):
+        for c in range(SLOTS):
+            top, low = up_ref[h, c, :128, :], up_ref[h, c, 128:, :]
+            wide = jnp.where(keep_wide, jnp.concatenate([top] * 2, axis=0), 0.0)
+            rest = jnp.where(keep_rest, jnp.concatenate([low] * 8, axis=0), 0.0)
+            both = dot(wide.astype(bf16), to_wide, NN) + dot(rest.astype(bf16), to_rest, NN)
+            upstream[h, CHUNK * c : CHUNK * c + CHUNK, :] = both.astype(bf16)
+
+    def attend(h):
+        cols = slice(PADDED * h, PADDED * h + 128)
+        more = slice(PADDED * h + 128, PADDED * h + PADDED)
+        scores = [dot(first[h, r, :], key_at[h, r, :], NT) for r in blocks]
+        grad_probs = [dot(upstream[h, r, :], second[h, r, :], NT) for r in blocks]
+        probs, grad_scores = [], []
+        for b, r in enumerate(blocks):
+            masked = scores[b] * scaling + same[r, :]
+            powers = jnp.exp(masked - jnp.max(masked, axis=-1, keepdims=True))
+            prob = powers * (1.0 / jnp.sum(powers, axis=-1, keepdims=True))
+            row_dot = jnp.sum(prob * grad_probs[b], axis=-1, keepdims=True)
+            grad_scores.append((prob * (grad_probs[b] - row_dot)).astype(bf16))
+            probs.append(prob.astype(bf16))
+        for b, r in enumerate(blocks):
+            grad_query = dot(grad_scores[b], key_at[h, r, :], NN)
+            grad_key = dot(grad_scores[b], query_at[h, r, :], TN)
+            grad_value = dot(probs[b], upstream[h, r, :], TN)
+            grad_ref[r, cols] = ((grad_query + grad_key[:, :128]) * scaling).astype(bf16)
+            grad_ref[r, more] = (grad_key[:, 128:] * scaling + grad_value).astype(bf16)
+
+    def weigh(h):
+        grads = grad_ref[:, PADDED * h : PADDED * h + PADDED]
+        part = dot(turned_ref[...], grads, NN).astype(bf16)
+        weight_ref[:, h] = part.reshape(16, width // 16, PADDED)
+
+    for b, r in enumerate(blocks):
         line = ring * 8 + (slot ^ XOR_ORDER[b // 2]) * 2 + b % 2
         labels = jnp.broadcast_to(window_ref[pl.ds(line, 1), :], (SUPER, SUPER))
-        masked = jnp.where(labels == labels.T, scores[b] * scaling, -1e30)
-        powers = jnp.exp(masked - jnp.max(masked, axis=-1, keepdims=True))
-        prob = powers / jnp.sum(powers, axis=-1, keepdims=True)
-        row_dot = jnp.sum(prob * grad_probs[b], axis=-1, keepdims=True)
-        grad_scores.append((prob * (grad_probs[b] - row_dot)).astype(bf16))
-        probs.append(prob.astype(bf16))
-    for b, r in enumerate(blocks):
-        grad_query = dot(grad_scores[b], key_at[r, :], NN)
-        grad_key = dot(grad_scores[b], query_at[r, :], TN)
-        grad_value = dot(probs[b], upstream[r, :], TN)
-        grad_ref[r, :128] = ((grad_query + grad_key[:, :128]) * scaling).astype(bf16)
-        grad_ref[r, 128:] = (grad_key[:, 128:] * scaling + grad_value).astype(bf16)
-    part = dot(grad_ref[...], normed_ref[...], TN)
-    weight_ref[:, 0] = part.astype(bf16).reshape(16, 16, part.shape[1])
-    gained = jnp.sum(part * w.astype(f32), axis=0, keepdims=True)
-
-    @pl.when(head == 0)
-    def _():
-        gain_ref[...] = gained
-
-    @pl.when(head > 0)
-    def _():
-        gain_ref[...] += gained
-
-
-def back_kernel(grad_ref, w_ref, keep_ref, send_ref):
+        same[r, :] = jnp.where(labels == labels.T, 0.0, -1e30)
+    project(0)
+    spread(0)
+    for h in range(RING):
+        if h + 1 < RING:
+            project(h + 1)
+            spread(h + 1)
+        attend(h)
+        weigh(h)
+
+
+def back_kernel(grad_ref, w_ref, normed_ref, keep_ref, send_ref, gain_ref):
     parts = [w_ref[:, h].reshape(PADDED, w_ref.shape[-1]) for h in range(RING)]
     total = dot(grad_ref[...], jnp.concatenate(parts, axis=0), NN)
     keep_ref[...] = total[: 2 * CHUNK]
     send_ref[...] = total[2 * CHUNK :].astype(bf16)
+    gain_ref[...] = jnp.sum(total * normed_ref[...].astype(f32), axis=0, keepdims=True)
 
 
 def final_kernel(rows_ref, gain_ref, keep_ref, core_ref, pair_ref, out_ref):
@@ -220,40 +252,29 @@
     )(rows, gain)
 
 
-def head_call(place, normed, weights, upstream, windows):
+def head_call(place, normed, turned, weights, upstream, windows):
     rows, width = normed.shape
     return pl.pallas_call(
         head_kernel,
-        grid=(RING,),
         out_shape=(
             jax.ShapeDtypeStruct((rows, RING * PADDED), bf16),
-            jax.ShapeDtypeStruct((16, RING, 16, width), bf16),
-            jax.ShapeDtypeStruct((1, width), f32),
+            jax.ShapeDtypeStruct((16, RING, width // 16, PADDED), bf16),
         ),
-        in_specs=[
-            smem(),
-            pl.BlockSpec((rows, width), lambda h: (0, 0)),
-            pl.BlockSpec((16, 1, 16, width), lambda h: (0, h, 0, 0)),
-            pl.BlockSpec((1, SLOTS, LINES, 128), lambda h: (h, 0, 0, 0)),
-            pl.BlockSpec((32, 128), lambda h: (0, 0)),
+        in_specs=[smem()] + [vmem()] * 5,
+        out_specs=(vmem(), vmem()),
+        scratch_shapes=[
+            pltpu.VMEM((RING, rows, 128), bf16),
+            pltpu.VMEM((RING, rows, 128), bf16),
+            pltpu.VMEM((RING, rows, 128), bf16),
+            pltpu.VMEM((RING, rows, PADDED), bf16),
+            pltpu.VMEM((RING, rows, 128), bf16),
+            pltpu.VMEM((rows, SUPER), f32),
         ],
-        out_specs=(
-            pl.BlockSpec((rows, PADDED), lambda h: (0, h)),
-            pl.BlockSpec((16, 1, 16, width), lambda h: (0, h, 0, 0)),
-            pl.BlockSpec((1, width), lambda h: (0, 0)),
-        ),
-        scratch_shapes=[
-            pltpu.VMEM((rows, 128), bf16),
-            pltpu.VMEM((rows, 128), bf16),
-            pltpu.VMEM((rows, 128), bf16),
-            pltpu.VMEM((rows, PADDED), bf16),
-            pltpu.VMEM((rows, 128), bf16),
-        ],
-        compiler_params=params(),
-    )(place, normed, weights, upstream, windows)
-
-
-def back_call(grads, weights):
+        compiler_params=params(),
+    )(place, normed, turned, weights, upstream, windows)
+
+
+def back_call(grads, weights, normed):
     rows, width = grads.shape[0], weights.shape[-1]
     piece = 256
     return pl.pallas_call(
@@ -262,17 +283,20 @@
         out_shape=(
             jax.ShapeDtypeStruct((2 * CHUNK, width), f32),
             jax.ShapeDtypeStruct((2 * CHUNK, width), bf16),
+            jax.ShapeDtypeStruct((1, width), f32),
         ),
         in_specs=[
             pl.BlockSpec((rows, RING * PADDED), lambda n: (0, 0)),
             pl.BlockSpec((16, RING, 16, piece), lambda n: (0, 0, 0, n)),
+            pl.BlockSpec((rows, piece), lambda n: (0, n)),
         ],
         out_specs=(
             pl.BlockSpec((2 * CHUNK, piece), lambda n: (0, n)),
             pl.BlockSpec((2 * CHUNK, piece), lambda n: (0, n)),
+            pl.BlockSpec((1, piece), lambda n: (0, n)),
         ),
         compiler_params=params(),
-    )(grads, weights)
+    )(grads, weights, normed)
 
 
 def final_call(rows, gain, keep, from_core, from_pair):
@@ -297,49 +321,49 @@
     place = jnp.stack([ring, slot]).astype(jnp.int32)
     gain_row = gain.reshape(1, width)
 
+    packed = pack_call(grad_packed)
     flipped = jnp.swapaxes(w_qkv, 1, 2).reshape(3 * HEAD, width)
     flipped = jnp.pad(flipped, ((0, PADDED - 3 * HEAD), (0, 0)))
     share = lax.dynamic_slice(flipped, (16 * dp, 0), (16, width))
+    packed, share = lax.optimization_barrier((packed, share))
     others = [lax.ppermute(share, "zq", [(i, (i + k) % RING) for i in range(RING)]) for k in (3, 2, 1)]
     circle = jnp.concatenate([share] + others + [share] + others, axis=0)
     ordered = lax.dynamic_slice(circle, (16 * ((RING - ring) % RING), 0), (16 * RING, width))
     weights = lax.all_gather(ordered, ("y", "x"), axis=0, tiled=True)
     weights = weights.reshape(16, RING, 16, width)
 
-    packed = pack_call(grad_packed)
-    packed, rows_in = lax.optimization_barrier((packed, layer_input))
     by_head = lax.all_to_all(packed, ("zq", "zp", "core"), split_axis=0, concat_axis=0)
+    own = norm_call(layer_input, gain_row)
+    by_head, own = lax.optimization_barrier((by_head, own))
     permuted = permute_call(place, source_row.reshape(-1), by_head)
     upstream = lax.all_to_all(permuted, "zq", split_axis=0, concat_axis=0)
 
-    own = norm_call(rows_in, gain_row)
     half = jnp.concatenate([own, swap(own, "zp")], axis=0)
     normed = jnp.concatenate([half, swap(half, "core")], axis=0)
-
     windows = window_id.reshape(32, 128).astype(f32)
-    grads, weight_part, gain_part = head_call(place, normed, weights, upstream, windows)
+    grads, weight_part = head_call(place, normed, normed.T, weights, upstream, windows)
 
     arrived = lax.all_to_all(weight_part, ("y", "x"), split_axis=0, concat_axis=0)
     summed = jnp.sum(arrived.astype(f32), axis=0).astype(bf16)
+    keep, send, gain_part = back_call(grads, weights, normed)
+    from_core = swap(send, "core")
+    pair = (keep[CHUNK:] + from_core[CHUNK:].astype(f32)).astype(bf16)
     gain_part = gain_part + swap(gain_part, "core")
     gain_part = gain_part + swap(gain_part, "zp")
-    beside = jnp.pad(gain_part.reshape(10, 128), ((0, 6), (0, 0))).astype(bf16)
-    beside = jnp.broadcast_to(beside[None], (RING, 16, 128))
-    keep, send = back_call(grads, weights)
-    from_core = swap(send, "core")
-    pair = (keep[CHUNK:] + from_core[CHUNK:].astype(f32)).astype(bf16)
+    beside = gain_part.reshape(width // 16, 16).astype(bf16)
+    beside = jnp.broadcast_to(beside[None], (RING, width // 16, 16))
+    message = jnp.concatenate([summed[..., : 3 * HEAD], beside], axis=2)
+    message, pair = lax.optimization_barrier((message, pair))
     from_pair = swap(pair, "zp")
-    grad_input = final_call(layer_input, gain_row, keep[:CHUNK], from_core[:CHUNK], from_pair)
-    message = jnp.concatenate([summed, beside], axis=2)
-    message, grad_input = lax.optimization_barrier((message, grad_input))
     arrived = lax.all_to_all(message, "zq", split_axis=0, concat_axis=0)
     summed = jnp.sum(arrived.astype(f32), axis=0).astype(bf16)
     copies = jnp.broadcast_to(summed[None], (16,) + summed.shape)
+    copies, from_pair = lax.optimization_barrier((copies, from_pair))
     whole = lax.all_to_all(copies, ("y", "x"), split_axis=0, concat_axis=0)
-    gradient = whole[:, :, :width].reshape(PADDED, width)[: 3 * HEAD].astype(f32)
-    grad_weight = jnp.swapaxes(gradient.reshape(3, HEAD, width), 1, 2)
-    grad_gain = jnp.sum(whole[:, :10, width:].astype(f32), axis=0).reshape(width) / gain
-
+    gradient = whole.reshape(width, PADDED).astype(f32)
+    grad_weight = jnp.stack([gradient[:, HEAD * j : HEAD * j + HEAD] for j in range(3)])
+    grad_gain = jnp.sum(whole[:, :, 3 * HEAD :].astype(f32), axis=0).reshape(width) / gain
+    grad_input = final_call(layer_input, gain_row, keep[:CHUNK], from_core[:CHUNK], from_pair)
     return (grad_input, grad_weight, grad_gain)
 
 

time: 201 us -> 215 us (1.070)
  local copies, waits for them, and re-layouts: 6.35 us -> 23.4 us
  waiting for transfers between devices: 63.3 us -> 77.1 us
  blocking collectives: 34.5 us -> 21.1 us
  Pallas kernels: 34.8 us -> 29.8 us
    all_to_all x1 -> x0, blocking collectives: 18.2 us -> none  [on_device(): whole = lax.all_to_all(copies, ('y', 'x'), split_axis=0, concat_axis=0)]
    all_to_all x1, waiting for transfers between devices: 5.31 us -> 18 us  [on_device(): lax.all_to_all(packed, ('zq', 'zp', 'core'), split_axis=0, concat_axis=0)]
    unnamed x25 -> x40, local copies, waits for them, and re-layouts: 3.74 us -> 15.2 us
    all_to_all x0 -> x1, starting transfers between devices: none -> 8.55 us  [on_device(): whole = lax.all_to_all(copies, ('y', 'x'), split_axis=0, concat_axis=0)]
    ppermute x6, waiting for transfers between devices: 30.4 us -> 22 us  [swap(): return lax.ppermute(x, axis, [(0, 1), (1, 0)])]
    all_to_all x0 -> x1, waiting for transfers between devices: none -> 7.8 us  [on_device(): whole = lax.all_to_all(copies, ('y', 'x'), split_axis=0, concat_axis=0)]
    ppermute x6, starting transfers between devices: 9.36 us -> 2.71 us  [swap(): return lax.ppermute(x, axis, [(0, 1), (1, 0)])]
    pallas_call x1, Pallas kernels: 17.9 us -> 12.6 us  [head_call(): pl.pallas_call(head_kernel, out_shape=(jax.ShapeDtypeStruct((rows, RING *...]
  transfers between devices with their start and end apart: 13 -> 14, of which waited for: 7 -> 8; matrix products, arithmetic and copies ran while one was open for 3% -> 5% of each run, Pallas kernels for 6% -> 7%
where the time goes in v3:
time: 215 us; the launch traced here: 212 us
  waiting for transfers between devices  77.1 us (36%)
  starting transfers between devices  39.6 us (18%)
  Pallas kernels  29.8 us (14%)
  local copies, waits for them, and re-layouts  23.4 us (11%)
  blocking collectives  21.1 us (10%)
  between operations  14.3 us (7%)
  other arithmetic  7.02 us (3%)
    ppermute x6, waiting for transfers between devices, swap(): return lax.ppermute(x, axis, [(0, 1), (1, 0)])  22 us
    all_to_all x1, blocking collectives, on_device(): arrived = lax.all_to_all(message, 'zq', split_axis=0, concat_axis=0)  21.1 us
    all_to_all x1, waiting for transfers between devices, on_device(): lax.all_to_all(packed, ('zq', 'zp', 'core'), split_axis=0, concat_axis=0)  18 us
    unnamed x40, local copies, waits for them, and re-layouts  15.2 us
    all_to_all x1, waiting for transfers between devices, on_device(): lax.all_to_all(weight_part, ('y', 'x'), split_axis=0, concat_axis=0)  13.5 us
    all_to_all x1, waiting for transfers between devices, on_device(): upstream = lax.all_to_all(permuted, 'zq', split_axis=0, concat_axis=0)  13.5 us
    pallas_call x1, Pallas kernels, head_call(): pl.pallas_call(head_kernel, out_shape=(jax.ShapeDtypeStruct((rows, RING *...  12.6 us
    ppermute x3, starting transfers between devices, on_device(): lax.ppermute(share, 'zq', [(i, (i + k) % RING) for i in range(RING)])  11.4 us
  transfers between devices with their start and end apart: 14, of which 8 were waited for; matrix products, arithmetic and copies ran while one was open for 5% of the time, Pallas kernels for 7%

profile of v3, /device:TPU:2, one launch (start us, length us, event | category | flops | bytes accessed | tf_op | source)
XLA Modules:
  0.0 212.3 jit_solution(18373497758838894922)
XLA Ops:
  8.3 2.5 %shard_map.85 = bf16[16,160,128]{2,1,0:T(8,128)(2,1)} custom-call(bf16[256,1280]{1,0:T(8,128)(2,1)S(1)} %copy-done.9), custom_call_target="tpu_custom_call" | custom-call | tf_op jit(solution)/shard_map/pallas_call | solution.py:225
  11.6 3.3 %collective-permute-start.4 = (bf16[16,1280]{1,0:T(8,128)(2,1)S(1)}, bf16[16,1280]{1,0:T(8,128)(2,1)S(1)}, u32[]{:S(2)}, u32[]{:S(2)}) collective-permute-start(bf16[16,1280]{1,0:T(8,128)(2,1)S(1)} %pad_dynamic-slice_fusion), channel_id=1, source_target_pairs={{0,4},{4,8},{8,12},{12,0},{1,5},{5,9},{9,13},{13,1},{2,6},{6,10},{... | collective-permute-start | bytes 122888 | tf_op jit(solution)/shard_map/ppermute | solution.py:329
  14.9 5.4 %collective-permute-start.3 = (bf16[16,1280]{1,0:T(8,128)(2,1)S(1)}, bf16[16,1280]{1,0:T(8,128)(2,1)S(1)}, u32[]{:S(2)}, u32[]{:S(2)}) collective-permute-start(bf16[16,1280]{1,0:T(8,128)(2,1)S(1)} %pad_dynamic-slice_fusion), channel_id=1, source_target_pairs={{0,8},{4,12},{8,0},{12,4},{1,9},{5,13},{9,1},{13,5},{2,10},{6,14},... | collective-permute-start | bytes 122888 | tf_op jit(solution)/shard_map/ppermute | solution.py:329
  20.3 2.7 %collective-permute-start.2 = (bf16[16,1280]{1,0:T(8,128)(2,1)S(1)}, bf16[16,1280]{1,0:T(8,128)(2,1)S(1)}, u32[]{:S(2)}, u32[]{:S(2)}) collective-permute-start(bf16[16,1280]{1,0:T(8,128)(2,1)S(1)} %pad_dynamic-slice_fusion), channel_id=1, source_target_pairs={{0,12},{4,0},{8,4},{12,8},{1,13},{5,1},{9,5},{13,9},{2,14},{6,2},{... | collective-permute-start | bytes 122888 | tf_op jit(solution)/shard_map/ppermute | solution.py:329
  23.0 2.2 %collective-permute-done.2 = bf16[16,1280]{1,0:T(8,128)(2,1)S(1)} collective-permute-done((bf16[16,1280]{1,0:T(8,128)(2,1)S(1)}, bf16[16,1280]{1,0:T(8,128)(2,1)S(1)}, u32[]{:S(2)}, u32[]{:S(2)}) %collective-permute-start.2) | collective-permute-done | bytes 40992 | tf_op jit(solution)/shard_map/ppermute | solution.py:329
  26.1 5.3 %all-to-all-start = ((bf16[16,160,128]{2,1,0:T(8,128)(2,1)}), bf16[16,160,128]{2,1,0:T(8,128)(2,1)S(1)}, u32[]{:S(2)}, u32[]{:S(2)}) async-start(bf16[16,160,128]{2,1,0:T(8,128)(2,1)} %shard_map.85), calls=%async_computation | async-start | bytes 1310720 | tf_op jit(solution)/shard_map/all_to_all | solution.py:335
  31.6 18.0 %all-to-all-done.in_ref = bf16[16,160,128]{2,1,0:T(8,128)(2,1)S(1)} async-done(((bf16[16,160,128]{2,1,0:T(8,128)(2,1)}), bf16[16,160,128]{2,1,0:T(8,128)(2,1)S(1)}, u32[]{:S(2)}, u32[]{:S(2)}) %all-to-all-start) | async-done | bytes 655392 | tf_op jit(solution)/shard_map/all_to_all | solution.py:335
  49.9 16.2 %collective-permute-done = bf16[256,1280]{1,0:T(8,128)(2,1)S(1)} collective-permute-done((bf16[256,1280]{1,0:T(8,128)(2,1)S(1)}, bf16[256,1280]{1,0:T(8,128)(2,1)S(1)}, u32[]{:S(2)}, u32[]{:S(2)}) %collective-permute-start) | collective-permute-done | bytes 655392 | tf_op jit(solution)/shard_map/ppermute | solution.py:313
  68.8 8.0 %shard_map.87 = bf16[4,4,160,128]{3,2,1,0:T(8,128)(2,1)} custom-call(s32[2]{0:T(128)S(1)} %pad_add_fusion.place_ref, s32[4096]{0:T(1024)S(1)} %bitcast.23, bf16[16,160,128]{2,1,0:T(8,128)(2,1)S(1)} %all-to-all-done.in_ref), custom_call_target="tpu_custom_call" | custom-call | tf_op jit(solution)/shard_map/pallas_call | solution.py:235
  76.8 4.3 %all-to-all-start.1 = ((bf16[4,4,160,128]{3,2,1,0:T(8,128)(2,1)}), bf16[4,4,160,128]{3,2,1,0:T(8,128)(2,1)}, u32[]{:S(2)}, u32[]{:S(2)}) async-start(bf16[4,4,160,128]{3,2,1,0:T(8,128)(2,1)} %shard_map.87), calls=%async_computation.1 | async-start | bytes 1310720 | tf_op jit(solution)/shard_map/all_to_all | solution.py:339
  82.4 1.4 constant_dynamic-update-slice_fusion.normed_ref
  83.8 2.7 %copy.12.turned_ref = bf16[1280,1024]{1,0:T(8,128)(2,1)} copy(bf16[1280,1024]{0,1:T(8,128)(2,1)S(1)} %bitcast.19) | data formatting | bytes 5242880 | tf_op jit(solution)/shard_map/transpose | solution.py:344
  86.5 13.5 %all-to-all-done.1.up_ref = bf16[4,4,160,128]{3,2,1,0:T(8,128)(2,1)} async-done(((bf16[4,4,160,128]{3,2,1,0:T(8,128)(2,1)}), bf16[4,4,160,128]{3,2,1,0:T(8,128)(2,1)}, u32[]{:S(2)}, u32[]{:S(2)}) %all-to-all-start.1) | async-done | bytes 655392 | tf_op jit(solution)/shard_map/all_to_all | solution.py:339
  100.0 1.7 copy-done
  101.7 1.7 copy-done.2
  103.5 12.6 %shard_map.88 = (bf16[1024,1024]{1,0:T(8,128)(2,1)S(1)}, bf16[16,4,80,256]{3,2,1,0:T(8,128)(2,1)S(1)}) custom-call(s32[2]{0:T(128)S(1)} %pad_add_fusion.place_ref, bf16[1024,1280]{1,0:T(8,128)(2,1)S(1)} %constant_dynamic-update-slice_fusion.normed_ref, bf16[1280,1024]{1,0:T(8,128)(2,1)S(1)} %copy-done.2, bf16[16,4,16,1280]{3,2,1,0:T(8,128)(2,1)S(1)} %bitcast.20, ...), custom_call_target="tpu_custom_call" | custom-call | tf_op jit(solution)/shard_map/pallas_call | solution.py:257
  116.1 1.5 copy-done.3
  119.1 7.3 %all-to-all-start.2 = ((bf16[16,4,80,256]{3,2,1,0:T(8,128)(2,1)}), bf16[16,4,80,256]{3,2,1,0:T(8,128)(2,1)}, u32[]{:S(2)}, u32[]{:S(2)}) async-start(bf16[16,4,80,256]{3,2,1,0:T(8,128)(2,1)} %copy-done.3), calls=%async_computation.2 | async-start | bytes 5242880 | tf_op jit(solution)/shard_map/all_to_all | solution.py:346
  126.4 1.7 copy-done.1
  128.1 1.6 copy-done.8
  129.7 4.9 %shard_map.89 = (f32[512,1280]{1,0:T(8,128)S(1)}, bf16[512,1280]{1,0:T(8,128)(2,1)}, f32[1,1280]{1,0:T(1,128)S(1)}) custom-call(bf16[1024,1024]{1,0:T(8,128)(2,1)S(1)} %copy-done.8, bf16[16,4,16,1280]{3,2,1,0:T(8,128)(2,1)S(1)} %bitcast.21, bf16[1024,1280]{1,0:T(8,128)(2,1)S(1)} %constant_dynamic-update-slice_fusion.normed_ref), custom_call_target="tpu_custom_call" | custom-call | tf_op jit(solution)/shard_map/pallas_call | solution.py:280
  134.6 1.5 copy-done.4
  136.6 2.2 %collective-permute-done.6 = f32[1,1280]{1,0:T(1,128)S(1)} collective-permute-done((f32[1,1280]{1,0:T(1,128)S(1)}, f32[1,1280]{1,0:T(1,128)S(1)}, u32[]{:S(2)}, u32[]{:S(2)}) %collective-permute-start.6) | collective-permute-done | bytes 5152 | tf_op jit(solution)/shard_map/ppermute | solution.py:313
  138.8 3.6 %collective-permute-done.7 = f32[1,1280]{1,0:T(1,128)S(1)} collective-permute-done((f32[1,1280]{1,0:T(1,128)S(1)}, f32[1,1280]{1,0:T(1,128)S(1)}, u32[]{:S(2)}, u32[]{:S(2)}) %collective-permute-start.7) | collective-permute-done | bytes 5152 | tf_op jit(solution)/shard_map/ppermute | solution.py:313
  142.5 2.4 %add_convert_fusion = (bf16[256,1280]{1,0:T(8,128)(2,1)S(1)}, f32[256,1280]{1,0:T(8,128)S(1)}) fusion(f32[512,1280]{1,0:T(8,128)} %copy-done.4, bf16[512,1280]{1,0:T(8,128)(2,1)S(1)} %collective-permute-done.5), kind=kLoop, calls=%fused_computation.2 | loop fusion | flops 983040 | bytes 5242880 | tf_op jit(solution)/shard_map/convert_element_type | solution.py:350
  144.9 13.5 %all-to-all-done.2 = bf16[16,4,80,256]{3,2,1,0:T(8,128)(2,1)} async-done(((bf16[16,4,80,256]{3,2,1,0:T(8,128)(2,1)}), bf16[16,4,80,256]{3,2,1,0:T(8,128)(2,1)}, u32[]{:S(2)}, u32[]{:S(2)}) %all-to-all-start.2) | async-done | bytes 2621472 | tf_op jit(solution)/shard_map/all_to_all | solution.py:346
  158.4 2.1 %reduce_sum.33 = bf16[4,80,256]{2,1,0:T(8,128)(2,1)S(1)} reduce(bf16[16,4,80,256]{3,2,1,0:T(8,128)(2,1)} %all-to-all-done.2, bf16[]{:T(256)} %constant.37.clone.1), dimensions={0}, to_apply=%region_0.1 | reduce | flops 1228800 | bytes 2785282 | tf_op jit(solution)/shard_map/reduce_sum | solution.py:347
  161.3 21.1 %all_to_all.25 = bf16[4,80,256]{2,1,0:T(8,128)(2,1)S(1)} all-to-all(bf16[4,80,256]{2,1,0:T(8,128)(2,1)S(1)} %pad_maximum_fusion.2), channel_id=1, replica_groups=mesh['y'=4,'x'=4,'zq'=4,'zp'=2,'core'=2] {'zq'}, dimensions={0} | all-to-all | bytes 327680 | tf_op jit(solution)/shard_map/all_to_all | solution.py:358
  183.3 8.5 %all-to-all-start.4 = ((bf16[16,80,256]{2,1,0:T(8,128)(2,1)}), bf16[16,80,256]{2,1,0:T(8,128)(2,1)S(1)}, u32[]{:S(2)}, u32[]{:S(2)}) async-start(bf16[16,80,256]{2,1,0:T(8,128)(2,1)} %broadcast_in_dim.5), calls=%async_computation.4 | async-start | bytes 1310720 | tf_op jit(solution)/shard_map/all_to_all | solution.py:362
  193.0 1.5 shard_map.90
  194.5 7.8 %all-to-all-done.4 = bf16[16,80,256]{2,1,0:T(8,128)(2,1)S(1)} async-done(((bf16[16,80,256]{2,1,0:T(8,128)(2,1)}), bf16[16,80,256]{2,1,0:T(8,128)(2,1)S(1)}, u32[]{:S(2)}, u32[]{:S(2)}) %all-to-all-start.4) | async-done | bytes 655392 | tf_op jit(solution)/shard_map/all_to_all | solution.py:362
  203.8 1.6 copy.13
  (69 shorter events, 13.4 us)
Async XLA Ops:
  7.2 92.8 %all-gather.2.cloned.1.call-start = ((), (), s32[]{:S(2)}) async-start(), calls=%async_computation.5 | async-start | bytes 2785280 | tf_op jit(solution)/shard_map/all_gather | solution.py:332
  7.2 1.1 copy-start.9
  8.3 23.0 %copy-start.13 = (f32[1280]{0:T(1024)S(1)}, f32[1280]{0:T(1024)}, u32[]{:S(2)}) copy-start(f32[1280]{0:T(1024)} %param.11) | copy-start | bytes 15364
  8.3 23.0 %copy-start.5 = (bf16[256,1280]{1,0:T(8,128)(2,1)S(1)}, bf16[256,1280]{1,0:T(8,128)(2,1)}, u32[]{:S(2)}) copy-start(bf16[256,1280]{1,0:T(8,128)(2,1)} %rows_ref.5) | copy-start | bytes 1966084
  11.6 13.7 %collective-permute-start.4 = (bf16[16,1280]{1,0:T(8,128)(2,1)S(1)}, bf16[16,1280]{1,0:T(8,128)(2,1)S(1)}, u32[]{:S(2)}, u32[]{:S(2)}) collective-permute-start(bf16[16,1280]{1,0:T(8,128)(2,1)S(1)} %pad_dynamic-slice_fusion), channel_id=1, source_target_pairs={{0,4},{4,8},{8,12},{12,0},{1,5},{5,9},{9,13},{13,1},{2,6},{6,10},{... | collective-permute-start | bytes 122888 | tf_op jit(solution)/shard_map/ppermute | solution.py:329
  14.9 10.3 %collective-permute-start.3 = (bf16[16,1280]{1,0:T(8,128)(2,1)S(1)}, bf16[16,1280]{1,0:T(8,128)(2,1)S(1)}, u32[]{:S(2)}, u32[]{:S(2)}) collective-permute-start(bf16[16,1280]{1,0:T(8,128)(2,1)S(1)} %pad_dynamic-slice_fusion), channel_id=1, source_target_pairs={{0,8},{4,12},{8,0},{12,4},{1,9},{5,13},{9,1},{13,5},{2,10},{6,14},... | collective-permute-start | bytes 122888 | tf_op jit(solution)/shard_map/ppermute | solution.py:329
  20.3 4.9 %collective-permute-start.2 = (bf16[16,1280]{1,0:T(8,128)(2,1)S(1)}, bf16[16,1280]{1,0:T(8,128)(2,1)S(1)}, u32[]{:S(2)}, u32[]{:S(2)}) collective-permute-start(bf16[16,1280]{1,0:T(8,128)(2,1)S(1)} %pad_dynamic-slice_fusion), channel_id=1, source_target_pairs={{0,12},{4,0},{8,4},{12,8},{1,13},{5,1},{9,5},{13,9},{2,14},{6,2},{... | collective-permute-start | bytes 122888 | tf_op jit(solution)/shard_map/ppermute | solution.py:329
  26.1 23.6 %all-to-all-start = ((bf16[16,160,128]{2,1,0:T(8,128)(2,1)}), bf16[16,160,128]{2,1,0:T(8,128)(2,1)S(1)}, u32[]{:S(2)}, u32[]{:S(2)}) async-start(bf16[16,160,128]{2,1,0:T(8,128)(2,1)} %shard_map.85), calls=%async_computation | async-start | bytes 1310720 | tf_op jit(solution)/shard_map/all_to_all | solution.py:335
  31.4 37.5 %copy-start.10 = (s32[1,4096]{1,0:T(1,128)S(1)}, s32[1,4096]{1,0:T(1,128)}, u32[]{:S(2)}) copy-start(s32[1,4096]{1,0:T(1,128)} %param.8) | copy-start | bytes 49156
  49.7 16.5 %collective-permute-start = (bf16[256,1280]{1,0:T(8,128)(2,1)S(1)}, bf16[256,1280]{1,0:T(8,128)(2,1)S(1)}, u32[]{:S(2)}, u32[]{:S(2)}) collective-permute-start(bf16[256,1280]{1,0:T(8,128)(2,1)S(1)} %shard_map.86), channel_id=1, source_target_pairs={{0,2},{2,0},{1,3},{3,1},{4,6},{6,4},{5,7},{7,5},{8,10},{10,8},{9,1... | collective-permute-start | bytes 1966088 | tf_op jit(solution)/shard_map/ppermute | solution.py:313
  66.1 15.1 %copy-start.11 = (bf16[256,1280]{1,0:T(8,128)(2,1)}, bf16[256,1280]{1,0:T(8,128)(2,1)S(1)}, u32[]{:S(2)}) copy-start(bf16[256,1280]{1,0:T(8,128)(2,1)S(1)} %collective-permute-done) | copy-start | bytes 1966084
  67.4 13.8 %copy-start.14 = (s32[1,4096]{1,0:T(1,128)S(1)}, s32[1,4096]{1,0:T(1,128)}, u32[]{:S(2)}) copy-start(s32[1,4096]{1,0:T(1,128)} %param.9) | copy-start | bytes 49156
  67.4 15.1 %collective-permute-start.1 = (bf16[512,1280]{1,0:T(8,128)(2,1)}, bf16[512,1280]{1,0:T(8,128)(2,1)}, u32[]{:S(2)}, u32[]{:S(2)}) collective-permute-start(bf16[512,1280]{1,0:T(8,128)(2,1)} %pad_maximum_fusion.1), channel_id=1, source_target_pairs={{0,1},{1,0},{2,3},{3,2},{4,5},{5,4},{6,7},{7,6},{8,9},{9,8},{10,11... | collective-permute-start | bytes 3932168 | tf_op jit(solution)/shard_map/ppermute | solution.py:313
  76.8 23.2 %all-to-all-start.1 = ((bf16[4,4,160,128]{3,2,1,0:T(8,128)(2,1)}), bf16[4,4,160,128]{3,2,1,0:T(8,128)(2,1)}, u32[]{:S(2)}, u32[]{:S(2)}) async-start(bf16[4,4,160,128]{3,2,1,0:T(8,128)(2,1)} %shard_map.87), calls=%async_computation.1 | async-start | bytes 1310720 | tf_op jit(solution)/shard_map/all_to_all | solution.py:339
  100.0 1.7 copy-start
  101.7 1.7 copy-start.2
  116.1 1.6 copy-start.3
  117.7 1.4 copy-start.7
  119.1 39.3 %all-to-all-start.2 = ((bf16[16,4,80,256]{3,2,1,0:T(8,128)(2,1)}), bf16[16,4,80,256]{3,2,1,0:T(8,128)(2,1)}, u32[]{:S(2)}, u32[]{:S(2)}) async-start(bf16[16,4,80,256]{3,2,1,0:T(8,128)(2,1)} %copy-done.3), calls=%async_computation.2 | async-start | bytes 5242880 | tf_op jit(solution)/shard_map/all_to_all | solution.py:346
  126.4 1.7 copy-start.1
  128.1 1.6 copy-start.8
  134.6 1.5 copy-start.4
  136.1 6.4 %collective-permute-start.5 = (bf16[512,1280]{1,0:T(8,128)(2,1)}, bf16[512,1280]{1,0:T(8,128)(2,1)S(1)}, u32[]{:S(2)}, u32[]{:S(2)}) collective-permute-start(bf16[512,1280]{1,0:T(8,128)(2,1)} %get-tuple-element.22), channel_id=1, source_target_pairs={{0,1},{1,0},{2,3},{3,2},{4,5},{5,4},{6,7},{7,6},{8,9},{9,8},{10,11... | collective-permute-start | bytes 3932168 | tf_op jit(solution)/shard_map/ppermute | solution.py:313
  136.1 2.7 %collective-permute-start.6 = (f32[1,1280]{1,0:T(1,128)S(1)}, f32[1,1280]{1,0:T(1,128)S(1)}, u32[]{:S(2)}, u32[]{:S(2)}) collective-permute-start(f32[1,1280]{1,0:T(1,128)S(1)} %get-tuple-element.24), channel_id=1, source_target_pairs={{0,1},{1,0},{2,3},{3,2},{4,5},{5,4},{6,7},{7,6},{8,9},{9,8},{10,11... | collective-permute-start | bytes 15368 | tf_op jit(solution)/shard_map/ppermute | solution.py:313
  138.8 3.6 %collective-permute-start.7 = (f32[1,1280]{1,0:T(1,128)S(1)}, f32[1,1280]{1,0:T(1,128)S(1)}, u32[]{:S(2)}, u32[]{:S(2)}) collective-permute-start(f32[1,1280]{1,0:T(1,128)S(1)} %add.32), channel_id=1, source_target_pairs={{0,2},{2,0},{1,3},{3,1},{4,6},{6,4},{5,7},{7,5},{8,10},{10,8},{9,1... | collective-permute-start | bytes 15368 | tf_op jit(solution)/shard_map/ppermute | solution.py:313
  142.5 2.4 %copy-start.12 = (bf16[512,1280]{1,0:T(8,128)(2,1)}, bf16[512,1280]{1,0:T(8,128)(2,1)S(1)}, u32[]{:S(2)}) copy-start(bf16[512,1280]{1,0:T(8,128)(2,1)S(1)} %collective-permute-done.5) | copy-start | bytes 3932164
  160.7 32.4 %copy-start.6 = (bf16[256,1280]{1,0:T(8,128)(2,1)S(1)}, bf16[256,1280]{1,0:T(8,128)(2,1)}, u32[]{:S(2)}) copy-start(bf16[256,1280]{1,0:T(8,128)(2,1)} %rows_ref.5) | copy-start | bytes 1966084
  160.7 21.8 %collective-permute-start.8 = (bf16[256,1280]{1,0:T(8,128)(2,1)S(1)}, bf16[256,1280]{1,0:T(8,128)(2,1)S(1)}, u32[]{:S(2)}, u32[]{:S(2)}) collective-permute-start(bf16[256,1280]{1,0:T(8,128)(2,1)S(1)} %get-tuple-element.26), channel_id=1, source_target_pairs={{0,2},{2,0},{1,3},{3,1},{4,6},{6,4},{5,7},{7,5},{8,10},{10,8},{9,1... | collective-permute-start | bytes 1966088 | tf_op jit(solution)/shard_map/ppermute | solution.py:313
  183.3 19.0 %all-to-all-start.4 = ((bf16[16,80,256]{2,1,0:T(8,128)(2,1)}), bf16[16,80,256]{2,1,0:T(8,128)(2,1)S(1)}, u32[]{:S(2)}, u32[]{:S(2)}) async-start(bf16[16,80,256]{2,1,0:T(8,128)(2,1)} %broadcast_in_dim.5), calls=%async_computation.4 | async-start | bytes 1310720 | tf_op jit(solution)/shard_map/all_to_all | solution.py:362
Sparse Core Ops, SparseCore 0:
  26.2 50.5 all-gather.1

commit v4 on v3

--- a/solution.py
+++ b/solution.py
@@ -22,7 +22,8 @@
 NT = (((1,), (1,)), ((), ()))
 TN = (((0,), (0,)), ((), ()))
 NN = (((1,), (0,)), ((), ()))
-BIG = 28 * 1024 * 1024
+BIG = 34 * 1024 * 1024
+SMALL = 20 * 1024 * 1024
 
 
 def dot(a, b, dims):
@@ -110,18 +111,31 @@
 
 
 def head_kernel(
-    place_ref, normed_ref, turned_ref, w_ref, up_ref, window_ref, grad_ref, weight_ref,
+    place_ref, normed_ref, turned_hbm, w_hbm, up_ref, window_ref, grad_hbm, weight_hbm,
     first, second, key_at, query_at, upstream, same,
+    turned_ref, w_ref, grad_ref, weight_ref, in_sems, out_sems,
 ):
     ring, slot = place_ref[0], place_ref[1]
     scaling = HEAD ** (-0.5)
     total_rows = SLOTS * CHUNK
-    width = w_ref.shape[-1]
+    width = normed_ref.shape[-1]
     blocks = [slice(SUPER * b, SUPER * b + SUPER) for b in range(total_rows // SUPER)]
-    to_key = shifted((PADDED, 128), lambda r, c: (c < HEAD) & (r == c + HEAD))
-    to_query = shifted(
-        (128, PADDED), lambda r, c: (c >= HEAD) & (c < 2 * HEAD) & (r == c - HEAD)
-    )
+    w_copies = [
+        pltpu.make_async_copy(w_hbm.at[:, h], w_ref.at[h], in_sems.at[h]) for h in range(RING)
+    ]
+    turned_copy = pltpu.make_async_copy(turned_hbm, turned_ref, in_sems.at[RING])
+    w_copies[0].start()
+    for h in range(1, RING):
+        w_copies[h].start()
+    turned_copy.start()
+    grad_copies = [
+        pltpu.make_async_copy(grad_ref.at[h], grad_hbm.at[h], out_sems.at[h])
+        for h in range(RING)
+    ]
+    weight_copies = [
+        pltpu.make_async_copy(weight_ref.at[h], weight_hbm.at[:, h], out_sems.at[RING + h])
+        for h in range(RING)
+    ]
     to_wide = shifted(
         (128, 128), lambda r, c: (c >= 32) & (c < 96) & (r % 64 == c - 32)
     )
@@ -133,7 +147,7 @@
     keep_rest = row // 32 == lanes((CHUNK, 128)) // 16
 
     def project(h):
-        w = w_ref[:, h].reshape(PADDED, width)
+        w = w_ref[h].reshape(PADDED, width)
         low = dot(normed_ref[...], w, NT).astype(bf16)
         first[h] = low[:, :128]
         second[h] = low[:, 128:]
@@ -153,8 +167,6 @@
             upstream[h, CHUNK * c : CHUNK * c + CHUNK, :] = both.astype(bf16)
 
     def attend(h):
-        cols = slice(PADDED * h, PADDED * h + 128)
-        more = slice(PADDED * h + 128, PADDED * h + PADDED)
         scores = [dot(first[h, r, :], key_at[h, r, :], NT) for r in blocks]
         grad_probs = [dot(upstream[h, r, :], second[h, r, :], NT) for r in blocks]
         probs, grad_scores = [], []
@@ -169,31 +181,38 @@
             grad_query = dot(grad_scores[b], key_at[h, r, :], NN)
             grad_key = dot(grad_scores[b], query_at[h, r, :], TN)
             grad_value = dot(probs[b], upstream[h, r, :], TN)
-            grad_ref[r, cols] = ((grad_query + grad_key[:, :128]) * scaling).astype(bf16)
-            grad_ref[r, more] = (grad_key[:, 128:] * scaling + grad_value).astype(bf16)
+            grad_ref[h, r, :128] = ((grad_query + grad_key[:, :128]) * scaling).astype(bf16)
+            grad_ref[h, r, 128:] = (grad_key[:, 128:] * scaling + grad_value).astype(bf16)
 
     def weigh(h):
-        grads = grad_ref[:, PADDED * h : PADDED * h + PADDED]
-        part = dot(turned_ref[...], grads, NN).astype(bf16)
-        weight_ref[:, h] = part.reshape(16, width // 16, PADDED)
+        part = dot(turned_ref[...], grad_ref[h], NN).astype(bf16)
+        weight_ref[h] = part.reshape(16, width // 16, PADDED)
 
     for b, r in enumerate(blocks):
         line = ring * 8 + (slot ^ XOR_ORDER[b // 2]) * 2 + b % 2
         labels = jnp.broadcast_to(window_ref[pl.ds(line, 1), :], (SUPER, SUPER))
         same[r, :] = jnp.where(labels == labels.T, 0.0, -1e30)
+    spread(0)
+    w_copies[0].wait()
     project(0)
-    spread(0)
+    for copy in w_copies[1:] + [turned_copy]:
+        copy.wait()
     for h in range(RING):
         if h + 1 < RING:
             project(h + 1)
             spread(h + 1)
         attend(h)
         weigh(h)
+    for copy in weight_copies + grad_copies:
+        copy.start()
+    for copy in weight_copies + grad_copies:
+        copy.wait()
 
 
 def back_kernel(grad_ref, w_ref, normed_ref, keep_ref, send_ref, gain_ref):
     parts = [w_ref[:, h].reshape(PADDED, w_ref.shape[-1]) for h in range(RING)]
-    total = dot(grad_ref[...], jnp.concatenate(parts, axis=0), NN)
+    grads = jnp.concatenate([grad_ref[h] for h in range(RING)], axis=1)
+    total = dot(grads, jnp.concatenate(parts, axis=0), NN)
     keep_ref[...] = total[: 2 * CHUNK]
     send_ref[...] = total[2 * CHUNK :].astype(bf16)
     gain_ref[...] = jnp.sum(total * normed_ref[...].astype(f32), axis=0, keepdims=True)
@@ -217,8 +236,8 @@
     return pl.BlockSpec(memory_space=pltpu.SMEM)
 
 
-def params():
-    return pltpu.CompilerParams(vmem_limit_bytes=BIG)
+def params(limit=SMALL):
+    return pltpu.CompilerParams(vmem_limit_bytes=limit)
 
 
 def pack_call(rows):
@@ -257,11 +276,11 @@
     return pl.pallas_call(
         head_kernel,
         out_shape=(
-            jax.ShapeDtypeStruct((rows, RING * PADDED), bf16),
+            jax.ShapeDtypeStruct((RING, rows, PADDED), bf16),
             jax.ShapeDtypeStruct((16, RING, width // 16, PADDED), bf16),
         ),
-        in_specs=[smem()] + [vmem()] * 5,
-        out_specs=(vmem(), vmem()),
+        in_specs=[smem(), vmem()] + [pl.BlockSpec(memory_space=pl.ANY)] * 2 + [vmem()] * 2,
+        out_specs=(pl.BlockSpec(memory_space=pl.ANY),) * 2,
         scratch_shapes=[
             pltpu.VMEM((RING, rows, 128), bf16),
             pltpu.VMEM((RING, rows, 128), bf16),
@@ -269,13 +288,19 @@
             pltpu.VMEM((RING, rows, PADDED), bf16),
             pltpu.VMEM((RING, rows, 128), bf16),
             pltpu.VMEM((rows, SUPER), f32),
+            pltpu.VMEM((width, rows), bf16),
+            pltpu.VMEM((RING, 16, 16, width), bf16),
+            pltpu.VMEM((RING, rows, PADDED), bf16),
+            pltpu.VMEM((RING, 16, width // 16, PADDED), bf16),
+            pltpu.SemaphoreType.DMA((RING + 1,)),
+            pltpu.SemaphoreType.DMA((2 * RING,)),
         ],
-        compiler_params=params(),
+        compiler_params=params(BIG),
     )(place, normed, turned, weights, upstream, windows)
 
 
 def back_call(grads, weights, normed):
-    rows, width = grads.shape[0], weights.shape[-1]
+    rows, width = grads.shape[1], weights.shape[-1]
     piece = 256
     return pl.pallas_call(
         back_kernel,
@@ -286,7 +311,7 @@
             jax.ShapeDtypeStruct((1, width), f32),
         ),
         in_specs=[
-            pl.BlockSpec((rows, RING * PADDED), lambda n: (0, 0)),
+            pl.BlockSpec((RING, rows, PADDED), lambda n: (0, 0, 0)),
             pl.BlockSpec((16, RING, 16, piece), lambda n: (0, 0, 0, n)),
             pl.BlockSpec((rows, piece), lambda n: (0, n)),
         ],
@@ -325,16 +350,15 @@
     flipped = jnp.swapaxes(w_qkv, 1, 2).reshape(3 * HEAD, width)
     flipped = jnp.pad(flipped, ((0, PADDED - 3 * HEAD), (0, 0)))
     share = lax.dynamic_slice(flipped, (16 * dp, 0), (16, width))
-    packed, share = lax.optimization_barrier((packed, share))
     others = [lax.ppermute(share, "zq", [(i, (i + k) % RING) for i in range(RING)]) for k in (3, 2, 1)]
+    own = norm_call(layer_input, gain_row)
+    others, packed, own = lax.optimization_barrier((others, packed, own))
     circle = jnp.concatenate([share] + others + [share] + others, axis=0)
     ordered = lax.dynamic_slice(circle, (16 * ((RING - ring) % RING), 0), (16 * RING, width))
     weights = lax.all_gather(ordered, ("y", "x"), axis=0, tiled=True)
     weights = weights.reshape(16, RING, 16, width)
 
     by_head = lax.all_to_all(packed, ("zq", "zp", "core"), split_axis=0, concat_axis=0)
-    own = norm_call(layer_input, gain_row)
-    by_head, own = lax.optimization_barrier((by_head, own))
     permuted = permute_call(place, source_row.reshape(-1), by_head)
     upstream = lax.all_to_all(permuted, "zq", split_axis=0, concat_axis=0)
 
@@ -354,11 +378,11 @@
     beside = jnp.broadcast_to(beside[None], (RING, width // 16, 16))
     message = jnp.concatenate([summed[..., : 3 * HEAD], beside], axis=2)
     message, pair = lax.optimization_barrier((message, pair))
-    from_pair = swap(pair, "zp")
     arrived = lax.all_to_all(message, "zq", split_axis=0, concat_axis=0)
     summed = jnp.sum(arrived.astype(f32), axis=0).astype(bf16)
     copies = jnp.broadcast_to(summed[None], (16,) + summed.shape)
-    copies, from_pair = lax.optimization_barrier((copies, from_pair))
+    copies, pair = lax.optimization_barrier((copies, pair))
+    from_pair = swap(pair, "zp")
     whole = lax.all_to_all(copies, ("y", "x"), split_axis=0, concat_axis=0)
     gradient = whole.reshape(width, PADDED).astype(f32)
     grad_weight = jnp.stack([gradient[:, HEAD * j : HEAD * j + HEAD] for j in range(3)])

time: 215 us -> 198 us (0.921)
  waiting for transfers between devices: 77.1 us -> 52.1 us
  starting transfers between devices: 39.6 us -> 48.9 us
  blocking collectives: 21.1 us -> 14.2 us
  other arithmetic: 7.02 us -> 9.2 us
    all_to_all x1, waiting for transfers between devices: 18 us -> 3.52 us  [on_device(): lax.all_to_all(packed, ('zq', 'zp', 'core'), split_axis=0, concat_axis=0)]
    ppermute x6, starting transfers between devices: 2.71 us -> 14.6 us  [swap(): return lax.ppermute(x, axis, [(0, 1), (1, 0)])]
    all_to_all x1, blocking collectives: 21.1 us -> 14.2 us  [on_device(): arrived = lax.all_to_all(message, 'zq', split_axis=0, concat_axis=0)]
    all_to_all x1, waiting for transfers between devices: 13.5 us -> 8.87 us  [on_device(): upstream = lax.all_to_all(permuted, 'zq', split_axis=0, concat_axis=0)]
    all_to_all x1, waiting for transfers between devices: 13.5 us -> 10.7 us  [on_device(): lax.all_to_all(weight_part, ('y', 'x'), split_axis=0, concat_axis=0)]
    all_to_all x1, waiting for transfers between devices: 7.8 us -> 5.43 us  [on_device(): whole = lax.all_to_all(copies, ('y', 'x'), split_axis=0, concat_axis=0)]
    ppermute x3, waiting for transfers between devices: 2.25 us -> 0.01 us  [on_device(): lax.ppermute(share, 'zq', [(i, (i + k) % RING) for i in range(RING)])]
  transfers between devices with their start and end apart: 14 -> 14, of which waited for: 8 -> 8; matrix products, arithmetic and copies ran while one was open for 5% -> 9% of each run, Pallas kernels for 7% -> 8%
where the time goes in v4:
time: 198 us; the launch traced here: 196 us
  waiting for transfers between devices  52.1 us (26%)
  starting transfers between devices  48.9 us (25%)
  Pallas kernels  31.8 us (16%)
  local copies, waits for them, and re-layouts  25.3 us (13%)
  between operations  14.3 us (7%)
  blocking collectives  14.2 us (7%)
  other arithmetic  9.2 us (5%)
    ppermute x6, waiting for transfers between devices, swap(): return lax.ppermute(x, axis, [(0, 1), (1, 0)])  23.5 us
    unnamed x40, local copies, waits for them, and re-layouts  17.2 us
    pallas_call x1, Pallas kernels, head_call(): pl.pallas_call(head_kernel, out_shape=(jax.ShapeDtypeStruct((RING, rows,...  14.7 us
    ppermute x6, starting transfers between devices, swap(): return lax.ppermute(x, axis, [(0, 1), (1, 0)])  14.6 us
    all_to_all x1, blocking collectives, on_device(): arrived = lax.all_to_all(message, 'zq', split_axis=0, concat_axis=0)  14.2 us
    ppermute x3, starting transfers between devices, on_device(): lax.ppermute(share, 'zq', [(i, (i + k) % RING) for i in range(RING)])  11.4 us
    all_to_all x1, waiting for transfers between devices, on_device(): lax.all_to_all(weight_part, ('y', 'x'), split_axis=0, concat_axis=0)  10.7 us
    all_to_all x1, waiting for transfers between devices, on_device(): upstream = lax.all_to_all(permuted, 'zq', split_axis=0, concat_axis=0)  8.87 us
  transfers between devices with their start and end apart: 14, of which 8 were waited for; matrix products, arithmetic and copies ran while one was open for 9% of the time, Pallas kernels for 8%

profile of v4, /device:TPU:2, one launch (start us, length us, event | category | flops | bytes accessed | tf_op | source)
XLA Modules:
  0.0 195.8 jit_solution(4897038659010293075)
XLA Ops:
  8.1 3.3 %collective-permute-start.2 = (bf16[16,1280]{1,0:T(8,128)(2,1)S(1)}, bf16[16,1280]{1,0:T(8,128)(2,1)S(1)}, u32[]{:S(2)}, u32[]{:S(2)}) collective-permute-start(bf16[16,1280]{1,0:T(8,128)(2,1)S(1)} %get-tuple-element.38), channel_id=1, source_target_pairs={{0,4},{4,8},{8,12},{12,0},{1,5},{5,9},{9,13},{13,1},{2,6},{6,10},{... | collective-permute-start | bytes 122888 | tf_op jit(solution)/shard_map/ppermute | solution.py:353
  11.4 5.4 %collective-permute-start.1 = (bf16[16,1280]{1,0:T(8,128)(2,1)S(1)}, bf16[16,1280]{1,0:T(8,128)(2,1)S(1)}, u32[]{:S(2)}, u32[]{:S(2)}) collective-permute-start(bf16[16,1280]{1,0:T(8,128)(2,1)S(1)} %get-tuple-element.38), channel_id=1, source_target_pairs={{0,8},{4,12},{8,0},{12,4},{1,9},{5,13},{9,1},{13,5},{2,10},{6,14},... | collective-permute-start | bytes 122888 | tf_op jit(solution)/shard_map/ppermute | solution.py:353
  16.8 2.7 %collective-permute-start = (bf16[16,1280]{1,0:T(8,128)(2,1)S(1)}, bf16[16,1280]{1,0:T(8,128)(2,1)S(1)}, u32[]{:S(2)}, u32[]{:S(2)}) collective-permute-start(bf16[16,1280]{1,0:T(8,128)(2,1)S(1)} %get-tuple-element.38), channel_id=1, source_target_pairs={{0,12},{4,0},{8,4},{12,8},{1,13},{5,1},{9,5},{13,9},{2,14},{6,2},{... | collective-permute-start | bytes 122888 | tf_op jit(solution)/shard_map/ppermute | solution.py:353
  21.3 2.5 %shard_map.85 = bf16[16,160,128]{2,1,0:T(8,128)(2,1)} custom-call(bf16[256,1280]{1,0:T(8,128)(2,1)S(1)} %copy-done.9), custom_call_target="tpu_custom_call" | custom-call | tf_op jit(solution)/shard_map/pallas_call | solution.py:244
  26.0 3.6 %all-to-all-start = ((bf16[16,160,128]{2,1,0:T(8,128)(2,1)}), bf16[16,160,128]{2,1,0:T(8,128)(2,1)S(1)}, u32[]{:S(2)}, u32[]{:S(2)}) async-start(bf16[16,160,128]{2,1,0:T(8,128)(2,1)} %shard_map.85), calls=%async_computation | async-start | bytes 1310720 | tf_op jit(solution)/shard_map/all_to_all | solution.py:361
  29.6 18.6 %collective-permute-done.3 = bf16[256,1280]{1,0:T(8,128)(2,1)S(1)} collective-permute-done((bf16[256,1280]{1,0:T(8,128)(2,1)S(1)}, bf16[256,1280]{1,0:T(8,128)(2,1)S(1)}, u32[]{:S(2)}, u32[]{:S(2)}) %collective-permute-start.3) | collective-permute-done | bytes 655392 | tf_op jit(solution)/shard_map/ppermute | solution.py:338
  49.5 3.5 %all-to-all-done.in_ref = bf16[16,160,128]{2,1,0:T(8,128)(2,1)S(1)} async-done(((bf16[16,160,128]{2,1,0:T(8,128)(2,1)}), bf16[16,160,128]{2,1,0:T(8,128)(2,1)S(1)}, u32[]{:S(2)}, u32[]{:S(2)}) %all-to-all-start) | async-done | bytes 655392 | tf_op jit(solution)/shard_map/all_to_all | solution.py:361
  53.0 8.0 %shard_map.87 = bf16[4,4,160,128]{3,2,1,0:T(8,128)(2,1)} custom-call(s32[2]{0:T(128)S(1)} %pad_add_fusion.place_ref, s32[4096]{0:T(1024)S(1)} %bitcast.23, bf16[16,160,128]{2,1,0:T(8,128)(2,1)S(1)} %all-to-all-done.in_ref), custom_call_target="tpu_custom_call" | custom-call | tf_op jit(solution)/shard_map/pallas_call | solution.py:254
  61.1 4.4 %all-to-all-start.1 = ((bf16[4,4,160,128]{3,2,1,0:T(8,128)(2,1)}), bf16[4,4,160,128]{3,2,1,0:T(8,128)(2,1)}, u32[]{:S(2)}, u32[]{:S(2)}) async-start(bf16[4,4,160,128]{3,2,1,0:T(8,128)(2,1)} %shard_map.87), calls=%async_computation.1 | async-start | bytes 1310720 | tf_op jit(solution)/shard_map/all_to_all | solution.py:363
  68.1 2.7 %copy.12.turned_hbm = bf16[1280,1024]{1,0:T(8,128)(2,1)} copy(bf16[1280,1024]{0,1:T(8,128)(2,1)S(1)} %bitcast.19) | data formatting | bytes 5242880 | tf_op jit(solution)/shard_map/transpose | solution.py:368
  70.8 8.9 %all-to-all-done.1.up_ref = bf16[4,4,160,128]{3,2,1,0:T(8,128)(2,1)} async-done(((bf16[4,4,160,128]{3,2,1,0:T(8,128)(2,1)}), bf16[4,4,160,128]{3,2,1,0:T(8,128)(2,1)}, u32[]{:S(2)}, u32[]{:S(2)}) %all-to-all-start.1) | async-done | bytes 655392 | tf_op jit(solution)/shard_map/all_to_all | solution.py:363
  79.7 1.7 copy-done
  81.4 1.7 copy-done.2
  83.2 14.7 %shard_map.88 = (bf16[4,1024,256]{2,1,0:T(8,128)(2,1)S(1)}, bf16[16,4,80,256]{3,2,1,0:T(8,128)(2,1)S(1)}) custom-call(s32[2]{0:T(128)S(1)} %pad_add_fusion.place_ref, bf16[1024,1280]{1,0:T(8,128)(2,1)S(1)} %constant_dynamic-update-slice_fusion.normed_ref, bf16[1280,1024]{1,0:T(8,128)(2,1)S(1)} %copy-done.2, bf16[16,4,16,1280]{3,2,1,0:T(8,128)(2,1)S(1)} %bitcast.20, ...), custom_call_target="tpu_custom_call" | custom-call | tf_op jit(solution)/shard_map/pallas_call | solution.py:276
  97.8 1.5 copy-done.3
  100.8 7.5 %all-to-all-start.2 = ((bf16[16,4,80,256]{3,2,1,0:T(8,128)(2,1)}), bf16[16,4,80,256]{3,2,1,0:T(8,128)(2,1)}, u32[]{:S(2)}, u32[]{:S(2)}) async-start(bf16[16,4,80,256]{3,2,1,0:T(8,128)(2,1)} %copy-done.3), calls=%async_computation.2 | async-start | bytes 5242880 | tf_op jit(solution)/shard_map/all_to_all | solution.py:370
  108.2 1.7 copy-done.1
  110.0 1.6 copy-done.8
  111.6 4.8 %shard_map.89 = (f32[512,1280]{1,0:T(8,128)S(1)}, bf16[512,1280]{1,0:T(8,128)(2,1)}, f32[1,1280]{1,0:T(1,128)S(1)}) custom-call(bf16[4,1024,256]{2,1,0:T(8,128)(2,1)S(1)} %copy-done.8, bf16[16,4,16,1280]{3,2,1,0:T(8,128)(2,1)S(1)} %bitcast.21, bf16[1024,1280]{1,0:T(8,128)(2,1)S(1)} %constant_dynamic-update-slice_fusion.normed_ref), custom_call_target="tpu_custom_call" | custom-call | tf_op jit(solution)/shard_map/pallas_call | solution.py:305
  117.9 1.8 collective-permute-start.5
  119.8 2.5 %collective-permute-done.6 = f32[1,1280]{1,0:T(1,128)S(1)} collective-permute-done((f32[1,1280]{1,0:T(1,128)S(1)}, f32[1,1280]{1,0:T(1,128)S(1)}, u32[]{:S(2)}, u32[]{:S(2)}) %collective-permute-start.6) | collective-permute-done | bytes 5152 | tf_op jit(solution)/shard_map/ppermute | solution.py:338
  122.3 6.3 %collective-permute-start.7 = (f32[1,1280]{1,0:T(1,128)S(1)}, f32[1,1280]{1,0:T(1,128)S(1)}, u32[]{:S(2)}, u32[]{:S(2)}) collective-permute-start(f32[1,1280]{1,0:T(1,128)S(1)} %add.32), channel_id=1, source_target_pairs={{0,2},{2,0},{1,3},{3,1},{4,6},{6,4},{5,7},{7,5},{8,10},{10,8},{9,1... | collective-permute-start | bytes 15368 | tf_op jit(solution)/shard_map/ppermute | solution.py:338
  128.6 1.6 collective-permute-done.7
  130.3 3.2 %add_convert_fusion = (bf16[256,1280]{1,0:T(8,128)(2,1)}, f32[256,1280]{1,0:T(8,128)S(1)}) fusion(f32[512,1280]{1,0:T(8,128)} %copy-done.4, bf16[512,1280]{1,0:T(8,128)(2,1)S(1)} %collective-permute-done.5), kind=kLoop, calls=%fused_computation.2 | loop fusion | flops 983040 | bytes 5242880 | tf_op jit(solution)/shard_map/convert_element_type | solution.py:374
  133.6 10.7 %all-to-all-done.2 = bf16[16,4,80,256]{3,2,1,0:T(8,128)(2,1)} async-done(((bf16[16,4,80,256]{3,2,1,0:T(8,128)(2,1)}), bf16[16,4,80,256]{3,2,1,0:T(8,128)(2,1)}, u32[]{:S(2)}, u32[]{:S(2)}) %all-to-all-start.2) | async-done | bytes 2621472 | tf_op jit(solution)/shard_map/all_to_all | solution.py:370
  144.3 2.1 %reduce_sum.33 = bf16[4,80,256]{2,1,0:T(8,128)(2,1)S(1)} reduce(bf16[16,4,80,256]{3,2,1,0:T(8,128)(2,1)} %all-to-all-done.2, bf16[]{:T(256)} %constant.37.clone.1), dimensions={0}, to_apply=%region_0.1 | reduce | flops 1228800 | bytes 2785282 | tf_op jit(solution)/shard_map/reduce_sum | solution.py:371
  146.5 14.2 %all_to_all.25 = bf16[4,80,256]{2,1,0:T(8,128)(2,1)S(1)} all-to-all(bf16[4,80,256]{2,1,0:T(8,128)(2,1)S(1)} %pad_maximum_fusion.2), channel_id=1, replica_groups=mesh['y'=4,'x'=4,'zq'=4,'zp'=2,'core'=2] {'zq'}, dimensions={0} | all-to-all | bytes 327680 | tf_op jit(solution)/shard_map/all_to_all | solution.py:381
  161.7 7.5 %all-to-all-start.4 = ((bf16[16,80,256]{2,1,0:T(8,128)(2,1)}), bf16[16,80,256]{2,1,0:T(8,128)(2,1)S(1)}, u32[]{:S(2)}, u32[]{:S(2)}) async-start(bf16[16,80,256]{2,1,0:T(8,128)(2,1)} %broadcast_in_dim.5), calls=%async_computation.4 | async-start | bytes 1310720 | tf_op jit(solution)/shard_map/all_to_all | solution.py:386
  170.3 5.4 %collective-permute-start.8 = (bf16[256,1280]{1,0:T(8,128)(2,1)}, bf16[256,1280]{1,0:T(8,128)(2,1)S(1)}, u32[]{:S(2)}, u32[]{:S(2)}) collective-permute-start(bf16[256,1280]{1,0:T(8,128)(2,1)} %get-tuple-element.29), channel_id=1, source_target_pairs={{0,2},{2,0},{1,3},{3,1},{4,6},{6,4},{5,7},{7,5},{8,10},{10,8},{9,1... | collective-permute-start | bytes 1966088 | tf_op jit(solution)/shard_map/ppermute | solution.py:338
  175.7 5.4 %all-to-all-done.4 = bf16[16,80,256]{2,1,0:T(8,128)(2,1)S(1)} async-done(((bf16[16,80,256]{2,1,0:T(8,128)(2,1)}), bf16[16,80,256]{2,1,0:T(8,128)(2,1)S(1)}, u32[]{:S(2)}, u32[]{:S(2)}) %all-to-all-start.4) | async-done | bytes 655392 | tf_op jit(solution)/shard_map/all_to_all | solution.py:386
  183.9 2.7 %copy.13 = f32[3,1280,80]{1,2,0:T(8,128)} copy(f32[3,1280,80]{2,1,0:T(8,128)} %pad_maximum_fusion) | data formatting | bytes 2457600
  187.5 1.5 shard_map.90
  (68 shorter events, 17.6 us)
Async XLA Ops:
  7.2 16.6 %copy-start.5 = (bf16[256,1280]{1,0:T(8,128)(2,1)S(1)}, bf16[256,1280]{1,0:T(8,128)(2,1)}, u32[]{:S(2)}) copy-start(bf16[256,1280]{1,0:T(8,128)(2,1)} %rows_ref.5) | copy-start | bytes 1966084
  7.2 72.5 %all-gather.2.cloned.1.call-start = ((), (), s32[]{:S(2)}) async-start(), calls=%async_computation.5 | async-start | bytes 2785280 | tf_op jit(solution)/shard_map/all_gather | solution.py:358
  8.1 16.0 %collective-permute-start.2 = (bf16[16,1280]{1,0:T(8,128)(2,1)S(1)}, bf16[16,1280]{1,0:T(8,128)(2,1)S(1)}, u32[]{:S(2)}, u32[]{:S(2)}) collective-permute-start(bf16[16,1280]{1,0:T(8,128)(2,1)S(1)} %get-tuple-element.38), channel_id=1, source_target_pairs={{0,4},{4,8},{8,12},{12,0},{1,5},{5,9},{9,13},{13,1},{2,6},{6,10},{... | collective-permute-start | bytes 122888 | tf_op jit(solution)/shard_map/ppermute | solution.py:353
  11.4 12.6 %collective-permute-start.1 = (bf16[16,1280]{1,0:T(8,128)(2,1)S(1)}, bf16[16,1280]{1,0:T(8,128)(2,1)S(1)}, u32[]{:S(2)}, u32[]{:S(2)}) collective-permute-start(bf16[16,1280]{1,0:T(8,128)(2,1)S(1)} %get-tuple-element.38), channel_id=1, source_target_pairs={{0,8},{4,12},{8,0},{12,4},{1,9},{5,13},{9,1},{13,5},{2,10},{6,14},... | collective-permute-start | bytes 122888 | tf_op jit(solution)/shard_map/ppermute | solution.py:353
  16.8 7.2 %collective-permute-start = (bf16[16,1280]{1,0:T(8,128)(2,1)S(1)}, bf16[16,1280]{1,0:T(8,128)(2,1)S(1)}, u32[]{:S(2)}, u32[]{:S(2)}) collective-permute-start(bf16[16,1280]{1,0:T(8,128)(2,1)S(1)} %get-tuple-element.38), channel_id=1, source_target_pairs={{0,12},{4,0},{8,4},{12,8},{1,13},{5,1},{9,5},{13,9},{2,14},{6,2},{... | collective-permute-start | bytes 122888 | tf_op jit(solution)/shard_map/ppermute | solution.py:353
  20.2 1.1 copy-start.9
  24.9 28.1 %copy-start.10 = (s32[1,4096]{1,0:T(1,128)S(1)}, s32[1,4096]{1,0:T(1,128)}, u32[]{:S(2)}) copy-start(s32[1,4096]{1,0:T(1,128)} %param.8) | copy-start | bytes 49156
  24.9 23.3 %collective-permute-start.3 = (bf16[256,1280]{1,0:T(8,128)(2,1)S(1)}, bf16[256,1280]{1,0:T(8,128)(2,1)S(1)}, u32[]{:S(2)}, u32[]{:S(2)}) collective-permute-start(bf16[256,1280]{1,0:T(8,128)(2,1)S(1)} %shard_map.86), channel_id=1, source_target_pairs={{0,2},{2,0},{1,3},{3,1},{4,6},{6,4},{5,7},{7,5},{8,10},{10,8},{9,1... | collective-permute-start | bytes 1966088 | tf_op jit(solution)/shard_map/ppermute | solution.py:338
  26.0 27.0 %all-to-all-start = ((bf16[16,160,128]{2,1,0:T(8,128)(2,1)}), bf16[16,160,128]{2,1,0:T(8,128)(2,1)S(1)}, u32[]{:S(2)}, u32[]{:S(2)}) async-start(bf16[16,160,128]{2,1,0:T(8,128)(2,1)} %shard_map.85), calls=%async_computation | async-start | bytes 1310720 | tf_op jit(solution)/shard_map/all_to_all | solution.py:361
  48.2 12.9 %copy-start.11 = (bf16[256,1280]{1,0:T(8,128)(2,1)}, bf16[256,1280]{1,0:T(8,128)(2,1)S(1)}, u32[]{:S(2)}) copy-start(bf16[256,1280]{1,0:T(8,128)(2,1)S(1)} %collective-permute-done.3) | copy-start | bytes 1966084
  49.4 16.0 %copy-start.14 = (s32[1,4096]{1,0:T(1,128)S(1)}, s32[1,4096]{1,0:T(1,128)}, u32[]{:S(2)}) copy-start(s32[1,4096]{1,0:T(1,128)} %param.9) | copy-start | bytes 49156
  49.4 17.2 %collective-permute-start.4 = (bf16[512,1280]{1,0:T(8,128)(2,1)}, bf16[512,1280]{1,0:T(8,128)(2,1)}, u32[]{:S(2)}, u32[]{:S(2)}) collective-permute-start(bf16[512,1280]{1,0:T(8,128)(2,1)} %pad_maximum_fusion.1), channel_id=1, source_target_pairs={{0,1},{1,0},{2,3},{3,2},{4,5},{5,4},{6,7},{7,6},{8,9},{9,8},{10,11... | collective-permute-start | bytes 3932168 | tf_op jit(solution)/shard_map/ppermute | solution.py:338
  61.1 18.6 %all-to-all-start.1 = ((bf16[4,4,160,128]{3,2,1,0:T(8,128)(2,1)}), bf16[4,4,160,128]{3,2,1,0:T(8,128)(2,1)}, u32[]{:S(2)}, u32[]{:S(2)}) async-start(bf16[4,4,160,128]{3,2,1,0:T(8,128)(2,1)} %shard_map.87), calls=%async_computation.1 | async-start | bytes 1310720 | tf_op jit(solution)/shard_map/all_to_all | solution.py:363
  79.7 1.7 copy-start
  81.4 1.7 copy-start.2
  97.8 1.6 copy-start.3
  99.4 1.4 copy-start.7
  100.8 43.5 %all-to-all-start.2 = ((bf16[16,4,80,256]{3,2,1,0:T(8,128)(2,1)}), bf16[16,4,80,256]{3,2,1,0:T(8,128)(2,1)}, u32[]{:S(2)}, u32[]{:S(2)}) async-start(bf16[16,4,80,256]{3,2,1,0:T(8,128)(2,1)} %copy-done.3), calls=%async_computation.2 | async-start | bytes 5242880 | tf_op jit(solution)/shard_map/all_to_all | solution.py:370
  108.2 1.7 copy-start.1
  110.0 1.6 copy-start.8
  116.4 1.5 copy-start.4
  117.9 12.4 %collective-permute-start.5 = (bf16[512,1280]{1,0:T(8,128)(2,1)}, bf16[512,1280]{1,0:T(8,128)(2,1)S(1)}, u32[]{:S(2)}, u32[]{:S(2)}) collective-permute-start(bf16[512,1280]{1,0:T(8,128)(2,1)} %get-tuple-element.24), channel_id=1, source_target_pairs={{0,1},{1,0},{2,3},{3,2},{4,5},{5,4},{6,7},{7,6},{8,9},{9,8},{10,11... | collective-permute-start | bytes 3932168 | tf_op jit(solution)/shard_map/ppermute | solution.py:338
  119.8 2.5 %collective-permute-start.6 = (f32[1,1280]{1,0:T(1,128)S(1)}, f32[1,1280]{1,0:T(1,128)S(1)}, u32[]{:S(2)}, u32[]{:S(2)}) collective-permute-start(f32[1,1280]{1,0:T(1,128)S(1)} %get-tuple-element.26), channel_id=1, source_target_pairs={{0,1},{1,0},{2,3},{3,2},{4,5},{5,4},{6,7},{7,6},{8,9},{9,8},{10,11... | collective-permute-start | bytes 15368 | tf_op jit(solution)/shard_map/ppermute | solution.py:338
  122.3 7.9 %collective-permute-start.7 = (f32[1,1280]{1,0:T(1,128)S(1)}, f32[1,1280]{1,0:T(1,128)S(1)}, u32[]{:S(2)}, u32[]{:S(2)}) collective-permute-start(f32[1,1280]{1,0:T(1,128)S(1)} %add.32), channel_id=1, source_target_pairs={{0,2},{2,0},{1,3},{3,1},{4,6},{6,4},{5,7},{7,5},{8,10},{10,8},{9,1... | collective-permute-start | bytes 15368 | tf_op jit(solution)/shard_map/ppermute | solution.py:338
  130.3 3.3 %copy-start.12 = (bf16[512,1280]{1,0:T(8,128)(2,1)}, bf16[512,1280]{1,0:T(8,128)(2,1)S(1)}, u32[]{:S(2)}) copy-start(bf16[512,1280]{1,0:T(8,128)(2,1)S(1)} %collective-permute-done.5) | copy-start | bytes 3932164
  160.7 20.6 %copy-start.13 = (f32[1280]{0:T(1024)S(1)}, f32[1280]{0:T(1024)}, u32[]{:S(2)}) copy-start(f32[1280]{0:T(1024)} %param.11) | copy-start | bytes 15364
  161.7 19.4 %all-to-all-start.4 = ((bf16[16,80,256]{2,1,0:T(8,128)(2,1)}), bf16[16,80,256]{2,1,0:T(8,128)(2,1)S(1)}, u32[]{:S(2)}, u32[]{:S(2)}) async-start(bf16[16,80,256]{2,1,0:T(8,128)(2,1)} %broadcast_in_dim.5), calls=%async_computation.4 | async-start | bytes 1310720 | tf_op jit(solution)/shard_map/all_to_all | solution.py:386
  170.3 17.2 %collective-permute-start.8 = (bf16[256,1280]{1,0:T(8,128)(2,1)}, bf16[256,1280]{1,0:T(8,128)(2,1)S(1)}, u32[]{:S(2)}, u32[]{:S(2)}) collective-permute-start(bf16[256,1280]{1,0:T(8,128)(2,1)} %get-tuple-element.29), channel_id=1, source_target_pairs={{0,2},{2,0},{1,3},{3,1},{4,6},{6,4},{5,7},{7,5},{8,10},{10,8},{9,1... | collective-permute-start | bytes 1966088 | tf_op jit(solution)/shard_map/ppermute | solution.py:338
  183.9 3.6 %copy-start.6 = (bf16[256,1280]{1,0:T(8,128)(2,1)S(1)}, bf16[256,1280]{1,0:T(8,128)(2,1)}, u32[]{:S(2)}) copy-start(bf16[256,1280]{1,0:T(8,128)(2,1)} %rows_ref.5) | copy-start | bytes 1966084
Sparse Core Ops, SparseCore 0:
  25.0 48.2 all-gather.1

commit v5 on v4

--- a/solution.py
+++ b/solution.py
@@ -22,7 +22,7 @@
 NT = (((1,), (1,)), ((), ()))
 TN = (((0,), (0,)), ((), ()))
 NN = (((1,), (0,)), ((), ()))
-BIG = 34 * 1024 * 1024
+BIG = 58 * 1024 * 1024
 SMALL = 20 * 1024 * 1024
 
 
@@ -87,13 +87,13 @@
             base = q * SLOTS * CHUNK + (slot ^ off) * CHUNK
 
             def step(i, carry):
-                at = i * 16
-                for u in range(16):
+                at = i * 64
+                for u in range(64):
                     row = source_ref[base + at + u]
                     picked[pl.ds(at + u, 1), :] = table[pl.ds(row, 1), :]
                 return carry
 
-            lax.fori_loop(0, CHUNK // 16, step, 0)
+            lax.fori_loop(0, CHUNK // 64, step, 0)
             top, low = pack(picked[...])
             out_ref[q, o, :128, :] = top.astype(bf16)
             out_ref[q, o, 128:, :] = low.astype(bf16)
@@ -111,9 +111,9 @@
 
 
 def head_kernel(
-    place_ref, normed_ref, turned_hbm, w_hbm, up_ref, window_ref, grad_hbm, weight_hbm,
+    place_ref, normed_hbm, turned_hbm, w_hbm, up_ref, window_ref, grad_hbm, weight_hbm,
     first, second, key_at, query_at, upstream, same,
-    turned_ref, w_ref, grad_ref, weight_ref, in_sems, out_sems,
+    normed_ref, turned_ref, w_ref, grad_ref, weight_ref, in_sems, out_sems,
 ):
     ring, slot = place_ref[0], place_ref[1]
     scaling = HEAD ** (-0.5)
@@ -124,7 +124,9 @@
         pltpu.make_async_copy(w_hbm.at[:, h], w_ref.at[h], in_sems.at[h]) for h in range(RING)
     ]
     turned_copy = pltpu.make_async_copy(turned_hbm, turned_ref, in_sems.at[RING])
+    normed_copy = pltpu.make_async_copy(normed_hbm, normed_ref, in_sems.at[RING + 1])
     w_copies[0].start()
+    normed_copy.start()
     for h in range(1, RING):
         w_copies[h].start()
     turned_copy.start()
@@ -194,6 +196,7 @@
         same[r, :] = jnp.where(labels == labels.T, 0.0, -1e30)
     spread(0)
     w_copies[0].wait()
+    normed_copy.wait()
     project(0)
     for copy in w_copies[1:] + [turned_copy]:
         copy.wait()
@@ -218,7 +221,12 @@
     gain_ref[...] = jnp.sum(total * normed_ref[...].astype(f32), axis=0, keepdims=True)
 
 
-def final_kernel(rows_ref, gain_ref, keep_ref, core_ref, pair_ref, out_ref):
+def final_kernel(
+    rows_ref, gain_ref, keep_ref, core_ref, pair_ref, whole_ref, out_ref, weight_ref
+):
+    whole = whole_ref[...].reshape(weight_ref.shape[1], PADDED).astype(f32)
+    for j in range(3):
+        weight_ref[j] = roll(whole, -HEAD * j)[:, :HEAD]
     values = rows_ref[...].astype(f32)
     inverse = lax.rsqrt(jnp.mean(values * values, axis=-1, keepdims=True) + epsilon)
     scaled = values * inverse
@@ -279,7 +287,7 @@
             jax.ShapeDtypeStruct((RING, rows, PADDED), bf16),
             jax.ShapeDtypeStruct((16, RING, width // 16, PADDED), bf16),
         ),
-        in_specs=[smem(), vmem()] + [pl.BlockSpec(memory_space=pl.ANY)] * 2 + [vmem()] * 2,
+        in_specs=[smem()] + [pl.BlockSpec(memory_space=pl.ANY)] * 3 + [vmem()] * 2,
         out_specs=(pl.BlockSpec(memory_space=pl.ANY),) * 2,
         scratch_shapes=[
             pltpu.VMEM((RING, rows, 128), bf16),
@@ -288,11 +296,12 @@
             pltpu.VMEM((RING, rows, PADDED), bf16),
             pltpu.VMEM((RING, rows, 128), bf16),
             pltpu.VMEM((rows, SUPER), f32),
+            pltpu.VMEM((rows, width), bf16),
             pltpu.VMEM((width, rows), bf16),
             pltpu.VMEM((RING, 16, 16, width), bf16),
             pltpu.VMEM((RING, rows, PADDED), bf16),
             pltpu.VMEM((RING, 16, width // 16, PADDED), bf16),
-            pltpu.SemaphoreType.DMA((RING + 1,)),
+            pltpu.SemaphoreType.DMA((RING + 2,)),
             pltpu.SemaphoreType.DMA((2 * RING,)),
         ],
         compiler_params=params(BIG),
@@ -324,14 +333,27 @@
     )(grads, weights, normed)
 
 
-def final_call(rows, gain, keep, from_core, from_pair):
+def final_call(rows, gain, keep, from_core, from_pair, whole):
+    part = pl.BlockSpec(rows.shape, lambda i: (0, 0))
+    width = rows.shape[1]
     return pl.pallas_call(
         final_kernel,
-        out_shape=jax.ShapeDtypeStruct(rows.shape, bf16),
-        in_specs=[vmem()] * 5,
-        out_specs=vmem(),
+        grid=(1,),
+        out_shape=(
+            jax.ShapeDtypeStruct(rows.shape, bf16),
+            jax.ShapeDtypeStruct((3, width, HEAD), f32),
+        ),
+        in_specs=[
+            part,
+            pl.BlockSpec((1, width), lambda i: (0, 0)),
+            part,
+            part,
+            part,
+            pl.BlockSpec(whole.shape, lambda i: (0, 0, 0)),
+        ],
+        out_specs=(part, pl.BlockSpec((3, width, HEAD), lambda i: (0, 0, 0))),
         compiler_params=params(),
-    )(rows, gain, keep, from_core, from_pair)
+    )(rows, gain, keep, from_core, from_pair, whole)
 
 
 def swap(x, axis):
@@ -384,10 +406,10 @@
     copies, pair = lax.optimization_barrier((copies, pair))
     from_pair = swap(pair, "zp")
     whole = lax.all_to_all(copies, ("y", "x"), split_axis=0, concat_axis=0)
-    gradient = whole.reshape(width, PADDED).astype(f32)
-    grad_weight = jnp.stack([gradient[:, HEAD * j : HEAD * j + HEAD] for j in range(3)])
     grad_gain = jnp.sum(whole[:, :, 3 * HEAD :].astype(f32), axis=0).reshape(width) / gain
-    grad_input = final_call(layer_input, gain_row, keep[:CHUNK], from_core[:CHUNK], from_pair)
+    grad_input, grad_weight = final_call(
+        layer_input, gain_row, keep, from_core, from_pair, whole
+    )
     return (grad_input, grad_weight, grad_gain)
 
 

time: 198 us -> 205 us (1.035)
  waiting for transfers between devices: 52.1 us -> 58.5 us
  blocking collectives: 14.2 us -> 19.7 us
  starting transfers between devices: 48.9 us -> 45 us
  Pallas kernels: 31.8 us -> 35.3 us
    all_to_all x1, blocking collectives: 14.2 us -> 19.7 us  [on_device(): arrived = lax.all_to_all(message, 'zq', split_axis=0, concat_axis=0)]
    ppermute x6, starting transfers between devices: 14.6 us -> 9.23 us  [swap(): return lax.ppermute(x, axis, [(0, 1), (1, 0)])]
    all_to_all x1, waiting for transfers between devices: 5.43 us -> 10.7 us  [on_device(): whole = lax.all_to_all(copies, ('y', 'x'), split_axis=0, concat_axis=0)]
    ppermute x6, waiting for transfers between devices: 23.5 us -> 26.9 us  [swap(): return lax.ppermute(x, axis, [(0, 1), (1, 0)])]
    pallas_call x1, Pallas kernels: 14.7 us -> 17.7 us  [head_call(): pl.pallas_call(head_kernel, out_shape=(jax.ShapeDtypeStruct((RING, rows,...]
    unnamed x40 -> x44, local copies, waits for them, and re-layouts: 17.2 us -> 16.6 us
  transfers between devices with their start and end apart: 14 -> 14, of which waited for: 8 -> 8; matrix products, arithmetic and copies ran while one was open for 9% -> 6% of each run, Pallas kernels for 8% -> 7%
where the time goes in v5:
time: 205 us; the launch traced here: 204 us
  waiting for transfers between devices  58.5 us (29%)
  starting transfers between devices  45 us (22%)
  Pallas kernels  35.3 us (17%)
  local copies, waits for them, and re-layouts  23.6 us (12%)
  blocking collectives  19.7 us (10%)
  between operations  14.3 us (7%)
  other arithmetic  7.25 us (4%)
    ppermute x6, waiting for transfers between devices, swap(): return lax.ppermute(x, axis, [(0, 1), (1, 0)])  26.9 us
    all_to_all x1, blocking collectives, on_device(): arrived = lax.all_to_all(message, 'zq', split_axis=0, concat_axis=0)  19.7 us
    pallas_call x1, Pallas kernels, head_call(): pl.pallas_call(head_kernel, out_shape=(jax.ShapeDtypeStruct((RING, rows,...  17.7 us
    unnamed x44, local copies, waits for them, and re-layouts  16.6 us
    ppermute x3, starting transfers between devices, on_device(): lax.ppermute(share, 'zq', [(i, (i + k) % RING) for i in range(RING)])  11.4 us
    all_to_all x1, waiting for transfers between devices, on_device(): whole = lax.all_to_all(copies, ('y', 'x'), split_axis=0, concat_axis=0)  10.7 us
    all_to_all x1, waiting for transfers between devices, on_device(): lax.all_to_all(weight_part, ('y', 'x'), split_axis=0, concat_axis=0)  9.67 us
    ppermute x6, starting transfers between devices, swap(): return lax.ppermute(x, axis, [(0, 1), (1, 0)])  9.23 us
  transfers between devices with their start and end apart: 14, of which 8 were waited for; matrix products, arithmetic and copies ran while one was open for 6% of the time, Pallas kernels for 7%

profile of v5, /device:TPU:2, one launch (start us, length us, event | category | flops | bytes accessed | tf_op | source)
XLA Modules:
  0.0 203.8 jit_solution(13156841376037740359)
XLA Ops:
  8.0 3.3 %collective-permute-start.2 = (bf16[16,1280]{1,0:T(8,128)(2,1)S(1)}, bf16[16,1280]{1,0:T(8,128)(2,1)S(1)}, u32[]{:S(2)}, u32[]{:S(2)}) collective-permute-start(bf16[16,1280]{1,0:T(8,128)(2,1)S(1)} %get-tuple-element.45), channel_id=1, source_target_pairs={{0,4},{4,8},{8,12},{12,0},{1,5},{5,9},{9,13},{13,1},{2,6},{6,10},{... | collective-permute-start | bytes 122888 | tf_op jit(solution)/shard_map/ppermute | solution.py:375
  11.4 5.4 %collective-permute-start.1 = (bf16[16,1280]{1,0:T(8,128)(2,1)S(1)}, bf16[16,1280]{1,0:T(8,128)(2,1)S(1)}, u32[]{:S(2)}, u32[]{:S(2)}) collective-permute-start(bf16[16,1280]{1,0:T(8,128)(2,1)S(1)} %get-tuple-element.45), channel_id=1, source_target_pairs={{0,8},{4,12},{8,0},{12,4},{1,9},{5,13},{9,1},{13,5},{2,10},{6,14},... | collective-permute-start | bytes 122888 | tf_op jit(solution)/shard_map/ppermute | solution.py:375
  16.8 2.7 %collective-permute-start = (bf16[16,1280]{1,0:T(8,128)(2,1)S(1)}, bf16[16,1280]{1,0:T(8,128)(2,1)S(1)}, u32[]{:S(2)}, u32[]{:S(2)}) collective-permute-start(bf16[16,1280]{1,0:T(8,128)(2,1)S(1)} %get-tuple-element.45), channel_id=1, source_target_pairs={{0,12},{4,0},{8,4},{12,8},{1,13},{5,1},{9,5},{13,9},{2,14},{6,2},{... | collective-permute-start | bytes 122888 | tf_op jit(solution)/shard_map/ppermute | solution.py:375
  21.2 2.5 %shard_map.85 = bf16[16,160,128]{2,1,0:T(8,128)(2,1)} custom-call(bf16[256,1280]{1,0:T(8,128)(2,1)S(1)} %copy-done.11), custom_call_target="tpu_custom_call" | custom-call | tf_op jit(solution)/shard_map/pallas_call | solution.py:252
  27.0 3.6 %all-to-all-start = ((bf16[16,160,128]{2,1,0:T(8,128)(2,1)}), bf16[16,160,128]{2,1,0:T(8,128)(2,1)S(1)}, u32[]{:S(2)}, u32[]{:S(2)}) async-start(bf16[16,160,128]{2,1,0:T(8,128)(2,1)} %shard_map.85), calls=%async_computation | async-start | bytes 1310720 | tf_op jit(solution)/shard_map/all_to_all | solution.py:383
  30.6 19.0 %collective-permute-done.3 = bf16[256,1280]{1,0:T(8,128)(2,1)S(1)} collective-permute-done((bf16[256,1280]{1,0:T(8,128)(2,1)S(1)}, bf16[256,1280]{1,0:T(8,128)(2,1)S(1)}, u32[]{:S(2)}, u32[]{:S(2)}) %collective-permute-start.3) | collective-permute-done | bytes 655392 | tf_op jit(solution)/shard_map/ppermute | solution.py:360
  51.0 3.3 %all-to-all-done.in_ref = bf16[16,160,128]{2,1,0:T(8,128)(2,1)S(1)} async-done(((bf16[16,160,128]{2,1,0:T(8,128)(2,1)}), bf16[16,160,128]{2,1,0:T(8,128)(2,1)S(1)}, u32[]{:S(2)}, u32[]{:S(2)}) %all-to-all-start) | async-done | bytes 655392 | tf_op jit(solution)/shard_map/all_to_all | solution.py:383
  54.3 7.1 %shard_map.87 = bf16[4,4,160,128]{3,2,1,0:T(8,128)(2,1)} custom-call(s32[2]{0:T(128)S(1)} %pad_add_fusion.place_ref, s32[4096]{0:T(1024)S(1)} %bitcast.13, bf16[16,160,128]{2,1,0:T(8,128)(2,1)S(1)} %all-to-all-done.in_ref), custom_call_target="tpu_custom_call" | custom-call | tf_op jit(solution)/shard_map/pallas_call | solution.py:262
  61.4 4.4 %all-to-all-start.1 = ((bf16[4,4,160,128]{3,2,1,0:T(8,128)(2,1)}), bf16[4,4,160,128]{3,2,1,0:T(8,128)(2,1)}, u32[]{:S(2)}, u32[]{:S(2)}) async-start(bf16[4,4,160,128]{3,2,1,0:T(8,128)(2,1)} %shard_map.87), calls=%async_computation.1 | async-start | bytes 1310720 | tf_op jit(solution)/shard_map/all_to_all | solution.py:385
  67.6 1.4 constant_dynamic-update-slice_fusion.normed_hbm.normed_ref
  69.0 3.1 %copy.13.turned_hbm = bf16[1280,1024]{1,0:T(8,128)(2,1)} copy(bf16[1280,1024]{0,1:T(8,128)(2,1)S(1)} %bitcast.10) | data formatting | bytes 5242880 | tf_op jit(solution)/shard_map/transpose | solution.py:390
  72.2 7.9 %all-to-all-done.1.up_ref = bf16[4,4,160,128]{3,2,1,0:T(8,128)(2,1)} async-done(((bf16[4,4,160,128]{3,2,1,0:T(8,128)(2,1)}), bf16[4,4,160,128]{3,2,1,0:T(8,128)(2,1)}, u32[]{:S(2)}, u32[]{:S(2)}) %all-to-all-start.1) | async-done | bytes 655392 | tf_op jit(solution)/shard_map/all_to_all | solution.py:385
  80.1 17.7 %shard_map.88 = (bf16[4,1024,256]{2,1,0:T(8,128)(2,1)}, bf16[16,4,80,256]{3,2,1,0:T(8,128)(2,1)}) custom-call(s32[2]{0:T(128)} %copy-done.13, bf16[1024,1280]{1,0:T(8,128)(2,1)} %copy-done, bf16[1280,1024]{1,0:T(8,128)(2,1)} %copy.13.turned_hbm, bf16[16,4,16,1280]{3,2,1,0:T(8,128)(2,1)} %bitcast.11, bf16[4,4,160,128]{3,2,1,0:T(8,128)(2,1)} %all-to-all-done.1.up_ref, ...), custom_call_target="tpu_custom_call" | custom-call | tf_op jit(solution)/shard_map/pallas_call | solution.py:284
  97.8 7.6 %all-to-all-start.2 = ((bf16[16,4,80,256]{3,2,1,0:T(8,128)(2,1)}), bf16[16,4,80,256]{3,2,1,0:T(8,128)(2,1)}, u32[]{:S(2)}, u32[]{:S(2)}) async-start(bf16[16,4,80,256]{3,2,1,0:T(8,128)(2,1)} %get-tuple-element.27), calls=%async_computation.2 | async-start | bytes 5242880 | tf_op jit(solution)/shard_map/all_to_all | solution.py:392
  105.4 1.7 copy-done.2
  107.2 1.6 copy-done.9
  108.8 4.8 %shard_map.89 = (f32[512,1280]{1,0:T(8,128)S(1)}, bf16[512,1280]{1,0:T(8,128)(2,1)}, f32[1,1280]{1,0:T(1,128)S(1)}) custom-call(bf16[4,1024,256]{2,1,0:T(8,128)(2,1)S(1)} %copy-done.9, bf16[16,4,16,1280]{3,2,1,0:T(8,128)(2,1)S(1)} %bitcast.12, bf16[1024,1280]{1,0:T(8,128)(2,1)S(1)} %copy-done.1), custom_call_target="tpu_custom_call" | custom-call | tf_op jit(solution)/shard_map/pallas_call | solution.py:314
  113.6 1.5 copy-done.3
  115.1 2.2 %collective-permute-start.5 = (bf16[512,1280]{1,0:T(8,128)(2,1)}, bf16[512,1280]{1,0:T(8,128)(2,1)S(1)}, u32[]{:S(2)}, u32[]{:S(2)}) collective-permute-start(bf16[512,1280]{1,0:T(8,128)(2,1)} %get-tuple-element.26), channel_id=1, source_target_pairs={{0,1},{1,0},{2,3},{3,2},{4,5},{5,4},{6,7},{7,6},{8,9},{9,8},{10,11... | collective-permute-start | bytes 3932168 | tf_op jit(solution)/shard_map/ppermute | solution.py:360
  117.3 2.5 %collective-permute-done.6 = f32[1,1280]{1,0:T(1,128)S(1)} collective-permute-done((f32[1,1280]{1,0:T(1,128)S(1)}, f32[1,1280]{1,0:T(1,128)S(1)}, u32[]{:S(2)}, u32[]{:S(2)}) %collective-permute-start.6) | collective-permute-done | bytes 5152 | tf_op jit(solution)/shard_map/ppermute | solution.py:360
  119.8 6.0 %collective-permute-start.7 = (f32[1,1280]{1,0:T(1,128)S(1)}, f32[1,1280]{1,0:T(1,128)S(1)}, u32[]{:S(2)}, u32[]{:S(2)}) collective-permute-start(f32[1,1280]{1,0:T(1,128)S(1)} %add.32), channel_id=1, source_target_pairs={{0,2},{2,0},{1,3},{3,1},{4,6},{6,4},{5,7},{7,5},{8,10},{10,8},{9,1... | collective-permute-start | bytes 15368 | tf_op jit(solution)/shard_map/ppermute | solution.py:360
  125.8 1.6 collective-permute-done.7
  127.5 2.3 %add_convert_fusion = bf16[256,1280]{1,0:T(8,128)(2,1)} fusion(f32[512,1280]{1,0:T(8,128)} %copy-done.3, bf16[512,1280]{1,0:T(8,128)(2,1)S(1)} %collective-permute-done.5.core_ref), kind=kLoop, calls=%fused_computation.1 | loop fusion | flops 983040 | bytes 2621440 | tf_op jit(solution)/shard_map/convert_element_type | solution.py:396
  131.0 9.7 %all-to-all-done.2 = bf16[16,4,80,256]{3,2,1,0:T(8,128)(2,1)} async-done(((bf16[16,4,80,256]{3,2,1,0:T(8,128)(2,1)}), bf16[16,4,80,256]{3,2,1,0:T(8,128)(2,1)}, u32[]{:S(2)}, u32[]{:S(2)}) %all-to-all-start.2) | async-done | bytes 2621472 | tf_op jit(solution)/shard_map/all_to_all | solution.py:392
  140.6 2.1 %reduce_sum.33 = bf16[4,80,256]{2,1,0:T(8,128)(2,1)S(1)} reduce(bf16[16,4,80,256]{3,2,1,0:T(8,128)(2,1)} %all-to-all-done.2, bf16[]{:T(256)} %constant.37.clone.1), dimensions={0}, to_apply=%region_0.1 | reduce | flops 1228800 | bytes 2785282 | tf_op jit(solution)/shard_map/reduce_sum | solution.py:393
  142.9 19.7 %all_to_all.25 = bf16[4,80,256]{2,1,0:T(8,128)(2,1)S(1)} all-to-all(bf16[4,80,256]{2,1,0:T(8,128)(2,1)S(1)} %pad_maximum_fusion.1), channel_id=1, replica_groups=mesh['y'=4,'x'=4,'zq'=4,'zp'=2,'core'=2] {'zq'}, dimensions={0} | all-to-all | bytes 327680 | tf_op jit(solution)/shard_map/all_to_all | solution.py:403
  163.5 8.8 %all-to-all-start.4 = ((bf16[16,80,256]{2,1,0:T(8,128)(2,1)}), bf16[16,80,256]{2,1,0:T(8,128)(2,1)S(1)}, u32[]{:S(2)}, u32[]{:S(2)}) async-start(bf16[16,80,256]{2,1,0:T(8,128)(2,1)} %broadcast_in_dim.5), calls=%async_computation.4 | async-start | bytes 1310720 | tf_op jit(solution)/shard_map/all_to_all | solution.py:408
  172.3 10.7 %all-to-all-done.4.whole_ref = bf16[16,80,256]{2,1,0:T(8,128)(2,1)S(1)} async-done(((bf16[16,80,256]{2,1,0:T(8,128)(2,1)}), bf16[16,80,256]{2,1,0:T(8,128)(2,1)S(1)}, u32[]{:S(2)}, u32[]{:S(2)}) %all-to-all-start.4) | async-done | bytes 655392 | tf_op jit(solution)/shard_map/all_to_all | solution.py:408
  183.9 3.8 %collective-permute-done.8.pair_ref = bf16[256,1280]{1,0:T(8,128)(2,1)} collective-permute-done((bf16[256,1280]{1,0:T(8,128)(2,1)}, bf16[256,1280]{1,0:T(8,128)(2,1)}, u32[]{:S(2)}, u32[]{:S(2)}) %collective-permute-start.8) | collective-permute-done | bytes 655392 | tf_op jit(solution)/shard_map/ppermute | solution.py:360
  187.6 1.3 copy-done.6
  190.0 3.0 %shard_map.90 = (bf16[256,1280]{1,0:T(8,128)(2,1)}, f32[3,1280,80]{2,1,0:T(8,128)S(1)}) custom-call(bf16[256,1280]{1,0:T(8,128)(2,1)S(1)} %copy-done.8, f32[1,1280]{1,0:T(1,128)S(1)} %reshape.31.gain_ref, f32[512,1280]{1,0:T(8,128)S(1)} %copy-done.4, bf16[512,1280]{1,0:T(8,128)(2,1)S(1)} %copy-done.6, bf16[256,1280]{1,0:T(8,128)(2,1)} %collective-permute-done.8.pair_ref, ...), custom_call_target="tpu_custom_call" | custom-call | tf_op jit(solution)/shard_map/pallas_call | solution.py:339
  194.3 2.7 %copy.14 = f32[3,1280,80]{1,2,0:T(8,128)} copy(f32[3,1280,80]{2,1,0:T(8,128)} %copy-done.10) | data formatting | bytes 2457600
  (68 shorter events, 14.5 us)
Async XLA Ops:
  7.2 72.9 %all-gather.2.cloned.1.call-start = ((), (), s32[]{:S(2)}) async-start(), calls=%async_computation.5 | async-start | bytes 2785280 | tf_op jit(solution)/shard_map/all_gather | solution.py:380
  8.0 17.1 %collective-permute-start.2 = (bf16[16,1280]{1,0:T(8,128)(2,1)S(1)}, bf16[16,1280]{1,0:T(8,128)(2,1)S(1)}, u32[]{:S(2)}, u32[]{:S(2)}) collective-permute-start(bf16[16,1280]{1,0:T(8,128)(2,1)S(1)} %get-tuple-element.45), channel_id=1, source_target_pairs={{0,4},{4,8},{8,12},{12,0},{1,5},{5,9},{9,13},{13,1},{2,6},{6,10},{... | collective-permute-start | bytes 122888 | tf_op jit(solution)/shard_map/ppermute | solution.py:375
  11.4 13.7 %collective-permute-start.1 = (bf16[16,1280]{1,0:T(8,128)(2,1)S(1)}, bf16[16,1280]{1,0:T(8,128)(2,1)S(1)}, u32[]{:S(2)}, u32[]{:S(2)}) collective-permute-start(bf16[16,1280]{1,0:T(8,128)(2,1)S(1)} %get-tuple-element.45), channel_id=1, source_target_pairs={{0,8},{4,12},{8,0},{12,4},{1,9},{5,13},{9,1},{13,5},{2,10},{6,14},... | collective-permute-start | bytes 122888 | tf_op jit(solution)/shard_map/ppermute | solution.py:375
  16.8 8.3 %collective-permute-start = (bf16[16,1280]{1,0:T(8,128)(2,1)S(1)}, bf16[16,1280]{1,0:T(8,128)(2,1)S(1)}, u32[]{:S(2)}, u32[]{:S(2)}) collective-permute-start(bf16[16,1280]{1,0:T(8,128)(2,1)S(1)} %get-tuple-element.45), channel_id=1, source_target_pairs={{0,12},{4,0},{8,4},{12,8},{1,13},{5,1},{9,5},{13,9},{2,14},{6,2},{... | collective-permute-start | bytes 122888 | tf_op jit(solution)/shard_map/ppermute | solution.py:375
  20.1 1.1 copy-start.11
  23.7 1.1 copy-start.7
  25.1 29.3 %copy-start.12 = (s32[1,4096]{1,0:T(1,128)S(1)}, s32[1,4096]{1,0:T(1,128)}, u32[]{:S(2)}) copy-start(s32[1,4096]{1,0:T(1,128)} %param.8) | copy-start | bytes 49156
  25.9 23.7 %collective-permute-start.3 = (bf16[256,1280]{1,0:T(8,128)(2,1)S(1)}, bf16[256,1280]{1,0:T(8,128)(2,1)S(1)}, u32[]{:S(2)}, u32[]{:S(2)}) collective-permute-start(bf16[256,1280]{1,0:T(8,128)(2,1)S(1)} %shard_map.86), channel_id=1, source_target_pairs={{0,2},{2,0},{1,3},{3,1},{4,6},{6,4},{5,7},{7,5},{8,10},{10,8},{9,1... | collective-permute-start | bytes 1966088 | tf_op jit(solution)/shard_map/ppermute | solution.py:360
  27.0 27.3 %all-to-all-start = ((bf16[16,160,128]{2,1,0:T(8,128)(2,1)}), bf16[16,160,128]{2,1,0:T(8,128)(2,1)S(1)}, u32[]{:S(2)}, u32[]{:S(2)}) async-start(bf16[16,160,128]{2,1,0:T(8,128)(2,1)} %shard_map.85), calls=%async_computation | async-start | bytes 1310720 | tf_op jit(solution)/shard_map/all_to_all | solution.py:383
  30.6 35.1 %copy-start.16 = (s32[1,4096]{1,0:T(1,128)S(1)}, s32[1,4096]{1,0:T(1,128)}, u32[]{:S(2)}) copy-start(s32[1,4096]{1,0:T(1,128)} %param.9) | copy-start | bytes 49156
  49.6 16.1 %copy-start.14 = (bf16[256,1280]{1,0:T(8,128)(2,1)}, bf16[256,1280]{1,0:T(8,128)(2,1)S(1)}, u32[]{:S(2)}) copy-start(bf16[256,1280]{1,0:T(8,128)(2,1)S(1)} %collective-permute-done.3) | copy-start | bytes 1966084
  50.9 16.7 %collective-permute-start.4 = (bf16[512,1280]{1,0:T(8,128)(2,1)}, bf16[512,1280]{1,0:T(8,128)(2,1)}, u32[]{:S(2)}, u32[]{:S(2)}) collective-permute-start(bf16[512,1280]{1,0:T(8,128)(2,1)} %pad_maximum_fusion), channel_id=1, source_target_pairs={{0,1},{1,0},{2,3},{3,2},{4,5},{5,4},{6,7},{7,6},{8,9},{9,8},{10,11... | collective-permute-start | bytes 3932168 | tf_op jit(solution)/shard_map/ppermute | solution.py:360
  51.0 16.6 %copy-start.13 = (s32[2]{0:T(128)}, s32[2]{0:T(128)S(1)}, u32[]{:S(2)}) copy-start(s32[2]{0:T(128)S(1)} %pad_add_fusion.place_ref) | copy-start | bytes 28
  61.4 18.7 %all-to-all-start.1 = ((bf16[4,4,160,128]{3,2,1,0:T(8,128)(2,1)}), bf16[4,4,160,128]{3,2,1,0:T(8,128)(2,1)}, u32[]{:S(2)}, u32[]{:S(2)}) async-start(bf16[4,4,160,128]{3,2,1,0:T(8,128)(2,1)} %shard_map.87), calls=%async_computation.1 | async-start | bytes 1310720 | tf_op jit(solution)/shard_map/all_to_all | solution.py:385
  69.0 3.2 %copy-start = (bf16[1024,1280]{1,0:T(8,128)(2,1)}, bf16[1024,1280]{1,0:T(8,128)(2,1)S(1)}, u32[]{:S(2)}) copy-start(bf16[1024,1280]{1,0:T(8,128)(2,1)S(1)} %constant_dynamic-update-slice_fusion.normed_hbm.normed_ref) | copy-start | bytes 7864324
  97.8 7.6 %copy-start.1 = (bf16[1024,1280]{1,0:T(8,128)(2,1)S(1)}, bf16[1024,1280]{1,0:T(8,128)(2,1)}, u32[]{:S(2)}) copy-start(bf16[1024,1280]{1,0:T(8,128)(2,1)} %copy-done) | copy-start | bytes 7864324
  97.8 42.9 %all-to-all-start.2 = ((bf16[16,4,80,256]{3,2,1,0:T(8,128)(2,1)}), bf16[16,4,80,256]{3,2,1,0:T(8,128)(2,1)}, u32[]{:S(2)}, u32[]{:S(2)}) async-start(bf16[16,4,80,256]{3,2,1,0:T(8,128)(2,1)} %get-tuple-element.27), calls=%async_computation.2 | async-start | bytes 5242880 | tf_op jit(solution)/shard_map/all_to_all | solution.py:392
  105.4 1.7 copy-start.2
  107.2 1.6 copy-start.9
  113.6 1.5 copy-start.3
  115.1 12.4 %collective-permute-start.5 = (bf16[512,1280]{1,0:T(8,128)(2,1)}, bf16[512,1280]{1,0:T(8,128)(2,1)S(1)}, u32[]{:S(2)}, u32[]{:S(2)}) collective-permute-start(bf16[512,1280]{1,0:T(8,128)(2,1)} %get-tuple-element.26), channel_id=1, source_target_pairs={{0,1},{1,0},{2,3},{3,2},{4,5},{5,4},{6,7},{7,6},{8,9},{9,8},{10,11... | collective-permute-start | bytes 3932168 | tf_op jit(solution)/shard_map/ppermute | solution.py:360
  117.3 2.5 %collective-permute-start.6 = (f32[1,1280]{1,0:T(1,128)S(1)}, f32[1,1280]{1,0:T(1,128)S(1)}, u32[]{:S(2)}, u32[]{:S(2)}) collective-permute-start(f32[1,1280]{1,0:T(1,128)S(1)} %get-tuple-element.28), channel_id=1, source_target_pairs={{0,1},{1,0},{2,3},{3,2},{4,5},{5,4},{6,7},{7,6},{8,9},{9,8},{10,11... | collective-permute-start | bytes 15368 | tf_op jit(solution)/shard_map/ppermute | solution.py:360
  119.8 7.5 %collective-permute-start.7 = (f32[1,1280]{1,0:T(1,128)S(1)}, f32[1,1280]{1,0:T(1,128)S(1)}, u32[]{:S(2)}, u32[]{:S(2)}) collective-permute-start(f32[1,1280]{1,0:T(1,128)S(1)} %add.32), channel_id=1, source_target_pairs={{0,2},{2,0},{1,3},{3,1},{4,6},{6,4},{5,7},{7,5},{8,10},{10,8},{9,1... | collective-permute-start | bytes 15368 | tf_op jit(solution)/shard_map/ppermute | solution.py:360
  129.8 1.2 copy-start.5
  131.0 52.3 %copy-start.15 = (f32[1280]{0:T(1024)S(1)}, f32[1280]{0:T(1024)}, u32[]{:S(2)}) copy-start(f32[1280]{0:T(1024)} %param.11) | copy-start | bytes 15364
  131.0 56.6 %copy-start.4 = (f32[512,1280]{1,0:T(8,128)S(1)}, f32[512,1280]{1,0:T(8,128)}, u32[]{:S(2)}) copy-start(f32[512,1280]{1,0:T(8,128)} %copy-done.3) | copy-start | bytes 7864324
  163.5 19.5 %all-to-all-start.4 = ((bf16[16,80,256]{2,1,0:T(8,128)(2,1)}), bf16[16,80,256]{2,1,0:T(8,128)(2,1)S(1)}, u32[]{:S(2)}, u32[]{:S(2)}) async-start(bf16[16,80,256]{2,1,0:T(8,128)(2,1)} %broadcast_in_dim.5), calls=%async_computation.4 | async-start | bytes 1310720 | tf_op jit(solution)/shard_map/all_to_all | solution.py:408
  172.3 15.3 %collective-permute-start.8 = (bf16[256,1280]{1,0:T(8,128)(2,1)}, bf16[256,1280]{1,0:T(8,128)(2,1)}, u32[]{:S(2)}, u32[]{:S(2)}) collective-permute-start(bf16[256,1280]{1,0:T(8,128)(2,1)} %add_convert_fusion), channel_id=1, source_target_pairs={{0,2},{2,0},{1,3},{3,1},{4,6},{6,4},{5,7},{7,5},{8,10},{10,8},{9,1... | collective-permute-start | bytes 1966088 | tf_op jit(solution)/shard_map/ppermute | solution.py:360
  187.6 1.3 copy-start.6
  188.9 1.1 copy-start.8
  193.0 1.3 copy-start.10
Sparse Core Ops, SparseCore 0:
  26.0 47.7 all-gather.1

commit v6 on v4

--- a/solution.py
+++ b/solution.py
@@ -22,7 +22,7 @@
 NT = (((1,), (1,)), ((), ()))
 TN = (((0,), (0,)), ((), ()))
 NN = (((1,), (0,)), ((), ()))
-BIG = 34 * 1024 * 1024
+BIG = 58 * 1024 * 1024
 SMALL = 20 * 1024 * 1024
 
 
@@ -87,13 +87,13 @@
             base = q * SLOTS * CHUNK + (slot ^ off) * CHUNK
 
             def step(i, carry):
-                at = i * 16
-                for u in range(16):
+                at = i * 64
+                for u in range(64):
                     row = source_ref[base + at + u]
                     picked[pl.ds(at + u, 1), :] = table[pl.ds(row, 1), :]
                 return carry
 
-            lax.fori_loop(0, CHUNK // 16, step, 0)
+            lax.fori_loop(0, CHUNK // 64, step, 0)
             top, low = pack(picked[...])
             out_ref[q, o, :128, :] = top.astype(bf16)
             out_ref[q, o, 128:, :] = low.astype(bf16)
@@ -111,9 +111,9 @@
 
 
 def head_kernel(
-    place_ref, normed_ref, turned_hbm, w_hbm, up_ref, window_ref, grad_hbm, weight_hbm,
+    place_ref, normed_hbm, turned_hbm, w_hbm, up_ref, window_ref, grad_hbm, weight_hbm,
     first, second, key_at, query_at, upstream, same,
-    turned_ref, w_ref, grad_ref, weight_ref, in_sems, out_sems,
+    normed_ref, turned_ref, w_ref, grad_ref, weight_ref, in_sems, out_sems,
 ):
     ring, slot = place_ref[0], place_ref[1]
     scaling = HEAD ** (-0.5)
@@ -124,7 +124,9 @@
         pltpu.make_async_copy(w_hbm.at[:, h], w_ref.at[h], in_sems.at[h]) for h in range(RING)
     ]
     turned_copy = pltpu.make_async_copy(turned_hbm, turned_ref, in_sems.at[RING])
+    normed_copy = pltpu.make_async_copy(normed_hbm, normed_ref, in_sems.at[RING + 1])
     w_copies[0].start()
+    normed_copy.start()
     for h in range(1, RING):
         w_copies[h].start()
     turned_copy.start()
@@ -194,6 +196,7 @@
         same[r, :] = jnp.where(labels == labels.T, 0.0, -1e30)
     spread(0)
     w_copies[0].wait()
+    normed_copy.wait()
     project(0)
     for copy in w_copies[1:] + [turned_copy]:
         copy.wait()
@@ -209,13 +212,17 @@
         copy.wait()
 
 
-def back_kernel(grad_ref, w_ref, normed_ref, keep_ref, send_ref, gain_ref):
+def back_kernel(grad_ref, w_ref, normed_ref, out_ref, gain_ref):
     parts = [w_ref[:, h].reshape(PADDED, w_ref.shape[-1]) for h in range(RING)]
     grads = jnp.concatenate([grad_ref[h] for h in range(RING)], axis=1)
     total = dot(grads, jnp.concatenate(parts, axis=0), NN)
-    keep_ref[...] = total[: 2 * CHUNK]
-    send_ref[...] = total[2 * CHUNK :].astype(bf16)
+    out_ref[...] = total.astype(out_ref.dtype)
     gain_ref[...] = jnp.sum(total * normed_ref[...].astype(f32), axis=0, keepdims=True)
+
+
+def turn_kernel(whole_ref, out_ref):
+    whole = whole_ref[...].reshape(out_ref.shape[1], PADDED).astype(f32)
+    out_ref[...] = whole.T[: 3 * HEAD]
 
 
 def final_kernel(rows_ref, gain_ref, keep_ref, core_ref, pair_ref, out_ref):
@@ -279,7 +286,7 @@
             jax.ShapeDtypeStruct((RING, rows, PADDED), bf16),
             jax.ShapeDtypeStruct((16, RING, width // 16, PADDED), bf16),
         ),
-        in_specs=[smem(), vmem()] + [pl.BlockSpec(memory_space=pl.ANY)] * 2 + [vmem()] * 2,
+        in_specs=[smem()] + [pl.BlockSpec(memory_space=pl.ANY)] * 3 + [vmem()] * 2,
         out_specs=(pl.BlockSpec(memory_space=pl.ANY),) * 2,
         scratch_shapes=[
             pltpu.VMEM((RING, rows, 128), bf16),
@@ -288,50 +295,62 @@
             pltpu.VMEM((RING, rows, PADDED), bf16),
             pltpu.VMEM((RING, rows, 128), bf16),
             pltpu.VMEM((rows, SUPER), f32),
+            pltpu.VMEM((rows, width), bf16),
             pltpu.VMEM((width, rows), bf16),
             pltpu.VMEM((RING, 16, 16, width), bf16),
             pltpu.VMEM((RING, rows, PADDED), bf16),
             pltpu.VMEM((RING, 16, width // 16, PADDED), bf16),
-            pltpu.SemaphoreType.DMA((RING + 1,)),
+            pltpu.SemaphoreType.DMA((RING + 2,)),
             pltpu.SemaphoreType.DMA((2 * RING,)),
         ],
         compiler_params=params(BIG),
     )(place, normed, turned, weights, upstream, windows)
 
 
-def back_call(grads, weights, normed):
-    rows, width = grads.shape[1], weights.shape[-1]
+def back_call(grads, weights, normed, half, dtype):
+    rows, width = 2 * CHUNK, weights.shape[-1]
     piece = 256
     return pl.pallas_call(
         back_kernel,
         grid=(width // piece,),
         out_shape=(
-            jax.ShapeDtypeStruct((2 * CHUNK, width), f32),
-            jax.ShapeDtypeStruct((2 * CHUNK, width), bf16),
+            jax.ShapeDtypeStruct((rows, width), dtype),
             jax.ShapeDtypeStruct((1, width), f32),
         ),
         in_specs=[
-            pl.BlockSpec((RING, rows, PADDED), lambda n: (0, 0, 0)),
+            pl.BlockSpec((RING, rows, PADDED), lambda n: (0, half, 0)),
             pl.BlockSpec((16, RING, 16, piece), lambda n: (0, 0, 0, n)),
-            pl.BlockSpec((rows, piece), lambda n: (0, n)),
+            pl.BlockSpec((rows, piece), lambda n: (half, n)),
         ],
         out_specs=(
-            pl.BlockSpec((2 * CHUNK, piece), lambda n: (0, n)),
-            pl.BlockSpec((2 * CHUNK, piece), lambda n: (0, n)),
+            pl.BlockSpec((rows, piece), lambda n: (0, n)),
             pl.BlockSpec((1, piece), lambda n: (0, n)),
         ),
-        compiler_params=params(),
+        compiler_params=params(BIG),
     )(grads, weights, normed)
 
 
 def final_call(rows, gain, keep, from_core, from_pair):
+    part = pl.BlockSpec(rows.shape, lambda i: (0, 0))
     return pl.pallas_call(
         final_kernel,
+        grid=(1,),
         out_shape=jax.ShapeDtypeStruct(rows.shape, bf16),
-        in_specs=[vmem()] * 5,
+        in_specs=[part, pl.BlockSpec(gain.shape, lambda i: (0, 0)), part, part, part],
+        out_specs=part,
+        compiler_params=params(BIG),
+    )(rows, gain, keep, from_core, from_pair)
+
+
+def turn_call(whole):
+    width = whole.shape[0] * whole.shape[1]
+    return pl.pallas_call(
+        turn_kernel,
+        out_shape=jax.ShapeDtypeStruct((3 * HEAD, width), f32),
+        in_specs=[vmem()],
         out_specs=vmem(),
-        compiler_params=params(),
-    )(rows, gain, keep, from_core, from_pair)
+        compiler_params=params(BIG),
+    )(whole)
 
 
 def swap(x, axis):
@@ -369,7 +388,9 @@
 
     arrived = lax.all_to_all(weight_part, ("y", "x"), split_axis=0, concat_axis=0)
     summed = jnp.sum(arrived.astype(f32), axis=0).astype(bf16)
-    keep, send, gain_part = back_call(grads, weights, normed)
+    send, gain_send = back_call(grads, weights, normed, 1, bf16)
+    keep, gain_keep = back_call(grads, weights, normed, 0, f32)
+    gain_part = gain_send + gain_keep
     from_core = swap(send, "core")
     pair = (keep[CHUNK:] + from_core[CHUNK:].astype(f32)).astype(bf16)
     gain_part = gain_part + swap(gain_part, "core")
@@ -377,17 +398,15 @@
     beside = gain_part.reshape(width // 16, 16).astype(bf16)
     beside = jnp.broadcast_to(beside[None], (RING, width // 16, 16))
     message = jnp.concatenate([summed[..., : 3 * HEAD], beside], axis=2)
-    message, pair = lax.optimization_barrier((message, pair))
+    from_pair = swap(pair, "zp")
+    message, from_pair = lax.optimization_barrier((message, from_pair))
     arrived = lax.all_to_all(message, "zq", split_axis=0, concat_axis=0)
     summed = jnp.sum(arrived.astype(f32), axis=0).astype(bf16)
     copies = jnp.broadcast_to(summed[None], (16,) + summed.shape)
-    copies, pair = lax.optimization_barrier((copies, pair))
-    from_pair = swap(pair, "zp")
     whole = lax.all_to_all(copies, ("y", "x"), split_axis=0, concat_axis=0)
-    gradient = whole.reshape(width, PADDED).astype(f32)
-    grad_weight = jnp.stack([gradient[:, HEAD * j : HEAD * j + HEAD] for j in range(3)])
     grad_gain = jnp.sum(whole[:, :, 3 * HEAD :].astype(f32), axis=0).reshape(width) / gain
-    grad_input = final_call(layer_input, gain_row, keep[:CHUNK], from_core[:CHUNK], from_pair)
+    grad_weight = jnp.swapaxes(turn_call(whole).reshape(3, HEAD, width), 1, 2)
+    grad_input = final_call(layer_input, gain_row, keep, from_core, from_pair)
     return (grad_input, grad_weight, grad_gain)
 
 

time: 198 us -> 193 us (0.975)
  Pallas kernels: 31.8 us -> 45.7 us
  local copies, waits for them, and re-layouts: 25.3 us -> 15 us
  other arithmetic: 9.2 us -> 4.59 us
  starting transfers between devices: 48.9 us -> 45.1 us
  blocking collectives: 14.2 us -> 16.7 us
    all_to_all x1, waiting for transfers between devices: 10.7 us -> 0.01 us  [on_device(): lax.all_to_all(weight_part, ('y', 'x'), split_axis=0, concat_axis=0)]
    ppermute x6, waiting for transfers between devices: 23.5 us -> 34.1 us  [swap(): return lax.ppermute(x, axis, [(0, 1), (1, 0)])]
    unnamed x40 -> x33, local copies, waits for them, and re-layouts: 17.2 us -> 6.83 us
    pallas_call x1 -> x2, Pallas kernels: 4.85 us -> 12.4 us  [back_call(): pl.pallas_call(back_kernel, grid=(width // piece,), out_shape=(jax.ShapeD...]
    ppermute x6, starting transfers between devices: 14.6 us -> 9.7 us  [swap(): return lax.ppermute(x, axis, [(0, 1), (1, 0)])]
    pallas_call x1 -> x2, Pallas kernels: 1.52 us -> 5.78 us  [the longest x1 3.42 us: final_call(): pl.pallas_call(final_kernel, grid=(1,), out_shape=jax.ShapeDtypeStruct(ro...]
    pallas_call x1, Pallas kernels: 14.7 us -> 17.7 us  [head_call(): pl.pallas_call(head_kernel, out_shape=(jax.ShapeDtypeStruct((RING, rows,...]
    all_to_all x1, waiting for transfers between devices: 8.87 us -> 6.08 us  [on_device(): upstream = lax.all_to_all(permuted, 'zq', split_axis=0, concat_axis=0)]
  transfers between devices with their start and end apart: 14 -> 14, of which waited for: 8 -> 6; matrix products, arithmetic and copies ran while one was open for 9% -> 6% of each run, Pallas kernels for 8% -> 13%
where the time goes in v6:
time: 193 us; the launch traced here: 192 us
  waiting for transfers between devices  50.9 us (26%)
  Pallas kernels  45.7 us (24%)
  starting transfers between devices  45.1 us (23%)
  blocking collectives  16.7 us (9%)
  local copies, waits for them, and re-layouts  15 us (8%)
  between operations  14.3 us (7%)
  other arithmetic  4.59 us (2%)
    ppermute x6, waiting for transfers between devices, swap(): return lax.ppermute(x, axis, [(0, 1), (1, 0)])  34.1 us
    pallas_call x1, Pallas kernels, head_call(): pl.pallas_call(head_kernel, out_shape=(jax.ShapeDtypeStruct((RING, rows,...  17.7 us
    all_to_all x1, blocking collectives, on_device(): arrived = lax.all_to_all(message, 'zq', split_axis=0, concat_axis=0)  16.7 us
    pallas_call x2, Pallas kernels, back_call(): pl.pallas_call(back_kernel, grid=(width // piece,), out_shape=(jax.ShapeD...  12.4 us
    ppermute x3, starting transfers between devices, on_device(): lax.ppermute(share, 'zq', [(i, (i + k) % RING) for i in range(RING)])  11.4 us
    ppermute x6, starting transfers between devices, swap(): return lax.ppermute(x, axis, [(0, 1), (1, 0)])  9.7 us
    all_to_all x1, starting transfers between devices, on_device(): whole = lax.all_to_all(copies, ('y', 'x'), split_axis=0, concat_axis=0)  8.54 us
    all_to_all x1, starting transfers between devices, on_device(): lax.all_to_all(weight_part, ('y', 'x'), split_axis=0, concat_axis=0)  7.49 us
  transfers between devices with their start and end apart: 14, of which 6 were waited for; matrix products, arithmetic and copies ran while one was open for 6% of the time, Pallas kernels for 13%

profile of v6, /device:TPU:2, one launch (start us, length us, event | category | flops | bytes accessed | tf_op | source)
XLA Modules:
  0.0 192.2 jit_solution(3300232707025603465)
XLA Ops:
  8.0 3.3 %collective-permute-start.2 = (bf16[16,1280]{1,0:T(8,128)(2,1)S(1)}, bf16[16,1280]{1,0:T(8,128)(2,1)S(1)}, u32[]{:S(2)}, u32[]{:S(2)}) collective-permute-start(bf16[16,1280]{1,0:T(8,128)(2,1)S(1)} %get-tuple-element.30), channel_id=1, source_target_pairs={{0,4},{4,8},{8,12},{12,0},{1,5},{5,9},{9,13},{13,1},{2,6},{6,10},{... | collective-permute-start | bytes 122888 | tf_op jit(solution)/shard_map/ppermute | solution.py:372
  11.4 5.4 %collective-permute-start.1 = (bf16[16,1280]{1,0:T(8,128)(2,1)S(1)}, bf16[16,1280]{1,0:T(8,128)(2,1)S(1)}, u32[]{:S(2)}, u32[]{:S(2)}) collective-permute-start(bf16[16,1280]{1,0:T(8,128)(2,1)S(1)} %get-tuple-element.30), channel_id=1, source_target_pairs={{0,8},{4,12},{8,0},{12,4},{1,9},{5,13},{9,1},{13,5},{2,10},{6,14},... | collective-permute-start | bytes 122888 | tf_op jit(solution)/shard_map/ppermute | solution.py:372
  16.8 2.7 %collective-permute-start = (bf16[16,1280]{1,0:T(8,128)(2,1)S(1)}, bf16[16,1280]{1,0:T(8,128)(2,1)S(1)}, u32[]{:S(2)}, u32[]{:S(2)}) collective-permute-start(bf16[16,1280]{1,0:T(8,128)(2,1)S(1)} %get-tuple-element.30), channel_id=1, source_target_pairs={{0,12},{4,0},{8,4},{12,8},{1,13},{5,1},{9,5},{13,9},{2,14},{6,2},{... | collective-permute-start | bytes 122888 | tf_op jit(solution)/shard_map/ppermute | solution.py:372
  20.1 1.1 copy-done.1
  21.2 2.5 %shard_map.85 = bf16[16,160,128]{2,1,0:T(8,128)(2,1)} custom-call(bf16[256,1280]{1,0:T(8,128)(2,1)S(1)} %copy-done.1), custom_call_target="tpu_custom_call" | custom-call | tf_op jit(solution)/shard_map/pallas_call | solution.py:251
  23.7 1.1 copy-done
  25.9 1.1 collective-permute-start.3
  27.0 3.6 %all-to-all-start = ((bf16[16,160,128]{2,1,0:T(8,128)(2,1)}), bf16[16,160,128]{2,1,0:T(8,128)(2,1)S(1)}, u32[]{:S(2)}, u32[]{:S(2)}) async-start(bf16[16,160,128]{2,1,0:T(8,128)(2,1)} %shard_map.85), calls=%async_computation | async-start | bytes 1310720 | tf_op jit(solution)/shard_map/all_to_all | solution.py:380
  30.6 19.0 %collective-permute-done.3 = bf16[256,1280]{1,0:T(8,128)(2,1)S(1)} collective-permute-done((bf16[256,1280]{1,0:T(8,128)(2,1)S(1)}, bf16[256,1280]{1,0:T(8,128)(2,1)S(1)}, u32[]{:S(2)}, u32[]{:S(2)}) %collective-permute-start.3) | collective-permute-done | bytes 655392 | tf_op jit(solution)/shard_map/ppermute | solution.py:357
  49.6 1.1 pad_maximum_fusion
  50.9 3.4 %all-to-all-done.in_ref = bf16[16,160,128]{2,1,0:T(8,128)(2,1)S(1)} async-done(((bf16[16,160,128]{2,1,0:T(8,128)(2,1)}), bf16[16,160,128]{2,1,0:T(8,128)(2,1)S(1)}, u32[]{:S(2)}, u32[]{:S(2)}) %all-to-all-start) | async-done | bytes 655392 | tf_op jit(solution)/shard_map/all_to_all | solution.py:380
  54.3 7.1 %shard_map.87 = bf16[4,4,160,128]{3,2,1,0:T(8,128)(2,1)} custom-call(s32[2]{0:T(128)S(1)} %pad_add_fusion.place_ref, s32[4096]{0:T(1024)S(1)} %bitcast.13, bf16[16,160,128]{2,1,0:T(8,128)(2,1)S(1)} %all-to-all-done.in_ref), custom_call_target="tpu_custom_call" | custom-call | tf_op jit(solution)/shard_map/pallas_call | solution.py:261
  61.4 4.3 %all-to-all-start.1 = ((bf16[4,4,160,128]{3,2,1,0:T(8,128)(2,1)}), bf16[4,4,160,128]{3,2,1,0:T(8,128)(2,1)S(1)}, u32[]{:S(2)}, u32[]{:S(2)}) async-start(bf16[4,4,160,128]{3,2,1,0:T(8,128)(2,1)} %shard_map.87), calls=%async_computation.1 | async-start | bytes 1310720 | tf_op jit(solution)/shard_map/all_to_all | solution.py:382
  67.3 1.0 constant_dynamic-update-slice_fusion.1
  68.2 1.2 constant_dynamic-update-slice_fusion.normed_hbm.normed_ref
  69.4 4.5 %copy.11.turned_hbm = bf16[1280,1024]{1,0:T(8,128)(2,1)} copy(bf16[1280,1024]{0,1:T(8,128)(2,1)} %bitcast.4) | data formatting | bytes 5242880 | tf_op jit(solution)/shard_map/transpose | solution.py:387
  73.9 6.1 %all-to-all-done.1.up_ref = bf16[4,4,160,128]{3,2,1,0:T(8,128)(2,1)S(1)} async-done(((bf16[4,4,160,128]{3,2,1,0:T(8,128)(2,1)}), bf16[4,4,160,128]{3,2,1,0:T(8,128)(2,1)S(1)}, u32[]{:S(2)}, u32[]{:S(2)}) %all-to-all-start.1) | async-done | bytes 655392 | tf_op jit(solution)/shard_map/all_to_all | solution.py:382
  80.8 17.7 %shard_map.88 = (bf16[4,1024,256]{2,1,0:T(8,128)(2,1)}, bf16[16,4,80,256]{3,2,1,0:T(8,128)(2,1)}) custom-call(s32[2]{0:T(128)} %copy-done.4, bf16[1024,1280]{1,0:T(8,128)(2,1)} %constant_dynamic-update-slice_fusion.normed_hbm.normed_ref, bf16[1280,1024]{1,0:T(8,128)(2,1)} %copy.11.turned_hbm, bf16[16,4,16,1280]{3,2,1,0:T(8,128)(2,1)} %bitcast.14, ...), custom_call_target="tpu_custom_call" | custom-call | tf_op jit(solution)/shard_map/pallas_call | solution.py:283
  98.5 7.5 %all-to-all-start.2 = ((bf16[16,4,80,256]{3,2,1,0:T(8,128)(2,1)}), bf16[16,4,80,256]{3,2,1,0:T(8,128)(2,1)S(1)}, u32[]{:S(2)}, u32[]{:S(2)}) async-start(bf16[16,4,80,256]{3,2,1,0:T(8,128)(2,1)} %get-tuple-element.24), calls=%async_computation.2 | async-start | bytes 5242880 | tf_op jit(solution)/shard_map/all_to_all | solution.py:389
  106.0 6.1 %shard_map.90 = (bf16[512,1280]{1,0:T(8,128)(2,1)}, f32[1,1280]{1,0:T(1,128)}) custom-call(bf16[4,1024,256]{2,1,0:T(8,128)(2,1)} %get-tuple-element.21.grad_ref, bf16[16,4,16,1280]{3,2,1,0:T(8,128)(2,1)} %bitcast.15, bf16[1024,1280]{1,0:T(8,128)(2,1)} %constant_dynamic-update-slice_fusion.normed_hbm.normed_ref), custom_call_target="tpu_custom_call" | custom-call | tf_op jit(solution)/shard_map/pallas_call | solution.py:313
  112.1 2.2 %collective-permute-start.5 = (bf16[512,1280]{1,0:T(8,128)(2,1)}, bf16[512,1280]{1,0:T(8,128)(2,1)S(1)}, u32[]{:S(2)}, u32[]{:S(2)}) collective-permute-start(bf16[512,1280]{1,0:T(8,128)(2,1)} %get-tuple-element.23), channel_id=1, source_target_pairs={{0,1},{1,0},{2,3},{3,2},{4,5},{5,4},{6,7},{7,6},{8,9},{9,8},{10,11... | collective-permute-start | bytes 3932168 | tf_op jit(solution)/shard_map/ppermute | solution.py:357
  114.3 6.3 %shard_map.89 = (f32[512,1280]{1,0:T(8,128)}, f32[1,1280]{1,0:T(1,128)}) custom-call(bf16[4,1024,256]{2,1,0:T(8,128)(2,1)} %get-tuple-element.21.grad_ref, bf16[16,4,16,1280]{3,2,1,0:T(8,128)(2,1)} %bitcast.16, bf16[1024,1280]{1,0:T(8,128)(2,1)} %constant_dynamic-update-slice_fusion.normed_hbm.normed_ref), custom_call_target="tpu_custom_call" | custom-call | tf_op jit(solution)/shard_map/pallas_call | solution.py:313
  120.6 1.1 copy-done.6
  121.7 1.4 add_convert_fusion
  123.1 5.9 %collective-permute-start.8 = (bf16[256,1280]{1,0:T(8,128)(2,1)S(1)}, bf16[256,1280]{1,0:T(8,128)(2,1)}, u32[]{:S(2)}, u32[]{:S(2)}) collective-permute-start(bf16[256,1280]{1,0:T(8,128)(2,1)S(1)} %add_convert_fusion), channel_id=1, source_target_pairs={{0,2},{2,0},{1,3},{3,1},{4,6},{6,4},{5,7},{7,5},{8,10},{10,8},{9,1... | collective-permute-start | bytes 1966088 | tf_op jit(solution)/shard_map/ppermute | solution.py:357
  129.4 1.0 collective-permute-done.6
  130.5 14.1 %collective-permute-done.7 = f32[1,1280]{1,0:T(1,128)S(1)} collective-permute-done((f32[1,1280]{1,0:T(1,128)S(1)}, f32[1,1280]{1,0:T(1,128)S(1)}, u32[]{:S(2)}, u32[]{:S(2)}) %collective-permute-start.7) | collective-permute-done | bytes 5152 | tf_op jit(solution)/shard_map/ppermute | solution.py:357
  145.3 16.7 %all_to_all.25 = bf16[4,80,256]{2,1,0:T(8,128)(2,1)S(1)} all-to-all(bf16[4,80,256]{2,1,0:T(8,128)(2,1)S(1)} %pad_maximum_fusion.1), channel_id=1, replica_groups=mesh['y'=4,'x'=4,'zq'=4,'zp'=2,'core'=2] {'zq'}, dimensions={0} | all-to-all | bytes 327680 | tf_op jit(solution)/shard_map/all_to_all | solution.py:403
  162.8 8.5 %all-to-all-start.4 = ((bf16[16,80,256]{2,1,0:T(8,128)(2,1)}), bf16[16,80,256]{2,1,0:T(8,128)(2,1)S(1)}, u32[]{:S(2)}, u32[]{:S(2)}) async-start(bf16[16,80,256]{2,1,0:T(8,128)(2,1)} %broadcast_in_dim.5), calls=%async_computation.4 | async-start | bytes 1310720 | tf_op jit(solution)/shard_map/all_to_all | solution.py:406
  171.4 3.4 %shard_map.91 = bf16[256,1280]{1,0:T(8,128)(2,1)} custom-call(bf16[256,1280]{1,0:T(8,128)(2,1)} %rows_ref.5, f32[1,1280]{1,0:T(1,128)} %copy-done.2, f32[512,1280]{1,0:T(8,128)} %get-tuple-element.22.keep_ref, bf16[512,1280]{1,0:T(8,128)(2,1)} %copy-done.6, bf16[256,1280]{1,0:T(8,128)(2,1)} %collective-permute-done.8.pair_ref), custom_call_target="tpu_custom_call" | custom-call | tf_op jit(solution)/shard_map/pallas_call | solution.py:335
  174.8 7.3 %all-to-all-done.4.whole_ref = bf16[16,80,256]{2,1,0:T(8,128)(2,1)S(1)} async-done(((bf16[16,80,256]{2,1,0:T(8,128)(2,1)}), bf16[16,80,256]{2,1,0:T(8,128)(2,1)S(1)}, u32[]{:S(2)}, u32[]{:S(2)}) %all-to-all-start.4) | async-done | bytes 655392 | tf_op jit(solution)/shard_map/all_to_all | solution.py:406
  183.0 2.4 %shard_map.92 = f32[240,1280]{1,0:T(8,128)} custom-call(bf16[16,80,256]{2,1,0:T(8,128)(2,1)} %copy-done.5), custom_call_target="tpu_custom_call" | custom-call | tf_op jit(solution)/shard_map/pallas_call | solution.py:347
  (60 shorter events, 7.9 us)
Async XLA Ops:
  7.2 72.8 %all-gather.2.cloned.1.call-start = ((), (), s32[]{:S(2)}) async-start(), calls=%async_computation.5 | async-start | bytes 2785280 | tf_op jit(solution)/shard_map/all_gather | solution.py:377
  8.0 17.1 %collective-permute-start.2 = (bf16[16,1280]{1,0:T(8,128)(2,1)S(1)}, bf16[16,1280]{1,0:T(8,128)(2,1)S(1)}, u32[]{:S(2)}, u32[]{:S(2)}) collective-permute-start(bf16[16,1280]{1,0:T(8,128)(2,1)S(1)} %get-tuple-element.30), channel_id=1, source_target_pairs={{0,4},{4,8},{8,12},{12,0},{1,5},{5,9},{9,13},{13,1},{2,6},{6,10},{... | collective-permute-start | bytes 122888 | tf_op jit(solution)/shard_map/ppermute | solution.py:372
  11.4 13.7 %collective-permute-start.1 = (bf16[16,1280]{1,0:T(8,128)(2,1)S(1)}, bf16[16,1280]{1,0:T(8,128)(2,1)S(1)}, u32[]{:S(2)}, u32[]{:S(2)}) collective-permute-start(bf16[16,1280]{1,0:T(8,128)(2,1)S(1)} %get-tuple-element.30), channel_id=1, source_target_pairs={{0,8},{4,12},{8,0},{12,4},{1,9},{5,13},{9,1},{13,5},{2,10},{6,14},... | collective-permute-start | bytes 122888 | tf_op jit(solution)/shard_map/ppermute | solution.py:372
  16.8 8.3 %collective-permute-start = (bf16[16,1280]{1,0:T(8,128)(2,1)S(1)}, bf16[16,1280]{1,0:T(8,128)(2,1)S(1)}, u32[]{:S(2)}, u32[]{:S(2)}) collective-permute-start(bf16[16,1280]{1,0:T(8,128)(2,1)S(1)} %get-tuple-element.30), channel_id=1, source_target_pairs={{0,12},{4,0},{8,4},{12,8},{1,13},{5,1},{9,5},{13,9},{2,14},{6,2},{... | collective-permute-start | bytes 122888 | tf_op jit(solution)/shard_map/ppermute | solution.py:372
  20.1 1.1 copy-start.1
  21.2 29.6 %copy-start.2 = (f32[1,1280]{1,0:T(1,128)}, f32[1,1280]{1,0:T(1,128)S(1)}, u32[]{:S(2)}) copy-start(f32[1,1280]{1,0:T(1,128)S(1)} %reshape.34.gain_ref) | copy-start | bytes 15364
  23.7 1.1 copy-start
  25.1 29.3 %copy-start.3 = (s32[1,4096]{1,0:T(1,128)S(1)}, s32[1,4096]{1,0:T(1,128)}, u32[]{:S(2)}) copy-start(s32[1,4096]{1,0:T(1,128)} %param.8) | copy-start | bytes 49156
  25.9 23.7 %collective-permute-start.3 = (bf16[256,1280]{1,0:T(8,128)(2,1)S(1)}, bf16[256,1280]{1,0:T(8,128)(2,1)S(1)}, u32[]{:S(2)}, u32[]{:S(2)}) collective-permute-start(bf16[256,1280]{1,0:T(8,128)(2,1)S(1)} %shard_map.86), channel_id=1, source_target_pairs={{0,2},{2,0},{1,3},{3,1},{4,6},{6,4},{5,7},{7,5},{8,10},{10,8},{9,1... | collective-permute-start | bytes 1966088 | tf_op jit(solution)/shard_map/ppermute | solution.py:357
  27.0 27.3 %all-to-all-start = ((bf16[16,160,128]{2,1,0:T(8,128)(2,1)}), bf16[16,160,128]{2,1,0:T(8,128)(2,1)S(1)}, u32[]{:S(2)}, u32[]{:S(2)}) async-start(bf16[16,160,128]{2,1,0:T(8,128)(2,1)} %shard_map.85), calls=%async_computation | async-start | bytes 1310720 | tf_op jit(solution)/shard_map/all_to_all | solution.py:380
  30.6 35.1 %copy-start.9 = (s32[1,4096]{1,0:T(1,128)S(1)}, s32[1,4096]{1,0:T(1,128)}, u32[]{:S(2)}) copy-start(s32[1,4096]{1,0:T(1,128)} %param.9) | copy-start | bytes 49156
  50.8 17.4 %collective-permute-start.4 = (bf16[512,1280]{1,0:T(8,128)(2,1)}, bf16[512,1280]{1,0:T(8,128)(2,1)S(1)}, u32[]{:S(2)}, u32[]{:S(2)}) collective-permute-start(bf16[512,1280]{1,0:T(8,128)(2,1)} %pad_maximum_fusion), channel_id=1, source_target_pairs={{0,1},{1,0},{2,3},{3,2},{4,5},{5,4},{6,7},{7,6},{8,9},{9,8},{10,11... | collective-permute-start | bytes 3932168 | tf_op jit(solution)/shard_map/ppermute | solution.py:357
  50.9 17.4 %copy-start.4 = (s32[2]{0:T(128)}, s32[2]{0:T(128)S(1)}, u32[]{:S(2)}) copy-start(s32[2]{0:T(128)S(1)} %pad_add_fusion.place_ref) | copy-start | bytes 28
  61.4 18.6 %all-to-all-start.1 = ((bf16[4,4,160,128]{3,2,1,0:T(8,128)(2,1)}), bf16[4,4,160,128]{3,2,1,0:T(8,128)(2,1)S(1)}, u32[]{:S(2)}, u32[]{:S(2)}) async-start(bf16[4,4,160,128]{3,2,1,0:T(8,128)(2,1)} %shard_map.87), calls=%async_computation.1 | async-start | bytes 1310720 | tf_op jit(solution)/shard_map/all_to_all | solution.py:382
  80.0 0.8 copy-start.7
  98.5 46.2 %all-to-all-start.2 = ((bf16[16,4,80,256]{3,2,1,0:T(8,128)(2,1)}), bf16[16,4,80,256]{3,2,1,0:T(8,128)(2,1)S(1)}, u32[]{:S(2)}, u32[]{:S(2)}) async-start(bf16[16,4,80,256]{3,2,1,0:T(8,128)(2,1)} %get-tuple-element.24), calls=%async_computation.2 | async-start | bytes 5242880 | tf_op jit(solution)/shard_map/all_to_all | solution.py:389
  112.1 8.6 %collective-permute-start.5 = (bf16[512,1280]{1,0:T(8,128)(2,1)}, bf16[512,1280]{1,0:T(8,128)(2,1)S(1)}, u32[]{:S(2)}, u32[]{:S(2)}) collective-permute-start(bf16[512,1280]{1,0:T(8,128)(2,1)} %get-tuple-element.23), channel_id=1, source_target_pairs={{0,1},{1,0},{2,3},{3,2},{4,5},{5,4},{6,7},{7,6},{8,9},{9,8},{10,11... | collective-permute-start | bytes 3932168 | tf_op jit(solution)/shard_map/ppermute | solution.py:357
  120.6 8.5 %copy-start.10 = (f32[1,1280]{1,0:T(1,128)S(1)}, f32[1,1280]{1,0:T(1,128)}, u32[]{:S(2)}) copy-start(f32[1,1280]{1,0:T(1,128)} %get-tuple-element.25) | copy-start | bytes 15364
  120.6 8.5 %copy-start.11 = (f32[1,1280]{1,0:T(1,128)S(1)}, f32[1,1280]{1,0:T(1,128)}, u32[]{:S(2)}) copy-start(f32[1,1280]{1,0:T(1,128)} %get-tuple-element.26) | copy-start | bytes 15364
  120.6 1.1 copy-start.6
  123.1 22.1 %collective-permute-start.8 = (bf16[256,1280]{1,0:T(8,128)(2,1)S(1)}, bf16[256,1280]{1,0:T(8,128)(2,1)}, u32[]{:S(2)}, u32[]{:S(2)}) collective-permute-start(bf16[256,1280]{1,0:T(8,128)(2,1)S(1)} %add_convert_fusion), channel_id=1, source_target_pairs={{0,2},{2,0},{1,3},{3,1},{4,6},{6,4},{5,7},{7,5},{8,10},{10,8},{9,1... | collective-permute-start | bytes 1966088 | tf_op jit(solution)/shard_map/ppermute | solution.py:357
  129.1 1.3 collective-permute-start.6
  130.3 14.3 %collective-permute-start.7 = (f32[1,1280]{1,0:T(1,128)S(1)}, f32[1,1280]{1,0:T(1,128)S(1)}, u32[]{:S(2)}, u32[]{:S(2)}) collective-permute-start(f32[1,1280]{1,0:T(1,128)S(1)} %add.36), channel_id=1, source_target_pairs={{0,2},{2,0},{1,3},{3,1},{4,6},{6,4},{5,7},{7,5},{8,10},{10,8},{9,1... | collective-permute-start | bytes 15368 | tf_op jit(solution)/shard_map/ppermute | solution.py:357
  162.8 19.2 %all-to-all-start.4 = ((bf16[16,80,256]{2,1,0:T(8,128)(2,1)}), bf16[16,80,256]{2,1,0:T(8,128)(2,1)S(1)}, u32[]{:S(2)}, u32[]{:S(2)}) async-start(bf16[16,80,256]{2,1,0:T(8,128)(2,1)} %broadcast_in_dim.5), calls=%async_computation.4 | async-start | bytes 1310720 | tf_op jit(solution)/shard_map/all_to_all | solution.py:406
  171.4 11.0 %copy-start.8 = (f32[1280]{0:T(1024)S(1)}, f32[1280]{0:T(1024)}, u32[]{:S(2)}) copy-start(f32[1280]{0:T(1024)} %param.11) | copy-start | bytes 15364
  182.1 0.9 copy-start.5
Sparse Core Ops, SparseCore 0:
  26.0 47.7 all-gather.1

commit v7 on v6

--- a/solution.py
+++ b/solution.py
@@ -110,43 +110,36 @@
     return jnp.where(move(row, lanes(shape)), 1.0, 0.0).astype(bf16)
 
 
-def head_kernel(
-    place_ref, normed_hbm, turned_hbm, w_hbm, up_ref, window_ref, grad_hbm, weight_hbm,
-    first, second, key_at, query_at, upstream, same,
-    normed_ref, turned_ref, w_ref, grad_ref, weight_ref, in_sems, out_sems,
+def gather_kernel(half_ref, core_ref, out_ref, turned_ref):
+    for c, part in enumerate((half_ref, core_ref)):
+        rows = slice(2 * CHUNK * c, 2 * CHUNK * c + 2 * CHUNK)
+        out_ref[rows, :] = part[...]
+        turned_ref[:, rows] = part[...].T
+
+
+def blocks_of(total_rows):
+    return [slice(SUPER * b, SUPER * b + SUPER) for b in range(total_rows // SUPER)]
+
+
+def forward_kernel(
+    place_ref, normed_hbm, w_hbm, window_ref, second_hbm, key_hbm, query_hbm, probs_hbm,
+    second, key_at, query_at, probs, first, same, normed_ref, w_ref, in_sems, out_sems,
 ):
     ring, slot = place_ref[0], place_ref[1]
     scaling = HEAD ** (-0.5)
-    total_rows = SLOTS * CHUNK
-    width = normed_ref.shape[-1]
-    blocks = [slice(SUPER * b, SUPER * b + SUPER) for b in range(total_rows // SUPER)]
-    w_copies = [
+    total_rows, width = normed_ref.shape
+    blocks = blocks_of(total_rows)
+    copies = [pltpu.make_async_copy(normed_hbm, normed_ref, in_sems.at[RING])] + [
         pltpu.make_async_copy(w_hbm.at[:, h], w_ref.at[h], in_sems.at[h]) for h in range(RING)
     ]
-    turned_copy = pltpu.make_async_copy(turned_hbm, turned_ref, in_sems.at[RING])
-    normed_copy = pltpu.make_async_copy(normed_hbm, normed_ref, in_sems.at[RING + 1])
-    w_copies[0].start()
-    normed_copy.start()
-    for h in range(1, RING):
-        w_copies[h].start()
-    turned_copy.start()
-    grad_copies = [
-        pltpu.make_async_copy(grad_ref.at[h], grad_hbm.at[h], out_sems.at[h])
-        for h in range(RING)
-    ]
-    weight_copies = [
-        pltpu.make_async_copy(weight_ref.at[h], weight_hbm.at[:, h], out_sems.at[RING + h])
-        for h in range(RING)
-    ]
-    to_wide = shifted(
-        (128, 128), lambda r, c: (c >= 32) & (c < 96) & (r % 64 == c - 32)
-    )
-    to_rest = shifted(
-        (128, 128), lambda r, c: (c >= 96) & (c < 112) & (r % 16 == c - 96)
-    )
-    row = lax.broadcasted_iota(jnp.int32, (CHUNK, 128), 0)
-    keep_wide = row // 128 == lanes((CHUNK, 128)) // 64
-    keep_rest = row // 32 == lanes((CHUNK, 128)) // 16
+    for copy in copies:
+        copy.start()
+    for b, r in enumerate(blocks):
+        line = ring * 8 + (slot ^ XOR_ORDER[b // 2]) * 2 + b % 2
+        labels = jnp.broadcast_to(window_ref[pl.ds(line, 1), :], (SUPER, SUPER))
+        same[r, :] = jnp.where(labels == labels.T, 0.0, -1e30)
+    for copy in copies:
+        copy.wait()
 
     def project(h):
         w = w_ref[h].reshape(PADDED, width)
@@ -160,6 +153,59 @@
             (at >= HEAD) & (at < 2 * HEAD), roll(rounded, HEAD), 0.0
         ).astype(bf16)
 
+    def soften(h):
+        scores = [dot(first[h, r, :], key_at[h, r, :], NT) for r in blocks]
+        for b, r in enumerate(blocks):
+            masked = scores[b] * scaling + same[r, :]
+            powers = jnp.exp(masked - jnp.max(masked, axis=-1, keepdims=True))
+            probs[h, r, :] = powers * (1.0 / jnp.sum(powers, axis=-1, keepdims=True))
+
+    project(0)
+    for h in range(RING):
+        if h + 1 < RING:
+            project(h + 1)
+        soften(h)
+    copies = [
+        pltpu.make_async_copy(src, dst, out_sems.at[i])
+        for i, (src, dst) in enumerate(
+            ((second, second_hbm), (key_at, key_hbm), (query_at, query_hbm), (probs, probs_hbm))
+        )
+    ]
+    for copy in copies:
+        copy.start()
+    for copy in copies:
+        copy.wait()
+
+
+def head_kernel(
+    turned_hbm, up_ref, second_hbm, key_hbm, query_hbm, probs_hbm, grad_hbm, weight_hbm,
+    second, key_at, query_at, probs, upstream, turned_ref, grad_ref, weight_ref,
+    in_sems, out_sems,
+):
+    scaling = HEAD ** (-0.5)
+    width, total_rows = turned_ref.shape
+    blocks = blocks_of(total_rows)
+    copies = [
+        pltpu.make_async_copy(src, dst, in_sems.at[i])
+        for i, (src, dst) in enumerate(
+            (
+                (second_hbm, second), (probs_hbm, probs), (key_hbm, key_at),
+                (query_hbm, query_at), (turned_hbm, turned_ref),
+            )
+        )
+    ]
+    for copy in copies:
+        copy.start()
+    to_wide = shifted(
+        (128, 128), lambda r, c: (c >= 32) & (c < 96) & (r % 64 == c - 32)
+    )
+    to_rest = shifted(
+        (128, 128), lambda r, c: (c >= 96) & (c < 112) & (r % 16 == c - 96)
+    )
+    row = lax.broadcasted_iota(jnp.int32, (CHUNK, 128), 0)
+    keep_wide = row // 128 == lanes((CHUNK, 128)) // 64
+    keep_rest = row // 32 == lanes((CHUNK, 128)) // 16
+
     def spread(h):
         for c in range(SLOTS):
             top, low = up_ref[h, c, :128, :], up_ref[h, c, 128:, :]
@@ -169,20 +215,17 @@
             upstream[h, CHUNK * c : CHUNK * c + CHUNK, :] = both.astype(bf16)
 
     def attend(h):
-        scores = [dot(first[h, r, :], key_at[h, r, :], NT) for r in blocks]
         grad_probs = [dot(upstream[h, r, :], second[h, r, :], NT) for r in blocks]
-        probs, grad_scores = [], []
+        grad_scores, probs_low = [], []
         for b, r in enumerate(blocks):
-            masked = scores[b] * scaling + same[r, :]
-            powers = jnp.exp(masked - jnp.max(masked, axis=-1, keepdims=True))
-            prob = powers * (1.0 / jnp.sum(powers, axis=-1, keepdims=True))
+            prob = probs[h, r, :]
             row_dot = jnp.sum(prob * grad_probs[b], axis=-1, keepdims=True)
             grad_scores.append((prob * (grad_probs[b] - row_dot)).astype(bf16))
-            probs.append(prob.astype(bf16))
+            probs_low.append(prob.astype(bf16))
         for b, r in enumerate(blocks):
             grad_query = dot(grad_scores[b], key_at[h, r, :], NN)
             grad_key = dot(grad_scores[b], query_at[h, r, :], TN)
-            grad_value = dot(probs[b], upstream[h, r, :], TN)
+            grad_value = dot(probs_low[b], upstream[h, r, :], TN)
             grad_ref[h, r, :128] = ((grad_query + grad_key[:, :128]) * scaling).astype(bf16)
             grad_ref[h, r, 128:] = (grad_key[:, 128:] * scaling + grad_value).astype(bf16)
 
@@ -190,25 +233,22 @@
         part = dot(turned_ref[...], grad_ref[h], NN).astype(bf16)
         weight_ref[h] = part.reshape(16, width // 16, PADDED)
 
-    for b, r in enumerate(blocks):
-        line = ring * 8 + (slot ^ XOR_ORDER[b // 2]) * 2 + b % 2
-        labels = jnp.broadcast_to(window_ref[pl.ds(line, 1), :], (SUPER, SUPER))
-        same[r, :] = jnp.where(labels == labels.T, 0.0, -1e30)
-    spread(0)
-    w_copies[0].wait()
-    normed_copy.wait()
-    project(0)
-    for copy in w_copies[1:] + [turned_copy]:
+    for h in range(RING):
+        spread(h)
+    for copy in copies:
         copy.wait()
+    attend(0)
     for h in range(RING):
         if h + 1 < RING:
-            project(h + 1)
-            spread(h + 1)
-        attend(h)
+            attend(h + 1)
         weigh(h)
-    for copy in weight_copies + grad_copies:
+    copies = [pltpu.make_async_copy(grad_ref, grad_hbm, out_sems.at[RING])] + [
+        pltpu.make_async_copy(weight_ref.at[h], weight_hbm.at[:, h], out_sems.at[h])
+        for h in range(RING)
+    ]
+    for copy in copies:
         copy.start()
-    for copy in weight_copies + grad_copies:
+    for copy in copies:
         copy.wait()
 
 
@@ -278,33 +318,74 @@
     )(rows, gain)
 
 
-def head_call(place, normed, turned, weights, upstream, windows):
+def gather_call(half, core):
+    rows, width = 2 * half.shape[0], half.shape[1]
+    return pl.pallas_call(
+        gather_kernel,
+        out_shape=(
+            jax.ShapeDtypeStruct((rows, width), bf16),
+            jax.ShapeDtypeStruct((width, rows), bf16),
+        ),
+        in_specs=[vmem(), vmem()],
+        out_specs=(vmem(), vmem()),
+        compiler_params=params(BIG),
+    )(half, core)
+
+
+def hbm():
+    return pl.BlockSpec(memory_space=pl.ANY)
+
+
+def kept(rows):
+    return (
+        ((RING, rows, 128), bf16),
+        ((RING, rows, 128), bf16),
+        ((RING, rows, PADDED), bf16),
+        ((RING, rows, SUPER), f32),
+    )
+
+
+def forward_call(place, normed, weights, windows):
     rows, width = normed.shape
+    return pl.pallas_call(
+        forward_kernel,
+        out_shape=tuple(jax.ShapeDtypeStruct(*each) for each in kept(rows)),
+        in_specs=[smem(), hbm(), hbm(), vmem()],
+        out_specs=(hbm(),) * 4,
+        scratch_shapes=[pltpu.VMEM(*each) for each in kept(rows)]
+        + [
+            pltpu.VMEM((RING, rows, 128), bf16),
+            pltpu.VMEM((rows, SUPER), f32),
+            pltpu.VMEM((rows, width), bf16),
+            pltpu.VMEM((RING, 16, 16, width), bf16),
+            pltpu.SemaphoreType.DMA((RING + 1,)),
+            pltpu.SemaphoreType.DMA((4,)),
+        ],
+        compiler_params=params(BIG),
+    )(place, normed, weights, windows)
+
+
+def head_call(turned, upstream, forward):
+    width, rows = turned.shape
     return pl.pallas_call(
         head_kernel,
         out_shape=(
             jax.ShapeDtypeStruct((RING, rows, PADDED), bf16),
             jax.ShapeDtypeStruct((16, RING, width // 16, PADDED), bf16),
         ),
-        in_specs=[smem()] + [pl.BlockSpec(memory_space=pl.ANY)] * 3 + [vmem()] * 2,
-        out_specs=(pl.BlockSpec(memory_space=pl.ANY),) * 2,
-        scratch_shapes=[
+        in_specs=[hbm(), vmem()] + [hbm()] * 4,
+        out_specs=(hbm(),) * 2,
+        scratch_shapes=[pltpu.VMEM(*each) for each in kept(rows)]
+        + [
             pltpu.VMEM((RING, rows, 128), bf16),
-            pltpu.VMEM((RING, rows, 128), bf16),
-            pltpu.VMEM((RING, rows, 128), bf16),
-            pltpu.VMEM((RING, rows, PADDED), bf16),
-            pltpu.VMEM((RING, rows, 128), bf16),
-            pltpu.VMEM((rows, SUPER), f32),
-            pltpu.VMEM((rows, width), bf16),
             pltpu.VMEM((width, rows), bf16),
-            pltpu.VMEM((RING, 16, 16, width), bf16),
             pltpu.VMEM((RING, rows, PADDED), bf16),
             pltpu.VMEM((RING, 16, width // 16, PADDED), bf16),
-            pltpu.SemaphoreType.DMA((RING + 2,)),
-            pltpu.SemaphoreType.DMA((2 * RING,)),
+            pltpu.SemaphoreType.DMA((5,)),
+            pltpu.SemaphoreType.DMA((RING + 1,)),
         ],
         compiler_params=params(BIG),
-    )(place, normed, turned, weights, upstream, windows)
+    )(turned, upstream, *forward)
 
 
 def back_call(grads, weights, normed, half, dtype):
@@ -382,9 +463,10 @@
     upstream = lax.all_to_all(permuted, "zq", split_axis=0, concat_axis=0)
 
     half = jnp.concatenate([own, swap(own, "zp")], axis=0)
-    normed = jnp.concatenate([half, swap(half, "core")], axis=0)
+    normed, turned = gather_call(half, swap(half, "core"))
     windows = window_id.reshape(32, 128).astype(f32)
-    grads, weight_part = head_call(place, normed, normed.T, weights, upstream, windows)
+    forward = forward_call(place, normed, weights, windows)
+    grads, weight_part = head_call(turned, upstream, forward)
 
     arrived = lax.all_to_all(weight_part, ("y", "x"), split_axis=0, concat_axis=0)
     summed = jnp.sum(arrived.astype(f32), axis=0).astype(bf16)

time: 193 us -> 188 us (0.974)
  Pallas kernels: 45.7 us -> 55.8 us
  local copies, waits for them, and re-layouts: 15 us -> 5.39 us
  starting transfers between devices: 45.1 us -> 38.9 us
    pallas_call x0 -> x2, Pallas kernels: none -> 16.1 us  [the longest x1 11 us: forward_call(): pl.pallas_call(forward_kernel, out_shape=tuple((jax.ShapeDtypeStruct(*eac...]
    all_to_all x1, waiting for transfers between devices: 6.08 us -> 0.01 us  [on_device(): upstream = lax.all_to_all(permuted, 'zq', split_axis=0, concat_axis=0)]
    pallas_call x1, Pallas kernels: 17.7 us -> 11.6 us  [head_call(): pl.pallas_call(head_kernel, out_shape=(jax.ShapeDtypeStruct((RING, rows,...]
    transpose x1 -> x0, local copies, waits for them, and re-layouts: 4.51 us -> none  [on_device(): grads, weight_part = head_call(place, normed, normed.T, weights, upstream...]
    ppermute x6, starting transfers between devices: 9.7 us -> 5.5 us  [swap(): return lax.ppermute(x, axis, [(0, 1), (1, 0)])]
    all_to_all x1, waiting for transfers between devices: 0.01 us -> 4 us  [on_device(): lax.all_to_all(weight_part, ('y', 'x'), split_axis=0, concat_axis=0)]
    unnamed x33 -> x34, local copies, waits for them, and re-layouts: 6.83 us -> 2.9 us
    all_gather x1, waiting for transfers between devices: 0.01 us -> 3.57 us  [on_device(): weights = lax.all_gather(ordered, ('y', 'x'), axis=0, tiled=True)]
  transfers between devices with their start and end apart: 14 -> 14, of which waited for: 6 -> 7; matrix products, arithmetic and copies ran while one was open for 6% -> 2% of each run, Pallas kernels for 13% -> 22%
where the time goes in v7:
time: 188 us; the launch traced here: 187 us
  Pallas kernels  55.8 us (30%)
  waiting for transfers between devices  52.1 us (28%)
  starting transfers between devices  38.9 us (21%)
  blocking collectives  16.1 us (9%)
  between operations  14.3 us (8%)
  local copies, waits for them, and re-layouts  5.39 us (3%)
  other arithmetic  3.92 us (2%)
    ppermute x6, waiting for transfers between devices, swap(): return lax.ppermute(x, axis, [(0, 1), (1, 0)])  33.6 us
    all_to_all x1, blocking collectives, on_device(): arrived = lax.all_to_all(message, 'zq', split_axis=0, concat_axis=0)  16.1 us
    pallas_call x2, Pallas kernels, back_call(): pl.pallas_call(back_kernel, grid=(width // piece,), out_shape=(jax.ShapeD...  12.5 us
    pallas_call x1, Pallas kernels, head_call(): pl.pallas_call(head_kernel, out_shape=(jax.ShapeDtypeStruct((RING, rows,...  11.6 us
    ppermute x3, starting transfers between devices, on_device(): lax.ppermute(share, 'zq', [(i, (i + k) % RING) for i in range(RING)])  11.4 us
    pallas_call x1, Pallas kernels, forward_call(): pl.pallas_call(forward_kernel, out_shape=tuple((jax.ShapeDtypeStruct(*eac...  11 us
    all_to_all x1, starting transfers between devices, on_device(): whole = lax.all_to_all(copies, ('y', 'x'), split_axis=0, concat_axis=0)  8.86 us
    pallas_call x1, Pallas kernels, permute_call(): pl.pallas_call(permute_kernel, out_shape=jax.ShapeDtypeStruct((RING, SLOT...  7.07 us
  transfers between devices with their start and end apart: 14, of which 7 were waited for; matrix products, arithmetic and copies ran while one was open for 2% of the time, Pallas kernels for 22%

profile of v7, /device:TPU:2, one launch (start us, length us, event | category | flops | bytes accessed | tf_op | source)
XLA Modules:
  0.0 186.6 jit_solution(3771830542076430368)
XLA Ops:
  7.2 0.9 constant_dynamic-update-slice_fusion.9
  8.1 3.3 %collective-permute-start.2 = (bf16[16,1280]{1,0:T(8,128)(2,1)S(1)}, bf16[16,1280]{1,0:T(8,128)(2,1)S(1)}, u32[]{:S(2)}, u32[]{:S(2)}) collective-permute-start(bf16[16,1280]{1,0:T(8,128)(2,1)S(1)} %get-tuple-element.42), channel_id=1, source_target_pairs={{0,4},{4,8},{8,12},{12,0},{1,5},{5,9},{9,13},{13,1},{2,6},{6,10},{... | collective-permute-start | bytes 122888 | tf_op jit(solution)/shard_map/ppermute | solution.py:453
  11.4 5.4 %collective-permute-start.1 = (bf16[16,1280]{1,0:T(8,128)(2,1)S(1)}, bf16[16,1280]{1,0:T(8,128)(2,1)S(1)}, u32[]{:S(2)}, u32[]{:S(2)}) collective-permute-start(bf16[16,1280]{1,0:T(8,128)(2,1)S(1)} %get-tuple-element.42), channel_id=1, source_target_pairs={{0,8},{4,12},{8,0},{12,4},{1,9},{5,13},{9,1},{13,5},{2,10},{6,14},... | collective-permute-start | bytes 122888 | tf_op jit(solution)/shard_map/ppermute | solution.py:453
  16.8 2.7 %collective-permute-start = (bf16[16,1280]{1,0:T(8,128)(2,1)S(1)}, bf16[16,1280]{1,0:T(8,128)(2,1)S(1)}, u32[]{:S(2)}, u32[]{:S(2)}) collective-permute-start(bf16[16,1280]{1,0:T(8,128)(2,1)S(1)} %get-tuple-element.42), channel_id=1, source_target_pairs={{0,12},{4,0},{8,4},{12,8},{1,13},{5,1},{9,5},{13,9},{2,14},{6,2},{... | collective-permute-start | bytes 122888 | tf_op jit(solution)/shard_map/ppermute | solution.py:453
  19.5 0.7 reshape.34.gain_ref
  20.2 1.1 copy-done.1
  21.3 2.5 %shard_map.85 = bf16[16,160,128]{2,1,0:T(8,128)(2,1)} custom-call(bf16[256,1280]{1,0:T(8,128)(2,1)S(1)} %copy-done.1), custom_call_target="tpu_custom_call" | custom-call | tf_op jit(solution)/shard_map/pallas_call | solution.py:291
  24.9 1.1 collective-permute-start.3
  26.0 3.6 %all-to-all-start = ((bf16[16,160,128]{2,1,0:T(8,128)(2,1)}), bf16[16,160,128]{2,1,0:T(8,128)(2,1)S(1)}, u32[]{:S(2)}, u32[]{:S(2)}) async-start(bf16[16,160,128]{2,1,0:T(8,128)(2,1)} %shard_map.85), calls=%async_computation | async-start | bytes 1310720 | tf_op jit(solution)/shard_map/all_to_all | solution.py:461
  29.7 18.5 %collective-permute-done.3 = bf16[256,1280]{1,0:T(8,128)(2,1)S(1)} collective-permute-done((bf16[256,1280]{1,0:T(8,128)(2,1)S(1)}, bf16[256,1280]{1,0:T(8,128)(2,1)S(1)}, u32[]{:S(2)}, u32[]{:S(2)}) %collective-permute-start.3) | collective-permute-done | bytes 655392 | tf_op jit(solution)/shard_map/ppermute | solution.py:438
  48.4 4.6 %all-to-all-done.in_ref = bf16[16,160,128]{2,1,0:T(8,128)(2,1)S(1)} async-done(((bf16[16,160,128]{2,1,0:T(8,128)(2,1)}), bf16[16,160,128]{2,1,0:T(8,128)(2,1)S(1)}, u32[]{:S(2)}, u32[]{:S(2)}) %all-to-all-start) | async-done | bytes 655392 | tf_op jit(solution)/shard_map/all_to_all | solution.py:461
  53.0 7.1 %shard_map.88 = bf16[4,4,160,128]{3,2,1,0:T(8,128)(2,1)} custom-call(s32[2]{0:T(128)S(1)} %pad_add_fusion.place_ref, s32[4096]{0:T(1024)S(1)} %bitcast.12, bf16[16,160,128]{2,1,0:T(8,128)(2,1)S(1)} %all-to-all-done.in_ref), custom_call_target="tpu_custom_call" | custom-call | tf_op jit(solution)/shard_map/pallas_call | solution.py:301
  60.1 3.8 %all-to-all-start.1 = ((bf16[4,4,160,128]{3,2,1,0:T(8,128)(2,1)}), bf16[4,4,160,128]{3,2,1,0:T(8,128)(2,1)S(1)}, u32[]{:S(2)}, u32[]{:S(2)}) async-start(bf16[4,4,160,128]{3,2,1,0:T(8,128)(2,1)} %shard_map.88), calls=%async_computation.1 | async-start | bytes 1310720 | tf_op jit(solution)/shard_map/all_to_all | solution.py:463
  64.5 5.2 %shard_map.87 = (bf16[1024,1280]{1,0:T(8,128)(2,1)}, bf16[1280,1024]{1,0:T(8,128)(2,1)}) custom-call(bf16[512,1280]{1,0:T(8,128)(2,1)} %copy-done.6, bf16[512,1280]{1,0:T(8,128)(2,1)} %collective-permute-done.4.core_ref), custom_call_target="tpu_custom_call" | custom-call | tf_op jit(solution)/shard_map/pallas_call | solution.py:323
  69.7 3.6 %all-gather.2.cloned.1.call-done = bf16[1024,1280]{1,0:T(8,128)(2,1)} async-done(((bf16[64,1280]{1,0:T(8,128)(2,1)}), bf16[1024,1280]{1,0:T(8,128)(2,1)}) %all-gather.2.cloned.1.call-update) | async-done | bytes 2621456 | tf_op jit(solution)/shard_map/all_gather | solution.py:458
  73.3 11.0 %shard_map.89 = (bf16[4,1024,128]{2,1,0:T(8,128)(2,1)}, bf16[4,1024,128]{2,1,0:T(8,128)(2,1)}, bf16[4,1024,256]{2,1,0:T(8,128)(2,1)}, f32[4,1024,128]{2,1,0:T(8,128)}) custom-call(s32[2]{0:T(128)} %copy-done.4, bf16[1024,1280]{1,0:T(8,128)(2,1)} %get-tuple-element.25.normed_hbm.normed_ref, bf16[16,4,16,1280]{3,2,1,0:T(8,128)(2,1)} %bitcast.13, ...), custom_call_target="tpu_custom_call" | custom-call | tf_op jit(solution)/shard_map/pallas_call | solution.py:350
  84.2 0.8 copy-done.8
  85.1 11.6 %shard_map.90 = (bf16[4,1024,256]{2,1,0:T(8,128)(2,1)}, bf16[16,4,80,256]{3,2,1,0:T(8,128)(2,1)}) custom-call(bf16[1280,1024]{1,0:T(8,128)(2,1)} %get-tuple-element.23.turned_hbm, bf16[4,4,160,128]{3,2,1,0:T(8,128)(2,1)} %copy-done.8, bf16[4,1024,128]{2,1,0:T(8,128)(2,1)} %get-tuple-element.29.second_hbm, bf16[4,1024,128]{2,1,0:T(8,128)(2,1)} %get-tuple-element.30.key_hbm, ...), custom_call_target="tpu_custom_call" | custom-call | tf_op jit(solution)/shard_map/pallas_call | solution.py:370
  96.7 5.7 %all-to-all-start.2 = ((bf16[16,4,80,256]{3,2,1,0:T(8,128)(2,1)}), bf16[16,4,80,256]{3,2,1,0:T(8,128)(2,1)S(1)}, u32[]{:S(2)}, u32[]{:S(2)}) async-start(bf16[16,4,80,256]{3,2,1,0:T(8,128)(2,1)} %get-tuple-element.36), calls=%async_computation.2 | async-start | bytes 5242880 | tf_op jit(solution)/shard_map/all_to_all | solution.py:471
  102.5 6.1 %shard_map.92 = (bf16[512,1280]{1,0:T(8,128)(2,1)}, f32[1,1280]{1,0:T(1,128)}) custom-call(bf16[4,1024,256]{2,1,0:T(8,128)(2,1)} %get-tuple-element.33.grad_ref, bf16[16,4,16,1280]{3,2,1,0:T(8,128)(2,1)} %bitcast.14, bf16[1024,1280]{1,0:T(8,128)(2,1)} %get-tuple-element.25.normed_hbm.normed_ref), custom_call_target="tpu_custom_call" | custom-call | tf_op jit(solution)/shard_map/pallas_call | solution.py:394
  108.9 6.4 %shard_map.91 = (f32[512,1280]{1,0:T(8,128)}, f32[1,1280]{1,0:T(1,128)}) custom-call(bf16[4,1024,256]{2,1,0:T(8,128)(2,1)} %get-tuple-element.33.grad_ref, bf16[16,4,16,1280]{3,2,1,0:T(8,128)(2,1)} %bitcast.15, bf16[1024,1280]{1,0:T(8,128)(2,1)} %get-tuple-element.25.normed_hbm.normed_ref), custom_call_target="tpu_custom_call" | custom-call | tf_op jit(solution)/shard_map/pallas_call | solution.py:394
  115.3 1.9 %add_convert_fusion = bf16[256,1280]{1,0:T(8,128)(2,1)S(1)} fusion(f32[512,1280]{1,0:T(8,128)} %get-tuple-element.34.keep_ref, bf16[512,1280]{1,0:T(8,128)(2,1)S(1)} %collective-permute-done.5.core_ref), kind=kLoop, calls=%fused_computation | loop fusion | flops 983040 | bytes 2621440 | tf_op jit(solution)/shard_map/convert_element_type | solution.py:477
  117.2 3.5 %collective-permute-start.8 = (bf16[256,1280]{1,0:T(8,128)(2,1)S(1)}, bf16[256,1280]{1,0:T(8,128)(2,1)}, u32[]{:S(2)}, u32[]{:S(2)}) collective-permute-start(bf16[256,1280]{1,0:T(8,128)(2,1)S(1)} %add_convert_fusion), channel_id=1, source_target_pairs={{0,2},{2,0},{1,3},{3,1},{4,6},{6,4},{5,7},{7,5},{8,10},{10,8},{9,1... | collective-permute-start | bytes 1966088 | tf_op jit(solution)/shard_map/ppermute | solution.py:438
  121.0 1.0 collective-permute-done.6
  122.2 14.1 %collective-permute-done.7 = f32[1,1280]{1,0:T(1,128)S(1)} collective-permute-done((f32[1,1280]{1,0:T(1,128)S(1)}, f32[1,1280]{1,0:T(1,128)S(1)}, u32[]{:S(2)}, u32[]{:S(2)}) %collective-permute-start.7) | collective-permute-done | bytes 5152 | tf_op jit(solution)/shard_map/ppermute | solution.py:438
  136.4 4.0 %all-to-all-done.2 = bf16[16,4,80,256]{3,2,1,0:T(8,128)(2,1)S(1)} async-done(((bf16[16,4,80,256]{3,2,1,0:T(8,128)(2,1)}), bf16[16,4,80,256]{3,2,1,0:T(8,128)(2,1)S(1)}, u32[]{:S(2)}, u32[]{:S(2)}) %all-to-all-start.2) | async-done | bytes 2621472 | tf_op jit(solution)/shard_map/all_to_all | solution.py:471
  140.9 16.1 %all_to_all.25 = bf16[4,80,256]{2,1,0:T(8,128)(2,1)S(1)} all-to-all(bf16[4,80,256]{2,1,0:T(8,128)(2,1)S(1)} %pad_maximum_fusion), channel_id=1, replica_groups=mesh['y'=4,'x'=4,'zq'=4,'zp'=2,'core'=2] {'zq'}, dimensions={0} | all-to-all | bytes 327680 | tf_op jit(solution)/shard_map/all_to_all | solution.py:485
  157.0 0.9 broadcast_in_dim.5
  157.9 8.9 %all-to-all-start.4 = ((bf16[16,80,256]{2,1,0:T(8,128)(2,1)}), bf16[16,80,256]{2,1,0:T(8,128)(2,1)S(1)}, u32[]{:S(2)}, u32[]{:S(2)}) async-start(bf16[16,80,256]{2,1,0:T(8,128)(2,1)} %broadcast_in_dim.5), calls=%async_computation.4 | async-start | bytes 1310720 | tf_op jit(solution)/shard_map/all_to_all | solution.py:488
  166.8 3.4 %shard_map.93 = bf16[256,1280]{1,0:T(8,128)(2,1)} custom-call(bf16[256,1280]{1,0:T(8,128)(2,1)} %rows_ref.5, f32[1,1280]{1,0:T(1,128)} %copy-done.2, f32[512,1280]{1,0:T(8,128)} %get-tuple-element.34.keep_ref, bf16[512,1280]{1,0:T(8,128)(2,1)} %copy-done.7, bf16[256,1280]{1,0:T(8,128)(2,1)} %collective-permute-done.8.pair_ref), custom_call_target="tpu_custom_call" | custom-call | tf_op jit(solution)/shard_map/pallas_call | solution.py:416
  170.2 6.4 %all-to-all-done.4.whole_ref = bf16[16,80,256]{2,1,0:T(8,128)(2,1)S(1)} async-done(((bf16[16,80,256]{2,1,0:T(8,128)(2,1)}), bf16[16,80,256]{2,1,0:T(8,128)(2,1)S(1)}, u32[]{:S(2)}, u32[]{:S(2)}) %all-to-all-start.4) | async-done | bytes 655392 | tf_op jit(solution)/shard_map/all_to_all | solution.py:488
  177.4 2.4 %shard_map.94 = f32[240,1280]{1,0:T(8,128)} custom-call(bf16[16,80,256]{2,1,0:T(8,128)(2,1)} %copy-done.5), custom_call_target="tpu_custom_call" | custom-call | tf_op jit(solution)/shard_map/pallas_call | solution.py:428
  (61 shorter events, 4.3 us)
Async XLA Ops:
  7.2 16.6 %copy-start = (bf16[256,1280]{1,0:T(8,128)(2,1)S(1)}, bf16[256,1280]{1,0:T(8,128)(2,1)}, u32[]{:S(2)}) copy-start(bf16[256,1280]{1,0:T(8,128)(2,1)} %rows_ref.5) | copy-start | bytes 1966084
  7.2 66.1 %all-gather.2.cloned.1.call-start = ((), (), s32[]{:S(2)}) async-start(), calls=%async_computation.5 | async-start | bytes 2785280 | tf_op jit(solution)/shard_map/all_gather | solution.py:458
  8.1 16.0 %collective-permute-start.2 = (bf16[16,1280]{1,0:T(8,128)(2,1)S(1)}, bf16[16,1280]{1,0:T(8,128)(2,1)S(1)}, u32[]{:S(2)}, u32[]{:S(2)}) collective-permute-start(bf16[16,1280]{1,0:T(8,128)(2,1)S(1)} %get-tuple-element.42), channel_id=1, source_target_pairs={{0,4},{4,8},{8,12},{12,0},{1,5},{5,9},{9,13},{13,1},{2,6},{6,10},{... | collective-permute-start | bytes 122888 | tf_op jit(solution)/shard_map/ppermute | solution.py:453
  11.4 12.6 %collective-permute-start.1 = (bf16[16,1280]{1,0:T(8,128)(2,1)S(1)}, bf16[16,1280]{1,0:T(8,128)(2,1)S(1)}, u32[]{:S(2)}, u32[]{:S(2)}) collective-permute-start(bf16[16,1280]{1,0:T(8,128)(2,1)S(1)} %get-tuple-element.42), channel_id=1, source_target_pairs={{0,8},{4,12},{8,0},{12,4},{1,9},{5,13},{9,1},{13,5},{2,10},{6,14},... | collective-permute-start | bytes 122888 | tf_op jit(solution)/shard_map/ppermute | solution.py:453
  16.8 7.2 %collective-permute-start = (bf16[16,1280]{1,0:T(8,128)(2,1)S(1)}, bf16[16,1280]{1,0:T(8,128)(2,1)S(1)}, u32[]{:S(2)}, u32[]{:S(2)}) collective-permute-start(bf16[16,1280]{1,0:T(8,128)(2,1)S(1)} %get-tuple-element.42), channel_id=1, source_target_pairs={{0,12},{4,0},{8,4},{12,8},{1,13},{5,1},{9,5},{13,9},{2,14},{6,2},{... | collective-permute-start | bytes 122888 | tf_op jit(solution)/shard_map/ppermute | solution.py:453
  20.2 1.1 copy-start.1
  21.3 2.8 %copy-start.2 = (f32[1,1280]{1,0:T(1,128)}, f32[1,1280]{1,0:T(1,128)S(1)}, u32[]{:S(2)}) copy-start(f32[1,1280]{1,0:T(1,128)S(1)} %reshape.34.gain_ref) | copy-start | bytes 15364
  24.9 23.3 %collective-permute-start.3 = (bf16[256,1280]{1,0:T(8,128)(2,1)S(1)}, bf16[256,1280]{1,0:T(8,128)(2,1)S(1)}, u32[]{:S(2)}, u32[]{:S(2)}) collective-permute-start(bf16[256,1280]{1,0:T(8,128)(2,1)S(1)} %shard_map.86), channel_id=1, source_target_pairs={{0,2},{2,0},{1,3},{3,1},{4,6},{6,4},{5,7},{7,5},{8,10},{10,8},{9,1... | collective-permute-start | bytes 1966088 | tf_op jit(solution)/shard_map/ppermute | solution.py:438
  26.0 27.0 %all-to-all-start = ((bf16[16,160,128]{2,1,0:T(8,128)(2,1)}), bf16[16,160,128]{2,1,0:T(8,128)(2,1)S(1)}, u32[]{:S(2)}, u32[]{:S(2)}) async-start(bf16[16,160,128]{2,1,0:T(8,128)(2,1)} %shard_map.85), calls=%async_computation | async-start | bytes 1310720 | tf_op jit(solution)/shard_map/all_to_all | solution.py:461
  29.6 23.4 %copy-start.3 = (s32[1,4096]{1,0:T(1,128)S(1)}, s32[1,4096]{1,0:T(1,128)}, u32[]{:S(2)}) copy-start(s32[1,4096]{1,0:T(1,128)} %param.8) | copy-start | bytes 49156
  48.2 11.9 %copy-start.6 = (bf16[512,1280]{1,0:T(8,128)(2,1)}, bf16[512,1280]{1,0:T(8,128)(2,1)S(1)}, u32[]{:S(2)}) copy-start(bf16[512,1280]{1,0:T(8,128)(2,1)S(1)} %constant_dynamic-update-slice_fusion.half_ref) | copy-start | bytes 3932164
  48.2 16.3 %collective-permute-start.4 = (bf16[512,1280]{1,0:T(8,128)(2,1)S(1)}, bf16[512,1280]{1,0:T(8,128)(2,1)}, u32[]{:S(2)}, u32[]{:S(2)}) collective-permute-start(bf16[512,1280]{1,0:T(8,128)(2,1)S(1)} %constant_dynamic-update-slice_fusion.half_ref), channel_id=1, source_target_pairs={{0,1},{1,0},{2,3},{3,2},{4,5},{5,4},{6,7},{7,6},{8,9},{9,8},{10,11... | collective-permute-start | bytes 3932168 | tf_op jit(solution)/shard_map/ppermute | solution.py:438
  48.4 11.7 %copy-start.4 = (s32[2]{0:T(128)}, s32[2]{0:T(128)S(1)}, u32[]{:S(2)}) copy-start(s32[2]{0:T(128)S(1)} %pad_add_fusion.place_ref) | copy-start | bytes 28
  53.0 10.9 %copy-start.10 = (s32[1,4096]{1,0:T(1,128)S(1)}, s32[1,4096]{1,0:T(1,128)}, u32[]{:S(2)}) copy-start(s32[1,4096]{1,0:T(1,128)} %param.9) | copy-start | bytes 49156
  60.1 24.1 %all-to-all-start.1 = ((bf16[4,4,160,128]{3,2,1,0:T(8,128)(2,1)}), bf16[4,4,160,128]{3,2,1,0:T(8,128)(2,1)S(1)}, u32[]{:S(2)}, u32[]{:S(2)}) async-start(bf16[4,4,160,128]{3,2,1,0:T(8,128)(2,1)} %shard_map.88), calls=%async_computation.1 | async-start | bytes 1310720 | tf_op jit(solution)/shard_map/all_to_all | solution.py:463
  84.2 0.8 copy-start.8
  96.7 43.7 %all-to-all-start.2 = ((bf16[16,4,80,256]{3,2,1,0:T(8,128)(2,1)}), bf16[16,4,80,256]{3,2,1,0:T(8,128)(2,1)S(1)}, u32[]{:S(2)}, u32[]{:S(2)}) async-start(bf16[16,4,80,256]{3,2,1,0:T(8,128)(2,1)} %get-tuple-element.36), calls=%async_computation.2 | async-start | bytes 5242880 | tf_op jit(solution)/shard_map/all_to_all | solution.py:471
  108.6 6.7 %collective-permute-start.5 = (bf16[512,1280]{1,0:T(8,128)(2,1)}, bf16[512,1280]{1,0:T(8,128)(2,1)S(1)}, u32[]{:S(2)}, u32[]{:S(2)}) collective-permute-start(bf16[512,1280]{1,0:T(8,128)(2,1)} %get-tuple-element.35), channel_id=1, source_target_pairs={{0,1},{1,0},{2,3},{3,2},{4,5},{5,4},{6,7},{7,6},{8,9},{9,8},{10,11... | collective-permute-start | bytes 3932168 | tf_op jit(solution)/shard_map/ppermute | solution.py:438
  115.3 2.0 %copy-start.7 = (bf16[512,1280]{1,0:T(8,128)(2,1)}, bf16[512,1280]{1,0:T(8,128)(2,1)S(1)}, u32[]{:S(2)}) copy-start(bf16[512,1280]{1,0:T(8,128)(2,1)S(1)} %collective-permute-done.5.core_ref) | copy-start | bytes 3932164
  115.3 5.5 %copy-start.11 = (f32[1,1280]{1,0:T(1,128)S(1)}, f32[1,1280]{1,0:T(1,128)}, u32[]{:S(2)}) copy-start(f32[1,1280]{1,0:T(1,128)} %get-tuple-element.37) | copy-start | bytes 15364
  115.3 5.4 %copy-start.12 = (f32[1,1280]{1,0:T(1,128)S(1)}, f32[1,1280]{1,0:T(1,128)}, u32[]{:S(2)}) copy-start(f32[1,1280]{1,0:T(1,128)} %get-tuple-element.38) | copy-start | bytes 15364
  117.2 23.7 %collective-permute-start.8 = (bf16[256,1280]{1,0:T(8,128)(2,1)S(1)}, bf16[256,1280]{1,0:T(8,128)(2,1)}, u32[]{:S(2)}, u32[]{:S(2)}) collective-permute-start(bf16[256,1280]{1,0:T(8,128)(2,1)S(1)} %add_convert_fusion), channel_id=1, source_target_pairs={{0,2},{2,0},{1,3},{3,1},{4,6},{6,4},{5,7},{7,5},{8,10},{10,8},{9,1... | collective-permute-start | bytes 1966088 | tf_op jit(solution)/shard_map/ppermute | solution.py:438
  120.7 1.3 collective-permute-start.6
  122.0 14.3 %collective-permute-start.7 = (f32[1,1280]{1,0:T(1,128)S(1)}, f32[1,1280]{1,0:T(1,128)S(1)}, u32[]{:S(2)}, u32[]{:S(2)}) collective-permute-start(f32[1,1280]{1,0:T(1,128)S(1)} %add.36), channel_id=1, source_target_pairs={{0,2},{2,0},{1,3},{3,1},{4,6},{6,4},{5,7},{7,5},{8,10},{10,8},{9,1... | collective-permute-start | bytes 15368 | tf_op jit(solution)/shard_map/ppermute | solution.py:438
  157.9 18.7 %all-to-all-start.4 = ((bf16[16,80,256]{2,1,0:T(8,128)(2,1)}), bf16[16,80,256]{2,1,0:T(8,128)(2,1)S(1)}, u32[]{:S(2)}, u32[]{:S(2)}) async-start(bf16[16,80,256]{2,1,0:T(8,128)(2,1)} %broadcast_in_dim.5), calls=%async_computation.4 | async-start | bytes 1310720 | tf_op jit(solution)/shard_map/all_to_all | solution.py:488
  166.7 10.0 %copy-start.9 = (f32[1280]{0:T(1024)S(1)}, f32[1280]{0:T(1024)}, u32[]{:S(2)}) copy-start(f32[1280]{0:T(1024)} %param.11) | copy-start | bytes 15364
  176.5 0.9 copy-start.5
Sparse Core Ops, SparseCore 0:
  25.0 48.2 all-gather.1

commit v8 on v7

--- a/solution.py
+++ b/solution.py
@@ -160,19 +160,21 @@
             powers = jnp.exp(masked - jnp.max(masked, axis=-1, keepdims=True))
             probs[h, r, :] = powers * (1.0 / jnp.sum(powers, axis=-1, keepdims=True))
 
-    project(0)
-    for h in range(RING):
-        if h + 1 < RING:
-            project(h + 1)
-        soften(h)
     copies = [
         pltpu.make_async_copy(src, dst, out_sems.at[i])
         for i, (src, dst) in enumerate(
             ((second, second_hbm), (key_at, key_hbm), (query_at, query_hbm), (probs, probs_hbm))
         )
     ]
-    for copy in copies:
-        copy.start()
+    project(0)
+    for h in range(RING):
+        if h + 1 < RING:
+            project(h + 1)
+        else:
+            for copy in copies[:3]:
+                copy.start()
+        soften(h)
+    copies[3].start()
     for copy in copies:
         copy.wait()
 
@@ -235,20 +237,23 @@
 
     for h in range(RING):
         spread(h)
-    for copy in copies:
+    for copy in copies[:4]:
         copy.wait()
+    out_copies = [pltpu.make_async_copy(grad_ref, grad_hbm, out_sems.at[RING])] + [
+        pltpu.make_async_copy(weight_ref.at[h], weight_hbm.at[:, h], out_sems.at[h])
+        for h in range(RING)
+    ]
     attend(0)
+    copies[4].wait()
     for h in range(RING):
         if h + 1 < RING:
             attend(h + 1)
+        else:
+            for copy in out_copies[:RING]:
+                copy.start()
         weigh(h)
-    copies = [pltpu.make_async_copy(grad_ref, grad_hbm, out_sems.at[RING])] + [
-        pltpu.make_async_copy(weight_ref.at[h], weight_hbm.at[:, h], out_sems.at[h])
-        for h in range(RING)
-    ]
-    for copy in copies:
-        copy.start()
-    for copy in copies:
+    out_copies[RING].start()
+    for copy in out_copies:
         copy.wait()
 
 
@@ -258,6 +263,13 @@
     total = dot(grads, jnp.concatenate(parts, axis=0), NN)
     out_ref[...] = total.astype(out_ref.dtype)
     gain_ref[...] = jnp.sum(total * normed_ref[...].astype(f32), axis=0, keepdims=True)
+
+
+def spread_kernel(in_ref, out_ref):
+    total = in_ref[0].astype(f32)
+    for q in range(1, RING):
+        total += in_ref[q].astype(f32)
+    out_ref[...] = jnp.broadcast_to(total.astype(bf16)[None], out_ref.shape)
 
 
 def turn_kernel(whole_ref, out_ref):
@@ -423,6 +435,16 @@
     )(rows, gain, keep, from_core, from_pair)
 
 
+def spread_call(arrived):
+    return pl.pallas_call(
+        spread_kernel,
+        out_shape=jax.ShapeDtypeStruct((16,) + arrived.shape[1:], bf16),
+        in_specs=[vmem()],
+        out_specs=vmem(),
+        compiler_params=params(),
+    )(arrived)
+
+
 def turn_call(whole):
     width = whole.shape[0] * whole.shape[1]
     return pl.pallas_call(
@@ -446,13 +468,14 @@
     place = jnp.stack([ring, slot]).astype(jnp.int32)
     gain_row = gain.reshape(1, width)
 
-    packed = pack_call(grad_packed)
+    own = norm_call(layer_input, gain_row)
+    grad_rows, own = lax.optimization_barrier((grad_packed, own))
+    packed = pack_call(grad_rows)
     flipped = jnp.swapaxes(w_qkv, 1, 2).reshape(3 * HEAD, width)
     flipped = jnp.pad(flipped, ((0, PADDED - 3 * HEAD), (0, 0)))
     share = lax.dynamic_slice(flipped, (16 * dp, 0), (16, width))
     others = [lax.ppermute(share, "zq", [(i, (i + k) % RING) for i in range(RING)]) for k in (3, 2, 1)]
-    own = norm_call(layer_input, gain_row)
-    others, packed, own = lax.optimization_barrier((others, packed, own))
+    others, packed = lax.optimization_barrier((others, packed))
     circle = jnp.concatenate([share] + others + [share] + others, axis=0)
     ordered = lax.dynamic_slice(circle, (16 * ((RING - ring) % RING), 0), (16 * RING, width))
     weights = lax.all_gather(ordered, ("y", "x"), axis=0, tiled=True)
@@ -483,8 +506,7 @@
     from_pair = swap(pair, "zp")
     message, from_pair = lax.optimization_barrier((message, from_pair))
     arrived = lax.all_to_all(message, "zq", split_axis=0, concat_axis=0)
-    summed = jnp.sum(arrived.astype(f32), axis=0).astype(bf16)
-    copies = jnp.broadcast_to(summed[None], (16,) + summed.shape)
+    copies = spread_call(arrived)
     whole = lax.all_to_all(copies, ("y", "x"), split_axis=0, concat_axis=0)
     grad_gain = jnp.sum(whole[:, :, 3 * HEAD :].astype(f32), axis=0).reshape(width) / gain
     grad_weight = jnp.swapaxes(turn_call(whole).reshape(3, HEAD, width), 1, 2)

time: 188 us -> 187 us (level)
  no operation moved by 1% of the time
where the time goes in v8:
time: 187 us; the launch traced here: 186 us
  Pallas kernels  56.1 us (30%)
  waiting for transfers between devices  52.4 us (28%)
  starting transfers between devices  38.7 us (21%)
  blocking collectives  16 us (9%)
  between operations  14.3 us (8%)
  local copies, waits for them, and re-layouts  4.51 us (2%)
  other arithmetic  3.89 us (2%)
    ppermute x6, waiting for transfers between devices, swap(): return lax.ppermute(x, axis, [(0, 1), (1, 0)])  33.6 us
    all_to_all x1, blocking collectives, on_device(): arrived = lax.all_to_all(message, 'zq', split_axis=0, concat_axis=0)  16 us
    pallas_call x2, Pallas kernels, back_call(): pl.pallas_call(back_kernel, grid=(width // piece,), out_shape=(jax.ShapeD...  12.4 us
    ppermute x3, starting transfers between devices, on_device(): lax.ppermute(share, 'zq', [(i, (i + k) % RING) for i in range(RING)])  11.4 us
    pallas_call x1, Pallas kernels, head_call(): pl.pallas_call(head_kernel, out_shape=(jax.ShapeDtypeStruct((RING, rows,...  11.1 us
    pallas_call x1, Pallas kernels, forward_call(): pl.pallas_call(forward_kernel, out_shape=tuple((jax.ShapeDtypeStruct(*eac...  11 us
    all_to_all x1, starting transfers between devices, on_device(): whole = lax.all_to_all(copies, ('y', 'x'), split_axis=0, concat_axis=0)  8.83 us
    pallas_call x1, Pallas kernels, permute_call(): pl.pallas_call(permute_kernel, out_shape=jax.ShapeDtypeStruct((RING, SLOT...  7.07 us
  transfers between devices with their start and end apart: 14, of which 7 were waited for; matrix products, arithmetic and copies ran while one was open for 2% of the time, Pallas kernels for 22%

profile of v8, /device:TPU:2, one launch (start us, length us, event | category | flops | bytes accessed | tf_op | source)
XLA Modules:
  0.0 185.9 jit_solution(15467212136379610179)
XLA Ops:
  7.2 0.9 constant_dynamic-update-slice_fusion.9
  8.1 3.3 %collective-permute-start.4 = (bf16[16,1280]{1,0:T(8,128)(2,1)S(1)}, bf16[16,1280]{1,0:T(8,128)(2,1)S(1)}, u32[]{:S(2)}, u32[]{:S(2)}) collective-permute-start(bf16[16,1280]{1,0:T(8,128)(2,1)S(1)} %get-tuple-element.44), channel_id=1, source_target_pairs={{0,4},{4,8},{8,12},{12,0},{1,5},{5,9},{9,13},{13,1},{2,6},{6,10},{... | collective-permute-start | bytes 122888 | tf_op jit(solution)/shard_map/ppermute | solution.py:477
  11.4 5.4 %collective-permute-start.3 = (bf16[16,1280]{1,0:T(8,128)(2,1)S(1)}, bf16[16,1280]{1,0:T(8,128)(2,1)S(1)}, u32[]{:S(2)}, u32[]{:S(2)}) collective-permute-start(bf16[16,1280]{1,0:T(8,128)(2,1)S(1)} %get-tuple-element.44), channel_id=1, source_target_pairs={{0,8},{4,12},{8,0},{12,4},{1,9},{5,13},{9,1},{13,5},{2,10},{6,14},... | collective-permute-start | bytes 122888 | tf_op jit(solution)/shard_map/ppermute | solution.py:477
  16.8 2.7 %collective-permute-start.2 = (bf16[16,1280]{1,0:T(8,128)(2,1)S(1)}, bf16[16,1280]{1,0:T(8,128)(2,1)S(1)}, u32[]{:S(2)}, u32[]{:S(2)}) collective-permute-start(bf16[16,1280]{1,0:T(8,128)(2,1)S(1)} %get-tuple-element.44), channel_id=1, source_target_pairs={{0,12},{4,0},{8,4},{12,8},{1,13},{5,1},{9,5},{13,9},{2,14},{6,2},{... | collective-permute-start | bytes 122888 | tf_op jit(solution)/shard_map/ppermute | solution.py:477
  19.5 0.7 reshape.33.gain_ref
  20.2 1.1 copy-done
  21.5 2.5 %shard_map.87 = bf16[16,160,128]{2,1,0:T(8,128)(2,1)} custom-call(bf16[256,1280]{1,0:T(8,128)(2,1)S(1)} %copy-done.1), custom_call_target="tpu_custom_call" | custom-call | tf_op jit(solution)/shard_map/pallas_call | solution.py:303
  24.9 1.1 collective-permute-start
  26.0 3.6 %all-to-all-start = ((bf16[16,160,128]{2,1,0:T(8,128)(2,1)}), bf16[16,160,128]{2,1,0:T(8,128)(2,1)S(1)}, u32[]{:S(2)}, u32[]{:S(2)}) async-start(bf16[16,160,128]{2,1,0:T(8,128)(2,1)} %shard_map.87), calls=%async_computation | async-start | bytes 1310720 | tf_op jit(solution)/shard_map/all_to_all | solution.py:484
  29.6 18.5 %collective-permute-done = bf16[256,1280]{1,0:T(8,128)(2,1)S(1)} collective-permute-done((bf16[256,1280]{1,0:T(8,128)(2,1)S(1)}, bf16[256,1280]{1,0:T(8,128)(2,1)S(1)}, u32[]{:S(2)}, u32[]{:S(2)}) %collective-permute-start) | collective-permute-done | bytes 655392 | tf_op jit(solution)/shard_map/ppermute | solution.py:460
  48.4 4.6 %all-to-all-done.in_ref = bf16[16,160,128]{2,1,0:T(8,128)(2,1)S(1)} async-done(((bf16[16,160,128]{2,1,0:T(8,128)(2,1)}), bf16[16,160,128]{2,1,0:T(8,128)(2,1)S(1)}, u32[]{:S(2)}, u32[]{:S(2)}) %all-to-all-start) | async-done | bytes 655392 | tf_op jit(solution)/shard_map/all_to_all | solution.py:484
  53.0 7.1 %shard_map.88 = bf16[4,4,160,128]{3,2,1,0:T(8,128)(2,1)} custom-call(s32[2]{0:T(128)S(1)} %pad_add_fusion.place_ref, s32[4096]{0:T(1024)S(1)} %bitcast.12, bf16[16,160,128]{2,1,0:T(8,128)(2,1)S(1)} %all-to-all-done.in_ref), custom_call_target="tpu_custom_call" | custom-call | tf_op jit(solution)/shard_map/pallas_call | solution.py:313
  60.1 3.8 %all-to-all-start.1 = ((bf16[4,4,160,128]{3,2,1,0:T(8,128)(2,1)}), bf16[4,4,160,128]{3,2,1,0:T(8,128)(2,1)S(1)}, u32[]{:S(2)}, u32[]{:S(2)}) async-start(bf16[4,4,160,128]{3,2,1,0:T(8,128)(2,1)} %shard_map.88), calls=%async_computation.1 | async-start | bytes 1310720 | tf_op jit(solution)/shard_map/all_to_all | solution.py:486
  64.5 5.2 %shard_map.86 = (bf16[1024,1280]{1,0:T(8,128)(2,1)}, bf16[1280,1024]{1,0:T(8,128)(2,1)}) custom-call(bf16[512,1280]{1,0:T(8,128)(2,1)} %copy-done.6, bf16[512,1280]{1,0:T(8,128)(2,1)} %collective-permute-done.1.core_ref), custom_call_target="tpu_custom_call" | custom-call | tf_op jit(solution)/shard_map/pallas_call | solution.py:335
  69.7 3.6 %all-gather.2.cloned.1.call-done = bf16[1024,1280]{1,0:T(8,128)(2,1)} async-done(((bf16[64,1280]{1,0:T(8,128)(2,1)}), bf16[1024,1280]{1,0:T(8,128)(2,1)}) %all-gather.2.cloned.1.call-update) | async-done | bytes 2621456 | tf_op jit(solution)/shard_map/all_gather | solution.py:481
  73.3 11.0 %shard_map.89 = (bf16[4,1024,128]{2,1,0:T(8,128)(2,1)}, bf16[4,1024,128]{2,1,0:T(8,128)(2,1)}, bf16[4,1024,256]{2,1,0:T(8,128)(2,1)}, f32[4,1024,128]{2,1,0:T(8,128)}) custom-call(s32[2]{0:T(128)} %copy-done.4, bf16[1024,1280]{1,0:T(8,128)(2,1)} %get-tuple-element.27.normed_hbm.normed_ref, bf16[16,4,16,1280]{3,2,1,0:T(8,128)(2,1)} %bitcast.13, ...), custom_call_target="tpu_custom_call" | custom-call | tf_op jit(solution)/shard_map/pallas_call | solution.py:362
  84.3 0.8 copy-done.8
  85.1 11.1 %shard_map.90 = (bf16[4,1024,256]{2,1,0:T(8,128)(2,1)}, bf16[16,4,80,256]{3,2,1,0:T(8,128)(2,1)}) custom-call(bf16[1280,1024]{1,0:T(8,128)(2,1)} %get-tuple-element.24.turned_hbm, bf16[4,4,160,128]{3,2,1,0:T(8,128)(2,1)} %copy-done.8, bf16[4,1024,128]{2,1,0:T(8,128)(2,1)} %get-tuple-element.31.second_hbm, bf16[4,1024,128]{2,1,0:T(8,128)(2,1)} %get-tuple-element.32.key_hbm, ...), custom_call_target="tpu_custom_call" | custom-call | tf_op jit(solution)/shard_map/pallas_call | solution.py:382
  96.2 5.7 %all-to-all-start.2 = ((bf16[16,4,80,256]{3,2,1,0:T(8,128)(2,1)}), bf16[16,4,80,256]{3,2,1,0:T(8,128)(2,1)S(1)}, u32[]{:S(2)}, u32[]{:S(2)}) async-start(bf16[16,4,80,256]{3,2,1,0:T(8,128)(2,1)} %get-tuple-element.38), calls=%async_computation.2 | async-start | bytes 5242880 | tf_op jit(solution)/shard_map/all_to_all | solution.py:494
  101.9 6.1 %shard_map.92 = (bf16[512,1280]{1,0:T(8,128)(2,1)}, f32[1,1280]{1,0:T(1,128)}) custom-call(bf16[4,1024,256]{2,1,0:T(8,128)(2,1)} %get-tuple-element.35.grad_ref, bf16[16,4,16,1280]{3,2,1,0:T(8,128)(2,1)} %bitcast.14, bf16[1024,1280]{1,0:T(8,128)(2,1)} %get-tuple-element.27.normed_hbm.normed_ref), custom_call_target="tpu_custom_call" | custom-call | tf_op jit(solution)/shard_map/pallas_call | solution.py:406
  108.3 6.4 %shard_map.91 = (f32[512,1280]{1,0:T(8,128)}, f32[1,1280]{1,0:T(1,128)}) custom-call(bf16[4,1024,256]{2,1,0:T(8,128)(2,1)} %get-tuple-element.35.grad_ref, bf16[16,4,16,1280]{3,2,1,0:T(8,128)(2,1)} %bitcast.15, bf16[1024,1280]{1,0:T(8,128)(2,1)} %get-tuple-element.27.normed_hbm.normed_ref), custom_call_target="tpu_custom_call" | custom-call | tf_op jit(solution)/shard_map/pallas_call | solution.py:406
  114.7 1.9 %add_convert_fusion = bf16[256,1280]{1,0:T(8,128)(2,1)S(1)} fusion(f32[512,1280]{1,0:T(8,128)} %get-tuple-element.36.keep_ref, bf16[512,1280]{1,0:T(8,128)(2,1)S(1)} %collective-permute-done.5.core_ref), kind=kLoop, calls=%fused_computation | loop fusion | flops 983040 | bytes 2621440 | tf_op jit(solution)/shard_map/convert_element_type | solution.py:500
  116.6 3.3 %collective-permute-start.8 = (bf16[256,1280]{1,0:T(8,128)(2,1)S(1)}, bf16[256,1280]{1,0:T(8,128)(2,1)}, u32[]{:S(2)}, u32[]{:S(2)}) collective-permute-start(bf16[256,1280]{1,0:T(8,128)(2,1)S(1)} %add_convert_fusion), channel_id=1, source_target_pairs={{0,2},{2,0},{1,3},{3,1},{4,6},{6,4},{5,7},{7,5},{8,10},{10,8},{9,1... | collective-permute-start | bytes 1966088 | tf_op jit(solution)/shard_map/ppermute | solution.py:460
  120.2 1.0 collective-permute-done.6
  121.4 14.1 %collective-permute-done.7 = f32[1,1280]{1,0:T(1,128)S(1)} collective-permute-done((f32[1,1280]{1,0:T(1,128)S(1)}, f32[1,1280]{1,0:T(1,128)S(1)}, u32[]{:S(2)}, u32[]{:S(2)}) %collective-permute-start.7) | collective-permute-done | bytes 5152 | tf_op jit(solution)/shard_map/ppermute | solution.py:460
  135.6 4.2 %all-to-all-done.2 = bf16[16,4,80,256]{3,2,1,0:T(8,128)(2,1)S(1)} async-done(((bf16[16,4,80,256]{3,2,1,0:T(8,128)(2,1)}), bf16[16,4,80,256]{3,2,1,0:T(8,128)(2,1)S(1)}, u32[]{:S(2)}, u32[]{:S(2)}) %all-to-all-start.2) | async-done | bytes 2621472 | tf_op jit(solution)/shard_map/all_to_all | solution.py:494
  140.3 16.0 %all_to_all.25.in_ref = bf16[4,80,256]{2,1,0:T(8,128)(2,1)S(1)} all-to-all(bf16[4,80,256]{2,1,0:T(8,128)(2,1)S(1)} %pad_maximum_fusion), channel_id=1, replica_groups=mesh['y'=4,'x'=4,'zq'=4,'zp'=2,'core'=2] {'zq'}, dimensions={0} | all-to-all | bytes 327680 | tf_op jit(solution)/shard_map/all_to_all | solution.py:508
  156.3 0.9 shard_map.94
  157.2 8.8 %all-to-all-start.4 = ((bf16[16,80,256]{2,1,0:T(8,128)(2,1)}), bf16[16,80,256]{2,1,0:T(8,128)(2,1)S(1)}, u32[]{:S(2)}, u32[]{:S(2)}) async-start(bf16[16,80,256]{2,1,0:T(8,128)(2,1)} %shard_map.94), calls=%async_computation.4 | async-start | bytes 1310720 | tf_op jit(solution)/shard_map/all_to_all | solution.py:510
  166.0 3.4 %shard_map.93 = bf16[256,1280]{1,0:T(8,128)(2,1)} custom-call(bf16[256,1280]{1,0:T(8,128)(2,1)} %rows_ref.4, f32[1,1280]{1,0:T(1,128)} %copy-done.2, f32[512,1280]{1,0:T(8,128)} %get-tuple-element.36.keep_ref, bf16[512,1280]{1,0:T(8,128)(2,1)} %copy-done.7, bf16[256,1280]{1,0:T(8,128)(2,1)} %collective-permute-done.8.pair_ref), custom_call_target="tpu_custom_call" | custom-call | tf_op jit(solution)/shard_map/pallas_call | solution.py:428
  169.4 6.4 %all-to-all-done.4.whole_ref = bf16[16,80,256]{2,1,0:T(8,128)(2,1)S(1)} async-done(((bf16[16,80,256]{2,1,0:T(8,128)(2,1)}), bf16[16,80,256]{2,1,0:T(8,128)(2,1)S(1)}, u32[]{:S(2)}, u32[]{:S(2)}) %all-to-all-start.4) | async-done | bytes 655392 | tf_op jit(solution)/shard_map/all_to_all | solution.py:510
  176.7 2.4 %shard_map.95 = f32[240,1280]{1,0:T(8,128)} custom-call(bf16[16,80,256]{2,1,0:T(8,128)(2,1)} %copy-done.5), custom_call_target="tpu_custom_call" | custom-call | tf_op jit(solution)/shard_map/pallas_call | solution.py:450
  (60 shorter events, 4.2 us)
Async XLA Ops:
  7.2 14.4 %copy-start.1 = (bf16[256,1280]{1,0:T(8,128)(2,1)S(1)}, bf16[256,1280]{1,0:T(8,128)(2,1)}, u32[]{:S(2)}) copy-start(bf16[256,1280]{1,0:T(8,128)(2,1)} %rows_ref.3) | copy-start | bytes 1966084
  7.2 66.1 %all-gather.2.cloned.1.call-start = ((), (), s32[]{:S(2)}) async-start(), calls=%async_computation.5 | async-start | bytes 2785280 | tf_op jit(solution)/shard_map/all_gather | solution.py:481
  8.1 16.0 %collective-permute-start.4 = (bf16[16,1280]{1,0:T(8,128)(2,1)S(1)}, bf16[16,1280]{1,0:T(8,128)(2,1)S(1)}, u32[]{:S(2)}, u32[]{:S(2)}) collective-permute-start(bf16[16,1280]{1,0:T(8,128)(2,1)S(1)} %get-tuple-element.44), channel_id=1, source_target_pairs={{0,4},{4,8},{8,12},{12,0},{1,5},{5,9},{9,13},{13,1},{2,6},{6,10},{... | collective-permute-start | bytes 122888 | tf_op jit(solution)/shard_map/ppermute | solution.py:477
  11.4 12.6 %collective-permute-start.3 = (bf16[16,1280]{1,0:T(8,128)(2,1)S(1)}, bf16[16,1280]{1,0:T(8,128)(2,1)S(1)}, u32[]{:S(2)}, u32[]{:S(2)}) collective-permute-start(bf16[16,1280]{1,0:T(8,128)(2,1)S(1)} %get-tuple-element.44), channel_id=1, source_target_pairs={{0,8},{4,12},{8,0},{12,4},{1,9},{5,13},{9,1},{13,5},{2,10},{6,14},... | collective-permute-start | bytes 122888 | tf_op jit(solution)/shard_map/ppermute | solution.py:477
  16.8 7.2 %collective-permute-start.2 = (bf16[16,1280]{1,0:T(8,128)(2,1)S(1)}, bf16[16,1280]{1,0:T(8,128)(2,1)S(1)}, u32[]{:S(2)}, u32[]{:S(2)}) collective-permute-start(bf16[16,1280]{1,0:T(8,128)(2,1)S(1)} %get-tuple-element.44), channel_id=1, source_target_pairs={{0,12},{4,0},{8,4},{12,8},{1,13},{5,1},{9,5},{13,9},{2,14},{6,2},{... | collective-permute-start | bytes 122888 | tf_op jit(solution)/shard_map/ppermute | solution.py:477
  20.2 1.1 copy-start
  21.3 2.8 %copy-start.2 = (f32[1,1280]{1,0:T(1,128)}, f32[1,1280]{1,0:T(1,128)S(1)}, u32[]{:S(2)}) copy-start(f32[1,1280]{1,0:T(1,128)S(1)} %reshape.33.gain_ref) | copy-start | bytes 15364
  24.9 23.3 %collective-permute-start = (bf16[256,1280]{1,0:T(8,128)(2,1)S(1)}, bf16[256,1280]{1,0:T(8,128)(2,1)S(1)}, u32[]{:S(2)}, u32[]{:S(2)}) collective-permute-start(bf16[256,1280]{1,0:T(8,128)(2,1)S(1)} %shard_map.85), channel_id=1, source_target_pairs={{0,2},{2,0},{1,3},{3,1},{4,6},{6,4},{5,7},{7,5},{8,10},{10,8},{9,1... | collective-permute-start | bytes 1966088 | tf_op jit(solution)/shard_map/ppermute | solution.py:460
  26.0 27.0 %all-to-all-start = ((bf16[16,160,128]{2,1,0:T(8,128)(2,1)}), bf16[16,160,128]{2,1,0:T(8,128)(2,1)S(1)}, u32[]{:S(2)}, u32[]{:S(2)}) async-start(bf16[16,160,128]{2,1,0:T(8,128)(2,1)} %shard_map.87), calls=%async_computation | async-start | bytes 1310720 | tf_op jit(solution)/shard_map/all_to_all | solution.py:484
  29.6 23.4 %copy-start.3 = (s32[1,4096]{1,0:T(1,128)S(1)}, s32[1,4096]{1,0:T(1,128)}, u32[]{:S(2)}) copy-start(s32[1,4096]{1,0:T(1,128)} %param.8) | copy-start | bytes 49156
  48.2 11.9 %copy-start.6 = (bf16[512,1280]{1,0:T(8,128)(2,1)}, bf16[512,1280]{1,0:T(8,128)(2,1)S(1)}, u32[]{:S(2)}) copy-start(bf16[512,1280]{1,0:T(8,128)(2,1)S(1)} %constant_dynamic-update-slice_fusion.half_ref) | copy-start | bytes 3932164
  48.2 16.3 %collective-permute-start.1 = (bf16[512,1280]{1,0:T(8,128)(2,1)S(1)}, bf16[512,1280]{1,0:T(8,128)(2,1)}, u32[]{:S(2)}, u32[]{:S(2)}) collective-permute-start(bf16[512,1280]{1,0:T(8,128)(2,1)S(1)} %constant_dynamic-update-slice_fusion.half_ref), channel_id=1, source_target_pairs={{0,1},{1,0},{2,3},{3,2},{4,5},{5,4},{6,7},{7,6},{8,9},{9,8},{10,11... | collective-permute-start | bytes 3932168 | tf_op jit(solution)/shard_map/ppermute | solution.py:460
  48.4 11.7 %copy-start.4 = (s32[2]{0:T(128)}, s32[2]{0:T(128)S(1)}, u32[]{:S(2)}) copy-start(s32[2]{0:T(128)S(1)} %pad_add_fusion.place_ref) | copy-start | bytes 28
  53.0 10.9 %copy-start.10 = (s32[1,4096]{1,0:T(1,128)S(1)}, s32[1,4096]{1,0:T(1,128)}, u32[]{:S(2)}) copy-start(s32[1,4096]{1,0:T(1,128)} %param.9) | copy-start | bytes 49156
  60.1 24.2 %all-to-all-start.1 = ((bf16[4,4,160,128]{3,2,1,0:T(8,128)(2,1)}), bf16[4,4,160,128]{3,2,1,0:T(8,128)(2,1)S(1)}, u32[]{:S(2)}, u32[]{:S(2)}) async-start(bf16[4,4,160,128]{3,2,1,0:T(8,128)(2,1)} %shard_map.88), calls=%async_computation.1 | async-start | bytes 1310720 | tf_op jit(solution)/shard_map/all_to_all | solution.py:486
  84.2 0.8 copy-start.8
  96.2 43.6 %all-to-all-start.2 = ((bf16[16,4,80,256]{3,2,1,0:T(8,128)(2,1)}), bf16[16,4,80,256]{3,2,1,0:T(8,128)(2,1)S(1)}, u32[]{:S(2)}, u32[]{:S(2)}) async-start(bf16[16,4,80,256]{3,2,1,0:T(8,128)(2,1)} %get-tuple-element.38), calls=%async_computation.2 | async-start | bytes 5242880 | tf_op jit(solution)/shard_map/all_to_all | solution.py:494
  108.0 6.7 %collective-permute-start.5 = (bf16[512,1280]{1,0:T(8,128)(2,1)}, bf16[512,1280]{1,0:T(8,128)(2,1)S(1)}, u32[]{:S(2)}, u32[]{:S(2)}) collective-permute-start(bf16[512,1280]{1,0:T(8,128)(2,1)} %get-tuple-element.37), channel_id=1, source_target_pairs={{0,1},{1,0},{2,3},{3,2},{4,5},{5,4},{6,7},{7,6},{8,9},{9,8},{10,11... | collective-permute-start | bytes 3932168 | tf_op jit(solution)/shard_map/ppermute | solution.py:460
  114.6 2.0 %copy-start.7 = (bf16[512,1280]{1,0:T(8,128)(2,1)}, bf16[512,1280]{1,0:T(8,128)(2,1)S(1)}, u32[]{:S(2)}) copy-start(bf16[512,1280]{1,0:T(8,128)(2,1)S(1)} %collective-permute-done.5.core_ref) | copy-start | bytes 3932164
  114.6 5.3 %copy-start.11 = (f32[1,1280]{1,0:T(1,128)S(1)}, f32[1,1280]{1,0:T(1,128)}, u32[]{:S(2)}) copy-start(f32[1,1280]{1,0:T(1,128)} %get-tuple-element.39) | copy-start | bytes 15364
  114.7 5.3 %copy-start.12 = (f32[1,1280]{1,0:T(1,128)S(1)}, f32[1,1280]{1,0:T(1,128)}, u32[]{:S(2)}) copy-start(f32[1,1280]{1,0:T(1,128)} %get-tuple-element.40) | copy-start | bytes 15364
  116.6 23.7 %collective-permute-start.8 = (bf16[256,1280]{1,0:T(8,128)(2,1)S(1)}, bf16[256,1280]{1,0:T(8,128)(2,1)}, u32[]{:S(2)}, u32[]{:S(2)}) collective-permute-start(bf16[256,1280]{1,0:T(8,128)(2,1)S(1)} %add_convert_fusion), channel_id=1, source_target_pairs={{0,2},{2,0},{1,3},{3,1},{4,6},{6,4},{5,7},{7,5},{8,10},{10,8},{9,1... | collective-permute-start | bytes 1966088 | tf_op jit(solution)/shard_map/ppermute | solution.py:460
  119.9 1.3 collective-permute-start.6
  121.2 14.3 %collective-permute-start.7 = (f32[1,1280]{1,0:T(1,128)S(1)}, f32[1,1280]{1,0:T(1,128)S(1)}, u32[]{:S(2)}, u32[]{:S(2)}) collective-permute-start(f32[1,1280]{1,0:T(1,128)S(1)} %add.36), channel_id=1, source_target_pairs={{0,2},{2,0},{1,3},{3,1},{4,6},{6,4},{5,7},{7,5},{8,10},{10,8},{9,1... | collective-permute-start | bytes 15368 | tf_op jit(solution)/shard_map/ppermute | solution.py:460
  157.2 18.7 %all-to-all-start.4 = ((bf16[16,80,256]{2,1,0:T(8,128)(2,1)}), bf16[16,80,256]{2,1,0:T(8,128)(2,1)S(1)}, u32[]{:S(2)}, u32[]{:S(2)}) async-start(bf16[16,80,256]{2,1,0:T(8,128)(2,1)} %shard_map.94), calls=%async_computation.4 | async-start | bytes 1310720 | tf_op jit(solution)/shard_map/all_to_all | solution.py:510
  166.0 10.1 %copy-start.9 = (f32[1280]{0:T(1024)S(1)}, f32[1280]{0:T(1024)}, u32[]{:S(2)}) copy-start(f32[1280]{0:T(1024)} %param.11) | copy-start | bytes 15364
  175.9 0.9 copy-start.5
Sparse Core Ops, SparseCore 0:
  25.0 48.2 all-gather.1

commit v9 on v8

--- a/solution.py
+++ b/solution.py
@@ -117,13 +117,17 @@
         turned_ref[:, rows] = part[...].T
 
 
+def front(x):
+    return jnp.where(lanes(x.shape) < HEAD, x, 0.0).astype(bf16)
+
+
 def blocks_of(total_rows):
     return [slice(SUPER * b, SUPER * b + SUPER) for b in range(total_rows // SUPER)]
 
 
 def forward_kernel(
-    place_ref, normed_hbm, w_hbm, window_ref, second_hbm, key_hbm, query_hbm, probs_hbm,
-    second, key_at, query_at, probs, first, same, normed_ref, w_ref, in_sems, out_sems,
+    place_ref, normed_hbm, w_hbm, window_ref, first_hbm, second_hbm, probs_hbm,
+    first, second, probs, same, normed_ref, w_ref, in_sems, out_sems,
 ):
     ring, slot = place_ref[0], place_ref[1]
     scaling = HEAD ** (-0.5)
@@ -138,23 +142,18 @@
         line = ring * 8 + (slot ^ XOR_ORDER[b // 2]) * 2 + b % 2
         labels = jnp.broadcast_to(window_ref[pl.ds(line, 1), :], (SUPER, SUPER))
         same[r, :] = jnp.where(labels == labels.T, 0.0, -1e30)
-    for copy in copies:
+    for copy in copies[:2]:
         copy.wait()
+    late = copies[2:]
 
     def project(h):
         w = w_ref[h].reshape(PADDED, width)
         low = dot(normed_ref[...], w, NT).astype(bf16)
         first[h] = low[:, :128]
         second[h] = low[:, 128:]
-        rounded = low.astype(f32)
-        at = lanes((total_rows, PADDED))
-        key_at[h] = jnp.where(at < HEAD, roll(rounded, -HEAD), 0.0)[:, :128].astype(bf16)
-        query_at[h] = jnp.where(
-            (at >= HEAD) & (at < 2 * HEAD), roll(rounded, HEAD), 0.0
-        ).astype(bf16)
 
     def soften(h):
-        scores = [dot(first[h, r, :], key_at[h, r, :], NT) for r in blocks]
+        scores = [dot(front(first[h, r, :]), second[h, r, :], NT) for r in blocks]
         for b, r in enumerate(blocks):
             masked = scores[b] * scaling + same[r, :]
             powers = jnp.exp(masked - jnp.max(masked, axis=-1, keepdims=True))
@@ -163,25 +162,27 @@
     copies = [
         pltpu.make_async_copy(src, dst, out_sems.at[i])
         for i, (src, dst) in enumerate(
-            ((second, second_hbm), (key_at, key_hbm), (query_at, query_hbm), (probs, probs_hbm))
+            ((first, first_hbm), (second, second_hbm), (probs, probs_hbm))
         )
     ]
     project(0)
+    for copy in late:
+        copy.wait()
     for h in range(RING):
         if h + 1 < RING:
             project(h + 1)
         else:
-            for copy in copies[:3]:
+            for copy in copies[:2]:
                 copy.start()
         soften(h)
-    copies[3].start()
+    copies[2].start()
     for copy in copies:
         copy.wait()
 
 
 def head_kernel(
-    turned_hbm, up_ref, second_hbm, key_hbm, query_hbm, probs_hbm, grad_hbm, weight_hbm,
-    second, key_at, query_at, probs, upstream, turned_ref, grad_ref, weight_ref,
+    turned_hbm, up_ref, first_hbm, second_hbm, probs_hbm, grad_hbm, weight_hbm,
+    first, second, probs, upstream, turned_ref, grad_ref, weight_ref,
     in_sems, out_sems,
 ):
     scaling = HEAD ** (-0.5)
@@ -191,18 +192,20 @@
         pltpu.make_async_copy(src, dst, in_sems.at[i])
         for i, (src, dst) in enumerate(
             (
-                (second_hbm, second), (probs_hbm, probs), (key_hbm, key_at),
-                (query_hbm, query_at), (turned_hbm, turned_ref),
+                (first_hbm, first), (second_hbm, second), (probs_hbm, probs),
+                (turned_hbm, turned_ref),
             )
         )
     ]
     for copy in copies:
         copy.start()
     to_wide = shifted(
-        (128, 128), lambda r, c: (c >= 32) & (c < 96) & (r % 64 == c - 32)
+        (128, PADDED),
+        lambda r, c: ((c >= 80) & (c < 128) & (r % 64 == c - 80))
+        | ((c >= 208) & (c < 224) & (r % 64 == c - 160)),
     )
     to_rest = shifted(
-        (128, 128), lambda r, c: (c >= 96) & (c < 112) & (r % 16 == c - 96)
+        (128, PADDED), lambda r, c: (c >= 224) & (c < 240) & (r % 16 == c - 224)
     )
     row = lax.broadcasted_iota(jnp.int32, (CHUNK, 128), 0)
     keep_wide = row // 128 == lanes((CHUNK, 128)) // 64
@@ -217,7 +220,11 @@
             upstream[h, CHUNK * c : CHUNK * c + CHUNK, :] = both.astype(bf16)
 
     def attend(h):
-        grad_probs = [dot(upstream[h, r, :], second[h, r, :], NT) for r in blocks]
+        grad_probs = [
+            dot(upstream[h, r, :128], first[h, r, :], NT)
+            + dot(upstream[h, r, 128:], second[h, r, :], NT)
+            for r in blocks
+        ]
         grad_scores, probs_low = [], []
         for b, r in enumerate(blocks):
             prob = probs[h, r, :]
@@ -225,11 +232,11 @@
             grad_scores.append((prob * (grad_probs[b] - row_dot)).astype(bf16))
             probs_low.append(prob.astype(bf16))
         for b, r in enumerate(blocks):
-            grad_query = dot(grad_scores[b], key_at[h, r, :], NN)
-            grad_key = dot(grad_scores[b], query_at[h, r, :], TN)
+            grad_query = dot(grad_scores[b], front(second[h, r, :]), NN)
+            grad_key = dot(grad_scores[b], front(first[h, r, :]), TN)
             grad_value = dot(probs_low[b], upstream[h, r, :], TN)
-            grad_ref[h, r, :128] = ((grad_query + grad_key[:, :128]) * scaling).astype(bf16)
-            grad_ref[h, r, 128:] = (grad_key[:, 128:] * scaling + grad_value).astype(bf16)
+            grad_ref[h, r, :128] = (grad_query * scaling + grad_value[:, :128]).astype(bf16)
+            grad_ref[h, r, 128:] = (grad_key * scaling + grad_value[:, 128:]).astype(bf16)
 
     def weigh(h):
         part = dot(turned_ref[...], grad_ref[h], NN).astype(bf16)
@@ -237,14 +244,14 @@
 
     for h in range(RING):
         spread(h)
-    for copy in copies[:4]:
+    for copy in copies[:3]:
         copy.wait()
     out_copies = [pltpu.make_async_copy(grad_ref, grad_hbm, out_sems.at[RING])] + [
         pltpu.make_async_copy(weight_ref.at[h], weight_hbm.at[:, h], out_sems.at[h])
         for h in range(RING)
     ]
     attend(0)
-    copies[4].wait()
+    copies[3].wait()
     for h in range(RING):
         if h + 1 < RING:
             attend(h + 1)
@@ -274,7 +281,11 @@
 
 def turn_kernel(whole_ref, out_ref):
     whole = whole_ref[...].reshape(out_ref.shape[1], PADDED).astype(f32)
-    out_ref[...] = whole.T[: 3 * HEAD]
+    turned = whole.T
+    out_ref[:HEAD] = turned[:HEAD]
+    out_ref[HEAD : 2 * HEAD] = turned[128 : 128 + HEAD]
+    out_ref[2 * HEAD : 2 * HEAD + 48] = turned[HEAD:128]
+    out_ref[2 * HEAD + 48 :] = turned[128 + HEAD : 3 * HEAD]
 
 
 def final_kernel(rows_ref, gain_ref, keep_ref, core_ref, pair_ref, out_ref):
@@ -352,7 +363,6 @@
     return (
         ((RING, rows, 128), bf16),
         ((RING, rows, 128), bf16),
-        ((RING, rows, PADDED), bf16),
         ((RING, rows, SUPER), f32),
     )
 
@@ -363,15 +373,14 @@
         forward_kernel,
         out_shape=tuple(jax.ShapeDtypeStruct(*each) for each in kept(rows)),
         in_specs=[smem(), hbm(), hbm(), vmem()],
-        out_specs=(hbm(),) * 4,
+        out_specs=(hbm(),) * 3,
         scratch_shapes=[pltpu.VMEM(*each) for each in kept(rows)]
         + [
-            pltpu.VMEM((RING, rows, 128), bf16),
             pltpu.VMEM((rows, SUPER), f32),
             pltpu.VMEM((rows, width), bf16),
             pltpu.VMEM((RING, 16, 16, width), bf16),
             pltpu.SemaphoreType.DMA((RING + 1,)),
-            pltpu.SemaphoreType.DMA((4,)),
+            pltpu.SemaphoreType.DMA((3,)),
         ],
         compiler_params=params(BIG),
     )(place, normed, weights, windows)
@@ -385,15 +394,15 @@
             jax.ShapeDtypeStruct((RING, rows, PADDED), bf16),
             jax.ShapeDtypeStruct((16, RING, width // 16, PADDED), bf16),
         ),
-        in_specs=[hbm(), vmem()] + [hbm()] * 4,
+        in_specs=[hbm(), vmem()] + [hbm()] * 3,
         out_specs=(hbm(),) * 2,
         scratch_shapes=[pltpu.VMEM(*each) for each in kept(rows)]
         + [
-            pltpu.VMEM((RING, rows, 128), bf16),
+            pltpu.VMEM((RING, rows, PADDED), bf16),
             pltpu.VMEM((width, rows), bf16),
             pltpu.VMEM((RING, rows, PADDED), bf16),
             pltpu.VMEM((RING, 16, width // 16, PADDED), bf16),
-            pltpu.SemaphoreType.DMA((5,)),
+            pltpu.SemaphoreType.DMA((4,)),
             pltpu.SemaphoreType.DMA((RING + 1,)),
         ],
         compiler_params=params(BIG),
@@ -449,9 +458,10 @@
     width = whole.shape[0] * whole.shape[1]
     return pl.pallas_call(
         turn_kernel,
+        grid=(2,),
         out_shape=jax.ShapeDtypeStruct((3 * HEAD, width), f32),
-        in_specs=[vmem()],
-        out_specs=vmem(),
+        in_specs=[pl.BlockSpec((8, width // 16, PADDED), lambda i: (i, 0, 0))],
+        out_specs=pl.BlockSpec((3 * HEAD, width // 2), lambda i: (0, i)),
         compiler_params=params(BIG),
     )(whole)
 
@@ -472,7 +482,9 @@
     grad_rows, own = lax.optimization_barrier((grad_packed, own))
     packed = pack_call(grad_rows)
     flipped = jnp.swapaxes(w_qkv, 1, 2).reshape(3 * HEAD, width)
-    flipped = jnp.pad(flipped, ((0, PADDED - 3 * HEAD), (0, 0)))
+    query, key, value = (flipped[HEAD * j : HEAD * j + HEAD] for j in range(3))
+    spare = jnp.zeros((PADDED - 3 * HEAD, width), bf16)
+    flipped = jnp.concatenate([query, value[:48], key, value[48:], spare], axis=0)
     share = lax.dynamic_slice(flipped, (16 * dp, 0), (16, width))
     others = [lax.ppermute(share, "zq", [(i, (i + k) % RING) for i in range(RING)]) for k in (3, 2, 1)]
     others, packed = lax.optimization_barrier((others, packed))

time: 187 us -> 185 us (0.989)
  waiting for transfers between devices: 52.4 us -> 46.7 us
  starting transfers between devices: 38.7 us -> 42.2 us
    all_to_all x1, waiting for transfers between devices: 4.16 us -> 0.01 us  [on_device(): lax.all_to_all(weight_part, ('y', 'x'), split_axis=0, concat_axis=0)]
    ppermute x6, waiting for transfers between devices: 33.6 us -> 31.3 us  [swap(): return lax.ppermute(x, axis, [(0, 1), (1, 0)])]
    all_to_all x1, starting transfers between devices: 3.81 us -> 5.72 us  [on_device(): upstream = lax.all_to_all(permuted, 'zq', split_axis=0, concat_axis=0)]
    unnamed x34 -> x38, local copies, waits for them, and re-layouts: 2.89 us -> 4.77 us
  transfers between devices with their start and end apart: 14 -> 14, of which waited for: 7 -> 6; matrix products, arithmetic and copies ran while one was open for 2% -> 2% of each run, Pallas kernels for 22% -> 22%
where the time goes in v9:
time: 185 us; the launch traced here: 184 us
  Pallas kernels  54.4 us (29%)
  waiting for transfers between devices  46.7 us (25%)
  starting transfers between devices  42.2 us (23%)
  blocking collectives  17 us (9%)
  between operations  14.4 us (8%)
  local copies, waits for them, and re-layouts  5.7 us (3%)
  other arithmetic  3.9 us (2%)
    ppermute x6, waiting for transfers between devices, swap(): return lax.ppermute(x, axis, [(0, 1), (1, 0)])  31.3 us
    all_to_all x1, blocking collectives, on_device(): arrived = lax.all_to_all(message, 'zq', split_axis=0, concat_axis=0)  17 us
    pallas_call x2, Pallas kernels, back_call(): pl.pallas_call(back_kernel, grid=(width // piece,), out_shape=(jax.ShapeD...  12.5 us
    ppermute x3, starting transfers between devices, on_device(): lax.ppermute(share, 'zq', [(i, (i + k) % RING) for i in range(RING)])  11.4 us
    pallas_call x1, Pallas kernels, head_call(): pl.pallas_call(head_kernel, out_shape=(jax.ShapeDtypeStruct((RING, rows,...  10.7 us
    pallas_call x1, Pallas kernels, forward_call(): pl.pallas_call(forward_kernel, out_shape=tuple((jax.ShapeDtypeStruct(*eac...  9.77 us
    all_to_all x1, starting transfers between devices, on_device(): whole = lax.all_to_all(copies, ('y', 'x'), split_axis=0, concat_axis=0)  8.76 us
    pallas_call x1, Pallas kernels, permute_call(): pl.pallas_call(permute_kernel, out_shape=jax.ShapeDtypeStruct((RING, SLOT...  7.07 us
  transfers between devices with their start and end apart: 14, of which 6 were waited for; matrix products, arithmetic and copies ran while one was open for 2% of the time, Pallas kernels for 22%

profile of v9, /device:TPU:2, one launch (start us, length us, event | category | flops | bytes accessed | tf_op | source)
XLA Modules:
  0.0 184.3 jit_solution(6012553073105549974)
XLA Ops:
  7.2 1.0 fusion.1
  8.3 0.9 fusion.2
  9.2 0.9 fusion
  10.2 0.9 fusion.3
  11.1 3.3 %collective-permute-start.4 = (bf16[16,1280]{1,0:T(8,128)(2,1)S(1)}, bf16[16,1280]{1,0:T(8,128)(2,1)S(1)}, u32[]{:S(2)}, u32[]{:S(2)}) collective-permute-start(bf16[16,1280]{1,0:T(8,128)(2,1)S(1)} %get-tuple-element.42), channel_id=1, source_target_pairs={{0,4},{4,8},{8,12},{12,0},{1,5},{5,9},{9,13},{13,1},{2,6},{6,10},{... | collective-permute-start | bytes 122888 | tf_op jit(solution)/shard_map/ppermute | solution.py:489
  14.4 5.4 %collective-permute-start.3 = (bf16[16,1280]{1,0:T(8,128)(2,1)S(1)}, bf16[16,1280]{1,0:T(8,128)(2,1)S(1)}, u32[]{:S(2)}, u32[]{:S(2)}) collective-permute-start(bf16[16,1280]{1,0:T(8,128)(2,1)S(1)} %get-tuple-element.42), channel_id=1, source_target_pairs={{0,8},{4,12},{8,0},{12,4},{1,9},{5,13},{9,1},{13,5},{2,10},{6,14},... | collective-permute-start | bytes 122888 | tf_op jit(solution)/shard_map/ppermute | solution.py:489
  19.8 2.7 %collective-permute-start.2 = (bf16[16,1280]{1,0:T(8,128)(2,1)S(1)}, bf16[16,1280]{1,0:T(8,128)(2,1)S(1)}, u32[]{:S(2)}, u32[]{:S(2)}) collective-permute-start(bf16[16,1280]{1,0:T(8,128)(2,1)S(1)} %get-tuple-element.42), channel_id=1, source_target_pairs={{0,12},{4,0},{8,4},{12,8},{1,13},{5,1},{9,5},{13,9},{2,14},{6,2},{... | collective-permute-start | bytes 122888 | tf_op jit(solution)/shard_map/ppermute | solution.py:489
  22.8 2.5 %shard_map.87 = bf16[16,160,128]{2,1,0:T(8,128)(2,1)} custom-call(bf16[256,1280]{1,0:T(8,128)(2,1)S(1)} %copy-done.1), custom_call_target="tpu_custom_call" | custom-call | tf_op jit(solution)/shard_map/pallas_call | solution.py:314
  26.1 1.1 collective-permute-start
  27.2 4.7 %all-to-all-start = ((bf16[16,160,128]{2,1,0:T(8,128)(2,1)}), bf16[16,160,128]{2,1,0:T(8,128)(2,1)S(1)}, u32[]{:S(2)}, u32[]{:S(2)}) async-start(bf16[16,160,128]{2,1,0:T(8,128)(2,1)} %shard_map.87), calls=%async_computation | async-start | bytes 1310720 | tf_op jit(solution)/shard_map/all_to_all | solution.py:496
  32.0 16.3 %collective-permute-done = bf16[256,1280]{1,0:T(8,128)(2,1)S(1)} collective-permute-done((bf16[256,1280]{1,0:T(8,128)(2,1)S(1)}, bf16[256,1280]{1,0:T(8,128)(2,1)S(1)}, u32[]{:S(2)}, u32[]{:S(2)}) %collective-permute-start) | collective-permute-done | bytes 655392 | tf_op jit(solution)/shard_map/ppermute | solution.py:470
  48.5 4.7 %all-to-all-done.in_ref = bf16[16,160,128]{2,1,0:T(8,128)(2,1)S(1)} async-done(((bf16[16,160,128]{2,1,0:T(8,128)(2,1)}), bf16[16,160,128]{2,1,0:T(8,128)(2,1)S(1)}, u32[]{:S(2)}, u32[]{:S(2)}) %all-to-all-start) | async-done | bytes 655392 | tf_op jit(solution)/shard_map/all_to_all | solution.py:496
  53.2 7.1 %shard_map.88 = bf16[4,4,160,128]{3,2,1,0:T(8,128)(2,1)} custom-call(s32[2]{0:T(128)S(1)} %pad_add_fusion.place_ref, s32[4096]{0:T(1024)S(1)} %bitcast.26, bf16[16,160,128]{2,1,0:T(8,128)(2,1)S(1)} %all-to-all-done.in_ref), custom_call_target="tpu_custom_call" | custom-call | tf_op jit(solution)/shard_map/pallas_call | solution.py:324
  60.3 5.7 %all-to-all-start.1 = ((bf16[4,4,160,128]{3,2,1,0:T(8,128)(2,1)}), bf16[4,4,160,128]{3,2,1,0:T(8,128)(2,1)S(1)}, u32[]{:S(2)}, u32[]{:S(2)}) async-start(bf16[4,4,160,128]{3,2,1,0:T(8,128)(2,1)} %shard_map.88), calls=%async_computation.1 | async-start | bytes 1310720 | tf_op jit(solution)/shard_map/all_to_all | solution.py:498
  66.7 5.2 %shard_map.86 = (bf16[1024,1280]{1,0:T(8,128)(2,1)}, bf16[1280,1024]{1,0:T(8,128)(2,1)}) custom-call(bf16[512,1280]{1,0:T(8,128)(2,1)} %copy-done.6, bf16[512,1280]{1,0:T(8,128)(2,1)} %collective-permute-done.1.core_ref), custom_call_target="tpu_custom_call" | custom-call | tf_op jit(solution)/shard_map/pallas_call | solution.py:346
  71.8 4.4 %all-gather.2.cloned.1.call-done = bf16[1024,1280]{1,0:T(8,128)(2,1)} async-done(((bf16[64,1280]{1,0:T(8,128)(2,1)}), bf16[1024,1280]{1,0:T(8,128)(2,1)}) %all-gather.2.cloned.1.call-update) | async-done | bytes 2621456 | tf_op jit(solution)/shard_map/all_gather | solution.py:493
  76.2 9.8 %shard_map.89 = (bf16[4,1024,128]{2,1,0:T(8,128)(2,1)}, bf16[4,1024,128]{2,1,0:T(8,128)(2,1)}, f32[4,1024,128]{2,1,0:T(8,128)}) custom-call(s32[2]{0:T(128)} %copy-done.4, bf16[1024,1280]{1,0:T(8,128)(2,1)} %get-tuple-element.26.normed_hbm.normed_ref, bf16[16,4,16,1280]{3,2,1,0:T(8,128)(2,1)} %bitcast.27, f32[32,128]{1,0:T(8,128)} %bitcast.36), custom_call_target="tpu_custom_call" | custom-call | tf_op jit(solution)/shard_map/pallas_call | solution.py:372
  86.0 0.8 copy-done.8
  86.8 10.7 %shard_map.90 = (bf16[4,1024,256]{2,1,0:T(8,128)(2,1)}, bf16[16,4,80,256]{3,2,1,0:T(8,128)(2,1)}) custom-call(bf16[1280,1024]{1,0:T(8,128)(2,1)} %get-tuple-element.23.turned_hbm, bf16[4,4,160,128]{3,2,1,0:T(8,128)(2,1)} %copy-done.8, bf16[4,1024,128]{2,1,0:T(8,128)(2,1)} %get-tuple-element.30.first_hbm, bf16[4,1024,128]{2,1,0:T(8,128)(2,1)} %get-tuple-element.31.second_hbm, ...), custom_call_target="tpu_custom_call" | custom-call | tf_op jit(solution)/shard_map/pallas_call | solution.py:391
  97.6 5.9 %all-to-all-start.2 = ((bf16[16,4,80,256]{3,2,1,0:T(8,128)(2,1)}), bf16[16,4,80,256]{3,2,1,0:T(8,128)(2,1)S(1)}, u32[]{:S(2)}, u32[]{:S(2)}) async-start(bf16[16,4,80,256]{3,2,1,0:T(8,128)(2,1)} %get-tuple-element.36), calls=%async_computation.2 | async-start | bytes 5242880 | tf_op jit(solution)/shard_map/all_to_all | solution.py:506
  103.5 6.1 %shard_map.92 = (bf16[512,1280]{1,0:T(8,128)(2,1)}, f32[1,1280]{1,0:T(1,128)}) custom-call(bf16[4,1024,256]{2,1,0:T(8,128)(2,1)} %get-tuple-element.33.grad_ref, bf16[16,4,16,1280]{3,2,1,0:T(8,128)(2,1)} %bitcast.28, bf16[1024,1280]{1,0:T(8,128)(2,1)} %get-tuple-element.26.normed_hbm.normed_ref), custom_call_target="tpu_custom_call" | custom-call | tf_op jit(solution)/shard_map/pallas_call | solution.py:415
  109.6 6.4 %shard_map.91 = (f32[512,1280]{1,0:T(8,128)}, f32[1,1280]{1,0:T(1,128)}) custom-call(bf16[4,1024,256]{2,1,0:T(8,128)(2,1)} %get-tuple-element.33.grad_ref, bf16[16,4,16,1280]{3,2,1,0:T(8,128)(2,1)} %bitcast.29, bf16[1024,1280]{1,0:T(8,128)(2,1)} %get-tuple-element.26.normed_hbm.normed_ref), custom_call_target="tpu_custom_call" | custom-call | tf_op jit(solution)/shard_map/pallas_call | solution.py:415
  116.0 1.9 %add_convert_fusion = bf16[256,1280]{1,0:T(8,128)(2,1)S(1)} fusion(f32[512,1280]{1,0:T(8,128)} %get-tuple-element.34.keep_ref, bf16[512,1280]{1,0:T(8,128)(2,1)S(1)} %collective-permute-done.5.core_ref), kind=kLoop, calls=%fused_computation | loop fusion | flops 983040 | bytes 2621440 | tf_op jit(solution)/shard_map/convert_element_type | solution.py:512
  117.9 4.0 %collective-permute-start.8 = (bf16[256,1280]{1,0:T(8,128)(2,1)S(1)}, bf16[256,1280]{1,0:T(8,128)(2,1)}, u32[]{:S(2)}, u32[]{:S(2)}) collective-permute-start(bf16[256,1280]{1,0:T(8,128)(2,1)S(1)} %add_convert_fusion), channel_id=1, source_target_pairs={{0,2},{2,0},{1,3},{3,1},{4,6},{6,4},{5,7},{7,5},{8,10},{10,8},{9,1... | collective-permute-start | bytes 1966088 | tf_op jit(solution)/shard_map/ppermute | solution.py:470
  122.2 1.0 collective-permute-done.6
  123.4 14.1 %collective-permute-done.7 = f32[1,1280]{1,0:T(1,128)S(1)} collective-permute-done((f32[1,1280]{1,0:T(1,128)S(1)}, f32[1,1280]{1,0:T(1,128)S(1)}, u32[]{:S(2)}, u32[]{:S(2)}) %collective-permute-start.7) | collective-permute-done | bytes 5152 | tf_op jit(solution)/shard_map/ppermute | solution.py:470
  138.1 17.0 %all_to_all.25.in_ref = bf16[4,80,256]{2,1,0:T(8,128)(2,1)S(1)} all-to-all(bf16[4,80,256]{2,1,0:T(8,128)(2,1)S(1)} %pad_maximum_fusion), channel_id=1, replica_groups=mesh['y'=4,'x'=4,'zq'=4,'zp'=2,'core'=2] {'zq'}, dimensions={0} | all-to-all | bytes 327680 | tf_op jit(solution)/shard_map/all_to_all | solution.py:520
  155.1 0.9 shard_map.94
  156.0 8.8 %all-to-all-start.4 = ((bf16[16,80,256]{2,1,0:T(8,128)(2,1)}), bf16[16,80,256]{2,1,0:T(8,128)(2,1)S(1)}, u32[]{:S(2)}, u32[]{:S(2)}) async-start(bf16[16,80,256]{2,1,0:T(8,128)(2,1)} %shard_map.94), calls=%async_computation.4 | async-start | bytes 1310720 | tf_op jit(solution)/shard_map/all_to_all | solution.py:522
  164.8 3.4 %shard_map.93 = bf16[256,1280]{1,0:T(8,128)(2,1)} custom-call(bf16[256,1280]{1,0:T(8,128)(2,1)} %rows_ref.4, f32[1,1280]{1,0:T(1,128)} %copy-done.2, f32[512,1280]{1,0:T(8,128)} %get-tuple-element.34.keep_ref, bf16[512,1280]{1,0:T(8,128)(2,1)} %copy-done.7, bf16[256,1280]{1,0:T(8,128)(2,1)} %collective-permute-done.8.pair_ref), custom_call_target="tpu_custom_call" | custom-call | tf_op jit(solution)/shard_map/pallas_call | solution.py:437
  168.2 6.2 %all-to-all-done.4.whole_ref = bf16[16,80,256]{2,1,0:T(8,128)(2,1)S(1)} async-done(((bf16[16,80,256]{2,1,0:T(8,128)(2,1)}), bf16[16,80,256]{2,1,0:T(8,128)(2,1)S(1)}, u32[]{:S(2)}, u32[]{:S(2)}) %all-to-all-start.4) | async-done | bytes 655392 | tf_op jit(solution)/shard_map/all_to_all | solution.py:522
  175.3 2.2 %shard_map.95 = f32[240,1280]{1,0:T(8,128)} custom-call(bf16[16,80,256]{2,1,0:T(8,128)(2,1)} %copy-done.5), custom_call_target="tpu_custom_call" | custom-call | tf_op jit(solution)/shard_map/pallas_call | solution.py:459
  (65 shorter events, 4.0 us)
Async XLA Ops:
  7.2 15.3 %copy-start.9 = (f32[1280]{0:T(1024)S(1)}, f32[1280]{0:T(1024)}, u32[]{:S(2)}) copy-start(f32[1280]{0:T(1024)} %param.11) | copy-start | bytes 15364
  7.2 15.3 %copy-start = (bf16[256,1280]{1,0:T(8,128)(2,1)S(1)}, bf16[256,1280]{1,0:T(8,128)(2,1)}, u32[]{:S(2)}) copy-start(bf16[256,1280]{1,0:T(8,128)(2,1)} %rows_ref.4) | copy-start | bytes 1966084
  7.2 69.0 %all-gather.2.cloned.1.call-start = ((), (), s32[]{:S(2)}) async-start(), calls=%async_computation.5 | async-start | bytes 2785280 | tf_op jit(solution)/shard_map/all_gather | solution.py:493
  7.2 15.5 %copy-start.1 = (bf16[256,1280]{1,0:T(8,128)(2,1)S(1)}, bf16[256,1280]{1,0:T(8,128)(2,1)}, u32[]{:S(2)}) copy-start(bf16[256,1280]{1,0:T(8,128)(2,1)} %rows_ref.3) | copy-start | bytes 1966084
  11.1 14.2 %collective-permute-start.4 = (bf16[16,1280]{1,0:T(8,128)(2,1)S(1)}, bf16[16,1280]{1,0:T(8,128)(2,1)S(1)}, u32[]{:S(2)}, u32[]{:S(2)}) collective-permute-start(bf16[16,1280]{1,0:T(8,128)(2,1)S(1)} %get-tuple-element.42), channel_id=1, source_target_pairs={{0,4},{4,8},{8,12},{12,0},{1,5},{5,9},{9,13},{13,1},{2,6},{6,10},{... | collective-permute-start | bytes 122888 | tf_op jit(solution)/shard_map/ppermute | solution.py:489
  14.4 10.9 %collective-permute-start.3 = (bf16[16,1280]{1,0:T(8,128)(2,1)S(1)}, bf16[16,1280]{1,0:T(8,128)(2,1)S(1)}, u32[]{:S(2)}, u32[]{:S(2)}) collective-permute-start(bf16[16,1280]{1,0:T(8,128)(2,1)S(1)} %get-tuple-element.42), channel_id=1, source_target_pairs={{0,8},{4,12},{8,0},{12,4},{1,9},{5,13},{9,1},{13,5},{2,10},{6,14},... | collective-permute-start | bytes 122888 | tf_op jit(solution)/shard_map/ppermute | solution.py:489
  19.8 5.5 %collective-permute-start.2 = (bf16[16,1280]{1,0:T(8,128)(2,1)S(1)}, bf16[16,1280]{1,0:T(8,128)(2,1)S(1)}, u32[]{:S(2)}, u32[]{:S(2)}) collective-permute-start(bf16[16,1280]{1,0:T(8,128)(2,1)S(1)} %get-tuple-element.42), channel_id=1, source_target_pairs={{0,12},{4,0},{8,4},{12,8},{1,13},{5,1},{9,5},{13,9},{2,14},{6,2},{... | collective-permute-start | bytes 122888 | tf_op jit(solution)/shard_map/ppermute | solution.py:489
  22.5 2.8 %copy-start.2 = (f32[1,1280]{1,0:T(1,128)}, f32[1,1280]{1,0:T(1,128)S(1)}, u32[]{:S(2)}) copy-start(f32[1,1280]{1,0:T(1,128)S(1)} %reshape.36.gain_ref) | copy-start | bytes 15364
  26.1 22.2 %collective-permute-start = (bf16[256,1280]{1,0:T(8,128)(2,1)S(1)}, bf16[256,1280]{1,0:T(8,128)(2,1)S(1)}, u32[]{:S(2)}, u32[]{:S(2)}) collective-permute-start(bf16[256,1280]{1,0:T(8,128)(2,1)S(1)} %shard_map.85), channel_id=1, source_target_pairs={{0,2},{2,0},{1,3},{3,1},{4,6},{6,4},{5,7},{7,5},{8,10},{10,8},{9,1... | collective-permute-start | bytes 1966088 | tf_op jit(solution)/shard_map/ppermute | solution.py:470
  27.2 26.0 %all-to-all-start = ((bf16[16,160,128]{2,1,0:T(8,128)(2,1)}), bf16[16,160,128]{2,1,0:T(8,128)(2,1)S(1)}, u32[]{:S(2)}, u32[]{:S(2)}) async-start(bf16[16,160,128]{2,1,0:T(8,128)(2,1)} %shard_map.87), calls=%async_computation | async-start | bytes 1310720 | tf_op jit(solution)/shard_map/all_to_all | solution.py:496
  31.9 21.3 %copy-start.3 = (s32[1,4096]{1,0:T(1,128)S(1)}, s32[1,4096]{1,0:T(1,128)}, u32[]{:S(2)}) copy-start(s32[1,4096]{1,0:T(1,128)} %param.8) | copy-start | bytes 49156
  48.3 12.0 %copy-start.6 = (bf16[512,1280]{1,0:T(8,128)(2,1)}, bf16[512,1280]{1,0:T(8,128)(2,1)S(1)}, u32[]{:S(2)}) copy-start(bf16[512,1280]{1,0:T(8,128)(2,1)S(1)} %constant_dynamic-update-slice_fusion.half_ref) | copy-start | bytes 3932164
  48.3 18.3 %collective-permute-start.1 = (bf16[512,1280]{1,0:T(8,128)(2,1)S(1)}, bf16[512,1280]{1,0:T(8,128)(2,1)}, u32[]{:S(2)}, u32[]{:S(2)}) collective-permute-start(bf16[512,1280]{1,0:T(8,128)(2,1)S(1)} %constant_dynamic-update-slice_fusion.half_ref), channel_id=1, source_target_pairs={{0,1},{1,0},{2,3},{3,2},{4,5},{5,4},{6,7},{7,6},{8,9},{9,8},{10,11... | collective-permute-start | bytes 3932168 | tf_op jit(solution)/shard_map/ppermute | solution.py:470
  48.5 11.8 %copy-start.4 = (s32[2]{0:T(128)}, s32[2]{0:T(128)S(1)}, u32[]{:S(2)}) copy-start(s32[2]{0:T(128)S(1)} %pad_add_fusion.place_ref) | copy-start | bytes 28
  53.2 12.8 %copy-start.10 = (s32[1,4096]{1,0:T(1,128)S(1)}, s32[1,4096]{1,0:T(1,128)}, u32[]{:S(2)}) copy-start(s32[1,4096]{1,0:T(1,128)} %param.9) | copy-start | bytes 49156
  60.3 25.7 %all-to-all-start.1 = ((bf16[4,4,160,128]{3,2,1,0:T(8,128)(2,1)}), bf16[4,4,160,128]{3,2,1,0:T(8,128)(2,1)S(1)}, u32[]{:S(2)}, u32[]{:S(2)}) async-start(bf16[4,4,160,128]{3,2,1,0:T(8,128)(2,1)} %shard_map.88), calls=%async_computation.1 | async-start | bytes 1310720 | tf_op jit(solution)/shard_map/all_to_all | solution.py:498
  86.0 0.8 copy-start.8
  97.6 40.0 %all-to-all-start.2 = ((bf16[16,4,80,256]{3,2,1,0:T(8,128)(2,1)}), bf16[16,4,80,256]{3,2,1,0:T(8,128)(2,1)S(1)}, u32[]{:S(2)}, u32[]{:S(2)}) async-start(bf16[16,4,80,256]{3,2,1,0:T(8,128)(2,1)} %get-tuple-element.36), calls=%async_computation.2 | async-start | bytes 5242880 | tf_op jit(solution)/shard_map/all_to_all | solution.py:506
  109.6 6.4 %collective-permute-start.5 = (bf16[512,1280]{1,0:T(8,128)(2,1)}, bf16[512,1280]{1,0:T(8,128)(2,1)S(1)}, u32[]{:S(2)}, u32[]{:S(2)}) collective-permute-start(bf16[512,1280]{1,0:T(8,128)(2,1)} %get-tuple-element.35), channel_id=1, source_target_pairs={{0,1},{1,0},{2,3},{3,2},{4,5},{5,4},{6,7},{7,6},{8,9},{9,8},{10,11... | collective-permute-start | bytes 3932168 | tf_op jit(solution)/shard_map/ppermute | solution.py:470
  116.0 2.0 %copy-start.7 = (bf16[512,1280]{1,0:T(8,128)(2,1)}, bf16[512,1280]{1,0:T(8,128)(2,1)S(1)}, u32[]{:S(2)}) copy-start(bf16[512,1280]{1,0:T(8,128)(2,1)S(1)} %collective-permute-done.5.core_ref) | copy-start | bytes 3932164
  116.0 6.0 %copy-start.11 = (f32[1,1280]{1,0:T(1,128)S(1)}, f32[1,1280]{1,0:T(1,128)}, u32[]{:S(2)}) copy-start(f32[1,1280]{1,0:T(1,128)} %get-tuple-element.37) | copy-start | bytes 15364
  116.0 6.0 %copy-start.12 = (f32[1,1280]{1,0:T(1,128)S(1)}, f32[1,1280]{1,0:T(1,128)}, u32[]{:S(2)}) copy-start(f32[1,1280]{1,0:T(1,128)} %get-tuple-element.38) | copy-start | bytes 15364
  117.9 20.2 %collective-permute-start.8 = (bf16[256,1280]{1,0:T(8,128)(2,1)S(1)}, bf16[256,1280]{1,0:T(8,128)(2,1)}, u32[]{:S(2)}, u32[]{:S(2)}) collective-permute-start(bf16[256,1280]{1,0:T(8,128)(2,1)S(1)} %add_convert_fusion), channel_id=1, source_target_pairs={{0,2},{2,0},{1,3},{3,1},{4,6},{6,4},{5,7},{7,5},{8,10},{10,8},{9,1... | collective-permute-start | bytes 1966088 | tf_op jit(solution)/shard_map/ppermute | solution.py:470
  122.0 1.3 collective-permute-start.6
  123.2 14.3 %collective-permute-start.7 = (f32[1,1280]{1,0:T(1,128)S(1)}, f32[1,1280]{1,0:T(1,128)S(1)}, u32[]{:S(2)}, u32[]{:S(2)}) collective-permute-start(f32[1,1280]{1,0:T(1,128)S(1)} %add.34), channel_id=1, source_target_pairs={{0,2},{2,0},{1,3},{3,1},{4,6},{6,4},{5,7},{7,5},{8,10},{10,8},{9,1... | collective-permute-start | bytes 15368 | tf_op jit(solution)/shard_map/ppermute | solution.py:470
  156.0 18.4 %all-to-all-start.4 = ((bf16[16,80,256]{2,1,0:T(8,128)(2,1)}), bf16[16,80,256]{2,1,0:T(8,128)(2,1)S(1)}, u32[]{:S(2)}, u32[]{:S(2)}) async-start(bf16[16,80,256]{2,1,0:T(8,128)(2,1)} %shard_map.94), calls=%async_computation.4 | async-start | bytes 1310720 | tf_op jit(solution)/shard_map/all_to_all | solution.py:522
  174.4 0.9 copy-start.5
Sparse Core Ops, SparseCore 0:
  26.2 49.9 all-gather.1

commit v10 on v9

--- a/solution.py
+++ b/solution.py
@@ -343,14 +343,20 @@
 
 def gather_call(half, core):
     rows, width = 2 * half.shape[0], half.shape[1]
+    piece = 256
+    part = pl.BlockSpec((half.shape[0], piece), lambda n: (0, n))
     return pl.pallas_call(
         gather_kernel,
+        grid=(width // piece,),
         out_shape=(
             jax.ShapeDtypeStruct((rows, width), bf16),
             jax.ShapeDtypeStruct((width, rows), bf16),
         ),
-        in_specs=[vmem(), vmem()],
-        out_specs=(vmem(), vmem()),
+        in_specs=[part, part],
+        out_specs=(
+            pl.BlockSpec((rows, piece), lambda n: (0, n)),
+            pl.BlockSpec((piece, rows), lambda n: (n, 0)),
+        ),
         compiler_params=params(BIG),
     )(half, core)
 
@@ -482,10 +488,9 @@
     grad_rows, own = lax.optimization_barrier((grad_packed, own))
     packed = pack_call(grad_rows)
     flipped = jnp.swapaxes(w_qkv, 1, 2).reshape(3 * HEAD, width)
-    query, key, value = (flipped[HEAD * j : HEAD * j + HEAD] for j in range(3))
-    spare = jnp.zeros((PADDED - 3 * HEAD, width), bf16)
-    flipped = jnp.concatenate([query, value[:48], key, value[48:], spare], axis=0)
-    share = lax.dynamic_slice(flipped, (16 * dp, 0), (16, width))
+    block = jnp.where(dp < 5, dp, jnp.where(dp < 8, dp + 5, jnp.where(dp < 13, dp - 3, dp)))
+    share = lax.dynamic_slice(flipped, (16 * jnp.minimum(block, 14), 0), (16, width))
+    share = jnp.where(dp < 15, share, jnp.zeros_like(share))
     others = [lax.ppermute(share, "zq", [(i, (i + k) % RING) for i in range(RING)]) for k in (3, 2, 1)]
     others, packed = lax.optimization_barrier((others, packed))
     circle = jnp.concatenate([share] + others + [share] + others, axis=0)

time: 185 us -> 186 us (level)
    ppermute x6, starting transfers between devices: 5.7 us -> 8.2 us  [swap(): return lax.ppermute(x, axis, [(0, 1), (1, 0)])]
    all_gather x1, waiting for transfers between devices: 4.38 us -> 1.92 us  [on_device(): weights = lax.all_gather(ordered, ('y', 'x'), axis=0, tiled=True)]
    ppermute x6, waiting for transfers between devices: 31.3 us -> 33.7 us  [swap(): return lax.ppermute(x, axis, [(0, 1), (1, 0)])]
    unnamed x38 -> x33, local copies, waits for them, and re-layouts: 4.77 us -> 2.87 us
  transfers between devices with their start and end apart: 14 -> 14, of which waited for: 6 -> 7; matrix products, arithmetic and copies ran while one was open for 2% -> 2% of each run, Pallas kernels for 22% -> 22%
where the time goes in v10:
time: 186 us; the launch traced here: 184 us
  Pallas kernels  54.8 us (29%)
  waiting for transfers between devices  47.3 us (25%)
  starting transfers between devices  41.8 us (22%)
  blocking collectives  17.2 us (9%)
  between operations  14.3 us (8%)
  other arithmetic  4.68 us (3%)
  local copies, waits for them, and re-layouts  4.49 us (2%)
    ppermute x6, waiting for transfers between devices, swap(): return lax.ppermute(x, axis, [(0, 1), (1, 0)])  33.7 us
    all_to_all x1, blocking collectives, on_device(): arrived = lax.all_to_all(message, 'zq', split_axis=0, concat_axis=0)  17.2 us
    pallas_call x2, Pallas kernels, back_call(): pl.pallas_call(back_kernel, grid=(width // piece,), out_shape=(jax.ShapeD...  12.5 us
    ppermute x3, starting transfers between devices, on_device(): lax.ppermute(share, 'zq', [(i, (i + k) % RING) for i in range(RING)])  11.4 us
    pallas_call x1, Pallas kernels, head_call(): pl.pallas_call(head_kernel, out_shape=(jax.ShapeDtypeStruct((RING, rows,...  10.7 us
    pallas_call x1, Pallas kernels, forward_call(): pl.pallas_call(forward_kernel, out_shape=tuple((jax.ShapeDtypeStruct(*eac...  9.77 us
    all_to_all x1, starting transfers between devices, on_device(): whole = lax.all_to_all(copies, ('y', 'x'), split_axis=0, concat_axis=0)  8.48 us
    ppermute x6, starting transfers between devices, swap(): return lax.ppermute(x, axis, [(0, 1), (1, 0)])  8.2 us
  transfers between devices with their start and end apart: 14, of which 7 were waited for; matrix products, arithmetic and copies ran while one was open for 2% of the time, Pallas kernels for 22%

profile of v10, /device:TPU:2, one launch (start us, length us, event | category | flops | bytes accessed | tf_op | source)
XLA Modules:
  0.0 184.5 jit_solution(1665984115322113911)
XLA Ops:
  7.2 0.8 constant_dynamic-update-slice_fusion.9
  8.0 3.3 %collective-permute-start.4 = (bf16[16,1280]{1,0:T(8,128)(2,1)S(1)}, bf16[16,1280]{1,0:T(8,128)(2,1)S(1)}, u32[]{:S(2)}, u32[]{:S(2)}) collective-permute-start(bf16[16,1280]{1,0:T(8,128)(2,1)S(1)} %get-tuple-element.42), channel_id=1, source_target_pairs={{0,4},{4,8},{8,12},{12,0},{1,5},{5,9},{9,13},{13,1},{2,6},{6,10},{... | collective-permute-start | bytes 122888 | tf_op jit(solution)/shard_map/ppermute | solution.py:494
  11.4 5.4 %collective-permute-start.3 = (bf16[16,1280]{1,0:T(8,128)(2,1)S(1)}, bf16[16,1280]{1,0:T(8,128)(2,1)S(1)}, u32[]{:S(2)}, u32[]{:S(2)}) collective-permute-start(bf16[16,1280]{1,0:T(8,128)(2,1)S(1)} %get-tuple-element.42), channel_id=1, source_target_pairs={{0,8},{4,12},{8,0},{12,4},{1,9},{5,13},{9,1},{13,5},{2,10},{6,14},... | collective-permute-start | bytes 122888 | tf_op jit(solution)/shard_map/ppermute | solution.py:494
  16.8 2.7 %collective-permute-start.2 = (bf16[16,1280]{1,0:T(8,128)(2,1)S(1)}, bf16[16,1280]{1,0:T(8,128)(2,1)S(1)}, u32[]{:S(2)}, u32[]{:S(2)}) collective-permute-start(bf16[16,1280]{1,0:T(8,128)(2,1)S(1)} %get-tuple-element.42), channel_id=1, source_target_pairs={{0,12},{4,0},{8,4},{12,8},{1,13},{5,1},{9,5},{13,9},{2,14},{6,2},{... | collective-permute-start | bytes 122888 | tf_op jit(solution)/shard_map/ppermute | solution.py:494
  20.1 1.1 copy-done
  21.5 0.8 copy-done.1
  22.3 2.5 %shard_map.87 = bf16[16,160,128]{2,1,0:T(8,128)(2,1)} custom-call(bf16[256,1280]{1,0:T(8,128)(2,1)S(1)} %copy-done.1), custom_call_target="tpu_custom_call" | custom-call | tf_op jit(solution)/shard_map/pallas_call | solution.py:314
  25.6 1.1 collective-permute-start
  26.7 3.6 %all-to-all-start = ((bf16[16,160,128]{2,1,0:T(8,128)(2,1)}), bf16[16,160,128]{2,1,0:T(8,128)(2,1)S(1)}, u32[]{:S(2)}, u32[]{:S(2)}) async-start(bf16[16,160,128]{2,1,0:T(8,128)(2,1)} %shard_map.87), calls=%async_computation | async-start | bytes 1310720 | tf_op jit(solution)/shard_map/all_to_all | solution.py:501
  30.4 18.7 %collective-permute-done = bf16[256,1280]{1,0:T(8,128)(2,1)S(1)} collective-permute-done((bf16[256,1280]{1,0:T(8,128)(2,1)S(1)}, bf16[256,1280]{1,0:T(8,128)(2,1)S(1)}, u32[]{:S(2)}, u32[]{:S(2)}) %collective-permute-start) | collective-permute-done | bytes 655392 | tf_op jit(solution)/shard_map/ppermute | solution.py:476
  49.3 4.7 %all-to-all-done.in_ref = bf16[16,160,128]{2,1,0:T(8,128)(2,1)S(1)} async-done(((bf16[16,160,128]{2,1,0:T(8,128)(2,1)}), bf16[16,160,128]{2,1,0:T(8,128)(2,1)S(1)}, u32[]{:S(2)}, u32[]{:S(2)}) %all-to-all-start) | async-done | bytes 655392 | tf_op jit(solution)/shard_map/all_to_all | solution.py:501
  54.1 7.1 %shard_map.88 = bf16[4,4,160,128]{3,2,1,0:T(8,128)(2,1)} custom-call(s32[2]{0:T(128)S(1)} %pad_add_fusion.place_ref, s32[4096]{0:T(1024)S(1)} %bitcast.12, bf16[16,160,128]{2,1,0:T(8,128)(2,1)S(1)} %all-to-all-done.in_ref), custom_call_target="tpu_custom_call" | custom-call | tf_op jit(solution)/shard_map/pallas_call | solution.py:324
  61.1 4.3 %all-to-all-start.1 = ((bf16[4,4,160,128]{3,2,1,0:T(8,128)(2,1)}), bf16[4,4,160,128]{3,2,1,0:T(8,128)(2,1)S(1)}, u32[]{:S(2)}, u32[]{:S(2)}) async-start(bf16[4,4,160,128]{3,2,1,0:T(8,128)(2,1)} %shard_map.88), calls=%async_computation.1 | async-start | bytes 1310720 | tf_op jit(solution)/shard_map/all_to_all | solution.py:503
  66.1 5.5 %shard_map.86 = (bf16[1024,1280]{1,0:T(8,128)(2,1)}, bf16[1280,1024]{1,0:T(8,128)(2,1)}) custom-call(bf16[512,1280]{1,0:T(8,128)(2,1)} %copy-done.6, bf16[512,1280]{1,0:T(8,128)(2,1)} %collective-permute-done.1.core_ref), custom_call_target="tpu_custom_call" | custom-call | tf_op jit(solution)/shard_map/pallas_call | solution.py:348
  71.6 1.9 %all-gather.2.cloned.1.call-done = bf16[1024,1280]{1,0:T(8,128)(2,1)} async-done(((bf16[64,1280]{1,0:T(8,128)(2,1)}), bf16[1024,1280]{1,0:T(8,128)(2,1)}) %all-gather.2.cloned.1.call-update) | async-done | bytes 2621456 | tf_op jit(solution)/shard_map/all_gather | solution.py:498
  73.5 9.8 %shard_map.89 = (bf16[4,1024,128]{2,1,0:T(8,128)(2,1)}, bf16[4,1024,128]{2,1,0:T(8,128)(2,1)}, f32[4,1024,128]{2,1,0:T(8,128)}) custom-call(s32[2]{0:T(128)} %copy-done.4, bf16[1024,1280]{1,0:T(8,128)(2,1)} %get-tuple-element.26.normed_hbm.normed_ref, bf16[16,4,16,1280]{3,2,1,0:T(8,128)(2,1)} %bitcast.13, f32[32,128]{1,0:T(8,128)} %bitcast.18), custom_call_target="tpu_custom_call" | custom-call | tf_op jit(solution)/shard_map/pallas_call | solution.py:378
  83.3 0.8 copy-done.8
  84.2 10.7 %shard_map.90 = (bf16[4,1024,256]{2,1,0:T(8,128)(2,1)}, bf16[16,4,80,256]{3,2,1,0:T(8,128)(2,1)}) custom-call(bf16[1280,1024]{1,0:T(8,128)(2,1)} %get-tuple-element.23.turned_hbm, bf16[4,4,160,128]{3,2,1,0:T(8,128)(2,1)} %copy-done.8, bf16[4,1024,128]{2,1,0:T(8,128)(2,1)} %get-tuple-element.30.first_hbm, bf16[4,1024,128]{2,1,0:T(8,128)(2,1)} %get-tuple-element.31.second_hbm, ...), custom_call_target="tpu_custom_call" | custom-call | tf_op jit(solution)/shard_map/pallas_call | solution.py:397
  94.9 5.7 %all-to-all-start.2 = ((bf16[16,4,80,256]{3,2,1,0:T(8,128)(2,1)}), bf16[16,4,80,256]{3,2,1,0:T(8,128)(2,1)S(1)}, u32[]{:S(2)}, u32[]{:S(2)}) async-start(bf16[16,4,80,256]{3,2,1,0:T(8,128)(2,1)} %get-tuple-element.36), calls=%async_computation.2 | async-start | bytes 5242880 | tf_op jit(solution)/shard_map/all_to_all | solution.py:511
  100.6 6.1 %shard_map.92 = (bf16[512,1280]{1,0:T(8,128)(2,1)}, f32[1,1280]{1,0:T(1,128)}) custom-call(bf16[4,1024,256]{2,1,0:T(8,128)(2,1)} %get-tuple-element.33.grad_ref, bf16[16,4,16,1280]{3,2,1,0:T(8,128)(2,1)} %bitcast.14, bf16[1024,1280]{1,0:T(8,128)(2,1)} %get-tuple-element.26.normed_hbm.normed_ref), custom_call_target="tpu_custom_call" | custom-call | tf_op jit(solution)/shard_map/pallas_call | solution.py:421
  106.7 1.6 collective-permute-start.5
  108.3 6.4 %shard_map.91 = (f32[512,1280]{1,0:T(8,128)}, f32[1,1280]{1,0:T(1,128)}) custom-call(bf16[4,1024,256]{2,1,0:T(8,128)(2,1)} %get-tuple-element.33.grad_ref, bf16[16,4,16,1280]{3,2,1,0:T(8,128)(2,1)} %bitcast.15, bf16[1024,1280]{1,0:T(8,128)(2,1)} %get-tuple-element.26.normed_hbm.normed_ref), custom_call_target="tpu_custom_call" | custom-call | tf_op jit(solution)/shard_map/pallas_call | solution.py:421
  114.7 1.9 %add_convert_fusion = bf16[256,1280]{1,0:T(8,128)(2,1)S(1)} fusion(f32[512,1280]{1,0:T(8,128)} %get-tuple-element.34.keep_ref, bf16[512,1280]{1,0:T(8,128)(2,1)S(1)} %collective-permute-done.5.core_ref), kind=kLoop, calls=%fused_computation | loop fusion | flops 983040 | bytes 2621440 | tf_op jit(solution)/shard_map/convert_element_type | solution.py:517
  116.6 5.0 %collective-permute-start.8 = (bf16[256,1280]{1,0:T(8,128)(2,1)S(1)}, bf16[256,1280]{1,0:T(8,128)(2,1)}, u32[]{:S(2)}, u32[]{:S(2)}) collective-permute-start(bf16[256,1280]{1,0:T(8,128)(2,1)S(1)} %add_convert_fusion), channel_id=1, source_target_pairs={{0,2},{2,0},{1,3},{3,1},{4,6},{6,4},{5,7},{7,5},{8,10},{10,8},{9,1... | collective-permute-start | bytes 1966088 | tf_op jit(solution)/shard_map/ppermute | solution.py:476
  121.9 1.0 collective-permute-done.6
  123.0 14.1 %collective-permute-done.7 = f32[1,1280]{1,0:T(1,128)S(1)} collective-permute-done((f32[1,1280]{1,0:T(1,128)S(1)}, f32[1,1280]{1,0:T(1,128)S(1)}, u32[]{:S(2)}, u32[]{:S(2)}) %collective-permute-start.7) | collective-permute-done | bytes 5152 | tf_op jit(solution)/shard_map/ppermute | solution.py:476
  138.2 17.2 %all_to_all.25.in_ref = bf16[4,80,256]{2,1,0:T(8,128)(2,1)S(1)} all-to-all(bf16[4,80,256]{2,1,0:T(8,128)(2,1)S(1)} %pad_maximum_fusion), channel_id=1, replica_groups=mesh['y'=4,'x'=4,'zq'=4,'zp'=2,'core'=2] {'zq'}, dimensions={0} | all-to-all | bytes 327680 | tf_op jit(solution)/shard_map/all_to_all | solution.py:525
  155.4 0.9 shard_map.94
  156.3 8.5 %all-to-all-start.4 = ((bf16[16,80,256]{2,1,0:T(8,128)(2,1)}), bf16[16,80,256]{2,1,0:T(8,128)(2,1)S(1)}, u32[]{:S(2)}, u32[]{:S(2)}) async-start(bf16[16,80,256]{2,1,0:T(8,128)(2,1)} %shard_map.94), calls=%async_computation.4 | async-start | bytes 1310720 | tf_op jit(solution)/shard_map/all_to_all | solution.py:527
  164.8 3.4 %shard_map.93 = bf16[256,1280]{1,0:T(8,128)(2,1)} custom-call(bf16[256,1280]{1,0:T(8,128)(2,1)} %rows_ref.4, f32[1,1280]{1,0:T(1,128)} %copy-done.2, f32[512,1280]{1,0:T(8,128)} %get-tuple-element.34.keep_ref, bf16[512,1280]{1,0:T(8,128)(2,1)} %copy-done.7, bf16[256,1280]{1,0:T(8,128)(2,1)} %collective-permute-done.8.pair_ref), custom_call_target="tpu_custom_call" | custom-call | tf_op jit(solution)/shard_map/pallas_call | solution.py:443
  168.2 6.4 %all-to-all-done.4.whole_ref = bf16[16,80,256]{2,1,0:T(8,128)(2,1)S(1)} async-done(((bf16[16,80,256]{2,1,0:T(8,128)(2,1)}), bf16[16,80,256]{2,1,0:T(8,128)(2,1)S(1)}, u32[]{:S(2)}, u32[]{:S(2)}) %all-to-all-start.4) | async-done | bytes 655392 | tf_op jit(solution)/shard_map/all_to_all | solution.py:527
  175.5 2.2 %shard_map.95 = f32[240,1280]{1,0:T(8,128)} custom-call(bf16[16,80,256]{2,1,0:T(8,128)(2,1)} %copy-done.5), custom_call_target="tpu_custom_call" | custom-call | tf_op jit(solution)/shard_map/pallas_call | solution.py:465
  (60 shorter events, 5.1 us)
Async XLA Ops:
  7.2 66.4 %all-gather.2.cloned.1.call-start = ((), (), s32[]{:S(2)}) async-start(), calls=%async_computation.5 | async-start | bytes 2785280 | tf_op jit(solution)/shard_map/all_gather | solution.py:498
  8.0 16.8 %collective-permute-start.4 = (bf16[16,1280]{1,0:T(8,128)(2,1)S(1)}, bf16[16,1280]{1,0:T(8,128)(2,1)S(1)}, u32[]{:S(2)}, u32[]{:S(2)}) collective-permute-start(bf16[16,1280]{1,0:T(8,128)(2,1)S(1)} %get-tuple-element.42), channel_id=1, source_target_pairs={{0,4},{4,8},{8,12},{12,0},{1,5},{5,9},{9,13},{13,1},{2,6},{6,10},{... | collective-permute-start | bytes 122888 | tf_op jit(solution)/shard_map/ppermute | solution.py:494
  11.4 13.4 %collective-permute-start.3 = (bf16[16,1280]{1,0:T(8,128)(2,1)S(1)}, bf16[16,1280]{1,0:T(8,128)(2,1)S(1)}, u32[]{:S(2)}, u32[]{:S(2)}) collective-permute-start(bf16[16,1280]{1,0:T(8,128)(2,1)S(1)} %get-tuple-element.42), channel_id=1, source_target_pairs={{0,8},{4,12},{8,0},{12,4},{1,9},{5,13},{9,1},{13,5},{2,10},{6,14},... | collective-permute-start | bytes 122888 | tf_op jit(solution)/shard_map/ppermute | solution.py:494
  16.8 8.1 %collective-permute-start.2 = (bf16[16,1280]{1,0:T(8,128)(2,1)S(1)}, bf16[16,1280]{1,0:T(8,128)(2,1)S(1)}, u32[]{:S(2)}, u32[]{:S(2)}) collective-permute-start(bf16[16,1280]{1,0:T(8,128)(2,1)S(1)} %get-tuple-element.42), channel_id=1, source_target_pairs={{0,12},{4,0},{8,4},{12,8},{1,13},{5,1},{9,5},{13,9},{2,14},{6,2},{... | collective-permute-start | bytes 122888 | tf_op jit(solution)/shard_map/ppermute | solution.py:494
  20.1 1.1 copy-start
  21.2 3.6 %copy-start.2 = (f32[1,1280]{1,0:T(1,128)}, f32[1,1280]{1,0:T(1,128)S(1)}, u32[]{:S(2)}) copy-start(f32[1,1280]{1,0:T(1,128)S(1)} %reshape.33.gain_ref) | copy-start | bytes 15364
  21.2 1.1 copy-start.1
  25.6 23.5 %collective-permute-start = (bf16[256,1280]{1,0:T(8,128)(2,1)S(1)}, bf16[256,1280]{1,0:T(8,128)(2,1)S(1)}, u32[]{:S(2)}, u32[]{:S(2)}) collective-permute-start(bf16[256,1280]{1,0:T(8,128)(2,1)S(1)} %shard_map.85), channel_id=1, source_target_pairs={{0,2},{2,0},{1,3},{3,1},{4,6},{6,4},{5,7},{7,5},{8,10},{10,8},{9,1... | collective-permute-start | bytes 1966088 | tf_op jit(solution)/shard_map/ppermute | solution.py:476
  26.7 27.3 %all-to-all-start = ((bf16[16,160,128]{2,1,0:T(8,128)(2,1)}), bf16[16,160,128]{2,1,0:T(8,128)(2,1)S(1)}, u32[]{:S(2)}, u32[]{:S(2)}) async-start(bf16[16,160,128]{2,1,0:T(8,128)(2,1)} %shard_map.87), calls=%async_computation | async-start | bytes 1310720 | tf_op jit(solution)/shard_map/all_to_all | solution.py:501
  30.4 23.7 %copy-start.3 = (s32[1,4096]{1,0:T(1,128)S(1)}, s32[1,4096]{1,0:T(1,128)}, u32[]{:S(2)}) copy-start(s32[1,4096]{1,0:T(1,128)} %param.8) | copy-start | bytes 49156
  49.2 12.0 %copy-start.6 = (bf16[512,1280]{1,0:T(8,128)(2,1)}, bf16[512,1280]{1,0:T(8,128)(2,1)S(1)}, u32[]{:S(2)}) copy-start(bf16[512,1280]{1,0:T(8,128)(2,1)S(1)} %constant_dynamic-update-slice_fusion.half_ref) | copy-start | bytes 3932164
  49.2 16.9 %collective-permute-start.1 = (bf16[512,1280]{1,0:T(8,128)(2,1)S(1)}, bf16[512,1280]{1,0:T(8,128)(2,1)}, u32[]{:S(2)}, u32[]{:S(2)}) collective-permute-start(bf16[512,1280]{1,0:T(8,128)(2,1)S(1)} %constant_dynamic-update-slice_fusion.half_ref), channel_id=1, source_target_pairs={{0,1},{1,0},{2,3},{3,2},{4,5},{5,4},{6,7},{7,6},{8,9},{9,8},{10,11... | collective-permute-start | bytes 3932168 | tf_op jit(solution)/shard_map/ppermute | solution.py:476
  49.3 11.8 %copy-start.4 = (s32[2]{0:T(128)}, s32[2]{0:T(128)S(1)}, u32[]{:S(2)}) copy-start(s32[2]{0:T(128)S(1)} %pad_add_fusion.place_ref) | copy-start | bytes 28
  54.1 11.4 %copy-start.10 = (s32[1,4096]{1,0:T(1,128)S(1)}, s32[1,4096]{1,0:T(1,128)}, u32[]{:S(2)}) copy-start(s32[1,4096]{1,0:T(1,128)} %param.9) | copy-start | bytes 49156
  61.1 22.2 %all-to-all-start.1 = ((bf16[4,4,160,128]{3,2,1,0:T(8,128)(2,1)}), bf16[4,4,160,128]{3,2,1,0:T(8,128)(2,1)S(1)}, u32[]{:S(2)}, u32[]{:S(2)}) async-start(bf16[4,4,160,128]{3,2,1,0:T(8,128)(2,1)} %shard_map.88), calls=%async_computation.1 | async-start | bytes 1310720 | tf_op jit(solution)/shard_map/all_to_all | solution.py:503
  83.3 0.8 copy-start.8
  94.9 42.8 %all-to-all-start.2 = ((bf16[16,4,80,256]{3,2,1,0:T(8,128)(2,1)}), bf16[16,4,80,256]{3,2,1,0:T(8,128)(2,1)S(1)}, u32[]{:S(2)}, u32[]{:S(2)}) async-start(bf16[16,4,80,256]{3,2,1,0:T(8,128)(2,1)} %get-tuple-element.36), calls=%async_computation.2 | async-start | bytes 5242880 | tf_op jit(solution)/shard_map/all_to_all | solution.py:511
  106.7 7.9 %collective-permute-start.5 = (bf16[512,1280]{1,0:T(8,128)(2,1)}, bf16[512,1280]{1,0:T(8,128)(2,1)S(1)}, u32[]{:S(2)}, u32[]{:S(2)}) collective-permute-start(bf16[512,1280]{1,0:T(8,128)(2,1)} %get-tuple-element.35), channel_id=1, source_target_pairs={{0,1},{1,0},{2,3},{3,2},{4,5},{5,4},{6,7},{7,6},{8,9},{9,8},{10,11... | collective-permute-start | bytes 3932168 | tf_op jit(solution)/shard_map/ppermute | solution.py:476
  114.7 2.0 %copy-start.7 = (bf16[512,1280]{1,0:T(8,128)(2,1)}, bf16[512,1280]{1,0:T(8,128)(2,1)S(1)}, u32[]{:S(2)}) copy-start(bf16[512,1280]{1,0:T(8,128)(2,1)S(1)} %collective-permute-done.5.core_ref) | copy-start | bytes 3932164
  114.7 6.9 %copy-start.11 = (f32[1,1280]{1,0:T(1,128)S(1)}, f32[1,1280]{1,0:T(1,128)}, u32[]{:S(2)}) copy-start(f32[1,1280]{1,0:T(1,128)} %get-tuple-element.37) | copy-start | bytes 15364
  114.7 6.9 %copy-start.12 = (f32[1,1280]{1,0:T(1,128)S(1)}, f32[1,1280]{1,0:T(1,128)}, u32[]{:S(2)}) copy-start(f32[1,1280]{1,0:T(1,128)} %get-tuple-element.38) | copy-start | bytes 15364
  116.6 21.6 %collective-permute-start.8 = (bf16[256,1280]{1,0:T(8,128)(2,1)S(1)}, bf16[256,1280]{1,0:T(8,128)(2,1)}, u32[]{:S(2)}, u32[]{:S(2)}) collective-permute-start(bf16[256,1280]{1,0:T(8,128)(2,1)S(1)} %add_convert_fusion), channel_id=1, source_target_pairs={{0,2},{2,0},{1,3},{3,1},{4,6},{6,4},{5,7},{7,5},{8,10},{10,8},{9,1... | collective-permute-start | bytes 1966088 | tf_op jit(solution)/shard_map/ppermute | solution.py:476
  121.6 1.3 collective-permute-start.6
  122.8 14.3 %collective-permute-start.7 = (f32[1,1280]{1,0:T(1,128)S(1)}, f32[1,1280]{1,0:T(1,128)S(1)}, u32[]{:S(2)}, u32[]{:S(2)}) collective-permute-start(f32[1,1280]{1,0:T(1,128)S(1)} %add.39), channel_id=1, source_target_pairs={{0,2},{2,0},{1,3},{3,1},{4,6},{6,4},{5,7},{7,5},{8,10},{10,8},{9,1... | collective-permute-start | bytes 15368 | tf_op jit(solution)/shard_map/ppermute | solution.py:476
  156.3 18.3 %all-to-all-start.4 = ((bf16[16,80,256]{2,1,0:T(8,128)(2,1)}), bf16[16,80,256]{2,1,0:T(8,128)(2,1)S(1)}, u32[]{:S(2)}, u32[]{:S(2)}) async-start(bf16[16,80,256]{2,1,0:T(8,128)(2,1)} %shard_map.94), calls=%async_computation.4 | async-start | bytes 1310720 | tf_op jit(solution)/shard_map/all_to_all | solution.py:527
  164.8 10.1 %copy-start.9 = (f32[1280]{0:T(1024)S(1)}, f32[1280]{0:T(1024)}, u32[]{:S(2)}) copy-start(f32[1280]{0:T(1024)} %param.11) | copy-start | bytes 15364
  174.6 0.9 copy-start.5
Sparse Core Ops, SparseCore 0:
  25.8 47.7 all-gather.1

commit v11 on v9

--- a/solution.py
+++ b/solution.py
@@ -87,13 +87,13 @@
             base = q * SLOTS * CHUNK + (slot ^ off) * CHUNK
 
             def step(i, carry):
-                at = i * 64
-                for u in range(64):
+                at = i * 128
+                for u in range(128):
                     row = source_ref[base + at + u]
                     picked[pl.ds(at + u, 1), :] = table[pl.ds(row, 1), :]
                 return carry
 
-            lax.fori_loop(0, CHUNK // 64, step, 0)
+            lax.fori_loop(0, CHUNK // 128, step, 0)
             top, low = pack(picked[...])
             out_ref[q, o, :128, :] = top.astype(bf16)
             out_ref[q, o, 128:, :] = low.astype(bf16)
@@ -482,10 +482,9 @@
     grad_rows, own = lax.optimization_barrier((grad_packed, own))
     packed = pack_call(grad_rows)
     flipped = jnp.swapaxes(w_qkv, 1, 2).reshape(3 * HEAD, width)
-    query, key, value = (flipped[HEAD * j : HEAD * j + HEAD] for j in range(3))
-    spare = jnp.zeros((PADDED - 3 * HEAD, width), bf16)
-    flipped = jnp.concatenate([query, value[:48], key, value[48:], spare], axis=0)
-    share = lax.dynamic_slice(flipped, (16 * dp, 0), (16, width))
+    block = jnp.where(dp < 5, dp, jnp.where(dp < 8, dp + 5, jnp.where(dp < 13, dp - 3, dp)))
+    share = lax.dynamic_slice(flipped, (16 * jnp.minimum(block, 14), 0), (16, width))
+    share = jnp.where(dp < 15, share, jnp.zeros_like(share))
     others = [lax.ppermute(share, "zq", [(i, (i + k) % RING) for i in range(RING)]) for k in (3, 2, 1)]
     others, packed = lax.optimization_barrier((others, packed))
     circle = jnp.concatenate([share] + others + [share] + others, axis=0)

time: 185 us -> 186 us (level)
  waiting for transfers between devices: 46.7 us -> 50 us
    ppermute x6, waiting for transfers between devices: 31.3 us -> 33.7 us  [swap(): return lax.ppermute(x, axis, [(0, 1), (1, 0)])]
    ppermute x6, starting transfers between devices: 5.7 us -> 7.79 us  [swap(): return lax.ppermute(x, axis, [(0, 1), (1, 0)])]
    all_gather x1, waiting for transfers between devices: 4.38 us -> 2.48 us  [on_device(): weights = lax.all_gather(ordered, ('y', 'x'), axis=0, tiled=True)]
    unnamed x38 -> x33, local copies, waits for them, and re-layouts: 4.77 us -> 2.87 us
  transfers between devices with their start and end apart: 14 -> 14, of which waited for: 6 -> 7; matrix products, arithmetic and copies ran while one was open for 2% -> 2% of each run, Pallas kernels for 22% -> 22%
where the time goes in v11:
time: 186 us; the launch traced here: 185 us
  Pallas kernels  54.2 us (29%)
  waiting for transfers between devices  50 us (27%)
  starting transfers between devices  41.3 us (22%)
  blocking collectives  16.2 us (9%)
  between operations  14.3 us (8%)
  other arithmetic  4.68 us (3%)
  local copies, waits for them, and re-layouts  4.49 us (2%)
    ppermute x6, waiting for transfers between devices, swap(): return lax.ppermute(x, axis, [(0, 1), (1, 0)])  33.7 us
    all_to_all x1, blocking collectives, on_device(): arrived = lax.all_to_all(message, 'zq', split_axis=0, concat_axis=0)  16.2 us
    pallas_call x2, Pallas kernels, back_call(): pl.pallas_call(back_kernel, grid=(width // piece,), out_shape=(jax.ShapeD...  12.5 us
    ppermute x3, starting transfers between devices, on_device(): lax.ppermute(share, 'zq', [(i, (i + k) % RING) for i in range(RING)])  11.4 us
    pallas_call x1, Pallas kernels, head_call(): pl.pallas_call(head_kernel, out_shape=(jax.ShapeDtypeStruct((RING, rows,...  10.7 us
    pallas_call x1, Pallas kernels, forward_call(): pl.pallas_call(forward_kernel, out_shape=tuple((jax.ShapeDtypeStruct(*eac...  9.77 us
    all_to_all x1, starting transfers between devices, on_device(): whole = lax.all_to_all(copies, ('y', 'x'), split_axis=0, concat_axis=0)  8.41 us
    ppermute x6, starting transfers between devices, swap(): return lax.ppermute(x, axis, [(0, 1), (1, 0)])  7.79 us
  transfers between devices with their start and end apart: 14, of which 7 were waited for; matrix products, arithmetic and copies ran while one was open for 2% of the time, Pallas kernels for 22%

profile of v11, /device:TPU:2, one launch (start us, length us, event | category | flops | bytes accessed | tf_op | source)
XLA Modules:
  0.0 185.2 jit_solution(13229803023119973534)
XLA Ops:
  8.0 3.3 %collective-permute-start.4 = (bf16[16,1280]{1,0:T(8,128)(2,1)S(1)}, bf16[16,1280]{1,0:T(8,128)(2,1)S(1)}, u32[]{:S(2)}, u32[]{:S(2)}) collective-permute-start(bf16[16,1280]{1,0:T(8,128)(2,1)S(1)} %get-tuple-element.42), channel_id=1, source_target_pairs={{0,4},{4,8},{8,12},{12,0},{1,5},{5,9},{9,13},{13,1},{2,6},{6,10},{... | collective-permute-start | bytes 122888 | tf_op jit(solution)/shard_map/ppermute | solution.py:488
  11.4 5.4 %collective-permute-start.3 = (bf16[16,1280]{1,0:T(8,128)(2,1)S(1)}, bf16[16,1280]{1,0:T(8,128)(2,1)S(1)}, u32[]{:S(2)}, u32[]{:S(2)}) collective-permute-start(bf16[16,1280]{1,0:T(8,128)(2,1)S(1)} %get-tuple-element.42), channel_id=1, source_target_pairs={{0,8},{4,12},{8,0},{12,4},{1,9},{5,13},{9,1},{13,5},{2,10},{6,14},... | collective-permute-start | bytes 122888 | tf_op jit(solution)/shard_map/ppermute | solution.py:488
  16.8 2.7 %collective-permute-start.2 = (bf16[16,1280]{1,0:T(8,128)(2,1)S(1)}, bf16[16,1280]{1,0:T(8,128)(2,1)S(1)}, u32[]{:S(2)}, u32[]{:S(2)}) collective-permute-start(bf16[16,1280]{1,0:T(8,128)(2,1)S(1)} %get-tuple-element.42), channel_id=1, source_target_pairs={{0,12},{4,0},{8,4},{12,8},{1,13},{5,1},{9,5},{13,9},{2,14},{6,2},{... | collective-permute-start | bytes 122888 | tf_op jit(solution)/shard_map/ppermute | solution.py:488
  20.1 1.1 copy-done
  21.5 0.8 copy-done.1
  22.3 2.5 %shard_map.87 = bf16[16,160,128]{2,1,0:T(8,128)(2,1)} custom-call(bf16[256,1280]{1,0:T(8,128)(2,1)S(1)} %copy-done.1), custom_call_target="tpu_custom_call" | custom-call | tf_op jit(solution)/shard_map/pallas_call | solution.py:314
  25.6 1.1 collective-permute-start
  26.7 3.6 %all-to-all-start = ((bf16[16,160,128]{2,1,0:T(8,128)(2,1)}), bf16[16,160,128]{2,1,0:T(8,128)(2,1)S(1)}, u32[]{:S(2)}, u32[]{:S(2)}) async-start(bf16[16,160,128]{2,1,0:T(8,128)(2,1)} %shard_map.87), calls=%async_computation | async-start | bytes 1310720 | tf_op jit(solution)/shard_map/all_to_all | solution.py:495
  30.4 18.7 %collective-permute-done = bf16[256,1280]{1,0:T(8,128)(2,1)S(1)} collective-permute-done((bf16[256,1280]{1,0:T(8,128)(2,1)S(1)}, bf16[256,1280]{1,0:T(8,128)(2,1)S(1)}, u32[]{:S(2)}, u32[]{:S(2)}) %collective-permute-start) | collective-permute-done | bytes 655392 | tf_op jit(solution)/shard_map/ppermute | solution.py:470
  49.3 4.7 %all-to-all-done.in_ref = bf16[16,160,128]{2,1,0:T(8,128)(2,1)S(1)} async-done(((bf16[16,160,128]{2,1,0:T(8,128)(2,1)}), bf16[16,160,128]{2,1,0:T(8,128)(2,1)S(1)}, u32[]{:S(2)}, u32[]{:S(2)}) %all-to-all-start) | async-done | bytes 655392 | tf_op jit(solution)/shard_map/all_to_all | solution.py:495
  54.1 6.9 %shard_map.88 = bf16[4,4,160,128]{3,2,1,0:T(8,128)(2,1)} custom-call(s32[2]{0:T(128)S(1)} %pad_add_fusion.place_ref, s32[4096]{0:T(1024)S(1)} %bitcast.12, bf16[16,160,128]{2,1,0:T(8,128)(2,1)S(1)} %all-to-all-done.in_ref), custom_call_target="tpu_custom_call" | custom-call | tf_op jit(solution)/shard_map/pallas_call | solution.py:324
  61.0 4.3 %all-to-all-start.1 = ((bf16[4,4,160,128]{3,2,1,0:T(8,128)(2,1)}), bf16[4,4,160,128]{3,2,1,0:T(8,128)(2,1)S(1)}, u32[]{:S(2)}, u32[]{:S(2)}) async-start(bf16[4,4,160,128]{3,2,1,0:T(8,128)(2,1)} %shard_map.88), calls=%async_computation.1 | async-start | bytes 1310720 | tf_op jit(solution)/shard_map/all_to_all | solution.py:497
  65.9 5.1 %shard_map.86 = (bf16[1024,1280]{1,0:T(8,128)(2,1)}, bf16[1280,1024]{1,0:T(8,128)(2,1)}) custom-call(bf16[512,1280]{1,0:T(8,128)(2,1)} %copy-done.6, bf16[512,1280]{1,0:T(8,128)(2,1)} %collective-permute-done.1.core_ref), custom_call_target="tpu_custom_call" | custom-call | tf_op jit(solution)/shard_map/pallas_call | solution.py:346
  71.1 2.5 %all-gather.2.cloned.1.call-done = bf16[1024,1280]{1,0:T(8,128)(2,1)} async-done(((bf16[64,1280]{1,0:T(8,128)(2,1)}), bf16[1024,1280]{1,0:T(8,128)(2,1)}) %all-gather.2.cloned.1.call-update) | async-done | bytes 2621456 | tf_op jit(solution)/shard_map/all_gather | solution.py:492
  73.5 9.8 %shard_map.89 = (bf16[4,1024,128]{2,1,0:T(8,128)(2,1)}, bf16[4,1024,128]{2,1,0:T(8,128)(2,1)}, f32[4,1024,128]{2,1,0:T(8,128)}) custom-call(s32[2]{0:T(128)} %copy-done.4, bf16[1024,1280]{1,0:T(8,128)(2,1)} %get-tuple-element.26.normed_hbm.normed_ref, bf16[16,4,16,1280]{3,2,1,0:T(8,128)(2,1)} %bitcast.13, f32[32,128]{1,0:T(8,128)} %bitcast.18), custom_call_target="tpu_custom_call" | custom-call | tf_op jit(solution)/shard_map/pallas_call | solution.py:372
  83.3 0.8 copy-done.8
  84.2 10.7 %shard_map.90 = (bf16[4,1024,256]{2,1,0:T(8,128)(2,1)}, bf16[16,4,80,256]{3,2,1,0:T(8,128)(2,1)}) custom-call(bf16[1280,1024]{1,0:T(8,128)(2,1)} %get-tuple-element.23.turned_hbm, bf16[4,4,160,128]{3,2,1,0:T(8,128)(2,1)} %copy-done.8, bf16[4,1024,128]{2,1,0:T(8,128)(2,1)} %get-tuple-element.30.first_hbm, bf16[4,1024,128]{2,1,0:T(8,128)(2,1)} %get-tuple-element.31.second_hbm, ...), custom_call_target="tpu_custom_call" | custom-call | tf_op jit(solution)/shard_map/pallas_call | solution.py:391
  94.9 5.7 %all-to-all-start.2 = ((bf16[16,4,80,256]{3,2,1,0:T(8,128)(2,1)}), bf16[16,4,80,256]{3,2,1,0:T(8,128)(2,1)S(1)}, u32[]{:S(2)}, u32[]{:S(2)}) async-start(bf16[16,4,80,256]{3,2,1,0:T(8,128)(2,1)} %get-tuple-element.36), calls=%async_computation.2 | async-start | bytes 5242880 | tf_op jit(solution)/shard_map/all_to_all | solution.py:505
  100.7 6.1 %shard_map.92 = (bf16[512,1280]{1,0:T(8,128)(2,1)}, f32[1,1280]{1,0:T(1,128)}) custom-call(bf16[4,1024,256]{2,1,0:T(8,128)(2,1)} %get-tuple-element.33.grad_ref, bf16[16,4,16,1280]{3,2,1,0:T(8,128)(2,1)} %bitcast.14, bf16[1024,1280]{1,0:T(8,128)(2,1)} %get-tuple-element.26.normed_hbm.normed_ref), custom_call_target="tpu_custom_call" | custom-call | tf_op jit(solution)/shard_map/pallas_call | solution.py:415
  106.7 1.0 collective-permute-start.5
  107.7 6.4 %shard_map.91 = (f32[512,1280]{1,0:T(8,128)}, f32[1,1280]{1,0:T(1,128)}) custom-call(bf16[4,1024,256]{2,1,0:T(8,128)(2,1)} %get-tuple-element.33.grad_ref, bf16[16,4,16,1280]{3,2,1,0:T(8,128)(2,1)} %bitcast.15, bf16[1024,1280]{1,0:T(8,128)(2,1)} %get-tuple-element.26.normed_hbm.normed_ref), custom_call_target="tpu_custom_call" | custom-call | tf_op jit(solution)/shard_map/pallas_call | solution.py:415
  114.1 1.9 %add_convert_fusion = bf16[256,1280]{1,0:T(8,128)(2,1)S(1)} fusion(f32[512,1280]{1,0:T(8,128)} %get-tuple-element.34.keep_ref, bf16[512,1280]{1,0:T(8,128)(2,1)S(1)} %collective-permute-done.5.core_ref), kind=kLoop, calls=%fused_computation | loop fusion | flops 983040 | bytes 2621440 | tf_op jit(solution)/shard_map/convert_element_type | solution.py:511
  116.1 5.1 %collective-permute-start.8 = (bf16[256,1280]{1,0:T(8,128)(2,1)S(1)}, bf16[256,1280]{1,0:T(8,128)(2,1)}, u32[]{:S(2)}, u32[]{:S(2)}) collective-permute-start(bf16[256,1280]{1,0:T(8,128)(2,1)S(1)} %add_convert_fusion), channel_id=1, source_target_pairs={{0,2},{2,0},{1,3},{3,1},{4,6},{6,4},{5,7},{7,5},{8,10},{10,8},{9,1... | collective-permute-start | bytes 1966088 | tf_op jit(solution)/shard_map/ppermute | solution.py:470
  121.5 1.0 collective-permute-done.6
  122.7 14.1 %collective-permute-done.7 = f32[1,1280]{1,0:T(1,128)S(1)} collective-permute-done((f32[1,1280]{1,0:T(1,128)S(1)}, f32[1,1280]{1,0:T(1,128)S(1)}, u32[]{:S(2)}, u32[]{:S(2)}) %collective-permute-start.7) | collective-permute-done | bytes 5152 | tf_op jit(solution)/shard_map/ppermute | solution.py:470
  136.9 1.7 all-to-all-done.2
  139.1 16.2 %all_to_all.25.in_ref = bf16[4,80,256]{2,1,0:T(8,128)(2,1)S(1)} all-to-all(bf16[4,80,256]{2,1,0:T(8,128)(2,1)S(1)} %pad_maximum_fusion), channel_id=1, replica_groups=mesh['y'=4,'x'=4,'zq'=4,'zp'=2,'core'=2] {'zq'}, dimensions={0} | all-to-all | bytes 327680 | tf_op jit(solution)/shard_map/all_to_all | solution.py:519
  155.3 0.9 shard_map.94
  156.2 8.4 %all-to-all-start.4 = ((bf16[16,80,256]{2,1,0:T(8,128)(2,1)}), bf16[16,80,256]{2,1,0:T(8,128)(2,1)S(1)}, u32[]{:S(2)}, u32[]{:S(2)}) async-start(bf16[16,80,256]{2,1,0:T(8,128)(2,1)} %shard_map.94), calls=%async_computation.4 | async-start | bytes 1310720 | tf_op jit(solution)/shard_map/all_to_all | solution.py:521
  164.6 3.4 %shard_map.93 = bf16[256,1280]{1,0:T(8,128)(2,1)} custom-call(bf16[256,1280]{1,0:T(8,128)(2,1)} %rows_ref.4, f32[1,1280]{1,0:T(1,128)} %copy-done.2, f32[512,1280]{1,0:T(8,128)} %get-tuple-element.34.keep_ref, bf16[512,1280]{1,0:T(8,128)(2,1)} %copy-done.7, bf16[256,1280]{1,0:T(8,128)(2,1)} %collective-permute-done.8.pair_ref), custom_call_target="tpu_custom_call" | custom-call | tf_op jit(solution)/shard_map/pallas_call | solution.py:437
  168.0 7.3 %all-to-all-done.4.whole_ref = bf16[16,80,256]{2,1,0:T(8,128)(2,1)S(1)} async-done(((bf16[16,80,256]{2,1,0:T(8,128)(2,1)}), bf16[16,80,256]{2,1,0:T(8,128)(2,1)S(1)}, u32[]{:S(2)}, u32[]{:S(2)}) %all-to-all-start.4) | async-done | bytes 655392 | tf_op jit(solution)/shard_map/all_to_all | solution.py:521
  176.2 2.2 %shard_map.95 = f32[240,1280]{1,0:T(8,128)} custom-call(bf16[16,80,256]{2,1,0:T(8,128)(2,1)} %copy-done.5), custom_call_target="tpu_custom_call" | custom-call | tf_op jit(solution)/shard_map/pallas_call | solution.py:459
  (60 shorter events, 5.4 us)
Async XLA Ops:
  7.2 66.4 %all-gather.2.cloned.1.call-start = ((), (), s32[]{:S(2)}) async-start(), calls=%async_computation.5 | async-start | bytes 2785280 | tf_op jit(solution)/shard_map/all_gather | solution.py:492
  8.0 16.8 %collective-permute-start.4 = (bf16[16,1280]{1,0:T(8,128)(2,1)S(1)}, bf16[16,1280]{1,0:T(8,128)(2,1)S(1)}, u32[]{:S(2)}, u32[]{:S(2)}) collective-permute-start(bf16[16,1280]{1,0:T(8,128)(2,1)S(1)} %get-tuple-element.42), channel_id=1, source_target_pairs={{0,4},{4,8},{8,12},{12,0},{1,5},{5,9},{9,13},{13,1},{2,6},{6,10},{... | collective-permute-start | bytes 122888 | tf_op jit(solution)/shard_map/ppermute | solution.py:488
  11.4 13.4 %collective-permute-start.3 = (bf16[16,1280]{1,0:T(8,128)(2,1)S(1)}, bf16[16,1280]{1,0:T(8,128)(2,1)S(1)}, u32[]{:S(2)}, u32[]{:S(2)}) collective-permute-start(bf16[16,1280]{1,0:T(8,128)(2,1)S(1)} %get-tuple-element.42), channel_id=1, source_target_pairs={{0,8},{4,12},{8,0},{12,4},{1,9},{5,13},{9,1},{13,5},{2,10},{6,14},... | collective-permute-start | bytes 122888 | tf_op jit(solution)/shard_map/ppermute | solution.py:488
  16.8 8.1 %collective-permute-start.2 = (bf16[16,1280]{1,0:T(8,128)(2,1)S(1)}, bf16[16,1280]{1,0:T(8,128)(2,1)S(1)}, u32[]{:S(2)}, u32[]{:S(2)}) collective-permute-start(bf16[16,1280]{1,0:T(8,128)(2,1)S(1)} %get-tuple-element.42), channel_id=1, source_target_pairs={{0,12},{4,0},{8,4},{12,8},{1,13},{5,1},{9,5},{13,9},{2,14},{6,2},{... | collective-permute-start | bytes 122888 | tf_op jit(solution)/shard_map/ppermute | solution.py:488
  20.1 1.1 copy-start
  21.2 3.6 %copy-start.2 = (f32[1,1280]{1,0:T(1,128)}, f32[1,1280]{1,0:T(1,128)S(1)}, u32[]{:S(2)}) copy-start(f32[1,1280]{1,0:T(1,128)S(1)} %reshape.33.gain_ref) | copy-start | bytes 15364
  21.2 1.1 copy-start.1
  25.6 23.5 %collective-permute-start = (bf16[256,1280]{1,0:T(8,128)(2,1)S(1)}, bf16[256,1280]{1,0:T(8,128)(2,1)S(1)}, u32[]{:S(2)}, u32[]{:S(2)}) collective-permute-start(bf16[256,1280]{1,0:T(8,128)(2,1)S(1)} %shard_map.85), channel_id=1, source_target_pairs={{0,2},{2,0},{1,3},{3,1},{4,6},{6,4},{5,7},{7,5},{8,10},{10,8},{9,1... | collective-permute-start | bytes 1966088 | tf_op jit(solution)/shard_map/ppermute | solution.py:470
  26.7 27.3 %all-to-all-start = ((bf16[16,160,128]{2,1,0:T(8,128)(2,1)}), bf16[16,160,128]{2,1,0:T(8,128)(2,1)S(1)}, u32[]{:S(2)}, u32[]{:S(2)}) async-start(bf16[16,160,128]{2,1,0:T(8,128)(2,1)} %shard_map.87), calls=%async_computation | async-start | bytes 1310720 | tf_op jit(solution)/shard_map/all_to_all | solution.py:495
  30.4 23.7 %copy-start.3 = (s32[1,4096]{1,0:T(1,128)S(1)}, s32[1,4096]{1,0:T(1,128)}, u32[]{:S(2)}) copy-start(s32[1,4096]{1,0:T(1,128)} %param.8) | copy-start | bytes 49156
  49.2 11.8 %copy-start.6 = (bf16[512,1280]{1,0:T(8,128)(2,1)}, bf16[512,1280]{1,0:T(8,128)(2,1)S(1)}, u32[]{:S(2)}) copy-start(bf16[512,1280]{1,0:T(8,128)(2,1)S(1)} %constant_dynamic-update-slice_fusion.half_ref) | copy-start | bytes 3932164
  49.2 16.8 %collective-permute-start.1 = (bf16[512,1280]{1,0:T(8,128)(2,1)S(1)}, bf16[512,1280]{1,0:T(8,128)(2,1)}, u32[]{:S(2)}, u32[]{:S(2)}) collective-permute-start(bf16[512,1280]{1,0:T(8,128)(2,1)S(1)} %constant_dynamic-update-slice_fusion.half_ref), channel_id=1, source_target_pairs={{0,1},{1,0},{2,3},{3,2},{4,5},{5,4},{6,7},{7,6},{8,9},{9,8},{10,11... | collective-permute-start | bytes 3932168 | tf_op jit(solution)/shard_map/ppermute | solution.py:470
  49.3 11.6 %copy-start.4 = (s32[2]{0:T(128)}, s32[2]{0:T(128)S(1)}, u32[]{:S(2)}) copy-start(s32[2]{0:T(128)S(1)} %pad_add_fusion.place_ref) | copy-start | bytes 28
  54.1 11.3 %copy-start.10 = (s32[1,4096]{1,0:T(1,128)S(1)}, s32[1,4096]{1,0:T(1,128)}, u32[]{:S(2)}) copy-start(s32[1,4096]{1,0:T(1,128)} %param.9) | copy-start | bytes 49156
  61.0 22.4 %all-to-all-start.1 = ((bf16[4,4,160,128]{3,2,1,0:T(8,128)(2,1)}), bf16[4,4,160,128]{3,2,1,0:T(8,128)(2,1)S(1)}, u32[]{:S(2)}, u32[]{:S(2)}) async-start(bf16[4,4,160,128]{3,2,1,0:T(8,128)(2,1)} %shard_map.88), calls=%async_computation.1 | async-start | bytes 1310720 | tf_op jit(solution)/shard_map/all_to_all | solution.py:497
  83.3 0.8 copy-start.8
  94.9 43.7 %all-to-all-start.2 = ((bf16[16,4,80,256]{3,2,1,0:T(8,128)(2,1)}), bf16[16,4,80,256]{3,2,1,0:T(8,128)(2,1)S(1)}, u32[]{:S(2)}, u32[]{:S(2)}) async-start(bf16[16,4,80,256]{3,2,1,0:T(8,128)(2,1)} %get-tuple-element.36), calls=%async_computation.2 | async-start | bytes 5242880 | tf_op jit(solution)/shard_map/all_to_all | solution.py:505
  106.7 7.4 %collective-permute-start.5 = (bf16[512,1280]{1,0:T(8,128)(2,1)}, bf16[512,1280]{1,0:T(8,128)(2,1)S(1)}, u32[]{:S(2)}, u32[]{:S(2)}) collective-permute-start(bf16[512,1280]{1,0:T(8,128)(2,1)} %get-tuple-element.35), channel_id=1, source_target_pairs={{0,1},{1,0},{2,3},{3,2},{4,5},{5,4},{6,7},{7,6},{8,9},{9,8},{10,11... | collective-permute-start | bytes 3932168 | tf_op jit(solution)/shard_map/ppermute | solution.py:470
  114.1 2.0 %copy-start.7 = (bf16[512,1280]{1,0:T(8,128)(2,1)}, bf16[512,1280]{1,0:T(8,128)(2,1)S(1)}, u32[]{:S(2)}) copy-start(bf16[512,1280]{1,0:T(8,128)(2,1)S(1)} %collective-permute-done.5.core_ref) | copy-start | bytes 3932164
  114.1 7.1 %copy-start.11 = (f32[1,1280]{1,0:T(1,128)S(1)}, f32[1,1280]{1,0:T(1,128)}, u32[]{:S(2)}) copy-start(f32[1,1280]{1,0:T(1,128)} %get-tuple-element.37) | copy-start | bytes 15364
  114.1 7.1 %copy-start.12 = (f32[1,1280]{1,0:T(1,128)S(1)}, f32[1,1280]{1,0:T(1,128)}, u32[]{:S(2)}) copy-start(f32[1,1280]{1,0:T(1,128)} %get-tuple-element.38) | copy-start | bytes 15364
  116.1 23.0 %collective-permute-start.8 = (bf16[256,1280]{1,0:T(8,128)(2,1)S(1)}, bf16[256,1280]{1,0:T(8,128)(2,1)}, u32[]{:S(2)}, u32[]{:S(2)}) collective-permute-start(bf16[256,1280]{1,0:T(8,128)(2,1)S(1)} %add_convert_fusion), channel_id=1, source_target_pairs={{0,2},{2,0},{1,3},{3,1},{4,6},{6,4},{5,7},{7,5},{8,10},{10,8},{9,1... | collective-permute-start | bytes 1966088 | tf_op jit(solution)/shard_map/ppermute | solution.py:470
  121.2 1.3 collective-permute-start.6
  122.5 14.3 %collective-permute-start.7 = (f32[1,1280]{1,0:T(1,128)S(1)}, f32[1,1280]{1,0:T(1,128)S(1)}, u32[]{:S(2)}, u32[]{:S(2)}) collective-permute-start(f32[1,1280]{1,0:T(1,128)S(1)} %add.39), channel_id=1, source_target_pairs={{0,2},{2,0},{1,3},{3,1},{4,6},{6,4},{5,7},{7,5},{8,10},{10,8},{9,1... | collective-permute-start | bytes 15368 | tf_op jit(solution)/shard_map/ppermute | solution.py:470
  156.2 19.2 %all-to-all-start.4 = ((bf16[16,80,256]{2,1,0:T(8,128)(2,1)}), bf16[16,80,256]{2,1,0:T(8,128)(2,1)S(1)}, u32[]{:S(2)}, u32[]{:S(2)}) async-start(bf16[16,80,256]{2,1,0:T(8,128)(2,1)} %shard_map.94), calls=%async_computation.4 | async-start | bytes 1310720 | tf_op jit(solution)/shard_map/all_to_all | solution.py:521
  164.6 11.0 %copy-start.9 = (f32[1280]{0:T(1024)S(1)}, f32[1280]{0:T(1024)}, u32[]{:S(2)}) copy-start(f32[1280]{0:T(1024)} %param.11) | copy-start | bytes 15364
  175.4 0.9 copy-start.5
Sparse Core Ops, SparseCore 0:
  25.8 47.7 all-gather.1
